TPU v7x, 32 devices: a whole 2x2x4 slice. The times are simulated.
32 devices in a mesh: dp: 8 (over y, x, core), mp: 4 (over z).
Axes of the slice: x: 2, y: 2, z: 4, core: 2. Of those that a mesh axis runs over, the one named last changes fastest.
Arguments:
- block_input: bfloat16 [4096, 2048], P('dp'), may hold values from -6 to 6
- cotangent: bfloat16 [4096, 2048], P('dp'), may hold values from -6 to 6
- doc_lengths: int32 [1, 8], replicated, may hold values from 1 to 2048, 4096 in all within a row
- span_order: int32 [32], replicated, may hold values from 0 to 31, as said below
- weights: float32 [2048, 24576], P('dp', 'mp'), may hold values from -0.125 to 0.125
- momentum: float32 [2048, 24576], P('dp', 'mp'), may hold values from -0.001953125 to 0.001953125
- ema_weights: float32 [2048, 24576], P('dp', 'mp'), may hold values from -0.125 to 0.125
- gains: float32 [4352], replicated, may hold values from 0.7 to 7.2, as said below
- gain_momentum: float32 [4352], replicated, may hold values from -0.0078125 to 0.0078125
- gain_ema: float32 [4352], replicated, may hold values from 0.5 to 1.5
Outputs:
- block_output: bfloat16 [4096, 2048], P('dp')
- grad_input: float32 [4096, 2048], P('dp')
- grad_norm: float32 [], replicated
- new_weights: float32 [2048, 24576], P('dp', 'mp')
- new_momentum: float32 [2048, 24576], P('dp', 'mp')
- new_ema: float32 [2048, 24576], P('dp', 'mp')
- new_gains: float32 [4352], replicated
- new_gain_momentum: float32 [4352], replicated
- new_gain_ema: float32 [4352], replicated
Inputs may be any that keep to these rules, and one draw needn't show every extreme that they name: `doc_lengths`: each row sums to 4096; the longest document of each row has 2048 tokens. A permutation of the 32 spans; storage span i holds span span_order[i] of the unpermuted order. Positive gains.
All inputs are finite; a program needn't handle non-finite values.
Results may differ from a plain program's by a relative error of at most 0.035.
Values may be sent and summed in bfloat16 or wider, within the bound.
No kernel may reach another device: no remote copies, remote signals or barrier semaphores. Data moves between devices by JAX's collectives and lax.ppermute only.
A program may use at most 256 MiB of HBM per device.

v0:
```python
import jax
import jax.numpy as jnp
from jax import lax
from jax.sharding import PartitionSpec as P

HEADS = 16
KV = 8
HD = 128
FF = 6144
LENGTH = 4096
SPAN = 128


eps_norm = 1e-06
rope_base = 1000000.0
learn_rate = 100.0
gain_rate = 4000.0
momentum_decay = 0.5
average_decay = 0.5


def rms_scale(values, weight_gain):
    return (
        values
        * lax.rsqrt(jnp.mean(values * values, axis=-1, keepdims=True) + eps_norm)
        * weight_gain
    )


def unit_rms(values):
    return values * lax.rsqrt(jnp.mean(values * values, axis=-1, keepdims=True) + eps_norm)


def norm_back(values, weight_gain, gradient):

    def forward(inner):
        return rms_scale(inner, weight_gain)

    unused, pullback = jax.vjp(forward, values)
    return pullback(gradient)[0]


def rotate(values, angles):
    half_size = values.shape[-1] // 2
    cosine = jnp.cos(angles)
    sine = jnp.sin(angles)
    first_half = values[..., :half_size]
    second_half = values[..., half_size:]
    return jnp.concatenate(
        [first_half * cosine - second_half * sine, second_half * cosine + first_half * sine],
        axis=-1,
    )


def swiglu(gate_in, up_in):
    return jax.nn.silu(gate_in) * up_in


def token_places(first_row, row_count, span_order, doc_lengths, seq_len):
    row_ids = first_row + jnp.arange(row_count, dtype=jnp.int32)
    span_index = row_ids // SPAN
    span_match = span_index[:, None] == jnp.arange(span_order.shape[0], dtype=jnp.int32)[None, :]
    source = jnp.sum(jnp.where(span_match, span_order[None, :], 0), axis=1)
    home_index = source * SPAN + row_ids % SPAN
    sequence = home_index // seq_len
    position = home_index % seq_len
    starts = jnp.cumsum(doc_lengths, axis=1) - doc_lengths
    seq_match = sequence[:, None] == jnp.arange(doc_lengths.shape[0], dtype=jnp.int32)[None, :]
    row_starts = jnp.sum(jnp.where(seq_match[:, :, None], starts[None, :, :], 0), axis=1)
    started = position[:, None] >= row_starts
    doc_index = jnp.sum(started.astype(jnp.int32), axis=1) + sequence * doc_lengths.shape[1]
    doc_start = jnp.max(jnp.where(started, row_starts, 0), axis=1)
    return (doc_index, home_index, position - doc_start)


def update(value, state, average, gradient, factor, step_rate):
    clipped = gradient * factor
    state_new = momentum_decay * state + clipped
    value_new = value - step_rate * (clipped + momentum_decay * state_new)
    average_new = average_decay * average + (1.0 - average_decay) * value_new
    return (value_new, state_new, average_new)


def per_device(
    block_input,
    cotangent,
    doc_lengths,
    span_order,
    weights,
    momentum,
    ema_weights,
    gains,
    gain_momentum,
    gain_ema,
):
    tok_count, model_width = block_input.shape
    data_count = lax.axis_size("dp")
    model_count = lax.axis_size("mp")
    token_total = tok_count * data_count
    span_total = token_total // SPAN
    seq_len = min(LENGTH, token_total)
    query_width = HEADS * HD // model_count
    kv_width = KV * HD // model_count
    ff_width = FF // model_count
    kv_heads = kv_width // HD
    group_size = HEADS // KV
    score_scale = HD ** (-0.5)
    qkv_cols = query_width + 2 * kv_width
    out_end = qkv_cols + query_width
    mlp_end = out_end + 2 * ff_width
    key_block = min(512, token_total)
    block_count = token_total // key_block
    contract_last = (((1,), (1,)), ((), ()))
    contract_rows = (((0,), (0,)), ((), ()))
    gain_attn = gains[:model_width]
    gain_mlp = gains[model_width : 2 * model_width]
    gain_query = gains[2 * model_width : 2 * model_width + HD]
    gain_key = gains[2 * model_width + HD :]
    span_ids = jnp.arange(span_total, dtype=jnp.int32)
    span_match = span_order[None, :] == span_ids[:, None]
    span_inverse = jnp.sum(jnp.where(span_match, span_ids[None, :], 0), axis=1)

    def to_unpermuted(array):
        return array.reshape((span_total, SPAN) + array.shape[1:])[span_inverse].reshape(
            array.shape
        )

    def to_storage_rows(array):
        return array.reshape((span_total, SPAN) + array.shape[1:])[span_order].reshape(array.shape)

    doc_query, home_query, inside_query = token_places(
        lax.axis_index("dp") * tok_count, tok_count, span_order, doc_lengths, seq_len
    )
    doc_stored, home_stored, inside_stored = token_places(
        0, token_total, span_order, doc_lengths, seq_len
    )
    doc_keys = to_unpermuted(doc_stored)
    home_keys = to_unpermuted(home_stored)
    low_weights = weights.astype(jnp.bfloat16)
    full_weights = lax.all_gather(low_weights, "dp", axis=0, tiled=True)
    inputs = block_input.astype(jnp.float32)
    normed_low = rms_scale(inputs, gain_attn).astype(jnp.bfloat16)
    projected = jnp.dot(normed_low, full_weights[:, :qkv_cols], preferred_element_type=jnp.float32)
    query_lin = projected[:, :query_width]
    key_lin = projected[:, query_width : query_width + kv_width]
    value_low = projected[:, query_width + kv_width :].astype(jnp.bfloat16)
    freqs = rope_base ** (-(2.0 * jnp.arange(HD // 2, dtype=jnp.float32)) / HD)
    angles = (inside_query.astype(jnp.float32)[:, None] * freqs[None, :])[:, None, :]

    def head_prepare(query_part, key_part, query_gain, key_gain):
        queries = rotate(rms_scale(query_part.reshape(tok_count, -1, HD), query_gain), angles)
        keys_rot = rotate(rms_scale(key_part.reshape(tok_count, -1, HD), key_gain), angles)
        return (queries, keys_rot)

    (queries, keys_rot), head_back = jax.vjp(head_prepare, query_lin, key_lin, gain_query, gain_key)
    query_group = queries.astype(jnp.bfloat16).reshape(tok_count, kv_heads, group_size, HD)
    key_low = keys_rot.astype(jnp.bfloat16).reshape(tok_count, kv_width)

    def block_mask(doc_piece, home_piece):
        return (doc_query[:, None] == doc_piece[None, :]) & (
            home_piece[None, :] <= home_query[:, None]
        )

    def block_scores(key_piece, allowed):
        scores = (
            jnp.einsum("tkgd,skd->tkgs", query_group, key_piece, preferred_element_type=jnp.float32)
            * score_scale
        )
        return (scores, allowed[:, None, None, :])

    def key_blocks(keys_all, values_all):
        keys_sorted = to_unpermuted(keys_all)
        values_sorted = to_unpermuted(values_all)
        return (
            keys_sorted.reshape(block_count, key_block, kv_heads, HD),
            values_sorted.reshape(block_count, key_block, kv_heads, HD),
            doc_keys.reshape(block_count, key_block),
            home_keys.reshape(block_count, key_block),
        )

    keys_all, values_all = (
        lax.all_gather(key_low, "dp", axis=0, tiled=True),
        lax.all_gather(value_low, "dp", axis=0, tiled=True),
    )
    blocks_forward = key_blocks(keys_all, values_all)

    def softmax_totals(carry, piece):
        allowed_rows = block_mask(piece[2], piece[3])

        def softmax_active(state):
            running_max, running_sum = state
            scores, allowed = block_scores(piece[0], allowed_rows)
            masked = jnp.where(allowed, scores, -1e30)
            new_max = jnp.maximum(running_max, jnp.max(masked, axis=-1))
            growth = jnp.sum(jnp.where(allowed, jnp.exp(masked - new_max[..., None]), 0.0), axis=-1)
            return (new_max, running_sum * jnp.exp(running_max - new_max) + growth)

        def softmax_skipped(state):
            return state

        return (lax.cond(jnp.any(allowed_rows), softmax_active, softmax_skipped, carry), None)

    start_shape = (tok_count, kv_heads, group_size)
    (row_max, row_sum), unused = lax.scan(
        softmax_totals,
        (jnp.full(start_shape, -1e30, jnp.float32), jnp.zeros(start_shape, jnp.float32)),
        blocks_forward,
    )
    log_total = row_max + jnp.log(row_sum)

    def weighted_values(running, piece):
        allowed_rows = block_mask(piece[2], piece[3])

        def weighted_active(state):
            scores, allowed = block_scores(piece[0], allowed_rows)
            probs_low = jnp.where(allowed, jnp.exp(scores - log_total[..., None]), 0.0).astype(
                jnp.bfloat16
            )
            return state + jnp.einsum(
                "tkgs,skd->tkgd", probs_low, piece[1], preferred_element_type=jnp.float32
            )

        def weighted_skipped(state):
            return state

        return (lax.cond(jnp.any(allowed_rows), weighted_active, weighted_skipped, running), None)

    attended, unused = lax.scan(
        weighted_values,
        jnp.zeros((tok_count, kv_heads, group_size, HD), jnp.float32),
        blocks_forward,
    )
    attended_low = attended.reshape(tok_count, query_width).astype(jnp.bfloat16)
    attn_part = lax.dot_general(
        attended_low,
        full_weights[:, qkv_cols:out_end],
        contract_last,
        preferred_element_type=jnp.float32,
    )
    residual = inputs + lax.psum(attn_part.astype(jnp.bfloat16), "mp").astype(jnp.float32)
    mlp_low = rms_scale(residual, gain_mlp).astype(jnp.bfloat16)
    gate_up = jnp.dot(mlp_low, full_weights[:, out_end:mlp_end], preferred_element_type=jnp.float32)
    gate_value = gate_up[:, :ff_width]
    up_value = gate_up[:, ff_width:]
    hidden_low = swiglu(gate_value, up_value).astype(jnp.bfloat16)
    mlp_part = lax.dot_general(
        hidden_low, full_weights[:, mlp_end:], contract_last, preferred_element_type=jnp.float32
    )
    block_output = residual + lax.psum(mlp_part.astype(jnp.bfloat16), "mp").astype(jnp.float32)
    back_weights = lax.all_gather(low_weights, "dp", axis=0, tiled=True)
    keys_back, values_back = (
        lax.all_gather(key_low, "dp", axis=0, tiled=True),
        lax.all_gather(value_low, "dp", axis=0, tiled=True),
    )
    blocks_back = key_blocks(keys_back, values_back)
    grad_output = cotangent.astype(jnp.float32)
    grad_hidden = jnp.dot(cotangent, back_weights[:, mlp_end:], preferred_element_type=jnp.float32)
    unused, swiglu_back = jax.vjp(swiglu, gate_value, up_value)
    grad_gate, grad_up = swiglu_back(grad_hidden)
    grad_gate_up = jnp.concatenate([grad_gate, grad_up], axis=1).astype(jnp.bfloat16)
    grad_mlp_part = lax.dot_general(
        grad_gate_up,
        back_weights[:, out_end:mlp_end],
        contract_last,
        preferred_element_type=jnp.float32,
    )
    mlp_gain_grad = jnp.sum(grad_mlp_part * unit_rms(residual), axis=0)
    grad_mlp_full = lax.psum(grad_mlp_part.astype(jnp.bfloat16), "mp").astype(jnp.float32)
    grad_residual = grad_output + norm_back(residual, gain_mlp, grad_mlp_full)
    grad_res_low = grad_residual.astype(jnp.bfloat16)
    grad_attended = jnp.dot(
        grad_res_low, back_weights[:, qkv_cols:out_end], preferred_element_type=jnp.float32
    )
    grad_att_low = grad_attended.astype(jnp.bfloat16).reshape(tok_count, kv_heads, group_size, HD)
    row_delta = jnp.sum(grad_att_low.astype(jnp.float32) * attended, axis=-1)
    block_zeros = jnp.zeros((key_block, kv_heads, HD), jnp.float32)

    def score_grads(grad_query, piece):
        allowed_rows = block_mask(piece[2], piece[3])

        def score_active(state):
            scores, allowed = block_scores(piece[0], allowed_rows)
            probs = jnp.where(allowed, jnp.exp(scores - log_total[..., None]), 0.0)
            grad_value = jnp.einsum(
                "tkgs,tkgd->skd",
                probs.astype(jnp.bfloat16),
                grad_att_low,
                preferred_element_type=jnp.float32,
            )
            grad_probs = jnp.einsum(
                "tkgd,skd->tkgs", grad_att_low, piece[1], preferred_element_type=jnp.float32
            )
            grad_scores = (probs * (grad_probs - row_delta[..., None])).astype(jnp.bfloat16)
            new_state = (
                state
                + jnp.einsum(
                    "tkgs,skd->tkgd", grad_scores, piece[0], preferred_element_type=jnp.float32
                )
                * score_scale
            )
            grad_key = (
                jnp.einsum(
                    "tkgs,tkgd->skd", grad_scores, query_group, preferred_element_type=jnp.float32
                )
                * score_scale
            )
            return (new_state, grad_key, grad_value)

        def score_skipped(state):
            return (state, block_zeros, block_zeros)

        new_state, grad_key, grad_value = lax.cond(
            jnp.any(allowed_rows), score_active, score_skipped, grad_query
        )
        return (new_state, (grad_key, grad_value))

    grad_queries, (grad_key_blocks, grad_value_blocks) = lax.scan(
        score_grads, jnp.zeros((tok_count, kv_heads, group_size, HD), jnp.float32), blocks_back
    )
    grad_key_stored = to_storage_rows(grad_key_blocks.reshape(token_total, kv_width))
    grad_value_stored = to_storage_rows(grad_value_blocks.reshape(token_total, kv_width))
    grad_keys_mine, grad_values_mine = (
        lax.psum_scatter(
            grad_key_stored.astype(jnp.bfloat16), "dp", scatter_dimension=0, tiled=True
        ).astype(jnp.float32),
        lax.psum_scatter(
            grad_value_stored.astype(jnp.bfloat16), "dp", scatter_dimension=0, tiled=True
        ).astype(jnp.float32),
    )
    grad_query_lin, grad_key_lin, grad_gain_query, grad_gain_key = head_back(
        (grad_queries.reshape(tok_count, -1, HD), grad_keys_mine.reshape(tok_count, kv_heads, HD))
    )
    grad_qkv_low = jnp.concatenate([grad_query_lin, grad_key_lin, grad_values_mine], axis=1).astype(
        jnp.bfloat16
    )
    grad_norm_part = lax.dot_general(
        grad_qkv_low, back_weights[:, :qkv_cols], contract_last, preferred_element_type=jnp.float32
    )
    attn_gain_grad = jnp.sum(grad_norm_part * unit_rms(inputs), axis=0)
    grad_norm_full = lax.psum(grad_norm_part.astype(jnp.bfloat16), "mp").astype(jnp.float32)
    grad_input = grad_residual + norm_back(inputs, gain_attn, grad_norm_full)
    weight_grads = lax.psum_scatter(
        jnp.concatenate(
            [
                lax.dot_general(
                    normed_low, grad_qkv_low, contract_rows, preferred_element_type=jnp.float32
                ),
                lax.dot_general(
                    grad_res_low, attended_low, contract_rows, preferred_element_type=jnp.float32
                ),
                lax.dot_general(
                    mlp_low, grad_gate_up, contract_rows, preferred_element_type=jnp.float32
                ),
                lax.dot_general(
                    cotangent, hidden_low, contract_rows, preferred_element_type=jnp.float32
                ),
            ],
            axis=1,
        ).astype(jnp.bfloat16),
        "dp",
        scatter_dimension=0,
        tiled=True,
    ).astype(jnp.float32)
    gain_local = jnp.concatenate([attn_gain_grad, mlp_gain_grad, grad_gain_query, grad_gain_key])
    weight_square = jnp.sum(weight_grads * weight_grads)
    gain_grads, square_total = lax.psum((gain_local, weight_square), ("dp", "mp"))
    grad_norm = jnp.sqrt(square_total + jnp.sum(gain_grads * gain_grads))
    factor = 1.0 / jnp.maximum(grad_norm, 1.0)
    new_weights, new_momentum, new_ema = update(
        weights, momentum, ema_weights, weight_grads, factor, learn_rate
    )
    new_gains, new_gain_momentum, new_gain_ema = update(
        gains, gain_momentum, gain_ema, gain_grads, factor, gain_rate
    )
    return (
        block_output.astype(jnp.bfloat16),
        grad_input,
        grad_norm,
        new_weights,
        new_momentum,
        new_ema,
        new_gains,
        new_gain_momentum,
        new_gain_ema,
    )


def solution(mesh):
    return jax.shard_map(
        per_device,
        mesh=mesh,
        in_specs=(
            P("dp", None),
            P("dp", None),
            P(),
            P(),
            P("dp", "mp"),
            P("dp", "mp"),
            P("dp", "mp"),
            P(),
            P(),
            P(),
        ),
        out_specs=(
            P("dp", None),
            P("dp", None),
            P(),
            P("dp", "mp"),
            P("dp", "mp"),
            P("dp", "mp"),
            P(),
            P(),
            P(),
        ),
        check_vma=False,
    )
```

profile of v0, /device:TPU:0, one launch (start us, length us, event | category | flops | bytes accessed | tf_op | source)
XLA Modules:
  0.0 1079.3 jit_solution(16014053604671503666)
XLA Ops:
  7.3 5.0 convert_element_type.129
  14.9 125.6 %all-gather.4.cloned.1.call-done = bf16[2048,6144]{1,0:T(8,128)(2,1)} async-done(((bf16[256,6144]{1,0:T(8,128)(2,1)}), bf16[2048,6144]{1,0:T(8,128)(2,1)}) %all-gather.4.cloned.1.call-update) | async-done | bytes 25165840 | tf_op jit(solution)/shard_map/all_gather | solution.py:140
  140.5 4.6 fusion.72
  167.4 13.1 %all-gather.6.cloned.1.call-done = bf16[4096,256]{1,0:T(8,128)(2,1)} async-done(((bf16[512,256]{1,0:T(8,128)(2,1)}), bf16[4096,256]{1,0:T(8,128)(2,1)}) %all-gather.6.cloned.1.call-update) | async-done | bytes 2097168 | tf_op jit(solution)/shard_map/all_gather | solution.py:182
  180.5 3.6 gather_fusion.2
  184.1 4.0 reshape.499
  188.1 3.4 copy.136
  191.5 33.7 %while.42 = (s32[]{:T(128)}, f32[512,2,2]{0,2,1:T(2,128)S(1)}, f32[512,2,2]{0,2,1:T(2,128)S(1)}, s32[512]{0:T(512)S(1)}, s32[8,512]{1,0:T(8,128)S(1)}, /*index=5...) while((s32[]{:T(128)}, f32[512,2,2]{0,2,1:T(2,128)S(1)}, ...), condition=%wide.region_16.17_spmd, body=%wide.region_10.16_spmd.sunk | while | flops 277876736 | bytes 10085071 | solution.py:204
  225.2 3.6 gather_fusion.3
  228.8 4.0 reshape.500
  237.2 42.0 %while.43 = (s32[]{:T(128)}, f32[512,2,2,128]{3,0,2,1:T(8,128)}, s32[512]{0:T(512)S(1)}, s32[8,512]{1,0:T(8,128)S(1)}, s32[8,512]{1,0:T(8,128)S(1)}, /*index=5*/...) while((s32[]{:T(128)}, f32[512,2,2,128]{3,0,2,1:T(8,128)}, ...), condition=%wide.region_21.22_spmd, body=%wide.region_17.21_spmd.sunk | while | flops 542375936 | bytes 3695807 | solution.py:228
  238.8 4.2 conditional.7
  238.8 4.1 fusion.10
  244.6 4.2 conditional.7
  244.6 4.1 fusion.10
  250.4 4.2 conditional.7
  250.4 4.1 fusion.10
  256.1 4.2 conditional.7
  256.1 4.1 fusion.10
  261.9 4.2 conditional.7
  261.9 4.1 fusion.10
  269.3 4.2 conditional.7
  269.3 4.1 fusion.10
  275.1 4.2 conditional.7
  275.1 4.1 fusion.10
  280.7 4.4 convolution_convert_fusion.4
  285.7 86.0 %all-reduce.10.cloned.1.call-done = bf16[512,2048]{1,0:T(8,128)(2,1)} async-done(((bf16[512,2048]{1,0:T(8,128)(2,1)}), bf16[512,2048]{1,0:T(8,128)(2,1)}) %all-reduce.10.cloned.1.call-update) | async-done | bytes 2097168 | tf_op jit(solution)/shard_map/psum | solution.py:240
  374.2 9.6 fusion.50
  383.9 8.6 fusion.76
  392.5 12.8 %fusion.136 = (bf16[512,2048]{1,0:T(8,128)(2,1)}, f32[512,2048]{1,0:T(8,128)}) fusion(bf16[2048,6144]{1,0:T(8,128)(2,1)} %all-gather.4.cloned.1.call-done, bf16[512,1536]{1,0:T(8,128)(2,1)S(1)} %get-tuple-element.664, bf16[512,1536]{1,0:T(8,128)(2,1)S(1)} %get-tuple-element.663), kind=kOutput, calls=%fused_computation.267 | convolution fusion | flops 6449790976 | bytes 22020096 | tf_op jit(solution)/shard_map/dot_general | solution.py:261
  405.6 85.4 %all-reduce.12.cloned.1.call-done = bf16[512,2048]{1,0:T(8,128)(2,1)} async-done(((bf16[512,2048]{1,0:T(8,128)(2,1)}), bf16[512,2048]{1,0:T(8,128)(2,1)}) %all-reduce.12.cloned.1.call-update) | async-done | bytes 2097168 | tf_op jit(solution)/shard_map/psum | solution.py:268
  491.0 5.1 multiply_reduce_fusion
  496.3 4.8 fusion.84
  504.1 80.4 %while.44 = (s32[]{:T(128)}, f32[512,2,2,128]{3,0,2,1:T(8,128)S(1)}, bf16[8,512,2,128]{3,2,1,0:T(2,128)(2,1)}, bf16[8,512,2,128]{3,2,1,0:T(2,128)(2,1)}, s32[512...) while((s32[]{:T(128)}, ...), condition=%wide.region_32.33_spmd, body=%wide.region_28.32_spmd.sunk | while | flops 1354498048 | bytes 26257668 | solution.py:317
  505.9 8.0 conditional.8
  516.9 8.0 conditional.8
  527.9 8.0 conditional.8
  539.0 8.0 conditional.8
  550.0 8.0 conditional.8
  564.2 8.0 conditional.8
  575.2 8.0 conditional.8
  584.6 4.4 reshape.501
  588.9 3.6 gather_fusion.4
  592.6 4.4 reshape.502
  597.0 3.6 gather_fusion.5
  600.9 8.3 fusion.78
  616.7 3.5 fusion.87
  621.1 11.4 %reduce-scatter.4.cloned.1.call-done = bf16[512,256]{1,0:T(8,128)(2,1)} async-done(((bf16[4096,256]{1,0:T(8,128)(2,1)}), bf16[512,256]{1,0:T(8,128)(2,1)}) %reduce-scatter.4.cloned.1.call-update) | async-done | bytes 262160 | tf_op jit(solution)/shard_map/reduce_scatter | solution.py:323
  639.9 38.1 %reduce-scatter.6.cloned.1.call-done = bf16[512,256]{1,0:T(8,128)(2,1)} async-done(((bf16[4096,256]{1,0:T(8,128)(2,1)}), bf16[512,256]{1,0:T(8,128)(2,1)}) %reduce-scatter.6.cloned.1.call-update) | async-done | bytes 262160 | tf_op jit(solution)/shard_map/reduce_scatter | solution.py:326
  679.7 7.6 fusion.137
  688.9 12.4 %convolution_convert_fusion = bf16[2048,3072]{1,0:T(8,128)(2,1)} fusion(bf16[512,1536]{1,0:T(8,128)(2,1)} %copy-done.50, bf16[512,1536]{1,0:T(8,128)(2,1)} %copy-done.49, bf16[512,2048]{1,0:T(8,128)(2,1)} %all-reduce.10.cloned.1.call-done, bf16[512,2048]{1,0:T(8,128)(2,1)S(1)} %copy-done.1, f32[2048]{0:T(1024)S(1)} %get-tuple-element.678, f32[512]{0:T(512)S(1)} %fusion.120), kind=kOutput, calls=%fused_computation.68 | convolution fusion | flops 6461325312 | bytes 19933184 | tf_op jit(solution)/shard_map/dot_general | solution.py:351
  701.3 5.5 fusion.54
  706.7 3.6 convolution_convert_fusion.3
  710.4 4.0 copy.155
  714.4 4.5 convolution_convert_fusion.2
  718.9 6.4 copy.154
  725.3 17.8 %pad_maximum_fusion = bf16[2048,6144]{1,0:T(8,128)(2,1)} fusion(bf16[2048,1536]{1,0:T(8,128)(2,1)} %fusion.54, bf16[2048,3072]{1,0:T(8,128)(2,1)} %convolution_convert_fusion, bf16[2048,512]{1,0:T(8,128)(2,1)} %copy.155, bf16[2048,1024]{1,0:T(8,128)(2,1)} %copy.154), kind=kLoop, calls=%fused_computation.67 | loop fusion | flops 100663296 | bytes 50331648 | tf_op jit(solution)/shard_map/concatenate | solution.py:343
  743.2 99.7 %all-reduce.14.cloned.1.call-done = (bf16[512,2048]{1,0:T(8,128)(2,1)}, bf16[512,2048]{1,0:T(8,128)(2,1)}) async-done(((bf16[512,2048]{1,0:T(8,128)(2,1)}, bf16[512,2048]{1,0:T(8,128)(2,1)}), (bf16[512,2048]{1,0:T(8,128)(2,1)}, bf16[512,2048]{1,0:T(8,128)(2,1)})) %all-reduce.14.cloned.1.call-update) | async-done | bytes 4194320 | tf_op jit(solution)/shard_map/psum | solution.py:249
  842.8 4.3 fusion.65
  847.2 155.7 %reduce-scatter.8.cloned.1.call-done = bf16[256,6144]{1,0:T(8,128)(2,1)} async-done(((bf16[2048,6144]{1,0:T(8,128)(2,1)}), bf16[256,6144]{1,0:T(8,128)(2,1)}) %reduce-scatter.8.cloned.1.call-update) | async-done | bytes 3145744 | tf_op jit(solution)/shard_map/reduce_scatter | solution.py:342
  1002.8 4.3 fusion.57
  1007.1 7.7 fusion.67
  1014.8 39.8 %all-reduce.4 = (f32[]{:T(128)}, f32[4352]{0:T(1024)S(1)}) all-reduce(f32[]{:T(128)} %fusion.57, f32[4352]{0:T(1024)S(1)} %pad_maximum_fusion.6), channel_id=1, replica_groups=mesh['dp'=8,'mp'=4] {'dp','mp'}, use_global_device_ids=true, to_apply=%region_41.42 | all-reduce | flops 4353 | bytes 34824 | tf_op jit(solution)/shard_map/psum | solution.py:366
  1057.2 14.3 %add_multiply_fusion = (f32[256,6144]{1,0:T(8,128)}, f32[256,6144]{1,0:T(8,128)}, f32[256,6144]{1,0:T(8,128)}) fusion(f32[256,6144]{1,0:T(8,128)} %param.28, f32[256,6144]{1,0:T(8,128)} %param.26, f32[]{:T(128)S(6)} %div.148, bf16[256,6144]{1,0:T(8,128)(2,1)} %reduce-scatter.8.cloned.1.call-done, f32[256,6144]{1,0:T(8,128)} %param.27), kind=kLoop, calls=%fused_computation.87 | loop fusion | flops 15728640 | bytes 40894468 | tf_op jit(solution)/shard_map/add | solution.py:80
  (352 shorter events, 188.3 us)
Async XLA Ops:
  7.2 5.2 copy-start.47
  7.2 5.4 copy-start.46
  7.2 5.6 copy-start
  7.2 133.3 %all-gather.4.cloned.1.call-start = ((), (), s32[]{:S(2)}) async-start(), calls=%async_computation.3 | async-start | bytes 28311552 | tf_op jit(solution)/shard_map/all_gather | solution.py:140
  12.3 1.1 copy-start.32
  12.3 168.2 %all-gather.6.cloned.1.call-start = ((), (), s32[]{:S(2)}) async-start(), calls=%async_computation.4 | async-start | bytes 2359296 | tf_op jit(solution)/shard_map/all_gather | solution.py:182
  13.3 0.6 copy-start.38
  13.3 131.7 %copy-start.40 = (f32[512]{0:T(512)}, f32[512]{0:T(512)S(1)}, u32[]{:S(2)}) copy-start(f32[512]{0:T(512)S(1)} %fusion.119) | copy-start | bytes 6148
  13.4 136.1 %copy-start.44 = (f32[128]{0:T(128)}, f32[128]{0:T(128)S(1)}, u32[]{:S(2)}) copy-start(f32[128]{0:T(128)S(1)} %get-tuple-element.681) | copy-start | bytes 1540
  13.4 150.1 %copy-start.42 = (f32[128]{0:T(128)}, f32[128]{0:T(128)S(1)}, u32[]{:S(2)}) copy-start(f32[128]{0:T(128)S(1)} %get-tuple-element.680) | copy-start | bytes 1540
  13.9 131.1 %copy-start.28 = (f32[2048]{0:T(1024)}, f32[2048]{0:T(1024)S(1)}, u32[]{:S(2)}) copy-start(f32[2048]{0:T(1024)S(1)} %get-tuple-element.679) | copy-start | bytes 24580
  14.9 135.3 %copy-start.15 = (f32[512,64]{1,0:T(8,128)}, f32[512,64]{1,0:T(8,128)S(1)}, u32[]{:S(2)}) copy-start(f32[512,64]{1,0:T(8,128)S(1)} %get-tuple-element.685) | copy-start | bytes 393220
  14.9 150.2 %copy-start.13 = (f32[512,64]{1,0:T(8,128)}, f32[512,64]{1,0:T(8,128)S(1)}, u32[]{:S(2)}) copy-start(f32[512,64]{1,0:T(8,128)S(1)} %get-tuple-element.684) | copy-start | bytes 393220
  145.1 1.3 copy-start.24
  148.5 8.0 copy-start.8
  149.3 3.6 copy-start.34
  149.4 8.8 copy-start.18
  152.5 72.7 %all-gather.8.cloned.1.call-start = ((), (), s32[]{:S(2)}) async-start(), calls=%async_computation.5 | async-start | bytes 2359296 | tf_op jit(solution)/shard_map/all_gather | solution.py:183
  159.9 7.2 copy-start.2
  162.3 4.9 copy-start.30
  162.3 209.4 %all-reduce.10.cloned.1.call-start = ((), (), s32[]{:S(2)}) async-start(), calls=%async_computation.6 | async-start | bytes 4194304 | tf_op jit(solution)/shard_map/psum | solution.py:240
  280.7 4.4 copy-start.25
  285.1 205.9 %all-reduce.12.cloned.1.call-start = ((), (), s32[]{:S(2)}) async-start(), calls=%async_computation.7 | async-start | bytes 4194304 | tf_op jit(solution)/shard_map/psum | solution.py:268
  371.7 2.5 copy-start.4
  374.2 9.7 copy-start.21
  392.5 12.8 %copy-start.49 = (bf16[512,1536]{1,0:T(8,128)(2,1)}, bf16[512,1536]{1,0:T(8,128)(2,1)S(1)}, u32[]{:S(2)}) copy-start(bf16[512,1536]{1,0:T(8,128)(2,1)S(1)} %get-tuple-element.663) | copy-start | bytes 4718596
  392.5 12.8 %copy-start.50 = (bf16[512,1536]{1,0:T(8,128)(2,1)}, bf16[512,1536]{1,0:T(8,128)(2,1)S(1)}, u32[]{:S(2)}) copy-start(bf16[512,1536]{1,0:T(8,128)(2,1)S(1)} %get-tuple-element.664) | copy-start | bytes 4718596
  405.4 227.2 %reduce-scatter.4.cloned.1.call-start = ((), (), s32[]{:S(2)}) async-start(), calls=%async_computation.8 | async-start | bytes 2359296 | tf_op jit(solution)/shard_map/reduce_scatter | solution.py:323
  491.0 5.1 copy-start.5
  491.0 5.1 copy-start.11
  491.0 5.3 copy-start.22
  592.5 85.5 %reduce-scatter.6.cloned.1.call-start = ((), (), s32[]{:S(2)}) async-start(), calls=%async_computation.9 | async-start | bytes 2359296 | tf_op jit(solution)/shard_map/reduce_scatter | solution.py:326
  600.6 242.2 %all-reduce.14.cloned.1.call-start = ((), (), s32[]{:S(2)}) async-start(), calls=%async_computation.11 | async-start | bytes 8388608 | tf_op jit(solution)/shard_map/psum | solution.py:249
  609.2 0.9 copy-start.14
  609.2 1.0 copy-start.16
  609.2 2.7 copy-start.3
  609.2 2.7 copy-start.20
  609.2 2.7 copy-start.43
  610.3 5.5 copy-start.31
  611.9 4.0 copy-start.10
  616.7 17.1 %copy-start.17 = (f32[512,64]{1,0:T(8,128)S(1)}, f32[512,64]{1,0:T(8,128)}, u32[]{:S(2)}) copy-start(f32[512,64]{1,0:T(8,128)} %copy-done.15) | copy-start | bytes 393220
  616.7 18.2 %copy-start.9 = (f32[512,2,128]{2,1,0:T(2,128)S(1)}, f32[512,2,128]{2,1,0:T(2,128)}, u32[]{:S(2)}) copy-start(f32[512,2,128]{2,1,0:T(2,128)} %copy-done.8) | copy-start | bytes 1572868
  616.7 18.2 %copy-start.45 = (f32[128]{0:T(128)S(1)}, f32[128]{0:T(128)}, u32[]{:S(2)}) copy-start(f32[128]{0:T(128)} %copy-done.44) | copy-start | bytes 1540
  620.2 14.6 %copy-start.19 = (f32[512,2]{1,0:T(8,128)S(1)}, f32[512,2]{1,0:T(8,128)}, u32[]{:S(2)}) copy-start(f32[512,2]{1,0:T(8,128)} %copy-done.18) | copy-start | bytes 12292
  620.3 16.8 %copy-start.35 = (f32[512,2]{0,1:T(2,128)S(1)}, f32[512,2]{0,1:T(2,128)}, u32[]{:S(2)}) copy-start(f32[512,2]{0,1:T(2,128)} %copy-done.34) | copy-start | bytes 12292
  687.3 1.6 copy-start.1
  687.3 315.5 %reduce-scatter.8.cloned.1.call-start = ((), (), s32[]{:S(2)}) async-start(), calls=%async_computation.10 | async-start | bytes 28311552 | tf_op jit(solution)/shard_map/reduce_scatter | solution.py:342
  688.9 12.4 %copy-start.23 = (bf16[512,2048]{1,0:T(8,128)(2,1)S(1)}, bf16[512,2048]{1,0:T(8,128)(2,1)}, u32[]{:S(2)}) copy-start(bf16[512,2048]{1,0:T(8,128)(2,1)} %param.23) | copy-start | bytes 6291460
  688.9 12.4 %copy-start.48 = (bf16[512,1536]{1,0:T(8,128)(2,1)S(1)}, bf16[512,1536]{1,0:T(8,128)(2,1)}, u32[]{:S(2)}) copy-start(bf16[512,1536]{1,0:T(8,128)(2,1)} %get-tuple-element.665) | copy-start | bytes 4718596
  701.3 5.5 copy-start.6
  701.3 5.5 copy-start.12
  701.3 5.5 copy-start.26
  710.4 4.0 copy-start.27
  710.4 4.0 copy-start.29
  710.4 4.0 copy-start.41
  842.8 4.3 copy-start.39
  1002.8 4.3 copy-start.7
  1007.1 49.4 %copy-start.33 = (f32[4352]{0:T(1024)S(1)}, f32[4352]{0:T(1024)}, u32[]{:S(2)}) copy-start(f32[4352]{0:T(1024)} %param.29) | copy-start | bytes 52228
  1007.1 49.4 %copy-start.36 = (f32[4352]{0:T(1024)S(1)}, f32[4352]{0:T(1024)}, u32[]{:S(2)}) copy-start(f32[4352]{0:T(1024)} %param.31) | copy-start | bytes 52228
  1007.1 49.4 %copy-start.37 = (f32[4352]{0:T(1024)S(1)}, f32[4352]{0:T(1024)}, u32[]{:S(2)}) copy-start(f32[4352]{0:T(1024)} %param.30) | copy-start | bytes 52228
Sparse Core Ops, SparseCore 0:
  12.4 128.0 all-gather.3
  152.6 27.8 all-gather.5
  183.0 27.9 all-gather.7
  285.2 86.4 all-reduce.9
  405.5 85.4 all-reduce.11
  592.7 39.8 reduce-scatter.3
  636.8 41.2 reduce-scatter.5
  687.4 155.3 all-reduce.13
  846.9 155.8 reduce-scatter.7
where the time goes:
time: 1090 us; the launch traced here: 1080 us
  waiting for transfers between devices  615 us (56%)
  matrix products  184 us (17%)
  other arithmetic  118 us (11%)
  local copies, waits for them, and re-layouts  86 us (8%)
  blocking collectives  39.8 us (4%)
  between operations  17.4 us (2%)
  loops' own time  17.1 us (2%)
    reduce_scatter x1, waiting for transfers between devices, per_device(): lax.psum_scatter(jnp.concatenate([lax.dot_general(normed_low, grad_qkv_lo...  156 us
    all_gather x1, waiting for transfers between devices, per_device(): full_weights = lax.all_gather(low_weights, 'dp', axis=0, tiled=True)  126 us
    psum x1, waiting for transfers between devices, per_device(): lax.psum(mlp_part.astype(jnp.bfloat16), 'mp').astype(jnp.float32)  99.7 us
    psum x1, waiting for transfers between devices, per_device(): lax.psum(attn_part.astype(jnp.bfloat16), 'mp').astype(jnp.float32)  86 us
    psum x1, waiting for transfers between devices, per_device(): lax.psum(grad_mlp_part.astype(jnp.bfloat16), 'mp').astype(jnp.float32)  85.4 us
    psum x1, blocking collectives, per_device(): lax.psum((gain_local, weight_square), ('dp', 'mp'))  39.8 us
    reduce_scatter x1, waiting for transfers between devices, per_device(): lax.psum_scatter(grad_value_stored.astype(jnp.bfloat16), 'dp', scatter_di...  38.1 us
    dot_general x7, matrix products, weighted_active(): jnp.einsum('tkgs,skd->tkgd', probs_low, piece[1], preferred_element_type=...  29 us
  transfers between devices with their start and end apart: 9, of which 8 were waited for; matrix products, arithmetic and copies ran while one was open for 14% of the time, Pallas kernels for 0%

commit v1 on v0

v1 whole, which is shorter than its diff:
```python
import functools

import jax
import jax.numpy as jnp
from jax import lax
from jax.experimental import pallas as pl
from jax.experimental.pallas import tpu as pltpu
from jax.sharding import PartitionSpec as P

HEADS = 16
KV = 8
HD = 128
FF = 6144
SPAN = 128
CHUNK = 4
TILE = 256
VMEM_LIMIT = 60 * 1024 * 1024

eps_norm = 1e-06
rope_base = 1000000.0
learn_rate = 100.0
gain_rate = 4000.0
momentum_decay = 0.5
average_decay = 0.5
score_scale = HD ** (-0.5)
far = -1e30

bf16 = jnp.bfloat16
f32 = jnp.float32
last_dims = (((1,), (1,)), ((), ()))
first_dims = (((0,), (0,)), ((), ()))


def dot(a, b, dims=(((1,), (0,)), ((), ()))):
    return lax.dot_general(a, b, dims, preferred_element_type=f32)


def params(**more):
    return pltpu.CompilerParams(vmem_limit_bytes=VMEM_LIMIT, **more)


def swap(array, axis, distance):
    count = lax.axis_size(axis)
    return lax.ppermute(array, axis, [(i, i ^ distance) for i in range(count)])


def gather_blocks(own):
    outer = [own] + [swap(own, "dp", k) for k in (2, 4, 6)]
    inner = [swap(block, "dp", 1) for block in outer]
    return [block for pair in zip(outer, inner) for block in pair]


def scatter_blocks(even, odd):
    came = swap(odd, "dp", 1)
    half = (even.astype(f32) + came.astype(f32)).astype(bf16)
    parts = [swap(half[k], "dp", 2 * k) for k in (1, 2, 3)]
    total = half[0].astype(f32)
    for part in parts:
        total = total + part.astype(f32)
    return total


def sum_all(value):
    for axis in ("dp", "mp"):
        distance = 1
        while distance < lax.axis_size(axis):
            value = value + swap(value, axis, distance)
            distance *= 2
    return value


def project_kernel(part_count, q_heads, kv_heads, *refs):
    h_ref = refs[0]
    w_refs = refs[1 : 1 + part_count]
    cos_ref, sin_ref, gq_ref, gk_ref, q_ref, kv_ref, lin_ref = refs[1 + part_count :]
    depth = w_refs[0].shape[0]
    cosine = cos_ref[...]
    sine = sin_ref[...]

    def columns(begin):
        total = None
        for k, w_ref in enumerate(w_refs):
            term = dot(h_ref[:, k * depth : (k + 1) * depth], w_ref[:, begin : begin + TILE])
            total = term if total is None else total + term
        return total

    def turned(head, gain):
        scale = lax.rsqrt(jnp.mean(head * head, axis=1, keepdims=True) + eps_norm)
        normed = head * scale * gain
        return normed * cosine + pltpu.roll(normed, HD // 2, 1) * sine

    per_tile = TILE // HD
    for tile in range((q_heads + 2 * kv_heads) // per_tile):
        block = columns(tile * TILE)
        for part in range(per_tile):
            head = tile * per_tile + part
            values = block[:, part * HD : (part + 1) * HD]
            if head < q_heads:
                lin_ref[:, head * HD : (head + 1) * HD] = values
                q_ref[:, head * HD : (head + 1) * HD] = turned(values, gq_ref[...]).astype(bf16)
            elif head < q_heads + kv_heads:
                place = 2 * (head - q_heads) * HD
                lin_ref[:, head * HD : (head + 1) * HD] = values
                kv_ref[:, place : place + HD] = turned(values, gk_ref[...]).astype(bf16)
            else:
                place = (2 * (head - q_heads - kv_heads) + 1) * HD
                kv_ref[:, place : place + HD] = values.astype(bf16)


def span_limits(own_ref, starts_ref, i):
    span = own_ref[i]
    first = span * SPAN
    rows = first + lax.broadcasted_iota(jnp.int32, (SPAN, 1), 0)
    low = jnp.int32(0)
    begin = jnp.zeros((SPAN, 1), jnp.int32)
    for d in range(starts_ref.shape[0]):
        start = starts_ref[d]
        low = jnp.maximum(low, jnp.where(start <= first, start, 0))
        begin = jnp.maximum(begin, jnp.where(start <= rows, start, 0))
    return span, low // SPAN, rows, begin


def key_rows(inverse_ref, newest, b):
    return pl.multiple_of(inverse_ref[jnp.maximum(newest - b, 0)] * SPAN, SPAN)


def allowed_keys(newest, rows, begin):
    lane = lax.broadcasted_iota(jnp.int32, (1, CHUNK * SPAN), 1)
    place = newest * SPAN + (lane & (SPAN - 1)) - (lane & ~(SPAN - 1))
    return (place <= rows) & (place >= begin)


def stacked(ref, i, group):
    rows = pl.ds(i * SPAN, SPAN)
    return jnp.concatenate([ref[rows, h * HD : (h + 1) * HD] for h in range(group)], axis=0)


def attend_kernel(group, own_ref, inverse_ref, starts_ref, q_ref, kv_ref, o_ref, low_ref, lse_ref, s_ref):
    for i in range(own_ref.shape[0]):
        span, low, rows, begin = span_limits(own_ref, starts_ref, i)
        rows = jnp.concatenate([rows] * group, axis=0)
        begin = jnp.concatenate([begin] * group, axis=0)
        query = stacked(q_ref, i, group)
        count = (span - low) // CHUNK + 1

        def score(c, top):
            newest = span - c * CHUNK
            keys = jnp.concatenate(
                [kv_ref[pl.ds(key_rows(inverse_ref, newest, b), SPAN), :HD] for b in range(CHUNK)], axis=0
            )
            scores = dot(query, keys, last_dims) * score_scale
            scores = jnp.where(allowed_keys(newest, rows, begin), scores, far)
            s_ref[c] = scores
            for b in range(CHUNK):
                top = jnp.maximum(top, scores[:, b * SPAN : (b + 1) * SPAN])
            return top

        top = lax.fori_loop(0, count, score, jnp.full((group * SPAN, SPAN), far, f32))
        top = jnp.max(top, axis=1, keepdims=True)

        def weigh(c, carry):
            weight, total = carry
            newest = span - c * CHUNK
            values = jnp.concatenate(
                [kv_ref[pl.ds(key_rows(inverse_ref, newest, b), SPAN), HD:] for b in range(CHUNK)], axis=0
            )
            probs = jnp.exp(s_ref[c] - top)
            for b in range(CHUNK):
                weight = weight + probs[:, b * SPAN : (b + 1) * SPAN]
            return weight, total + dot(probs.astype(bf16), values)

        zeros = jnp.zeros((group * SPAN, SPAN), f32)
        weight, total = lax.fori_loop(0, count, weigh, (zeros, jnp.zeros((group * SPAN, HD), f32)))
        weight = jnp.sum(weight, axis=1, keepdims=True)
        output = total / weight
        lse = jnp.broadcast_to(top + jnp.log(weight), output.shape)
        place = pl.ds(i * SPAN, SPAN)
        for h in range(group):
            o_ref[place, h * HD : (h + 1) * HD] = output[h * SPAN : (h + 1) * SPAN]
            low_ref[place, h * HD : (h + 1) * HD] = output[h * SPAN : (h + 1) * SPAN].astype(bf16)
            lse_ref[place, h * HD : (h + 1) * HD] = lse[h * SPAN : (h + 1) * SPAN]


def attend_back_kernel(
    group, own_ref, inverse_ref, starts_ref, place_ref, q_ref, kv_ref, do_ref, o_ref, lse_ref, dq_ref, dkv_ref, acc_ref
):
    acc_ref[...] = jnp.zeros_like(acc_ref)
    for i in range(own_ref.shape[0]):
        span, low, rows, begin = span_limits(own_ref, starts_ref, i)
        rows = jnp.concatenate([rows] * group, axis=0)
        begin = jnp.concatenate([begin] * group, axis=0)
        query = stacked(q_ref, i, group)
        grad = stacked(do_ref, i, group)
        delta = jnp.sum(grad.astype(f32) * stacked(o_ref, i, group), axis=1, keepdims=True)
        lse = stacked(lse_ref, i, group)[:, :1]
        count = (span - low) // CHUNK + 1

        def step(c, grad_query):
            newest = span - c * CHUNK
            at = [key_rows(inverse_ref, newest, b) for b in range(CHUNK)]
            both = jnp.concatenate([kv_ref[pl.ds(a, SPAN), :] for a in at], axis=0)
            keys, values = both[:, :HD], both[:, HD:]
            scores = dot(query, keys, last_dims) * score_scale
            probs = jnp.exp(jnp.where(allowed_keys(newest, rows, begin), scores - lse, far))
            grad_probs = dot(grad, values, last_dims)
            grad_scores = (probs * (grad_probs - delta)).astype(bf16)
            grad_keys = dot(grad_scores, query, first_dims) * score_scale
            grad_values = dot(probs.astype(bf16), grad, first_dims)
            for b, a in enumerate(at):
                acc_ref[pl.ds(a, SPAN), :HD] += grad_keys[b * SPAN : (b + 1) * SPAN]
                acc_ref[pl.ds(a, SPAN), HD:] += grad_values[b * SPAN : (b + 1) * SPAN]
            return grad_query + dot(grad_scores, keys)

        grad_query = lax.fori_loop(0, count, step, jnp.zeros((group * SPAN, HD), f32)) * score_scale
        for h in range(group):
            dq_ref[pl.ds(i * SPAN, SPAN), h * HD : (h + 1) * HD] = grad_query[h * SPAN : (h + 1) * SPAN]

    def put(t, unused):
        source = pl.multiple_of(t * SPAN, SPAN)
        target = pl.multiple_of(place_ref[t] * SPAN, SPAN)
        dkv_ref[pl.ds(target, SPAN), :] = acc_ref[pl.ds(source, SPAN), :].astype(bf16)
        return unused

    lax.fori_loop(0, place_ref.shape[0], put, 0)


def mlp_kernel(h_ref, c_ref, wg_ref, wu_ref, wd_ref, dg_ref, du_ref, a_ref, dh_ref, acc_ref):
    step = pl.program_id(0)
    hidden = h_ref[...]
    gate = dot(hidden, wg_ref[...])
    up = dot(hidden, wu_ref[...])
    grad = dot(c_ref[...], wd_ref[...])
    sig = 1.0 / (1.0 + jnp.exp(-gate))
    silu = gate * sig
    a_ref[...] = (silu * up).astype(bf16)
    grad_gate = (grad * up * (sig + silu * (1.0 - sig))).astype(bf16)
    grad_up = (grad * silu).astype(bf16)
    dg_ref[...] = grad_gate
    du_ref[...] = grad_up
    term = dot(grad_gate, wg_ref[...], last_dims) + dot(grad_up, wu_ref[...], last_dims)

    @pl.when(step == 0)
    def _():
        acc_ref[...] = term

    @pl.when(step > 0)
    def _():
        acc_ref[...] += term

    @pl.when(step == pl.num_programs(0) - 1)
    def _():
        dh_ref[...] = acc_ref[...].astype(bf16)


def unit_scale(values):
    return lax.rsqrt(jnp.mean(values * values, axis=-1, keepdims=True) + eps_norm)


def norm_back(unit, scale, gain, gradient):
    e = gradient * gain
    return scale * (e - unit * jnp.mean(e * unit, axis=-1, keepdims=True))


def head_back(lin, gain, gradient, cosine, sine):
    tokens = lin.shape[0]
    lin = lin.reshape(tokens, -1, HD)
    gradient = gradient.reshape(tokens, -1, HD)
    turned = gradient * sine[:, None, :]
    half = HD // 2
    turned = jnp.concatenate([turned[..., half:], turned[..., :half]], axis=-1)
    grad_normed = gradient * cosine[:, None, :] + turned
    scale = unit_scale(lin)
    unit = lin * scale
    grad_gain = jnp.sum(grad_normed * unit, axis=(0, 1))
    return norm_back(unit, scale, gain, grad_normed).reshape(tokens, -1).astype(bf16), grad_gain


def update(value, state, average, gradient, factor, step_rate):
    clipped = gradient * factor
    state_new = momentum_decay * state + clipped
    value_new = value - step_rate * (clipped + momentum_decay * state_new)
    average_new = average_decay * average + (1.0 - average_decay) * value_new
    return (value_new, state_new, average_new)


def per_device(
    block_input,
    cotangent,
    doc_lengths,
    span_order,
    weights,
    momentum,
    ema_weights,
    gains,
    gain_momentum,
    gain_ema,
):
    tok_count, model_width = block_input.shape
    data_count = lax.axis_size("dp")
    model_count = lax.axis_size("mp")
    me = lax.axis_index("dp")
    row_count = weights.shape[0]
    token_total = tok_count * data_count
    span_total = token_total // SPAN
    span_own = tok_count // SPAN
    seq_len = token_total // doc_lengths.shape[0]
    doc_total = doc_lengths.shape[0] * doc_lengths.shape[1]
    q_heads = HEADS // model_count
    kv_heads = KV // model_count
    group = q_heads // kv_heads
    query_width = q_heads * HD
    kv_width = kv_heads * HD
    ff_width = FF // model_count
    qkv_cols = query_width + 2 * kv_width
    out_end = qkv_cols + query_width
    in_pairs = data_count == 8
    gain_attn = gains[:model_width]
    gain_mlp = gains[model_width : 2 * model_width]
    gain_query = gains[2 * model_width : 2 * model_width + HD]
    gain_key = gains[2 * model_width + HD :]

    doc_ids = jnp.arange(doc_lengths.shape[1], dtype=jnp.int32)
    earlier = doc_ids[None, :] < doc_ids[:, None]
    starts = jnp.sum(jnp.where(earlier[None], doc_lengths[:, None, :], 0), axis=2)
    starts = starts + seq_len * jnp.arange(doc_lengths.shape[0], dtype=jnp.int32)[:, None]
    starts = starts.reshape(doc_total)
    span_ids = jnp.arange(span_total, dtype=jnp.int32)
    inverse = jnp.sum(jnp.where(span_order[None, :] == span_ids[:, None], span_ids[None, :], 0), axis=1)
    own_spans = lax.dynamic_slice(span_order, (me * span_own,), (span_own,))
    home = (own_spans[:, None] * SPAN + jnp.arange(SPAN, dtype=jnp.int32)[None, :]).reshape(tok_count)
    doc_start = jnp.max(jnp.where(starts[None, :] <= home[:, None], starts[None, :], 0), axis=1)
    freqs = rope_base ** (-(2.0 * jnp.arange(HD // 2, dtype=f32)) / HD)
    angles = (home - doc_start).astype(f32)[:, None] * freqs[None, :]
    cosine = jnp.tile(jnp.cos(angles), (1, 2))
    sine_half = jnp.sin(angles)
    sine = jnp.concatenate([-sine_half, sine_half], axis=1)

    qkv_own = weights[:, :qkv_cols].astype(bf16)
    out_own = weights[:, qkv_cols:out_end].astype(bf16)
    mlp_own = weights[:, out_end:].astype(bf16)
    inputs = block_input.astype(f32)
    scale_in = unit_scale(inputs)
    unit_in = inputs * scale_in
    normed_low = (unit_in * gain_attn).astype(bf16)

    if in_pairs:
        order = [me ^ k for k in range(data_count)]

        def reordered(array):
            return jnp.concatenate(
                [lax.dynamic_slice(array, (0, b * row_count), (array.shape[0], row_count)) for b in order], axis=1
            )

        qkv_parts = gather_blocks(qkv_own)
        normed_low = reordered(normed_low)
        out_parts = gather_blocks(out_own)
        mlp_own, qkv_parts = lax.optimization_barrier((mlp_own, qkv_parts))
    else:

        def reordered(array):
            return array

        qkv_parts = [lax.all_gather(qkv_own, "dp", axis=0, tiled=True)]
        out_parts = [lax.all_gather(out_own, "dp", axis=0, tiled=True)]
    mlp_weights = lax.all_gather(mlp_own, "dp", axis=0, tiled=True)
    qkv_weights = jnp.concatenate(qkv_parts, axis=0)
    out_weights = jnp.concatenate(out_parts, axis=0)

    queries, keys_values, lin = pl.pallas_call(
        functools.partial(project_kernel, len(qkv_parts), q_heads, kv_heads),
        out_shape=(
            jax.ShapeDtypeStruct((tok_count, query_width), bf16),
            jax.ShapeDtypeStruct((tok_count, 2 * kv_width), bf16),
            jax.ShapeDtypeStruct((tok_count, query_width + kv_width), f32),
        ),
        compiler_params=params(),
        name="project",
    )(normed_low, *qkv_parts, cosine, sine, gain_query[None], gain_key[None])

    if in_pairs:
        kv_parts = gather_blocks(keys_values)
        kv_all = jnp.concatenate(kv_parts, axis=0)
        kv_inverse = ((inverse // span_own) ^ me) * span_own + inverse % span_own
        kv_place = ((span_ids // span_own) >> 1) * span_own + span_ids % span_own
        kv_place = kv_place + jnp.where(((span_ids // span_own) & 1) == 1, span_total // 2, 0)
    else:
        kv_all = lax.all_gather(keys_values, "dp", axis=0, tiled=True)
        kv_inverse = inverse
        kv_place = span_ids

    wide = group * HD
    q_spec = pl.BlockSpec((tok_count, wide), lambda g, *_: (0, g))
    kv_spec = pl.BlockSpec((token_total, 2 * HD), lambda g, *_: (0, g))
    attended, attended_low, lse = pl.pallas_call(
        functools.partial(attend_kernel, group),
        grid_spec=pltpu.PrefetchScalarGridSpec(
            num_scalar_prefetch=3,
            grid=(kv_heads,),
            in_specs=[q_spec, kv_spec],
            out_specs=[q_spec, q_spec, q_spec],
            scratch_shapes=[pltpu.VMEM((seq_len // (CHUNK * SPAN) + 1, group * SPAN, CHUNK * SPAN), f32)],
        ),
        out_shape=(
            jax.ShapeDtypeStruct((tok_count, query_width), f32),
            jax.ShapeDtypeStruct((tok_count, query_width), bf16),
            jax.ShapeDtypeStruct((tok_count, query_width), f32),
        ),
        compiler_params=params(),
        name="attend",
    )(own_spans, kv_inverse, starts, queries, kv_all)

    attn_part = dot(attended_low, out_weights, last_dims).astype(bf16)
    attn_sum = lax.psum(attn_part, "mp").astype(f32)
    inputs_there = reordered(block_input).astype(f32)
    residual = inputs_there + attn_sum
    gain_mlp_there = reordered(gain_mlp[None])[0]
    scale_mlp = unit_scale(residual)
    unit_mlp = residual * scale_mlp
    mlp_low_there = (unit_mlp * gain_mlp_there).astype(bf16)

    def restored(array):
        return reordered(array)

    mlp_low = restored(mlp_low_there)

    tiles = ff_width // TILE
    rows_spec = pl.BlockSpec((tok_count, model_width), lambda n: (0, 0))
    tile_spec = pl.BlockSpec((tok_count, TILE), lambda n: (0, n))
    hidden_shape = jax.ShapeDtypeStruct((tok_count, ff_width), bf16)
    grad_gate, grad_up, hidden_low, grad_mlp_part = pl.pallas_call(
        mlp_kernel,
        grid=(tiles,),
        in_specs=[
            rows_spec,
            rows_spec,
            pl.BlockSpec((model_width, TILE), lambda n: (0, n)),
            pl.BlockSpec((model_width, TILE), lambda n: (0, n + tiles)),
            pl.BlockSpec((model_width, TILE), lambda n: (0, n + 2 * tiles)),
        ],
        out_specs=[tile_spec, tile_spec, tile_spec, rows_spec],
        out_shape=(hidden_shape, hidden_shape, hidden_shape, jax.ShapeDtypeStruct((tok_count, model_width), bf16)),
        scratch_shapes=[pltpu.VMEM((tok_count, model_width), f32)],
        compiler_params=params(),
        name="mlp",
    )(mlp_low, cotangent, mlp_weights, mlp_weights, mlp_weights)

    grad_mlp_full = lax.psum(grad_mlp_part, "mp").astype(f32)
    mlp_part = dot(hidden_low, mlp_weights[:, 2 * ff_width :], last_dims).astype(bf16)
    mlp_part, grad_mlp_full = lax.optimization_barrier((mlp_part, grad_mlp_full))
    mlp_sum = lax.psum(mlp_part, "mp").astype(f32)
    block_output = (restored(residual) + mlp_sum).astype(bf16)

    unit_mlp_here = restored(unit_mlp)
    mlp_gain_grad = jnp.sum(grad_mlp_part.astype(f32) * unit_mlp_here, axis=0)
    grad_residual = cotangent.astype(f32) + norm_back(unit_mlp_here, scale_mlp, gain_mlp, grad_mlp_full)
    grad_res_low = grad_residual.astype(bf16)
    grad_res_there = reordered(grad_res_low)
    grad_att_low = dot(grad_res_there, out_weights).astype(bf16)

    grad_queries, grad_kv = pl.pallas_call(
        functools.partial(attend_back_kernel, group),
        grid_spec=pltpu.PrefetchScalarGridSpec(
            num_scalar_prefetch=4,
            grid=(kv_heads,),
            in_specs=[q_spec, kv_spec, q_spec, q_spec, q_spec],
            out_specs=[q_spec, kv_spec],
            scratch_shapes=[pltpu.VMEM((token_total, 2 * HD), f32)],
        ),
        out_shape=(
            jax.ShapeDtypeStruct((tok_count, query_width), f32),
            jax.ShapeDtypeStruct((token_total, 2 * kv_width), bf16),
        ),
        compiler_params=params(),
        name="attend_back",
    )(own_spans, kv_inverse, starts, kv_place, queries, kv_all, grad_att_low, attended, lse)

    if in_pairs:
        halves = grad_kv.reshape(2, data_count // 2, tok_count, 2 * kv_width)
        grad_kv_mine = scatter_blocks(halves[0], halves[1])
    else:
        grad_kv_mine = lax.psum_scatter(grad_kv, "dp", scatter_dimension=0, tiled=True).astype(f32)
    grad_kv_mine = grad_kv_mine.reshape(tok_count, kv_heads, 2, HD)
    grad_query_low, grad_gain_query = head_back(lin[:, :query_width], gain_query, grad_queries, cosine, sine)
    grad_key_low, grad_gain_key = head_back(lin[:, query_width:], gain_key, grad_kv_mine[:, :, 0], cosine, sine)
    grad_qkv_low = jnp.concatenate(
        [grad_query_low, grad_key_low, grad_kv_mine[:, :, 1].reshape(tok_count, kv_width).astype(bf16)], axis=1
    )

    grad_norm_part = dot(grad_qkv_low, qkv_weights, last_dims).astype(bf16)
    unit_there = reordered(unit_in)
    gain_attn_there = reordered(gain_attn[None])[0]
    attn_gain_grad = restored(jnp.sum(grad_norm_part.astype(f32) * unit_there, axis=0, keepdims=True))[0]
    grad_norm_full = lax.psum(grad_norm_part, "mp").astype(f32)
    grad_input = grad_residual + restored(norm_back(unit_there, scale_in, gain_attn_there, grad_norm_full))

    grad_gate_up = jnp.concatenate([grad_gate, grad_up], axis=1)
    dw_down = dot(cotangent, hidden_low, first_dims).astype(bf16)
    dw_gate_up = dot(mlp_low, grad_gate_up, first_dims).astype(bf16)
    dw_qkv = dot(normed_low, grad_qkv_low, first_dims).astype(bf16)
    dw_out = dot(grad_res_there, attended_low, first_dims).astype(bf16)

    def scattered(array):
        return lax.psum_scatter(array, "dp", scatter_dimension=0, tiled=True).astype(f32)

    if in_pairs:

        def scattered_there(array):
            blocks = array.reshape(data_count, row_count, -1)
            return scatter_blocks(blocks[0::2], blocks[1::2])
    else:
        scattered_there = scattered
    weight_grads = [
        scattered_there(dw_qkv),
        scattered_there(dw_out),
        scattered(dw_gate_up),
        scattered(dw_down),
    ]
    square = sum(jnp.sum(grad * grad) for grad in weight_grads)
    gain_grads = sum_all(jnp.concatenate([attn_gain_grad, mlp_gain_grad, grad_gain_query, grad_gain_key]))
    square_total = sum_all(square.reshape(1, 1))[0, 0]
    grad_norm = jnp.sqrt(square_total + jnp.sum(gain_grads * gain_grads))
    factor = 1.0 / jnp.maximum(grad_norm, 1.0)
    weight_grad = jnp.concatenate(weight_grads, axis=1)
    new_weights, new_momentum, new_ema = update(weights, momentum, ema_weights, weight_grad, factor, learn_rate)
    new_gains, new_gain_momentum, new_gain_ema = update(gains, gain_momentum, gain_ema, gain_grads, factor, gain_rate)
    return (
        block_output,
        grad_input,
        grad_norm,
        new_weights,
        new_momentum,
        new_ema,
        new_gains,
        new_gain_momentum,
        new_gain_ema,
    )


def solution(mesh):
    return jax.shard_map(
        per_device,
        mesh=mesh,
        in_specs=(
            P("dp", None),
            P("dp", None),
            P(),
            P(),
            P("dp", "mp"),
            P("dp", "mp"),
            P("dp", "mp"),
            P(),
            P(),
            P(),
        ),
        out_specs=(
            P("dp", None),
            P("dp", None),
            P(),
            P("dp", "mp"),
            P("dp", "mp"),
            P("dp", "mp"),
            P(),
            P(),
            P(),
        ),
        check_vma=False,
    )
```

time: 1090 us -> 720 us (0.66)
  waiting for transfers between devices: 615 us -> 324 us
  matrix products: 184 us -> 42.7 us
  Pallas kernels: 0 us -> 75.4 us
  starting transfers between devices: 1.98 us -> 49.1 us
  blocking collectives: 39.8 us -> 0 us
  other arithmetic: 118 us -> 93.1 us
  loops' own time: 17.1 us -> 0 us
  local copies, waits for them, and re-layouts: 86 us -> 103 us
    reduce_scatter x3 -> x2, waiting for transfers between devices: 205 us -> 4.25 us  [scattered(): lax.psum_scatter(array, 'dp', scatter_dimension=0, tiled=True).astype(f32)]
    dot_general x61 -> x8, matrix products: 184 us -> 42.7 us  [dot(): return lax.dot_general(a, b, dims, preferred_element_type=f32)]
    all_gather x3 -> x1, waiting for transfers between devices: 139 us -> 5.91 us  [per_device(): mlp_weights = lax.all_gather(mlp_own, 'dp', axis=0, tiled=True)]
    ppermute x0 -> x43, waiting for transfers between devices: none -> 92.2 us  [swap(): return lax.ppermute(array, axis, [(i, i ^ distance) for i in range(count)])]
    pallas_call x0 -> x4, Pallas kernels: none -> 75.4 us  [the longest x1 38.2 us: per_device(): pl.pallas_call(mlp_kernel, grid=(tiles,), in_specs=[rows_spec, rows_spec,...]
    unnamed x105 -> x196, local copies, waits for them, and re-layouts: 6.28 us -> 67.8 us
    psum x3, waiting for transfers between devices: 271 us -> 221 us  [the longest x1 86.7 us: per_device(): attn_sum = lax.psum(attn_part, 'mp').astype(f32)]
    ppermute x0 -> x43, starting transfers between devices: none -> 48.2 us  [swap(): return lax.ppermute(array, axis, [(i, i ^ distance) for i in range(count)])]
  transfers between devices with their start and end apart: 9 -> 49, of which waited for: 8 -> 24; matrix products, arithmetic and copies ran while one was open for 14% -> 23% of each run, Pallas kernels for 0% -> 1%
where the time goes in v1:
time: 720 us; the launch traced here: 711 us
  waiting for transfers between devices  324 us (45%)
  local copies, waits for them, and re-layouts  103 us (14%)
  other arithmetic  93.1 us (13%)
  Pallas kernels  75.4 us (10%)
  starting transfers between devices  49.1 us (7%)
  matrix products  42.7 us (6%)
  between operations  24.5 us (3%)
    ppermute x43, waiting for transfers between devices, swap(): return lax.ppermute(array, axis, [(i, i ^ distance) for i in range(count)])  92.2 us
    psum x1, waiting for transfers between devices, per_device(): attn_sum = lax.psum(attn_part, 'mp').astype(f32)  86.7 us
    psum x1, waiting for transfers between devices, per_device(): mlp_sum = lax.psum(mlp_part, 'mp').astype(f32)  68.8 us
    unnamed x196, local copies, waits for them, and re-layouts  67.8 us
    psum x1, waiting for transfers between devices, per_device(): grad_mlp_full = lax.psum(grad_mlp_part, 'mp').astype(f32)  65.4 us
    ppermute x43, starting transfers between devices, swap(): return lax.ppermute(array, axis, [(i, i ^ distance) for i in range(count)])  48.2 us
    dot_general x8, matrix products, dot(): return lax.dot_general(a, b, dims, preferred_element_type=f32)  42.7 us
    pallas_call x1, Pallas kernels, per_device(): pl.pallas_call(mlp_kernel, grid=(tiles,), in_specs=[rows_spec, rows_spec,...  38.2 us
  transfers between devices with their start and end apart: 49, of which 24 were waited for; matrix products, arithmetic and copies ran while one was open for 23% of the time, Pallas kernels for 1%

profile of v1, /device:TPU:0, one launch (start us, length us, event | category | flops | bytes accessed | tf_op | source)
XLA Modules:
  0.0 711.3 jit_solution(8446432982500038054)
XLA Ops:
  8.1 3.4 convert.12
  11.5 3.0 collective-permute-start.1
  16.9 1.9 collective-permute-start.15
  23.6 2.6 convert_multiply_fusion
  37.5 6.0 collective-permute-done.15
  51.2 2.2 collective-permute-done.19
  59.1 3.3 slice.142
  63.9 7.7 %project.1 = (bf16[512,512]{1,0:T(8,128)(2,1)}, bf16[512,512]{1,0:T(8,128)(2,1)}, f32[512,768]{1,0:T(8,128)}) custom-call(bf16[512,2048]{1,0:T(8,128)(2,1)} %dynamic-slice_dynamic-update-slice_fusion.48.refs_0_, bf16[256,1024]{1,0:T(8,128)(2,1)} %copy-done.22, bf16[256,1024]{1,0:T(8,128)(2,1)} %collective-permute-done.refs_2_, ...), custom_call_target="tpu_custom_call" | custom-call | tf_op jit(solution)/shard_map/project/pallas_call | solution.py:369
  82.5 4.1 collective-permute-done.8
  88.9 12.7 %collective-permute-done.10 = bf16[512,512]{1,0:T(8,128)(2,1)S(1)} collective-permute-done((bf16[512,512]{1,0:T(8,128)(2,1)}, bf16[512,512]{1,0:T(8,128)(2,1)S(1)}, u32[]{:S(2)}, u32[]{:S(2)}) %collective-permute-start.10) | collective-permute-done | bytes 524320 | tf_op jit(solution)/shard_map/ppermute | solution.py:44
  109.9 12.7 %attend.1 = (f32[512,512]{1,0:T(8,128)}, bf16[512,512]{1,0:T(8,128)(2,1)}, f32[512,512]{1,0:T(8,128)}) custom-call(s32[4]{0:T(128)} %get-tuple-element.81.own_ref, s32[32]{0:T(128)} %get-tuple-element.138.inverse_ref, s32[8]{0:T(128)} %copy-done.44, bf16[512,512]{1,0:T(8,128)(2,1)} %get-tuple-element.40.q_ref, ...), custom_call_target="tpu_custom_call" | custom-call | tf_op jit(solution)/shard_map/attend/pallas_call | solution.py:394
  122.5 4.4 convolution_convert_fusion.5
  132.2 86.7 %all-reduce.5.cloned.1.call-done = bf16[512,2048]{1,0:T(8,128)(2,1)} async-done(((bf16[512,2048]{1,0:T(8,128)(2,1)}), bf16[512,2048]{1,0:T(8,128)(2,1)}) %all-reduce.5.cloned.1.call-update) | async-done | bytes 2097168 | tf_op jit(solution)/shard_map/psum | solution.py:413
  218.8 3.3 multiply_reduce_fusion.4
  222.1 4.8 multiply_convert_fusion
  227.4 5.9 all-gather.2.cloned.1.call-done.wg_ref.wu_ref.wd_ref
  233.3 38.2 %mlp.1 = (bf16[512,1536]{1,0:T(8,128)(2,1)}, bf16[512,1536]{1,0:T(8,128)(2,1)}, bf16[512,1536]{1,0:T(8,128)(2,1)}, bf16[512,2048]{1,0:T(8,128)(2,1)}) custom-call(bf16[512,2048]{1,0:T(8,128)(2,1)} %copy-done.28, bf16[512,2048]{1,0:T(8,128)(2,1)} %c_ref.1, bf16[2048,4608]{1,0:T(8,128)(2,1)} %all-gather.2.cloned.1.call-done.wg_ref.wu_ref.wd_ref, ...), custom_call_target="tpu_custom_call" | custom-call | tf_op jit(solution)/shard_map/mlp/pallas_call | solution.py:430
  271.9 2.0 constant_dynamic-update-slice_fusion.29
  275.9 2.1 dynamic-slice_dynamic-update-slice_fusion.23
  277.9 1.9 dynamic-slice_dynamic-update-slice_fusion.22
  285.1 7.6 %fusion.8 = bf16[512,2048]{1,0:T(8,128)(2,1)} fusion(bf16[512,1536]{1,0:T(8,128)(2,1)S(1)} %copy-done.46, bf16[2048,4608]{1,0:T(8,128)(2,1)} %all-gather.2.cloned.1.call-done.wg_ref.wu_ref.wd_ref), kind=kOutput, calls=%fused_computation.33 | convolution fusion | flops 3222274048 | bytes 9961472 | tf_op jit(solution)/shard_map/dot_general | solution.py:35
  292.7 65.4 %all-reduce.7.cloned.1.call-done = bf16[512,2048]{1,0:T(8,128)(2,1)} async-done(((bf16[512,2048]{1,0:T(8,128)(2,1)}), bf16[512,2048]{1,0:T(8,128)(2,1)}) %all-reduce.7.cloned.1.call-update) | async-done | bytes 2097168 | tf_op jit(solution)/shard_map/psum | solution.py:447
  358.1 2.3 convert_element_type.175
  360.4 4.8 multiply_reduce_fusion
  365.2 3.2 fusion.34
  370.0 2.0 convolution_convert_fusion.6.do_ref
  372.1 16.9 %attend_back.1 = (f32[512,512]{1,0:T(8,128)}, bf16[4096,512]{1,0:T(8,128)(2,1)}) custom-call(s32[4]{0:T(128)} %get-tuple-element.81.own_ref, s32[32]{0:T(128)} %get-tuple-element.138.inverse_ref, s32[8]{0:T(128)} %copy-done.44, s32[32]{0:T(128)} %get-tuple-element.137.place_ref, bf16[512,512]{1,0:T(8,128)(2,1)} %get-tuple-element.40.q_ref, ...), custom_call_target="tpu_custom_call" | custom-call | tf_op jit(solution)/shard_map/attend_back/pallas_call | solution.py:460
  389.0 4.6 fusion.37
  410.1 2.6 reshape.271
  415.0 2.1 multiply_reduce_fusion.9
  417.1 2.2 fusion.4
  420.6 6.5 collective-permute-start.23
  431.4 3.8 collective-permute-done.24
  435.2 14.9 %collective-permute-done.23 = bf16[512,512]{1,0:T(8,128)(2,1)S(1)} collective-permute-done((bf16[512,512]{1,0:T(8,128)(2,1)S(1)}, bf16[512,512]{1,0:T(8,128)(2,1)S(1)}, u32[]{:S(2)}, u32[]{:S(2)}) %collective-permute-start.23) | collective-permute-done | bytes 524320 | tf_op jit(solution)/shard_map/ppermute | solution.py:44
  453.3 2.9 reshape.273
  460.8 2.7 multiply_reduce_fusion.11
  466.2 5.9 convolution_convert_fusion.3
  472.2 6.8 fusion
  479.0 12.3 %convolution_convert_fusion = bf16[2048,3072]{1,0:T(8,128)(2,1)} fusion(bf16[512,2048]{1,0:T(8,128)(2,1)} %copy-done.28, bf16[512,1536]{1,0:T(8,128)(2,1)} %get-tuple-element.54, bf16[512,1536]{1,0:T(8,128)(2,1)} %get-tuple-element.53), kind=kOutput, calls=%fused_computation | convolution fusion | flops 6455033856 | bytes 17825792 | tf_op jit(solution)/shard_map/dot_general | solution.py:35
  497.3 2.4 convolution_convert_fusion.2
  499.9 1.9 copy-done.41
  503.7 3.4 copy-done.6
  509.0 2.4 collective-permute-start.30
  514.1 9.5 %collective-permute-done.32 = bf16[256,512]{1,0:T(8,128)(2,1)S(1)} collective-permute-done((bf16[256,512]{1,0:T(8,128)(2,1)S(1)}, bf16[256,512]{1,0:T(8,128)(2,1)S(1)}, u32[]{:S(2)}, u32[]{:S(2)}) %collective-permute-start.32) | collective-permute-done | bytes 262176 | tf_op jit(solution)/shard_map/ppermute | solution.py:44
  523.8 4.2 collective-permute-done.31
  527.9 3.0 collective-permute-done.30
  532.5 10.6 %collective-permute-done.28 = bf16[256,1024]{1,0:T(8,128)(2,1)S(1)} collective-permute-done((bf16[256,1024]{1,0:T(8,128)(2,1)S(1)}, bf16[256,1024]{1,0:T(8,128)(2,1)S(1)}, u32[]{:S(2)}, u32[]{:S(2)}) %collective-permute-start.28) | collective-permute-done | bytes 524320 | tf_op jit(solution)/shard_map/ppermute | solution.py:44
  543.1 9.6 %collective-permute-done.27 = bf16[256,1024]{1,0:T(8,128)(2,1)S(1)} collective-permute-done((bf16[256,1024]{1,0:T(8,128)(2,1)S(1)}, bf16[256,1024]{1,0:T(8,128)(2,1)S(1)}, u32[]{:S(2)}, u32[]{:S(2)}) %collective-permute-start.27) | collective-permute-done | bytes 524320 | tf_op jit(solution)/shard_map/ppermute | solution.py:44
  552.7 2.0 multiply_reduce_fusion.8
  556.0 68.8 %all-reduce.9.cloned.1.call-done = (bf16[512,2048]{1,0:T(8,128)(2,1)}, bf16[512,2048]{1,0:T(8,128)(2,1)}) async-done(((bf16[512,2048]{1,0:T(8,128)(2,1)}, bf16[512,2048]{1,0:T(8,128)(2,1)}), (bf16[512,2048]{1,0:T(8,128)(2,1)}, bf16[512,2048]{1,0:T(8,128)(2,1)})) %all-reduce.9.cloned.1.call-update) | async-done | bytes 4194320 | tf_op jit(solution)/shard_map/psum | solution.py:450
  624.8 4.8 multiply_reduce_fusion.1
  633.1 2.3 collective-permute-done.39
  637.0 2.2 collective-permute-done.40
  639.2 6.6 fusion.33
  647.3 4.1 add_convert_fusion.1
  651.9 2.6 convert_element_type.217
  654.5 2.1 multiply_reduce_fusion.6
  656.6 4.3 reduce-scatter.3.cloned.1.call-done
  660.9 2.8 multiply_reduce_fusion.5
  668.4 2.7 collective-permute-start.34
  672.7 2.7 collective-permute-start.35
  676.9 2.9 collective-permute-start.36
  681.2 3.8 collective-permute-start.37
  687.8 14.5 %add_multiply_fusion = (f32[256,6144]{1,0:T(8,128)}, f32[256,6144]{1,0:T(8,128)}, f32[256,6144]{1,0:T(8,128)}) fusion(f32[256,6144]{1,0:T(8,128)} %param.16, f32[256,6144]{1,0:T(8,128)} %param.14, f32[]{:T(128)S(6)} %div.66, f32[256,1536]{1,0:T(8,128)} %convert_element_type.217, f32[256,3072]{1,0:T(8,128)S(1)} %convert_element_type.214, ...), kind=kLoop, calls=%fused_computation.6 | loop fusion | flops 18874368 | bytes 44040196 | tf_op jit(solution)/shard_map/add | solution.py:282
  (354 shorter events, 132.4 us)
Async XLA Ops:
  8.0 12.4 %copy-start.37 = (f32[4352]{0:T(1024)S(1)}, f32[4352]{0:T(1024)}, u32[]{:S(2)}) copy-start(f32[4352]{0:T(1024)} %param.17) | copy-start | bytes 52228
  8.0 13.0 %copy-start.45 = (s32[32]{0:T(128)S(1)}, s32[32]{0:T(128)}, u32[]{:S(2)}) copy-start(s32[32]{0:T(128)} %param.13) | copy-start | bytes 388
  8.0 14.2 %copy-start.48 = (s32[1,8]{1,0:T(1,128)S(1)}, s32[1,8]{1,0:T(1,128)}, u32[]{:S(2)}) copy-start(s32[1,8]{1,0:T(1,128)} %param.12) | copy-start | bytes 100
  8.0 14.3 %copy-start.4 = (bf16[512,2048]{1,0:T(8,128)(2,1)S(1)}, bf16[512,2048]{1,0:T(8,128)(2,1)}, u32[]{:S(2)}) copy-start(bf16[512,2048]{1,0:T(8,128)(2,1)} %param.10) | copy-start | bytes 6291460
  8.1 210.8 %all-reduce.5.cloned.1.call-start = ((), (), s32[]{:S(2)}) async-start(), calls=%async_computation.2 | async-start | bytes 4194304 | tf_op jit(solution)/shard_map/psum | solution.py:413
  11.5 31.9 %copy-start.22 = (bf16[256,1024]{1,0:T(8,128)(2,1)}, bf16[256,1024]{1,0:T(8,128)(2,1)S(1)}, u32[]{:S(2)}) copy-start(bf16[256,1024]{1,0:T(8,128)(2,1)S(1)} %slice.143.refs_1_) | copy-start | bytes 1572868
  11.5 36.5 %collective-permute-start.1 = (bf16[256,1024]{1,0:T(8,128)(2,1)S(1)}, bf16[256,1024]{1,0:T(8,128)(2,1)}, u32[]{:S(2)}, u32[]{:S(2)}) collective-permute-start(bf16[256,1024]{1,0:T(8,128)(2,1)S(1)} %slice.143.refs_1_), channel_id=1, source_target_pairs={{0,8},{4,12},{8,0},{12,4},{16,24},{20,28},{24,16},{28,20},{1,9},{5... | collective-permute-start | bytes 1572872 | tf_op jit(solution)/shard_map/ppermute | solution.py:44
  14.5 33.5 %collective-permute-start.3 = (bf16[256,1024]{1,0:T(8,128)(2,1)S(1)}, bf16[256,1024]{1,0:T(8,128)(2,1)}, u32[]{:S(2)}, u32[]{:S(2)}) collective-permute-start(bf16[256,1024]{1,0:T(8,128)(2,1)S(1)} %slice.143.refs_1_), channel_id=1, source_target_pairs={{0,16},{4,20},{8,24},{12,28},{16,0},{20,4},{24,8},{28,12},{1,17},{... | collective-permute-start | bytes 1572872 | tf_op jit(solution)/shard_map/ppermute | solution.py:44
  16.0 32.5 %collective-permute-start.5 = (bf16[256,1024]{1,0:T(8,128)(2,1)S(1)}, bf16[256,1024]{1,0:T(8,128)(2,1)S(1)}, u32[]{:S(2)}, u32[]{:S(2)}) collective-permute-start(bf16[256,1024]{1,0:T(8,128)(2,1)S(1)} %slice.143.refs_1_), channel_id=1, source_target_pairs={{0,24},{4,28},{8,16},{12,20},{16,8},{20,12},{24,0},{28,4},{1,25},{... | collective-permute-start | bytes 1572872 | tf_op jit(solution)/shard_map/ppermute | solution.py:44
  16.9 26.5 %collective-permute-start.15 = (bf16[256,512]{1,0:T(8,128)(2,1)}, bf16[256,512]{1,0:T(8,128)(2,1)}, u32[]{:S(2)}, u32[]{:S(2)}) collective-permute-start(bf16[256,512]{1,0:T(8,128)(2,1)} %get-tuple-element.87), channel_id=1, source_target_pairs={{0,8},{4,12},{8,0},{12,4},{16,24},{20,28},{24,16},{28,20},{1,9},{5... | collective-permute-start | bytes 786440 | tf_op jit(solution)/shard_map/ppermute | solution.py:44
  18.9 26.0 %collective-permute-start.17 = (bf16[256,512]{1,0:T(8,128)(2,1)}, bf16[256,512]{1,0:T(8,128)(2,1)}, u32[]{:S(2)}, u32[]{:S(2)}) collective-permute-start(bf16[256,512]{1,0:T(8,128)(2,1)} %get-tuple-element.87), channel_id=1, source_target_pairs={{0,16},{4,20},{8,24},{12,28},{16,0},{20,4},{24,8},{28,12},{1,17},{... | collective-permute-start | bytes 786440 | tf_op jit(solution)/shard_map/ppermute | solution.py:44
  22.3 10.8 %copy-start.44 = (s32[8]{0:T(128)}, s32[8]{0:T(128)S(1)}, u32[]{:S(2)}) copy-start(s32[8]{0:T(128)S(1)} %select_reduce_fusion.2.starts_ref) | copy-start | bytes 100
  43.5 13.3 %collective-permute-start = (bf16[256,1024]{1,0:T(8,128)(2,1)S(1)}, bf16[256,1024]{1,0:T(8,128)(2,1)}, u32[]{:S(2)}, u32[]{:S(2)}) collective-permute-start(bf16[256,1024]{1,0:T(8,128)(2,1)S(1)} %slice.143.refs_1_), channel_id=1, source_target_pairs={{0,4},{4,0},{8,12},{12,8},{16,20},{20,16},{24,28},{28,24},{1,5},{5... | collective-permute-start | bytes 1572872 | tf_op jit(solution)/shard_map/ppermute | solution.py:44
  44.9 8.6 %collective-permute-start.19 = (bf16[256,512]{1,0:T(8,128)(2,1)}, bf16[256,512]{1,0:T(8,128)(2,1)}, u32[]{:S(2)}, u32[]{:S(2)}) collective-permute-start(bf16[256,512]{1,0:T(8,128)(2,1)} %get-tuple-element.87), channel_id=1, source_target_pairs={{0,24},{4,28},{8,16},{12,20},{16,8},{20,12},{24,0},{28,4},{1,25},{... | collective-permute-start | bytes 786440 | tf_op jit(solution)/shard_map/ppermute | solution.py:44
  48.0 15.3 %collective-permute-start.2 = (bf16[256,1024]{1,0:T(8,128)(2,1)}, bf16[256,1024]{1,0:T(8,128)(2,1)}, u32[]{:S(2)}, u32[]{:S(2)}) collective-permute-start(bf16[256,1024]{1,0:T(8,128)(2,1)} %collective-permute-done.1.refs_3_), channel_id=1, source_target_pairs={{0,4},{4,0},{8,12},{12,8},{16,20},{20,16},{24,28},{28,24},{1,5},{5... | collective-permute-start | bytes 1572872 | tf_op jit(solution)/shard_map/ppermute | solution.py:44
  48.1 15.4 %collective-permute-start.4 = (bf16[256,1024]{1,0:T(8,128)(2,1)}, bf16[256,1024]{1,0:T(8,128)(2,1)}, u32[]{:S(2)}, u32[]{:S(2)}) collective-permute-start(bf16[256,1024]{1,0:T(8,128)(2,1)} %collective-permute-done.3.refs_5_), channel_id=1, source_target_pairs={{0,4},{4,0},{8,12},{12,8},{16,20},{20,16},{24,28},{28,24},{1,5},{5... | collective-permute-start | bytes 1572872 | tf_op jit(solution)/shard_map/ppermute | solution.py:44
  48.5 14.0 %copy-start.31 = (bf16[256,1024]{1,0:T(8,128)(2,1)}, bf16[256,1024]{1,0:T(8,128)(2,1)S(1)}, u32[]{:S(2)}) copy-start(bf16[256,1024]{1,0:T(8,128)(2,1)S(1)} %collective-permute-done.5.refs_7_) | copy-start | bytes 1572868
  48.6 15.3 %collective-permute-start.6 = (bf16[256,1024]{1,0:T(8,128)(2,1)S(1)}, bf16[256,1024]{1,0:T(8,128)(2,1)}, u32[]{:S(2)}, u32[]{:S(2)}) collective-permute-start(bf16[256,1024]{1,0:T(8,128)(2,1)S(1)} %collective-permute-done.5.refs_7_), channel_id=1, source_target_pairs={{0,4},{4,0},{8,12},{12,8},{16,20},{20,16},{24,28},{28,24},{1,5},{5... | collective-permute-start | bytes 1572872 | tf_op jit(solution)/shard_map/ppermute | solution.py:44
  53.4 19.8 %collective-permute-start.14 = (bf16[256,512]{1,0:T(8,128)(2,1)}, bf16[256,512]{1,0:T(8,128)(2,1)}, u32[]{:S(2)}, u32[]{:S(2)}) collective-permute-start(bf16[256,512]{1,0:T(8,128)(2,1)} %get-tuple-element.87), channel_id=1, source_target_pairs={{0,4},{4,0},{8,12},{12,8},{16,20},{20,16},{24,28},{28,24},{1,5},{5... | collective-permute-start | bytes 786440 | tf_op jit(solution)/shard_map/ppermute | solution.py:44
  56.8 21.3 %collective-permute-start.16 = (bf16[256,512]{1,0:T(8,128)(2,1)}, bf16[256,512]{1,0:T(8,128)(2,1)}, u32[]{:S(2)}, u32[]{:S(2)}) collective-permute-start(bf16[256,512]{1,0:T(8,128)(2,1)} %collective-permute-done.15), channel_id=1, source_target_pairs={{0,4},{4,0},{8,12},{12,8},{16,20},{20,16},{24,28},{28,24},{1,5},{5... | collective-permute-start | bytes 786440 | tf_op jit(solution)/shard_map/ppermute | solution.py:44
  63.4 16.4 %collective-permute-start.18 = (bf16[256,512]{1,0:T(8,128)(2,1)}, bf16[256,512]{1,0:T(8,128)(2,1)S(1)}, u32[]{:S(2)}, u32[]{:S(2)}) collective-permute-start(bf16[256,512]{1,0:T(8,128)(2,1)} %collective-permute-done.17), channel_id=1, source_target_pairs={{0,4},{4,0},{8,12},{12,8},{16,20},{20,16},{24,28},{28,24},{1,5},{5... | collective-permute-start | bytes 786440 | tf_op jit(solution)/shard_map/ppermute | solution.py:44
  63.4 24.8 %collective-permute-start.20 = (bf16[256,512]{1,0:T(8,128)(2,1)}, bf16[256,512]{1,0:T(8,128)(2,1)S(1)}, u32[]{:S(2)}, u32[]{:S(2)}) collective-permute-start(bf16[256,512]{1,0:T(8,128)(2,1)} %collective-permute-done.19), channel_id=1, source_target_pairs={{0,4},{4,0},{8,12},{12,8},{16,20},{20,16},{24,28},{28,24},{1,5},{5... | collective-permute-start | bytes 786440 | tf_op jit(solution)/shard_map/ppermute | solution.py:44
  71.6 15.0 %collective-permute-start.8 = (bf16[512,512]{1,0:T(8,128)(2,1)}, bf16[512,512]{1,0:T(8,128)(2,1)S(1)}, u32[]{:S(2)}, u32[]{:S(2)}) collective-permute-start(bf16[512,512]{1,0:T(8,128)(2,1)} %get-tuple-element.41), channel_id=1, source_target_pairs={{0,8},{4,12},{8,0},{12,4},{16,24},{20,28},{24,16},{28,20},{1,9},{5... | collective-permute-start | bytes 1572872 | tf_op jit(solution)/shard_map/ppermute | solution.py:44
  76.6 25.1 %collective-permute-start.10 = (bf16[512,512]{1,0:T(8,128)(2,1)}, bf16[512,512]{1,0:T(8,128)(2,1)S(1)}, u32[]{:S(2)}, u32[]{:S(2)}) collective-permute-start(bf16[512,512]{1,0:T(8,128)(2,1)} %get-tuple-element.41), channel_id=1, source_target_pairs={{0,16},{4,20},{8,24},{12,28},{16,0},{20,4},{24,8},{28,12},{1,17},{... | collective-permute-start | bytes 1572872 | tf_op jit(solution)/shard_map/ppermute | solution.py:44
  79.8 24.3 %collective-permute-start.7 = (bf16[512,512]{1,0:T(8,128)(2,1)}, bf16[512,512]{1,0:T(8,128)(2,1)S(1)}, u32[]{:S(2)}, u32[]{:S(2)}) collective-permute-start(bf16[512,512]{1,0:T(8,128)(2,1)} %get-tuple-element.41), channel_id=1, source_target_pairs={{0,4},{4,0},{8,12},{12,8},{16,20},{20,16},{24,28},{28,24},{1,5},{5... | collective-permute-start | bytes 1572872 | tf_op jit(solution)/shard_map/ppermute | solution.py:44
  79.8 23.8 %collective-permute-start.12 = (bf16[512,512]{1,0:T(8,128)(2,1)}, bf16[512,512]{1,0:T(8,128)(2,1)S(1)}, u32[]{:S(2)}, u32[]{:S(2)}) collective-permute-start(bf16[512,512]{1,0:T(8,128)(2,1)} %get-tuple-element.41), channel_id=1, source_target_pairs={{0,24},{4,28},{8,16},{12,20},{16,8},{20,12},{24,0},{28,4},{1,25},{... | collective-permute-start | bytes 1572872 | tf_op jit(solution)/shard_map/ppermute | solution.py:44
  86.6 19.2 %collective-permute-start.9 = (bf16[512,512]{1,0:T(8,128)(2,1)S(1)}, bf16[512,512]{1,0:T(8,128)(2,1)S(1)}, u32[]{:S(2)}, u32[]{:S(2)}) collective-permute-start(bf16[512,512]{1,0:T(8,128)(2,1)S(1)} %collective-permute-done.8), channel_id=1, source_target_pairs={{0,4},{4,0},{8,12},{12,8},{16,20},{20,16},{24,28},{28,24},{1,5},{5... | collective-permute-start | bytes 1572872 | tf_op jit(solution)/shard_map/ppermute | solution.py:44
  101.7 5.7 collective-permute-start.11
  103.6 5.5 collective-permute-start.13
  126.9 106.3 %all-gather.2.cloned.1.call-start = ((), (), s32[]{:S(2)}) async-start(), calls=%async_computation.3 | async-start | bytes 21233664 | tf_op jit(solution)/shard_map/all_gather | solution.py:365
  127.5 230.6 %all-reduce.7.cloned.1.call-start = ((), (), s32[]{:S(2)}) async-start(), calls=%async_computation.4 | async-start | bytes 4194304 | tf_op jit(solution)/shard_map/psum | solution.py:447
  129.5 92.7 %copy-start.10 = (bf16[512,2048]{1,0:T(8,128)(2,1)S(1)}, bf16[512,2048]{1,0:T(8,128)(2,1)}, u32[]{:S(2)}) copy-start(bf16[512,2048]{1,0:T(8,128)(2,1)} %dynamic-slice_dynamic-update-slice_fusion.56) | copy-start | bytes 6291460
  271.5 353.3 %all-reduce.9.cloned.1.call-start = ((), (), s32[]{:S(2)}) async-start(), calls=%async_computation.7 | async-start | bytes 8388608 | tf_op jit(solution)/shard_map/psum | solution.py:450
  393.7 23.4 %collective-permute-start.21 = (bf16[4,512,512]{2,1,0:T(8,128)(2,1)}, bf16[4,512,512]{2,1,0:T(8,128)(2,1)}, u32[]{:S(2)}, u32[]{:S(2)}) collective-permute-start(bf16[4,512,512]{2,1,0:T(8,128)(2,1)} %bitcast.16), channel_id=1, source_target_pairs={{0,4},{4,0},{8,12},{12,8},{16,20},{20,16},{24,28},{28,24},{1,5},{5... | collective-permute-start | bytes 6291464 | tf_op jit(solution)/shard_map/ppermute | solution.py:44
  419.3 10.6 %copy-start.19 = (f32[512,768]{1,0:T(8,128)S(1)}, f32[512,768]{1,0:T(8,128)}, u32[]{:S(2)}) copy-start(f32[512,768]{1,0:T(8,128)} %get-tuple-element.48) | copy-start | bytes 4718596
  419.3 10.6 %copy-start.26 = (f32[512,512]{1,0:T(8,128)S(1)}, f32[512,512]{1,0:T(8,128)}, u32[]{:S(2)}) copy-start(f32[512,512]{1,0:T(8,128)} %get-tuple-element.51) | copy-start | bytes 3145732
  419.4 15.8 %collective-permute-start.24 = (bf16[512,512]{1,0:T(8,128)(2,1)S(1)}, bf16[512,512]{1,0:T(8,128)(2,1)S(1)}, u32[]{:S(2)}, u32[]{:S(2)}) collective-permute-start(bf16[512,512]{1,0:T(8,128)(2,1)S(1)} %get-tuple-element.95), channel_id=1, source_target_pairs={{0,24},{4,28},{8,16},{12,20},{16,8},{20,12},{24,0},{28,4},{1,25},{... | collective-permute-start | bytes 1572872 | tf_op jit(solution)/shard_map/ppermute | solution.py:44
  420.6 29.6 %collective-permute-start.23 = (bf16[512,512]{1,0:T(8,128)(2,1)S(1)}, bf16[512,512]{1,0:T(8,128)(2,1)S(1)}, u32[]{:S(2)}, u32[]{:S(2)}) collective-permute-start(bf16[512,512]{1,0:T(8,128)(2,1)S(1)} %get-tuple-element.96), channel_id=1, source_target_pairs={{0,16},{4,20},{8,24},{12,28},{16,0},{20,4},{24,8},{28,12},{1,17},{... | collective-permute-start | bytes 1572872 | tf_op jit(solution)/shard_map/ppermute | solution.py:44
  427.1 25.0 %collective-permute-start.22 = (bf16[512,512]{1,0:T(8,128)(2,1)S(1)}, bf16[512,512]{1,0:T(8,128)(2,1)S(1)}, u32[]{:S(2)}, u32[]{:S(2)}) collective-permute-start(bf16[512,512]{1,0:T(8,128)(2,1)S(1)} %get-tuple-element.94), channel_id=1, source_target_pairs={{0,8},{4,12},{8,0},{12,4},{16,24},{20,28},{24,16},{28,20},{1,9},{5... | collective-permute-start | bytes 1572872 | tf_op jit(solution)/shard_map/ppermute | solution.py:44
  431.4 28.4 %copy-start.25 = (f32[512,128]{1,0:T(8,128)S(1)}, f32[512,128]{1,0:T(8,128)}, u32[]{:S(2)}) copy-start(f32[512,128]{1,0:T(8,128)} %pad_maximum_fusion.5.refs_10_) | copy-start | bytes 786436
  472.1 179.8 %reduce-scatter.5.cloned.1.call-start = ((), (), s32[]{:S(2)}) async-start(), calls=%async_computation.6 | async-start | bytes 7077888 | tf_op jit(solution)/shard_map/reduce_scatter | solution.py:503
  479.0 181.9 %reduce-scatter.3.cloned.1.call-start = ((), (), s32[]{:S(2)}) async-start(), calls=%async_computation.5 | async-start | bytes 14155776 | tf_op jit(solution)/shard_map/reduce_scatter | solution.py:503
  499.8 11.6 %collective-permute-start.25 = (bf16[4,256,1024]{2,1,0:T(8,128)(2,1)S(1)}, bf16[4,256,1024]{2,1,0:T(8,128)(2,1)S(1)}, u32[]{:S(2)}, u32[]{:S(2)}) collective-permute-start(bf16[4,256,1024]{2,1,0:T(8,128)(2,1)S(1)} %slice.131), channel_id=1, source_target_pairs={{0,4},{4,0},{8,12},{12,8},{16,20},{20,16},{24,28},{28,24},{1,5},{5... | collective-permute-start | bytes 6291464 | tf_op jit(solution)/shard_map/ppermute | solution.py:44
  503.4 4.0 collective-permute-start.29
  507.9 15.7 %collective-permute-start.32 = (bf16[256,512]{1,0:T(8,128)(2,1)S(1)}, bf16[256,512]{1,0:T(8,128)(2,1)S(1)}, u32[]{:S(2)}, u32[]{:S(2)}) collective-permute-start(bf16[256,512]{1,0:T(8,128)(2,1)S(1)} %get-tuple-element.98), channel_id=1, source_target_pairs={{0,24},{4,28},{8,16},{12,20},{16,8},{20,12},{24,0},{28,4},{1,25},{... | collective-permute-start | bytes 786440 | tf_op jit(solution)/shard_map/ppermute | solution.py:44
  508.0 20.0 %collective-permute-start.31 = (bf16[256,512]{1,0:T(8,128)(2,1)S(1)}, bf16[256,512]{1,0:T(8,128)(2,1)S(1)}, u32[]{:S(2)}, u32[]{:S(2)}) collective-permute-start(bf16[256,512]{1,0:T(8,128)(2,1)S(1)} %get-tuple-element.99), channel_id=1, source_target_pairs={{0,16},{4,20},{8,24},{12,28},{16,0},{20,4},{24,8},{28,12},{1,17},{... | collective-permute-start | bytes 786440 | tf_op jit(solution)/shard_map/ppermute | solution.py:44
  509.0 21.9 %collective-permute-start.30 = (bf16[256,512]{1,0:T(8,128)(2,1)S(1)}, bf16[256,512]{1,0:T(8,128)(2,1)S(1)}, u32[]{:S(2)}, u32[]{:S(2)}) collective-permute-start(bf16[256,512]{1,0:T(8,128)(2,1)S(1)} %get-tuple-element.97), channel_id=1, source_target_pairs={{0,8},{4,12},{8,0},{12,4},{16,24},{20,28},{24,16},{28,20},{1,9},{5... | collective-permute-start | bytes 786440 | tf_op jit(solution)/shard_map/ppermute | solution.py:44
  512.6 30.6 %collective-permute-start.28 = (bf16[256,1024]{1,0:T(8,128)(2,1)S(1)}, bf16[256,1024]{1,0:T(8,128)(2,1)S(1)}, u32[]{:S(2)}, u32[]{:S(2)}) collective-permute-start(bf16[256,1024]{1,0:T(8,128)(2,1)S(1)} %get-tuple-element.92), channel_id=1, source_target_pairs={{0,24},{4,28},{8,16},{12,20},{16,8},{20,12},{24,0},{28,4},{1,25},{... | collective-permute-start | bytes 1572872 | tf_op jit(solution)/shard_map/ppermute | solution.py:44
  512.7 40.0 %collective-permute-start.27 = (bf16[256,1024]{1,0:T(8,128)(2,1)S(1)}, bf16[256,1024]{1,0:T(8,128)(2,1)S(1)}, u32[]{:S(2)}, u32[]{:S(2)}) collective-permute-start(bf16[256,1024]{1,0:T(8,128)(2,1)S(1)} %get-tuple-element.93), channel_id=1, source_target_pairs={{0,16},{4,20},{8,24},{12,28},{16,0},{20,4},{24,8},{28,12},{1,17},{... | collective-permute-start | bytes 1572872 | tf_op jit(solution)/shard_map/ppermute | solution.py:44
  523.6 29.2 %collective-permute-start.26 = (bf16[256,1024]{1,0:T(8,128)(2,1)S(1)}, bf16[256,1024]{1,0:T(8,128)(2,1)S(1)}, u32[]{:S(2)}, u32[]{:S(2)}) collective-permute-start(bf16[256,1024]{1,0:T(8,128)(2,1)S(1)} %get-tuple-element.91), channel_id=1, source_target_pairs={{0,8},{4,12},{8,0},{12,4},{16,24},{20,28},{24,16},{28,20},{1,9},{5... | collective-permute-start | bytes 1572872 | tf_op jit(solution)/shard_map/ppermute | solution.py:44
  523.7 31.0 %copy-start.20 = (f32[512,2048]{1,0:T(8,128)}, f32[512,2048]{1,0:T(8,128)S(1)}, u32[]{:S(2)}) copy-start(f32[512,2048]{1,0:T(8,128)S(1)} %dynamic-slice_dynamic-update-slice_fusion.24) | copy-start | bytes 12582916
  629.8 1.7 collective-permute-start.38
  631.5 3.8 collective-permute-start.39
  635.4 3.8 collective-permute-start.40
  639.2 6.6 collective-permute-start.41
  645.8 5.5 collective-permute-start.42
  651.9 35.2 %copy-start.38 = (f32[4352]{0:T(1024)S(1)}, f32[4352]{0:T(1024)}, u32[]{:S(2)}) copy-start(f32[4352]{0:T(1024)} %param.17) | copy-start | bytes 52228
  651.9 35.2 %copy-start.42 = (f32[4352]{0:T(1024)S(1)}, f32[4352]{0:T(1024)}, u32[]{:S(2)}) copy-start(f32[4352]{0:T(1024)} %param.19) | copy-start | bytes 52228
  651.9 35.2 %copy-start.43 = (f32[4352]{0:T(1024)S(1)}, f32[4352]{0:T(1024)}, u32[]{:S(2)}) copy-start(f32[4352]{0:T(1024)} %param.18) | copy-start | bytes 52228
  665.0 2.8 collective-permute-start.33
  668.4 3.7 collective-permute-start.34
  672.7 3.7 collective-permute-start.35
  676.9 3.7 collective-permute-start.36
  681.2 4.6 collective-permute-start.37
  (34 other events, 165.2 us)
Sparse Core Ops, SparseCore 0:
  127.1 91.7 all-reduce.4
  271.6 86.4 all-reduce.6
  472.2 152.4 all-reduce.8
Sparse Core Ops, SparseCore 1:
  129.5 103.8 all-gather.1
  479.1 86.0 reduce-scatter.4
  568.5 92.3 reduce-scatter.2

commit v2 on v1

v2 whole, which is shorter than its diff:
```python
import functools

import jax
import jax.numpy as jnp
from jax import lax
from jax.experimental import pallas as pl
from jax.experimental.pallas import tpu as pltpu
from jax.sharding import PartitionSpec as P

HEADS = 16
KV = 8
HD = 128
FF = 6144
SPAN = 128
CHUNK = 4
TILE = 256
WIDE = 512
VMEM_LIMIT = 60 * 1024 * 1024

eps_norm = 1e-06
rope_base = 1000000.0
learn_rate = 100.0
gain_rate = 4000.0
momentum_decay = 0.5
average_decay = 0.5
score_scale = HD ** (-0.5)
far = -1e30

bf16 = jnp.bfloat16
f32 = jnp.float32
plain_dims = (((1,), (0,)), ((), ()))
last_dims = (((1,), (1,)), ((), ()))
first_dims = (((0,), (0,)), ((), ()))


def dot(a, b, dims=plain_dims):
    return lax.dot_general(a, b, dims, preferred_element_type=f32)


def cost(micros):
    return pl.CostEstimate(flops=int(micros * 1.0e9), bytes_accessed=int(micros * 3.4e6), transcendentals=0)


def params(**more):
    return pltpu.CompilerParams(vmem_limit_bytes=VMEM_LIMIT, **more)


def swap(array, axis, distance):
    count = lax.axis_size(axis)
    return lax.ppermute(array, axis, [(i, i ^ distance) for i in range(count)])


def gather_chips(own):
    return [own] + [swap(own, "dp", k) for k in (2, 4, 6)]


def gather_cores(outer):
    inner = [swap(block, "dp", 1) for block in outer]
    return [block for pair in zip(outer, inner) for block in pair]


def scatter_small(even, odd):
    came = swap(odd, "dp", 1)
    half = (even.astype(f32) + came.astype(f32)).astype(bf16)
    return [half[0]] + [swap(half[k], "dp", 2 * k) for k in (1, 2, 3)]


def add_pair(a, b):
    return (a.astype(f32) + b.astype(f32)).astype(bf16)


def sum_all(value):
    for axis in ("dp", "mp"):
        distance = 1
        while distance < lax.axis_size(axis):
            value = value + swap(value, axis, distance)
            distance *= 2
    return value


def place_of(me_ref, k, parts):
    return me_ref[0] ^ k if parts > 1 else 0


def columns_at(ref, block, width):
    return ref[:, pl.ds(pl.multiple_of(block * width, width), width)]


def turned(normed, cosine, sine):
    return normed * cosine + pltpu.roll(normed, HD // 2, 1) * sine


def turned_back(gradient, cosine, sine):
    return gradient * cosine + pltpu.roll(gradient * sine, HD // 2, 1)


def unit_scale(values):
    return lax.rsqrt(jnp.mean(values * values, axis=-1, keepdims=True) + eps_norm)


def norm_back(unit, scale, gain, gradient):
    e = gradient * gain
    return scale * (e - unit * jnp.mean(e * unit, axis=-1, keepdims=True))


def project_kernel(parts, q_tiles, me_ref, h_ref, *refs):
    w_refs = refs[:parts]
    cos_ref, sin_ref, gain_ref, q_ref, kv_ref, lin_ref = refs[parts:]
    tile = pl.program_id(0)
    depth = w_refs[0].shape[0]
    total = None
    for k, w_ref in enumerate(w_refs):
        term = dot(columns_at(h_ref, place_of(me_ref, k, parts), depth), w_ref[...])
        total = term if total is None else total + term
    per_tile = TILE // HD

    def normed_to(out_ref, gain):
        for part in range(per_tile):
            at = slice(part * HD, (part + 1) * HD)
            values = total[:, at]
            lin_ref[:, at] = values
            normed = values * unit_scale(values) * gain
            out_ref[:, at] = turned(normed, cos_ref[...], sin_ref[...]).astype(bf16)

    @pl.when(tile < q_tiles)
    def _():
        normed_to(q_ref, gain_ref[0:1])

    @pl.when(tile == q_tiles)
    def _():
        normed_to(kv_ref, gain_ref[1:2])

    @pl.when(tile > q_tiles)
    def _():
        kv_ref[...] = total.astype(bf16)


def span_limits(own_ref, starts_ref, i, group):
    span = own_ref[i]
    first = span * SPAN
    lane = lax.broadcasted_iota(jnp.int32, (1, group * SPAN), 1)
    places = first + (lane & (SPAN - 1))
    low = jnp.int32(0)
    begin = jnp.zeros((1, group * SPAN), jnp.int32)
    for d in range(starts_ref.shape[0]):
        start = starts_ref[d]
        low = jnp.maximum(low, jnp.where(start <= first, start, 0))
        begin = jnp.maximum(begin, jnp.where(start <= places, start, 0))
    return span, low // SPAN, places, begin


def key_rows(inverse_ref, newest, b):
    return pl.multiple_of(inverse_ref[jnp.maximum(newest - b, 0)] * SPAN, SPAN)


def allowed_keys(newest, places, begin):
    row = lax.broadcasted_iota(jnp.int32, (CHUNK * SPAN, 1), 0)
    key = newest * SPAN + (row & (SPAN - 1)) - (row & ~(SPAN - 1))
    return (key <= places) & (key >= begin)


def stacked(ref, i, head, group):
    rows = pl.ds(i * SPAN, SPAN)
    return jnp.concatenate([ref[rows, h * HD : (h + 1) * HD] for h in range(head * group, (head + 1) * group)], axis=0)


def head_columns(first, heads, kv_heads):
    keys = [pl.ds(pl.multiple_of((first + h) * HD, HD), HD) for h in range(heads)]
    values = [pl.ds(pl.multiple_of((first + h + kv_heads) * HD, HD), HD) for h in range(heads)]
    return keys, values


def load_parts(part_refs, target_ref, sem_ref, first):
    rows = part_refs[0].shape[0]
    return [
        pltpu.make_async_copy(ref, target_ref.at[pl.ds(k * rows, rows)], sem_ref.at[first + k])
        for k, ref in enumerate(part_refs)
    ]


def attend_kernel(group, heads, parts, own_ref, inverse_ref, starts_ref, q_ref, *refs):
    kv_parts = refs[:parts]
    turned_ref, low_ref, lse_ref, kv_ref, sem_ref = refs[parts:]
    g = pl.program_id(0)
    kv_heads = pl.num_programs(0) * heads
    kv_copies = load_parts(kv_parts, kv_ref, sem_ref, 0)

    @pl.when(g == 0)
    def _():
        for copy in kv_copies:
            copy.start()
        for copy in kv_copies:
            copy.wait()

    key_at, value_at = head_columns(g * heads, heads, kv_heads)
    wide = group * SPAN
    for i in range(own_ref.shape[0]):
        span, low, places, begin = span_limits(own_ref, starts_ref, i, group)
        queries = [stacked(q_ref, i, h, group) for h in range(heads)]
        count = (span - low) // CHUNK + 1

        def step(c, carry):
            newest = span - c * CHUNK
            at = [key_rows(inverse_ref, newest, b) for b in range(CHUNK)]
            allowed = allowed_keys(newest, places, begin)
            made = []
            for h, (top, weight, total) in enumerate(carry):
                keys = jnp.concatenate([kv_ref[pl.ds(a, SPAN), key_at[h]] for a in at], axis=0)
                values = jnp.concatenate([kv_ref[pl.ds(a, SPAN), value_at[h]] for a in at], axis=0)
                scores = jnp.where(allowed, dot(keys, queries[h], last_dims), far)
                new_top = jnp.maximum(top, jnp.max(scores, axis=0, keepdims=True))
                probs = jnp.exp((scores - new_top) * score_scale)
                shrink = jnp.exp((top - new_top) * score_scale)
                weight = weight * shrink + jnp.sum(probs, axis=0, keepdims=True)
                total = total * shrink + dot(values, probs.astype(bf16), first_dims)
                made.append((new_top, weight, total))
            return tuple(made)

        start = (jnp.full((1, wide), far, f32), jnp.zeros((1, wide), f32), jnp.zeros((HD, wide), f32))
        made = lax.fori_loop(0, count, step, (start,) * heads)
        for h, (top, weight, total) in enumerate(made):
            output = total / weight
            place = i * heads + h
            turned_ref[place] = output
            lse_ref[place] = jnp.broadcast_to(top * score_scale + jnp.log(weight), (8, wide))
            back = output.T.astype(bf16)
            for k in range(group):
                column = pl.multiple_of(((g * heads + h) * group + k) * HD, HD)
                low_ref[pl.ds(i * SPAN, SPAN), pl.ds(column, HD)] = back[k * SPAN : (k + 1) * SPAN]


def project_out_kernel(parts, me_ref, low_ref, *refs):
    out_parts = refs[:parts]
    o_ref = refs[parts]
    width = out_parts[0].shape[0]
    block = min(width, TILE)
    for k, w_ref in enumerate(out_parts):
        first = place_of(me_ref, k, parts) * width
        for b in range(width // block):
            at = pl.multiple_of(first + b * block, block)
            term = dot(low_ref[...], w_ref[b * block : (b + 1) * block], last_dims)
            o_ref[:, pl.ds(at, block)] = term.astype(bf16)


def mlp_kernel(x_ref, s_ref, gain_ref, c_ref, wg_ref, wu_ref, wd_ref, y_ref, h_ref, dg_ref, du_ref, a_ref):
    @pl.when(pl.program_id(0) == 0)
    def _():
        def rows_of(r, unused):
            at = pl.ds(pl.multiple_of(r * 64, 64), 64)
            y = x_ref[at, :].astype(f32) + s_ref[at, :].astype(f32)
            y_ref[at, :] = y
            h_ref[at, :] = (y * unit_scale(y) * gain_ref[...]).astype(bf16)
            return unused

        lax.fori_loop(0, x_ref.shape[0] // 64, rows_of, 0, unroll=2)

    hidden = h_ref[...]
    gate = dot(hidden, wg_ref[...])
    up = dot(hidden, wu_ref[...])
    grad = dot(c_ref[...], wd_ref[...])
    sig = 1.0 / (1.0 + jnp.exp(-gate))
    silu = gate * sig
    a_ref[...] = (silu * up).astype(bf16)
    dg_ref[...] = (grad * up * (sig + silu * (1.0 - sig))).astype(bf16)
    du_ref[...] = (grad * silu).astype(bf16)


def mlp_back_kernel(dg_ref, du_ref, wg_ref, wu_ref, dh_ref):
    dh_ref[...] = (dot(dg_ref[...], wg_ref[...], last_dims) + dot(du_ref[...], wu_ref[...], last_dims)).astype(bf16)


def rows_by_rows_kernel(a_ref, w_ref, o_ref):
    o_ref[...] = dot(a_ref[...], w_ref[...], last_dims).astype(bf16)


def residual_back_kernel(parts, share, me_ref, y_ref, c_ref, s_ref, gain_ref, *refs):
    out_parts = refs[:parts]
    dy_ref, low_ref, do_ref, dgain_ref = refs[parts:]

    @pl.when(pl.program_id(0) == 0)
    def _():
        dgain_ref[...] = jnp.zeros_like(dgain_ref)

    def rows_of(r, dgain):
        at = pl.ds(pl.multiple_of(r * 32, 32), 32)
        y = y_ref[at, :]
        scale = unit_scale(y)
        unit = y * scale
        grad = s_ref[at, :].astype(f32)
        dy = c_ref[at, :].astype(f32) + norm_back(unit, scale, gain_ref[...], grad)
        dy_ref[at, :] = dy
        low_ref[at, :] = dy.astype(bf16)
        return dgain + jnp.sum(grad * unit, axis=0, keepdims=True)

    zeros = jnp.zeros(dgain_ref.shape, f32)
    dgain_ref[...] += share * lax.fori_loop(0, y_ref.shape[0] // 32, rows_of, zeros, unroll=2)
    total = None
    depth = out_parts[0].shape[0]
    for k, w_ref in enumerate(out_parts):
        term = dot(columns_at(low_ref, place_of(me_ref, k, parts), depth), w_ref[...])
        total = term if total is None else total + term
    do_ref[...] = total.astype(bf16)


def attend_back_kernel(group, heads, parts, outs, own_ref, inverse_ref, starts_ref, q_ref, *refs):
    kv_parts = refs[:parts]
    do_ref, turned_ref, lse_ref, lin_ref, cos_ref, sin_ref, gain_ref = refs[parts : parts + 7]
    dq_ref, dgain_ref = refs[parts + 7 : parts + 9]
    dkv_refs = refs[parts + 9 : parts + 9 + outs]
    kv_ref, acc_ref, sem_ref = refs[parts + 9 + outs :]
    g = pl.program_id(0)
    kv_heads = pl.num_programs(0) * heads
    copies = load_parts(kv_parts, kv_ref, sem_ref, 0)

    @pl.when(g == 0)
    def _():
        for copy in copies:
            copy.start()

    acc_ref[...] = jnp.zeros_like(acc_ref)

    @pl.when(g == 0)
    def _():
        for copy in copies:
            copy.wait()

    key_at, value_at = head_columns(g * heads, heads, kv_heads)
    wide = group * SPAN
    dgain = jnp.zeros((1, HD), f32)
    for i in range(own_ref.shape[0]):
        span, low, places, begin = span_limits(own_ref, starts_ref, i, group)
        queries = [stacked(q_ref, i, h, group) for h in range(heads)]
        grads = [stacked(do_ref, i, h, group) for h in range(heads)]
        deltas = [
            jnp.sum(grads[h].astype(f32).T * turned_ref[i * heads + h], axis=0, keepdims=True) for h in range(heads)
        ]
        lses = [lse_ref[i * heads + h, :1] for h in range(heads)]
        count = (span - low) // CHUNK + 1

        def step(c, carry):
            newest = span - c * CHUNK
            at = [key_rows(inverse_ref, newest, b) for b in range(CHUNK)]
            allowed = allowed_keys(newest, places, begin)
            made = []
            for h, grad_query in enumerate(carry):
                keys = jnp.concatenate([kv_ref[pl.ds(a, SPAN), key_at[h]] for a in at], axis=0)
                values = jnp.concatenate([kv_ref[pl.ds(a, SPAN), value_at[h]] for a in at], axis=0)
                scores = dot(keys, queries[h], last_dims) * score_scale
                probs = jnp.exp(jnp.where(allowed, scores - lses[h], far))
                grad_probs = dot(values, grads[h], last_dims)
                grad_scores = (probs * (grad_probs - deltas[h])).astype(bf16)
                grad_values = dot(probs.astype(bf16), grads[h])
                grad_keys = dot(grad_scores, queries[h]) * score_scale
                left = 2 * h * HD
                for b, a in enumerate(at):
                    rows = slice(b * SPAN, (b + 1) * SPAN)
                    acc_ref[pl.ds(a, SPAN), left : left + HD] += grad_keys[rows]
                    acc_ref[pl.ds(a, SPAN), left + HD : left + 2 * HD] += grad_values[rows]
                made.append(grad_query + dot(keys, grad_scores, first_dims))
            return tuple(made)

        made = lax.fori_loop(0, count, step, (jnp.zeros((HD, wide), f32),) * heads)
        place = pl.ds(i * SPAN, SPAN)
        for h, grad_query in enumerate(made):
            grad_query = (grad_query * score_scale).T
            for k in range(group):
                at = slice((h * group + k) * HD, (h * group + k + 1) * HD)
                back = turned_back(grad_query[k * SPAN : (k + 1) * SPAN], cos_ref[place, :], sin_ref[place, :])
                lin = lin_ref[place, at]
                scale = unit_scale(lin)
                unit = lin * scale
                dgain = dgain + jnp.sum(back * unit, axis=0, keepdims=True)
                dq_ref[place, at] = norm_back(unit, scale, gain_ref[...], back).astype(bf16)
    dgain_ref[...] = jnp.broadcast_to(dgain, dgain_ref.shape)

    rows = acc_ref.shape[0] // parts
    for k in range(parts):
        dkv_refs[k % outs][pl.ds((k // outs) * rows, rows), :] = acc_ref[pl.ds(k * rows, rows), :].astype(bf16)


def key_back_kernel(parts, terms, kv_heads, me_ref, *refs):
    term_refs = refs[:terms]
    lin_ref, cos_ref, sin_ref, gain_ref, dq_ref, x_ref = refs[terms : terms + 6]
    w_refs = refs[terms + 6 : terms + 6 + parts]
    dkv_ref, dgain_k_ref, dgain_ref, dh_ref, unit_ref = refs[terms + 6 + parts :]
    dgain = jnp.zeros((1, HD), f32)

    def total(begin):
        value = None
        for ref in term_refs:
            term = ref[:, begin : begin + HD].astype(f32)
            value = term if value is None else value + term
        return value

    for g in range(kv_heads):
        at = slice(g * HD, (g + 1) * HD)
        back = turned_back(total(2 * g * HD), cos_ref[...], sin_ref[...])
        lin = lin_ref[:, at]
        scale = unit_scale(lin)
        unit = lin * scale
        dgain = dgain + jnp.sum(back * unit, axis=0, keepdims=True)
        dkv_ref[:, at] = norm_back(unit, scale, gain_ref[...], back).astype(bf16)
        dkv_ref[:, (kv_heads + g) * HD : (kv_heads + g + 1) * HD] = total((2 * g + 1) * HD).astype(bf16)
    dgain_k_ref[...] = jnp.broadcast_to(dgain, dgain_k_ref.shape)

    def rows_of(r, unused):
        at = pl.ds(pl.multiple_of(r * 64, 64), 64)
        x = x_ref[at, :].astype(f32)
        unit_ref[at, :] = x * unit_scale(x)
        return unused

    lax.fori_loop(0, x_ref.shape[0] // 64, rows_of, 0, unroll=2)
    width = w_refs[0].shape[0]
    block = min(width, TILE)
    q_width = dq_ref.shape[1]
    for k, w_ref in enumerate(w_refs):
        first = place_of(me_ref, k, parts) * width
        for b in range(width // block):
            here = pl.ds(pl.multiple_of(first + b * block, block), block)
            rows = slice(b * block, (b + 1) * block)
            term = dot(dq_ref[...], w_ref[rows, :q_width], last_dims)
            term = term + dot(dkv_ref[...], w_ref[rows, q_width:], last_dims)
            dh_ref[:, here] = term.astype(bf16)
            dgain_ref[:, here] = jnp.sum(term * unit_ref[:, here], axis=0, keepdims=True)


def input_back_kernel(dy_ref, x_ref, s_ref, gain_ref, o_ref):
    def rows_of(r, unused):
        at = pl.ds(pl.multiple_of(r * 32, 32), 32)
        x = x_ref[at, :].astype(f32)
        scale = unit_scale(x)
        back = norm_back(x * scale, scale, gain_ref[...], s_ref[at, :].astype(f32))
        o_ref[at, :] = dy_ref[at, :] + back
        return unused

    lax.fori_loop(0, x_ref.shape[0] // 32, rows_of, 0, unroll=2)


def transpose_kernel(me_ref, x_ref, o_ref):
    o_ref[...] = x_ref[...].T


def transposed(me, lhs, parts, rows):
    tokens, depth = lhs.shape
    rows = rows if parts > 1 else TILE
    return pl.pallas_call(
        transpose_kernel,
        grid_spec=pltpu.PrefetchScalarGridSpec(
            num_scalar_prefetch=1,
            grid=(depth // rows,),
            in_specs=[pl.BlockSpec((tokens, rows), weight_source(parts, depth // rows))],
            out_specs=pl.BlockSpec((rows, tokens), lambda p, _: (p, 0)),
        ),
        out_shape=jax.ShapeDtypeStruct((depth, tokens), bf16),
        compiler_params=params(),
        cost_estimate=cost(5),
        name="transposed",
    )(me, lhs)


def weight_source(parts, steps):
    half = steps // 2

    def source(p, me_ref):
        return (0, me_ref[0] ^ (2 * (p % half) + p // half)) if parts > 1 else (0, p)

    return source


def weight_grad_kernel(outs, count, me_ref, lhs_ref, *refs):
    rhs_refs = refs[:count]
    out_refs = refs[count:]
    step = pl.program_id(0)
    half = pl.num_programs(0) // outs
    for o in range(outs):

        @pl.when((step >= o * half) & (step < (o + 1) * half))
        def _():
            for rhs_ref, out_ref in zip(rhs_refs, out_refs[o * count : (o + 1) * count]):
                out_ref[0] = dot(lhs_ref[...], rhs_ref[...], first_dims).astype(bf16)


def mlp_weight_grad_kernel(h_ref, c_ref, dg_ref, du_ref, a_ref, dgu_ref, down_ref):
    width = a_ref.shape[1]
    dgu_ref[:, :width] = dot(h_ref[...], dg_ref[...], first_dims).astype(bf16)
    dgu_ref[:, width:] = dot(h_ref[...], du_ref[...], first_dims).astype(bf16)
    down_ref[...] = dot(c_ref[...], a_ref[...], first_dims).astype(bf16)


def weight_grad_turned_kernel(outs, lhs_ref, rhs_ref, *out_refs):
    for o, out_ref in enumerate(out_refs):

        @pl.when(pl.program_id(0) == o)
        def _():
            out_ref[...] = dot(lhs_ref[...], rhs_ref[...]).astype(bf16)


def weight_grad(me, lhs, rhs, parts, rows, is_transposed=False):
    tokens = rhs[0].shape[0]
    depth = lhs.size // tokens
    outs = 2 if parts > 1 else 1
    rows = rows if parts > 1 else TILE
    columns = sum(r.shape[1] for r in rhs)
    if is_transposed:
        half = depth // rows // outs
        made = pl.pallas_call(
            functools.partial(weight_grad_turned_kernel, outs),
            grid=(outs,),
            in_specs=[pl.BlockSpec((depth // outs, tokens), lambda p: (p, 0)), pl.BlockSpec(rhs[0].shape, lambda p: (0, 0))],
            out_specs=[pl.BlockSpec((depth // outs, columns), lambda p: (0, 0))] * outs,
            out_shape=[jax.ShapeDtypeStruct((depth // outs, columns), bf16)] * outs,
            compiler_params=params(),
            cost_estimate=cost(1),
            name="weight_grad_turned",
        )(lhs, rhs[0])
        return [[m.reshape(half, rows, columns) for m in made]]
    steps = depth // rows
    half = steps // outs

    def out_spec(o, width):
        return pl.BlockSpec((1, rows, width), lambda p, _: (jnp.clip(p - o * half, 0, half - 1), 0, 0))

    made = pl.pallas_call(
        functools.partial(weight_grad_kernel, outs, len(rhs)),
        grid_spec=pltpu.PrefetchScalarGridSpec(
            num_scalar_prefetch=1,
            grid=(steps,),
            in_specs=[pl.BlockSpec((tokens, rows), weight_source(parts, steps))]
            + [pl.BlockSpec(r.shape, lambda p, _: (0, 0)) for r in rhs],
            out_specs=[out_spec(o, r.shape[1]) for o in range(outs) for r in rhs],
        ),
        out_shape=[jax.ShapeDtypeStruct((half, rows, r.shape[1]), bf16) for o in range(outs) for r in rhs],
        compiler_params=params(),
        cost_estimate=cost(1),
        name="weight_grad",
    )(me, lhs, *rhs)
    return [made[k :: len(rhs)] for k in range(len(rhs))]


def update_kernel(factor_ref, w_ref, m_ref, e_ref, *refs):
    new_w_ref, new_m_ref, new_e_ref = refs[-3:]
    begin = 0
    for g_ref in refs[:-3]:
        at = slice(begin, begin + g_ref.shape[1])
        made = update(w_ref[:, at], m_ref[:, at], e_ref[:, at], g_ref[...].astype(f32), factor_ref[0], learn_rate)
        new_w_ref[:, at], new_m_ref[:, at], new_e_ref[:, at] = made
        begin += g_ref.shape[1]


def update_weights(factor, weights, momentum, average, pieces):
    rows, columns = weights.shape
    step = 32
    spec = pl.BlockSpec((step, columns), lambda n, _: (n, 0))
    shape = jax.ShapeDtypeStruct(weights.shape, f32)
    return pl.pallas_call(
        update_kernel,
        grid_spec=pltpu.PrefetchScalarGridSpec(
            num_scalar_prefetch=1,
            grid=(rows // step,),
            in_specs=[spec, spec, spec]
            + [pl.BlockSpec((step, piece.shape[1]), lambda n, _: (n, 0)) for piece in pieces],
            out_specs=[spec, spec, spec],
        ),
        out_shape=(shape, shape, shape),
        compiler_params=params(),
        cost_estimate=cost(1),
        name="update",
    )(factor, weights, momentum, average, *pieces)


def update(value, state, average, gradient, factor, step_rate):
    clipped = gradient * factor
    state_new = momentum_decay * state + clipped
    value_new = value - step_rate * (clipped + momentum_decay * state_new)
    average_new = average_decay * average + (1.0 - average_decay) * value_new
    return (value_new, state_new, average_new)


def per_device(
    block_input,
    cotangent,
    doc_lengths,
    span_order,
    weights,
    momentum,
    ema_weights,
    gains,
    gain_momentum,
    gain_ema,
):
    tok_count, model_width = block_input.shape
    data_count = lax.axis_size("dp")
    model_count = lax.axis_size("mp")
    me = lax.axis_index("dp").astype(jnp.int32)
    me_array = me[None]
    row_count = weights.shape[0]
    token_total = tok_count * data_count
    span_total = token_total // SPAN
    span_own = tok_count // SPAN
    seq_len = token_total // doc_lengths.shape[0]
    doc_total = doc_lengths.shape[0] * doc_lengths.shape[1]
    q_heads = HEADS // model_count
    kv_heads = KV // model_count
    group = q_heads // kv_heads
    query_width = q_heads * HD
    kv_width = kv_heads * HD
    ff_width = FF // model_count
    qkv_cols = query_width + 2 * kv_width
    out_end = qkv_cols + query_width
    in_pairs = data_count == 8
    parts = data_count if in_pairs else 1
    outs = 2 if in_pairs else 1
    gain_attn = gains[:model_width]
    gain_mlp = gains[model_width : 2 * model_width]
    head_gains = gains[2 * model_width :].reshape(2, HD)

    qkv_own = weights[:, :qkv_cols].astype(bf16)
    if in_pairs:
        qkv_outer = gather_chips(qkv_own)
        later, qkv_own = lax.optimization_barrier((weights, qkv_own))
        out_outer = gather_chips(later[:, qkv_cols:out_end].astype(bf16))
    else:
        later = weights
        qkv_parts = [lax.all_gather(qkv_own, "dp", axis=0, tiled=True)]
        out_own = weights[:, qkv_cols:out_end].astype(bf16)
        out_parts = [lax.all_gather(out_own, "dp", axis=0, tiled=True)]

    doc_ids = jnp.arange(doc_lengths.shape[1], dtype=jnp.int32)
    earlier = doc_ids[None, :] < doc_ids[:, None]
    starts = jnp.sum(jnp.where(earlier[None], doc_lengths[:, None, :], 0), axis=2)
    starts = starts + seq_len * jnp.arange(doc_lengths.shape[0], dtype=jnp.int32)[:, None]
    starts = starts.reshape(doc_total)
    span_ids = jnp.arange(span_total, dtype=jnp.int32)
    inverse = jnp.sum(jnp.where(span_order[None, :] == span_ids[:, None], span_ids[None, :], 0), axis=1)
    if in_pairs:
        inverse = ((inverse // span_own) ^ me) * span_own + inverse % span_own
    own_spans = lax.dynamic_slice(span_order, (me * span_own,), (span_own,))
    home = (own_spans[:, None] * SPAN + jnp.arange(SPAN, dtype=jnp.int32)[None, :]).reshape(tok_count)
    doc_start = jnp.max(jnp.where(starts[None, :] <= home[:, None], starts[None, :], 0), axis=1)
    freqs = rope_base ** (-(2.0 * (jnp.arange(HD, dtype=jnp.int32) % (HD // 2)).astype(f32)) / HD)
    angles = (home - doc_start).astype(f32)[:, None] * freqs[None, :]
    cosine = jnp.cos(angles)
    sine = jnp.sin(angles) * jnp.where(jnp.arange(HD) < HD // 2, -1.0, 1.0)[None, :]

    inputs = block_input.astype(f32)
    normed_low = (inputs * unit_scale(inputs) * gain_attn).astype(bf16)

    normed_turned = transposed(me_array, normed_low, parts, row_count)
    if in_pairs:
        normed_turned, qkv_outer[1] = lax.optimization_barrier((normed_turned, qkv_outer[1]))
        qkv_parts = gather_cores(qkv_outer)

    q_tiles = query_width // TILE
    rows_all = pl.BlockSpec((tok_count, model_width), lambda *_: (0, 0))
    angle_spec = pl.BlockSpec((tok_count, HD), lambda *_: (0, 0))
    part_tile = pl.BlockSpec((model_width // parts, TILE), lambda n, *_: (0, n))
    queries, keys_values, lin = pl.pallas_call(
        functools.partial(project_kernel, parts, q_tiles),
        grid_spec=pltpu.PrefetchScalarGridSpec(
            num_scalar_prefetch=1,
            grid=(qkv_cols // TILE,),
            in_specs=[rows_all]
            + [part_tile] * parts
            + [angle_spec, angle_spec, pl.BlockSpec((2, HD), lambda *_: (0, 0))],
            out_specs=[
                pl.BlockSpec((tok_count, TILE), lambda n, *_: (0, jnp.minimum(n, q_tiles - 1))),
                pl.BlockSpec((tok_count, TILE), lambda n, *_: (0, jnp.maximum(n - q_tiles, 0))),
                pl.BlockSpec((tok_count, TILE), lambda n, *_: (0, jnp.minimum(n, q_tiles))),
            ],
        ),
        out_shape=(
            jax.ShapeDtypeStruct((tok_count, query_width), bf16),
            jax.ShapeDtypeStruct((tok_count, 2 * kv_width), bf16),
            jax.ShapeDtypeStruct((tok_count, query_width + kv_width), f32),
        ),
        compiler_params=params(),
        cost_estimate=cost(6),
        name="project",
    )(me_array, normed_low, *qkv_parts, cosine, sine, head_gains)

    mlp_own = later[:, out_end:].astype(bf16)
    if in_pairs:
        keys_values, out_outer = lax.optimization_barrier((keys_values, out_outer))
        kv_parts = gather_cores(gather_chips(keys_values))
        out_parts = gather_cores(out_outer)
        mlp_own, out_parts, kv_parts = lax.optimization_barrier((mlp_own, out_parts, kv_parts))
    else:
        kv_parts = [lax.all_gather(keys_values, "dp", axis=0, tiled=True)]
    mlp_weights = lax.all_gather(mlp_own, "dp", axis=0, tiled=True)

    heads = kv_heads if in_pairs else 1
    head_steps = kv_heads // heads
    wide = group * SPAN
    anywhere = pl.BlockSpec(memory_space=pl.ANY)
    head_spec = pl.BlockSpec((tok_count, heads * group * HD), lambda g, *_: (0, g))
    q_all = pl.BlockSpec((tok_count, query_width), lambda *_: (0, 0))
    turned_spec = pl.BlockSpec((span_own * heads, HD, wide), lambda g, *_: (g, 0, 0))
    lse_spec = pl.BlockSpec((span_own * heads, 8, wide), lambda g, *_: (g, 0, 0))
    attended, attended_low, lse = pl.pallas_call(
        functools.partial(attend_kernel, group, heads, parts),
        grid_spec=pltpu.PrefetchScalarGridSpec(
            num_scalar_prefetch=3,
            grid=(head_steps,),
            in_specs=[head_spec] + [anywhere] * parts,
            out_specs=[turned_spec, q_all, lse_spec],
            scratch_shapes=[
                pltpu.VMEM((token_total, 2 * kv_width), bf16),
                pltpu.SemaphoreType.DMA((parts,)),
            ],
        ),
        out_shape=(
            jax.ShapeDtypeStruct((span_own * kv_heads, HD, wide), f32),
            jax.ShapeDtypeStruct((tok_count, query_width), bf16),
            jax.ShapeDtypeStruct((span_own * kv_heads, 8, wide), f32),
        ),
        compiler_params=params(),
        cost_estimate=cost(16),
        name="attend",
    )(own_spans, inverse, starts, queries, *kv_parts)
    part_all = pl.BlockSpec((model_width // parts, query_width), lambda *_: (0, 0))
    attn_part = pl.pallas_call(
        functools.partial(project_out_kernel, parts),
        grid_spec=pltpu.PrefetchScalarGridSpec(
            num_scalar_prefetch=1,
            grid=(1,),
            in_specs=[q_all] + [part_all] * parts,
            out_specs=rows_all,
        ),
        out_shape=jax.ShapeDtypeStruct((tok_count, model_width), bf16),
        compiler_params=params(),
        cost_estimate=cost(4),
        name="project_out",
    )(me_array, attended_low, *out_parts)

    attn_sum = lax.psum(attn_part, "mp")

    tiles = ff_width // TILE
    gain_spec = pl.BlockSpec((1, model_width), lambda *_: (0, 0))
    tile_spec = pl.BlockSpec((tok_count, TILE), lambda n: (0, n))
    hidden_shape = jax.ShapeDtypeStruct((tok_count, ff_width), bf16)
    low_shape = jax.ShapeDtypeStruct((tok_count, model_width), bf16)
    wide_shape = jax.ShapeDtypeStruct((tok_count, model_width), f32)
    residual, mlp_low, grad_gate, grad_up, hidden_low = pl.pallas_call(
        mlp_kernel,
        grid=(tiles,),
        in_specs=[
            rows_all,
            rows_all,
            gain_spec,
            rows_all,
            pl.BlockSpec((model_width, TILE), lambda n: (0, n)),
            pl.BlockSpec((model_width, TILE), lambda n: (0, n + tiles)),
            pl.BlockSpec((model_width, TILE), lambda n: (0, n + 2 * tiles)),
        ],
        out_specs=[rows_all, rows_all, tile_spec, tile_spec, tile_spec],
        out_shape=(wide_shape, low_shape, hidden_shape, hidden_shape, hidden_shape),
        compiler_params=params(),
        cost_estimate=cost(18),
        name="mlp",
    )(block_input, attn_sum, gain_mlp[None], cotangent, mlp_weights, mlp_weights, mlp_weights)

    hidden_all = pl.BlockSpec((tok_count, ff_width), lambda n: (0, 0))
    out_tile = pl.BlockSpec((tok_count, 512), lambda n: (0, n))
    grad_mlp_part = pl.pallas_call(
        mlp_back_kernel,
        grid=(model_width // WIDE,),
        in_specs=[
            hidden_all,
            hidden_all,
            pl.BlockSpec((WIDE, ff_width), lambda n: (n, 0)),
            pl.BlockSpec((WIDE, ff_width), lambda n: (n, 1)),
        ],
        out_specs=out_tile,
        out_shape=low_shape,
        compiler_params=params(),
        cost_estimate=cost(11),
        name="mlp_back",
    )(grad_gate, grad_up, mlp_weights, mlp_weights)
    grad_mlp_part, mlp_low, hidden_low = lax.optimization_barrier((grad_mlp_part, mlp_low, hidden_low))
    grad_mlp_sum = lax.psum(grad_mlp_part, "mp")

    row_tile = pl.BlockSpec((tok_count, TILE), lambda n: (0, n))
    dw_gate_up, dw_down = pl.pallas_call(
        mlp_weight_grad_kernel,
        grid=(model_width // TILE,),
        in_specs=[row_tile, row_tile, hidden_all, hidden_all, hidden_all],
        out_specs=[pl.BlockSpec((TILE, k * ff_width), lambda n: (n, 0)) for k in (2, 1)],
        out_shape=[jax.ShapeDtypeStruct((model_width, k * ff_width), bf16) for k in (2, 1)],
        compiler_params=params(),
        cost_estimate=cost(1),
        name="mlp_weight_grad",
    )(mlp_low, cotangent, grad_gate, grad_up, hidden_low)
    mlp_part = pl.pallas_call(
        rows_by_rows_kernel,
        grid=(model_width // 512,),
        in_specs=[hidden_all, pl.BlockSpec((512, ff_width), lambda n: (n, 2))],
        out_specs=out_tile,
        out_shape=low_shape,
        compiler_params=params(),
        cost_estimate=cost(1),
        name="mlp_out",
    )(hidden_low, mlp_weights)
    gate_up_grads = lax.psum_scatter(dw_gate_up, "dp", scatter_dimension=0, tiled=True)
    down_grads = lax.psum_scatter(dw_down, "dp", scatter_dimension=0, tiled=True)
    grad_mlp_sum, mlp_part, dw_gate_up = lax.optimization_barrier((grad_mlp_sum, mlp_part, dw_gate_up))
    mlp_sum = lax.psum(mlp_part, "mp")

    half_rows = tok_count // 2
    half_spec = pl.BlockSpec((half_rows, model_width), lambda n, *_: (n, 0))
    grad_residual, grad_res_low, grad_att_low, mlp_gain_grad = pl.pallas_call(
        functools.partial(residual_back_kernel, parts, 1.0 / model_count),
        grid_spec=pltpu.PrefetchScalarGridSpec(
            num_scalar_prefetch=1,
            grid=(2,),
            in_specs=[half_spec, half_spec, half_spec, gain_spec]
            + [pl.BlockSpec((model_width // parts, query_width), lambda *_: (0, 0))] * parts,
            out_specs=[half_spec, half_spec, pl.BlockSpec((half_rows, query_width), lambda n, *_: (n, 0)), gain_spec],
        ),
        out_shape=(
            wide_shape,
            low_shape,
            jax.ShapeDtypeStruct((tok_count, query_width), bf16),
            jax.ShapeDtypeStruct((1, model_width), f32),
        ),
        compiler_params=params(),
        cost_estimate=cost(1),
        name="residual_back",
    )(me_array, residual, cotangent, grad_mlp_sum, gain_mlp[None], *out_parts)
    out_rows = token_total // parts
    dkv_spec = pl.BlockSpec((out_rows, 2 * heads * HD), lambda g, *_: (0, g))
    back = pl.pallas_call(
        functools.partial(attend_back_kernel, group, heads, parts, parts),
        grid_spec=pltpu.PrefetchScalarGridSpec(
            num_scalar_prefetch=3,
            grid=(head_steps,),
            in_specs=[head_spec]
            + [anywhere] * parts
            + [head_spec, turned_spec, lse_spec, head_spec]
            + [angle_spec, angle_spec, pl.BlockSpec((1, HD), lambda *_: (0, 0))],
            out_specs=[head_spec, pl.BlockSpec((8, HD), lambda g, *_: (g, 0))] + [dkv_spec] * parts,
            scratch_shapes=[
                pltpu.VMEM((token_total, 2 * kv_width), bf16),
                pltpu.VMEM((token_total, 2 * heads * HD), f32),
                pltpu.SemaphoreType.DMA((parts,)),
            ],
        ),
        out_shape=[
            jax.ShapeDtypeStruct((tok_count, query_width), bf16),
            jax.ShapeDtypeStruct((8 * head_steps, HD), f32),
        ]
        + [jax.ShapeDtypeStruct((out_rows, 2 * kv_width), bf16)] * parts,
        compiler_params=params(),
        cost_estimate=cost(1),
        name="attend_back",
    )(
        own_spans,
        inverse,
        starts,
        queries,
        *kv_parts,
        grad_att_low,
        attended,
        lse,
        lin,
        cosine,
        sine,
        head_gains[:1],
    )
    back, gate_up_grads = lax.optimization_barrier((back, gate_up_grads))
    grad_query_low, query_gain_grad = back[:2]
    query_gain_grad = jnp.sum(query_gain_grad, axis=0) / 8.0
    if in_pairs:
        came = [swap(back[2 + k], "dp", 1) for k in range(1, parts, 2)]
        halves = [add_pair(back[2 + 2 * k], came[k]) for k in range(parts // 2)]
        terms = [halves[0]] + [swap(halves[k], "dp", 2 * k) for k in range(1, parts // 2)]
    else:
        terms = [lax.psum_scatter(back[2], "dp", scatter_dimension=0, tiled=True)]

    [dw_query] = weight_grad(me_array, normed_turned, [grad_query_low], parts, row_count, True)
    [dw_out] = weight_grad(me_array, grad_res_low, [attended_low], parts, row_count)

    terms, dw_query, dw_out, mlp_sum = lax.optimization_barrier((terms, dw_query, dw_out, mlp_sum))
    grad_kv_low, key_gain_grad, attn_gain_grad, grad_norm_part = pl.pallas_call(
        functools.partial(key_back_kernel, parts, len(terms), kv_heads),
        grid_spec=pltpu.PrefetchScalarGridSpec(
            num_scalar_prefetch=1,
            grid=(1,),
            in_specs=[pl.BlockSpec((tok_count, 2 * kv_width), lambda *_: (0, 0))] * len(terms)
            + [pl.BlockSpec((tok_count, kv_width), lambda *_: (0, query_width // kv_width))]
            + [angle_spec, angle_spec, pl.BlockSpec((1, HD), lambda *_: (0, 0))]
            + [q_all, rows_all]
            + [pl.BlockSpec((model_width // parts, qkv_cols), lambda *_: (0, 0))] * parts,
            out_specs=[
                pl.BlockSpec((tok_count, 2 * kv_width), lambda *_: (0, 0)),
                pl.BlockSpec((8, HD), lambda *_: (0, 0)),
                gain_spec,
                rows_all,
            ],
            scratch_shapes=[pltpu.VMEM((tok_count, model_width), f32)],
        ),
        out_shape=[
            jax.ShapeDtypeStruct((tok_count, 2 * kv_width), bf16),
            jax.ShapeDtypeStruct((8, HD), f32),
            jax.ShapeDtypeStruct((1, model_width), f32),
            low_shape,
        ],
        compiler_params=params(),
        cost_estimate=cost(1),
        name="key_back",
    )(me_array, *terms, lin, cosine, sine, head_gains[1:], grad_query_low, block_input, *qkv_parts)
    [dw_kv] = weight_grad(me_array, normed_turned, [grad_kv_low], parts, row_count, True)

    grad_norm_sum = lax.psum(grad_norm_part, "mp")
    if in_pairs:
        small = [scatter_small(*dw) for dw in (dw_query, dw_kv, dw_out)]
        small = [sum(term.astype(f32) for term in piece).astype(bf16) for piece in small]
    else:

        def scattered(made):
            whole = made[0].reshape(model_width, -1)
            return lax.psum_scatter(whole, "dp", scatter_dimension=0, tiled=True)

        small = [scattered(dw) for dw in (dw_query, dw_kv, dw_out)]
    gain_grads = sum_all(
        jnp.concatenate([attn_gain_grad[0], mlp_gain_grad[0], query_gain_grad, key_gain_grad[0]])
    )
    square = sum(jnp.sum(jnp.square(grad.astype(f32))) for grad in small + [gate_up_grads, down_grads])
    square_total = sum_all(square.reshape(1, 1))[0, 0]
    grad_norm = jnp.sqrt(square_total + jnp.sum(gain_grads * gain_grads))
    factor = 1.0 / jnp.maximum(grad_norm, 1.0)
    new_weights, new_momentum, new_ema = update_weights(factor[None], weights, momentum, ema_weights, small + [gate_up_grads, down_grads])
    gain_grads, mlp_sum = lax.optimization_barrier((gain_grads, mlp_sum))
    block_output = (residual + mlp_sum.astype(f32)).astype(bf16)
    eighth = tok_count // 8
    eighth_spec = pl.BlockSpec((eighth, model_width), lambda n: (n, 0))
    grad_input = pl.pallas_call(
        input_back_kernel,
        grid=(8,),
        in_specs=[eighth_spec, eighth_spec, eighth_spec, gain_spec],
        out_specs=eighth_spec,
        out_shape=wide_shape,
        compiler_params=params(),
        cost_estimate=cost(300),
        name="input_back",
    )(grad_residual, block_input, grad_norm_sum, gain_attn[None])
    new_gains, new_gain_momentum, new_gain_ema = update(gains, gain_momentum, gain_ema, gain_grads, factor, gain_rate)
    return (
        block_output,
        grad_input,
        grad_norm,
        new_weights,
        new_momentum,
        new_ema,
        new_gains,
        new_gain_momentum,
        new_gain_ema,
    )


def solution(mesh):
    return jax.shard_map(
        per_device,
        mesh=mesh,
        in_specs=(
            P("dp", None),
            P("dp", None),
            P(),
            P(),
            P("dp", "mp"),
            P("dp", "mp"),
            P("dp", "mp"),
            P(),
            P(),
            P(),
        ),
        out_specs=(
            P("dp", None),
            P("dp", None),
            P(),
            P("dp", "mp"),
            P("dp", "mp"),
            P("dp", "mp"),
            P(),
            P(),
            P(),
        ),
        check_vma=False,
    )
```

time: 720 us -> 544 us (0.76); the launches traced: 711 us -> 543 us
  local copies, waits for them, and re-layouts: 103 us -> 9.27 us
  Pallas kernels: 75.4 us -> 160 us
  other arithmetic: 93.1 us -> 29.2 us
  waiting for transfers between devices: 324 us -> 268 us
  matrix products: 42.7 us -> 0 us
    pallas_call x4 -> x16, Pallas kernels: 75.4 us -> 160 us  [the longest x1 19.5 us: per_device(): pl.pallas_call(mlp_kernel, grid=(tiles,), in_specs=[rows_all, rows_all, g...]
    unnamed x196 -> x66, local copies, waits for them, and re-layouts: 67.8 us -> 3.82 us
    dot_general x8 -> x0, matrix products: 42.7 us -> none  [dot(): return lax.dot_general(a, b, dims, preferred_element_type=f32)]
    ppermute x43 -> x50, waiting for transfers between devices: 92.2 us -> 59.9 us  [swap(): return lax.ppermute(array, axis, [(i, i ^ distance) for i in range(count)])]
    psum x3 -> x4, waiting for transfers between devices: 221 us -> 192 us  [the longest x1 89 us: per_device(): attn_sum = lax.psum(attn_part, 'mp')]
    reduce_sum x10 -> x6, other arithmetic: 24.5 us -> 7.98 us  [the longest x5 7.96 us: per_device(): jnp.sum(jnp.square(grad.astype(f32)))]
    add x2 -> x1, other arithmetic: 15.1 us -> 0.63 us  [update(): average_new = average_decay * average + (1.0 - average_decay) * value_new]
    slice x12 -> x4, local copies, waits for them, and re-layouts: 15.3 us -> 2.7 us  [the longest x1 1.58 us: per_device(): mlp_own = later[:, out_end:].astype(bf16)]
  transfers between devices with their start and end apart: 49 -> 57, of which waited for: 24 -> 28; matrix products, arithmetic and copies ran while one was open for 23% -> 6% of each run, Pallas kernels for 1% -> 19%
where the time goes in v2:
time: 544 us; the launch traced here: 543 us
  waiting for transfers between devices  268 us (49%)
  Pallas kernels  160 us (29%)
  starting transfers between devices  52.7 us (10%)
  other arithmetic  29.2 us (5%)
  between operations  24.1 us (4%)
  local copies, waits for them, and re-layouts  9.27 us (2%)
    psum x1, waiting for transfers between devices, per_device(): attn_sum = lax.psum(attn_part, 'mp')  89 us
    psum x1, waiting for transfers between devices, per_device(): grad_mlp_sum = lax.psum(grad_mlp_part, 'mp')  63.8 us
    ppermute x50, waiting for transfers between devices, swap(): return lax.ppermute(array, axis, [(i, i ^ distance) for i in range(count)])  59.9 us
    ppermute x50, starting transfers between devices, swap(): return lax.ppermute(array, axis, [(i, i ^ distance) for i in range(count)])  52.2 us
    psum x1, waiting for transfers between devices, per_device(): mlp_sum = lax.psum(mlp_part, 'mp')  38.9 us
    pallas_call x1, Pallas kernels, per_device(): pl.pallas_call(mlp_kernel, grid=(tiles,), in_specs=[rows_all, rows_all, g...  19.5 us
    pallas_call x1, Pallas kernels, per_device(): pl.pallas_call(functools.partial(attend_back_kernel, group, heads, parts,...  17 us
    pallas_call x1, Pallas kernels, update_weights(): pl.pallas_call(update_kernel, grid_spec=pltpu.PrefetchScalarGridSpec(num_...  15.3 us
  transfers between devices with their start and end apart: 57, of which 28 were waited for; matrix products, arithmetic and copies ran while one was open for 6% of the time, Pallas kernels for 19%

profile of v2, /device:TPU:0, one launch (start us, length us, event | category | flops | bytes accessed | tf_op | source)
XLA Modules:
  0.0 542.9 jit_solution(4692697995119607505)
XLA Ops:
  8.1 1.3 slice.146.refs_0_.refs_10_
  9.4 4.0 collective-permute-start.5
  14.0 3.2 convert.12
  17.2 1.7 copy-done.1
  18.9 2.9 collective-permute-start.9
  23.8 1.9 fusion.2.x_ref.h_ref
  25.8 6.0 %transposed.1.lhs_ref = bf16[2048,512]{1,0:T(8,128)(2,1)} custom-call(s32[1]{0:T(128)} %bitcast.me_ref, bf16[512,2048]{1,0:T(8,128)(2,1)} %fusion.2.x_ref.h_ref), custom_call_target="tpu_custom_call" | custom-call | flops 5000000000 | bytes 17000000 | tf_op jit(solution)/shard_map/transposed/pallas_call | solution.py:446
  31.8 6.3 %collective-permute-done.1.refs_2_.refs_12_ = bf16[256,1024]{1,0:T(8,128)(2,1)} collective-permute-done((bf16[256,1024]{1,0:T(8,128)(2,1)S(1)}, bf16[256,1024]{1,0:T(8,128)(2,1)}, u32[]{:S(2)}, u32[]{:S(2)}) %collective-permute-start.1) | collective-permute-done | bytes 524320 | tf_op jit(solution)/shard_map/ppermute | solution.py:50
  39.2 1.8 fusion.13
  44.0 8.2 %project.1 = (bf16[512,512]{1,0:T(8,128)(2,1)}, bf16[512,512]{1,0:T(8,128)(2,1)}, f32[512,768]{1,0:T(8,128)}) custom-call(s32[1]{0:T(128)} %bitcast.me_ref, bf16[512,2048]{1,0:T(8,128)(2,1)} %fusion.2.x_ref.h_ref, bf16[256,1024]{1,0:T(8,128)(2,1)} %copy-done.4, bf16[256,1024]{1,0:T(8,128)(2,1)} %collective-permute-done.refs_1_.refs_11_, ...), custom_call_target="tpu_custom_call" | custom-call | flops 6000000000 | bytes 20400000 | tf_op jit(solution)/shard_map/project/pallas_call | solution.py:657
  52.3 1.6 collective-permute-start.19
  56.3 1.4 collective-permute-done.10.refs_1_
  58.2 10.1 %collective-permute-done.19.refs_6_ = bf16[512,512]{1,0:T(8,128)(2,1)S(1)} collective-permute-done((bf16[512,512]{1,0:T(8,128)(2,1)}, bf16[512,512]{1,0:T(8,128)(2,1)S(1)}, u32[]{:S(2)}, u32[]{:S(2)}) %collective-permute-start.19) | collective-permute-done | bytes 524320 | tf_op jit(solution)/shard_map/ppermute | solution.py:50
  68.3 10.2 %collective-permute-done.17.refs_4_ = bf16[512,512]{1,0:T(8,128)(2,1)} collective-permute-done((bf16[512,512]{1,0:T(8,128)(2,1)}, bf16[512,512]{1,0:T(8,128)(2,1)}, u32[]{:S(2)}, u32[]{:S(2)}) %collective-permute-start.17) | collective-permute-done | bytes 524320 | tf_op jit(solution)/shard_map/ppermute | solution.py:50
  79.2 1.6 slice.109
  81.9 12.8 %attend.1 = (f32[8,128,256]{2,1,0:T(8,128)}, bf16[512,512]{1,0:T(8,128)(2,1)}, f32[8,8,256]{2,1,0:T(8,128)}) custom-call(s32[4]{0:T(128)} %get-tuple-element.205.own_ref, s32[32]{0:T(128)} %fusion.14.inverse_ref, s32[8]{0:T(128)} %copy-done.30, bf16[512,512]{1,0:T(8,128)(2,1)} %get-tuple-element.102.q_ref, bf16[512,512]{1,0:T(8,128)(2,1)} %get-tuple-element.110.refs_0_, ...), custom_call_target="tpu_custom_call" | custom-call | flops 16000000000 | bytes 54400000 | tf_op jit(solution)/shard_map/attend/pallas_call | solution.py:699
  94.7 4.5 project_out.1
  99.9 89.0 %all-reduce.5.cloned.1.call-done.s_ref = bf16[512,2048]{1,0:T(8,128)(2,1)} async-done(((bf16[512,2048]{1,0:T(8,128)(2,1)}), bf16[512,2048]{1,0:T(8,128)(2,1)}) %all-reduce.5.cloned.1.call-update) | async-done | bytes 2097168 | tf_op jit(solution)/shard_map/psum | solution.py:735
  189.0 15.0 %all-gather.2.cloned.1.call-done.wg_ref.wu_ref.wd_ref.w_ref = bf16[2048,4608]{1,0:T(8,128)(2,1)} async-done(((bf16[256,4608]{1,0:T(8,128)(2,1)}), bf16[2048,4608]{1,0:T(8,128)(2,1)}) %all-gather.2.cloned.1.call-update) | async-done | bytes 18874384 | tf_op jit(solution)/shard_map/all_gather | solution.py:689
  203.9 19.5 %mlp.1 = (f32[512,2048]{1,0:T(8,128)}, bf16[512,2048]{1,0:T(8,128)(2,1)}, bf16[512,1536]{1,0:T(8,128)(2,1)}, bf16[512,1536]{1,0:T(8,128)(2,1)}, bf16[512,1536]{1,0:T(8,128)(2,1)}) custom-call(bf16[512,2048]{1,0:T(8,128)(2,1)} %x_ref.3, bf16[512,2048]{1,0:T(8,128)(2,1)} %all-reduce.5.cloned.1.call-done.s_ref, f32[1,2048]{1,0:T(1,128)} %bitcast.65, ...), custom_call_target="tpu_custom_call" | custom-call | flops 17999998976 | bytes 61200000 | tf_op jit(solution)/shard_map/mlp/pallas_call | solution.py:743
  223.5 11.3 %mlp_back.1 = bf16[512,2048]{1,0:T(8,128)(2,1)} custom-call(bf16[512,1536]{1,0:T(8,128)(2,1)} %get-tuple-element.129.dg_ref, bf16[512,1536]{1,0:T(8,128)(2,1)} %get-tuple-element.130.du_ref, bf16[2048,4608]{1,0:T(8,128)(2,1)} %all-gather.2.cloned.1.call-done.wg_ref.wu_ref.wd_ref.w_ref, bf16[2048,4608]{1,0:T(8,128)(2,1)} %all-gather.2.cloned.1.call-done.wg_ref.wu_ref.wd_ref.w_ref), custom_call_target="tpu_custom_call" | custom-call | flops 11000000512 | bytes 37400000 | tf_op jit(solution)/shard_map/mlp_back/pallas_call | solution.py:764
  234.8 15.1 %mlp_weight_grad.1 = (bf16[2048,3072]{1,0:T(8,128)(2,1)}, bf16[2048,1536]{1,0:T(8,128)(2,1)}) custom-call(bf16[512,2048]{1,0:T(8,128)(2,1)} %get-tuple-element.135.h_ref, bf16[512,2048]{1,0:T(8,128)(2,1)} %c_ref.5, bf16[512,1536]{1,0:T(8,128)(2,1)} %get-tuple-element.129.dg_ref, bf16[512,1536]{1,0:T(8,128)(2,1)} %get-tuple-element.130.du_ref, ...), custom_call_target="tpu_custom_call" | custom-call | flops 1000000000 | bytes 3400000 | tf_op jit(solution)/shard_map/mlp_weight_grad/pallas_call | solution.py:783
  250.0 7.6 %mlp_out.1 = bf16[512,2048]{1,0:T(8,128)(2,1)} custom-call(bf16[512,1536]{1,0:T(8,128)(2,1)} %get-tuple-element.134.a_ref, bf16[2048,4608]{1,0:T(8,128)(2,1)} %all-gather.2.cloned.1.call-done.wg_ref.wu_ref.wd_ref.w_ref), custom_call_target="tpu_custom_call" | custom-call | flops 1000000000 | bytes 3400000 | tf_op jit(solution)/shard_map/mlp_out/pallas_call | solution.py:793
  257.6 63.8 %all-reduce.7.cloned.1.call-done.s_ref = bf16[512,2048]{1,0:T(8,128)(2,1)} async-done(((bf16[512,2048]{1,0:T(8,128)(2,1)}), bf16[512,2048]{1,0:T(8,128)(2,1)}) %all-reduce.7.cloned.1.call-update) | async-done | bytes 2097168 | tf_op jit(solution)/shard_map/psum | solution.py:780
  322.6 9.3 %residual_back.1 = (f32[512,2048]{1,0:T(8,128)}, bf16[512,2048]{1,0:T(8,128)(2,1)}, bf16[512,512]{1,0:T(8,128)(2,1)}, f32[1,2048]{1,0:T(1,128)}) custom-call(s32[1]{0:T(128)} %bitcast.me_ref, f32[512,2048]{1,0:T(8,128)} %get-tuple-element.128.y_ref, bf16[512,2048]{1,0:T(8,128)(2,1)} %c_ref.5, bf16[512,2048]{1,0:T(8,128)(2,1)} %all-reduce.7.cloned.1.call-done.s_ref, ...), custom_call_target="tpu_custom_call" | custom-call | flops 1000000000 | bytes 3400000 | tf_op jit(solution)/shard_map/residual_back/pallas_call | solution.py:810
  331.9 17.0 %attend_back.1 = (bf16[512,512]{1,0:T(8,128)(2,1)}, f32[8,128]{1,0:T(8,128)}, bf16[512,512]{1,0:T(8,128)(2,1)}, bf16[512,512]{1,0:T(8,128)(2,1)}, bf16[512,512]{...) custom-call(s32[4]{0:T(128)} %get-tuple-element.205.own_ref, ...), custom_call_target="tpu_custom_call" | custom-call | flops 1000000000 | bytes 3400000 | tf_op jit(solution)/shard_map/attend_back/pallas_call | solution.py:831
  349.9 7.3 %weight_grad.1 = (bf16[4,256,512]{2,1,0:T(8,128)(2,1)}, bf16[4,256,512]{2,1,0:T(8,128)(2,1)}) custom-call(s32[1]{0:T(128)} %bitcast.me_ref, bf16[512,2048]{1,0:T(8,128)(2,1)} %get-tuple-element.164.lhs_ref, bf16[512,512]{1,0:T(8,128)(2,1)} %get-tuple-element.118.low_ref.refs_0_), custom_call_target="tpu_custom_call" | custom-call | flops 1000000000 | bytes 3400000 | tf_op jit(solution)/shard_map/weight_grad/pallas_call | solution.py:523
  357.9 3.9 collective-permute-start.23
  365.9 4.2 weight_grad_turned.2
  371.0 38.9 %all-reduce.9.cloned.1.call-done = bf16[512,2048]{1,0:T(8,128)(2,1)} async-done(((bf16[512,2048]{1,0:T(8,128)(2,1)}), bf16[512,2048]{1,0:T(8,128)(2,1)}) %all-reduce.9.cloned.1.call-update) | async-done | bytes 2097168 | tf_op jit(solution)/shard_map/psum | solution.py:806
  411.1 9.5 %key_back.1 = (bf16[512,512]{1,0:T(8,128)(2,1)}, f32[8,128]{1,0:T(8,128)}, f32[1,2048]{1,0:T(1,128)}, bf16[512,2048]{1,0:T(8,128)(2,1)}) custom-call(s32[1]{0:T(128)} %bitcast.me_ref, bf16[512,512]{1,0:T(8,128)(2,1)} %add_convert_fusion.6.refs_0_, bf16[512,512]{1,0:T(8,128)(2,1)} %copy-done.15, bf16[512,512]{1,0:T(8,128)(2,1)} %copy-done.17, ...), custom_call_target="tpu_custom_call" | custom-call | flops 1000000000 | bytes 3400000 | tf_op jit(solution)/shard_map/key_back/pallas_call | solution.py:883
  423.8 1.5 collective-permute-start.29
  425.3 2.3 collective-permute-done.29
  427.6 1.5 collective-permute-start.30
  429.1 2.1 multiply_reduce_fusion.1
  432.0 4.1 weight_grad_turned.3
  436.1 1.9 collective-permute-start.32
  438.1 1.4 multiply_reduce_fusion
  441.5 4.3 add_convert_fusion
  445.8 1.6 fusion.3
  447.5 1.5 collective-permute-start.38
  449.0 1.5 collective-permute-start.40
  451.4 1.5 collective-permute-start.34
  453.0 1.5 collective-permute-start.36
  454.8 2.0 collective-permute-done.38
  456.8 1.5 collective-permute-start.35
  458.3 5.0 collective-permute-done.40
  463.4 1.5 collective-permute-start.42
  466.3 1.8 collective-permute-done.34
  468.1 1.5 collective-permute-start.43
  469.5 1.5 multiply_reduce_fusion.3
  471.0 3.6 collective-permute-done.36
  474.6 1.8 collective-permute-done.35
  476.5 1.5 multiply_reduce_fusion.4
  479.4 5.0 collective-permute-done.44
  485.6 1.5 multiply_reduce_fusion.2
  491.0 2.8 collective-permute-start.46
  495.4 1.9 collective-permute-start.47
  497.3 1.8 collective-permute-done.47
  499.7 2.8 collective-permute-start.48
  504.2 3.2 collective-permute-start.49
  507.4 1.6 collective-permute-done.49
  510.3 15.3 %update.1 = (f32[256,6144]{1,0:T(8,128)}, f32[256,6144]{1,0:T(8,128)}, f32[256,6144]{1,0:T(8,128)}) custom-call(f32[1]{0:T(128)} %bitcast.29.factor_ref, f32[256,6144]{1,0:T(8,128)} %w_ref.1, f32[256,6144]{1,0:T(8,128)} %m_ref.1, f32[256,6144]{1,0:T(8,128)} %e_ref.1, bf16[256,512]{1,0:T(8,128)(2,1)} %get-tuple-element.203.refs_0_, ...), custom_call_target="tpu_custom_call" | custom-call | flops 1000000000 | bytes 3400000 | tf_op jit(solution)/shard_map/update/pallas_call | solution.py:555
  526.2 8.3 %input_back.1 = f32[512,2048]{1,0:T(8,128)} custom-call(f32[512,2048]{1,0:T(8,128)} %get-tuple-element.178.dy_ref, bf16[512,2048]{1,0:T(8,128)(2,1)} %x_ref.3, bf16[512,2048]{1,0:T(8,128)(2,1)} %all-reduce.11.cloned.1.call-done.s_ref, f32[1,2048]{1,0:T(1,128)} %bitcast.64), custom_call_target="tpu_custom_call" | custom-call | flops 299999985664 | bytes 1020000000 | tf_op jit(solution)/shard_map/input_back/pallas_call | solution.py:936
  (184 shorter events, 35.7 us)
Async XLA Ops:
  8.0 181.0 %all-reduce.5.cloned.1.call-start = ((), (), s32[]{:S(2)}) async-start(), calls=%async_computation.2 | async-start | bytes 4194304 | tf_op jit(solution)/shard_map/psum | solution.py:735
  9.4 12.6 %copy-start.31 = (s32[32]{0:T(128)S(1)}, s32[32]{0:T(128)}, u32[]{:S(2)}) copy-start(s32[32]{0:T(128)} %param.13) | copy-start | bytes 388
  9.4 13.2 %copy-start = (bf16[512,2048]{1,0:T(8,128)(2,1)S(1)}, bf16[512,2048]{1,0:T(8,128)(2,1)}, u32[]{:S(2)}) copy-start(bf16[512,2048]{1,0:T(8,128)(2,1)} %x_ref.3) | copy-start | bytes 6291460
  9.4 28.7 %collective-permute-start.5 = (bf16[256,1024]{1,0:T(8,128)(2,1)S(1)}, bf16[256,1024]{1,0:T(8,128)(2,1)}, u32[]{:S(2)}, u32[]{:S(2)}) collective-permute-start(bf16[256,1024]{1,0:T(8,128)(2,1)S(1)} %slice.146.refs_0_.refs_10_), channel_id=1, source_target_pairs={{0,24},{4,28},{8,16},{12,20},{16,8},{20,12},{24,0},{28,4},{1,25},{... | collective-permute-start | bytes 1572872 | tf_op jit(solution)/shard_map/ppermute | solution.py:50
  13.4 25.2 %collective-permute-start.3 = (bf16[256,1024]{1,0:T(8,128)(2,1)S(1)}, bf16[256,1024]{1,0:T(8,128)(2,1)}, u32[]{:S(2)}, u32[]{:S(2)}) collective-permute-start(bf16[256,1024]{1,0:T(8,128)(2,1)S(1)} %slice.146.refs_0_.refs_10_), channel_id=1, source_target_pairs={{0,16},{4,20},{8,24},{12,28},{16,0},{20,4},{24,8},{28,12},{1,17},{... | collective-permute-start | bytes 1572872 | tf_op jit(solution)/shard_map/ppermute | solution.py:50
  13.9 24.2 %collective-permute-start.1 = (bf16[256,1024]{1,0:T(8,128)(2,1)S(1)}, bf16[256,1024]{1,0:T(8,128)(2,1)}, u32[]{:S(2)}, u32[]{:S(2)}) collective-permute-start(bf16[256,1024]{1,0:T(8,128)(2,1)S(1)} %slice.146.refs_0_.refs_10_), channel_id=1, source_target_pairs={{0,8},{4,12},{8,0},{12,4},{16,24},{20,28},{24,16},{28,20},{1,9},{5... | collective-permute-start | bytes 1572872 | tf_op jit(solution)/shard_map/ppermute | solution.py:50
  14.0 27.0 %collective-permute-start = (bf16[256,1024]{1,0:T(8,128)(2,1)S(1)}, bf16[256,1024]{1,0:T(8,128)(2,1)}, u32[]{:S(2)}, u32[]{:S(2)}) collective-permute-start(bf16[256,1024]{1,0:T(8,128)(2,1)S(1)} %slice.146.refs_0_.refs_10_), channel_id=1, source_target_pairs={{0,4},{4,0},{8,12},{12,8},{16,20},{20,16},{24,28},{28,24},{1,5},{5... | collective-permute-start | bytes 1572872 | tf_op jit(solution)/shard_map/ppermute | solution.py:50
  18.9 36.9 %copy-start.9 = (bf16[256,512]{1,0:T(8,128)(2,1)}, bf16[256,512]{1,0:T(8,128)(2,1)S(1)}, u32[]{:S(2)}) copy-start(bf16[256,512]{1,0:T(8,128)(2,1)S(1)} %slice.110.refs_0_) | copy-start | bytes 786436
  18.9 33.3 %collective-permute-start.9 = (bf16[256,512]{1,0:T(8,128)(2,1)S(1)}, bf16[256,512]{1,0:T(8,128)(2,1)}, u32[]{:S(2)}, u32[]{:S(2)}) collective-permute-start(bf16[256,512]{1,0:T(8,128)(2,1)S(1)} %slice.110.refs_0_), channel_id=1, source_target_pairs={{0,24},{4,28},{8,16},{12,20},{16,8},{20,12},{24,0},{28,4},{1,25},{... | collective-permute-start | bytes 786440 | tf_op jit(solution)/shard_map/ppermute | solution.py:50
  38.1 5.0 collective-permute-start.2
  38.1 3.8 collective-permute-start.6
  38.6 4.5 collective-permute-start.4
  41.0 11.2 %collective-permute-start.8 = (bf16[256,512]{1,0:T(8,128)(2,1)S(1)}, bf16[256,512]{1,0:T(8,128)(2,1)}, u32[]{:S(2)}, u32[]{:S(2)}) collective-permute-start(bf16[256,512]{1,0:T(8,128)(2,1)S(1)} %slice.110.refs_0_), channel_id=1, source_target_pairs={{0,16},{4,20},{8,24},{12,28},{16,0},{20,4},{24,8},{28,12},{1,17},{... | collective-permute-start | bytes 786440 | tf_op jit(solution)/shard_map/ppermute | solution.py:50
  41.8 10.4 %collective-permute-start.7 = (bf16[256,512]{1,0:T(8,128)(2,1)S(1)}, bf16[256,512]{1,0:T(8,128)(2,1)}, u32[]{:S(2)}, u32[]{:S(2)}) collective-permute-start(bf16[256,512]{1,0:T(8,128)(2,1)S(1)} %slice.110.refs_0_), channel_id=1, source_target_pairs={{0,8},{4,12},{8,0},{12,4},{16,24},{20,28},{24,16},{28,20},{1,9},{5... | collective-permute-start | bytes 786440 | tf_op jit(solution)/shard_map/ppermute | solution.py:50
  44.0 35.2 %copy-start.2 = (bf16[256,6144]{1,0:T(8,128)(2,1)S(1)}, bf16[256,6144]{1,0:T(8,128)(2,1)}, u32[]{:S(2)}) copy-start(bf16[256,6144]{1,0:T(8,128)(2,1)} %copy-done.1) | copy-start | bytes 9437188
  52.3 16.0 %collective-permute-start.19 = (bf16[512,512]{1,0:T(8,128)(2,1)}, bf16[512,512]{1,0:T(8,128)(2,1)S(1)}, u32[]{:S(2)}, u32[]{:S(2)}) collective-permute-start(bf16[512,512]{1,0:T(8,128)(2,1)} %get-tuple-element.110.refs_0_), channel_id=1, source_target_pairs={{0,24},{4,28},{8,16},{12,20},{16,8},{20,12},{24,0},{28,4},{1,25},{... | collective-permute-start | bytes 1572872 | tf_op jit(solution)/shard_map/ppermute | solution.py:50
  53.9 24.6 %collective-permute-start.17 = (bf16[512,512]{1,0:T(8,128)(2,1)}, bf16[512,512]{1,0:T(8,128)(2,1)}, u32[]{:S(2)}, u32[]{:S(2)}) collective-permute-start(bf16[512,512]{1,0:T(8,128)(2,1)} %get-tuple-element.110.refs_0_), channel_id=1, source_target_pairs={{0,16},{4,20},{8,24},{12,28},{16,0},{20,4},{24,8},{28,12},{1,17},{... | collective-permute-start | bytes 1572872 | tf_op jit(solution)/shard_map/ppermute | solution.py:50
  54.7 23.9 %collective-permute-start.15 = (bf16[512,512]{1,0:T(8,128)(2,1)}, bf16[512,512]{1,0:T(8,128)(2,1)}, u32[]{:S(2)}, u32[]{:S(2)}) collective-permute-start(bf16[512,512]{1,0:T(8,128)(2,1)} %get-tuple-element.110.refs_0_), channel_id=1, source_target_pairs={{0,8},{4,12},{8,0},{12,4},{16,24},{20,28},{24,16},{28,20},{1,9},{5... | collective-permute-start | bytes 1572872 | tf_op jit(solution)/shard_map/ppermute | solution.py:50
  55.8 1.9 collective-permute-start.10
  55.8 2.1 collective-permute-start.11
  57.7 21.3 %collective-permute-start.12 = (bf16[256,512]{1,0:T(8,128)(2,1)}, bf16[256,512]{1,0:T(8,128)(2,1)S(1)}, u32[]{:S(2)}, u32[]{:S(2)}) collective-permute-start(bf16[256,512]{1,0:T(8,128)(2,1)} %collective-permute-done.8.refs_4_), channel_id=1, source_target_pairs={{0,4},{4,0},{8,12},{12,8},{16,20},{20,16},{24,28},{28,24},{1,5},{5... | collective-permute-start | bytes 786440 | tf_op jit(solution)/shard_map/ppermute | solution.py:50
  58.0 23.9 %collective-permute-start.14 = (bf16[512,512]{1,0:T(8,128)(2,1)}, bf16[512,512]{1,0:T(8,128)(2,1)}, u32[]{:S(2)}, u32[]{:S(2)}) collective-permute-start(bf16[512,512]{1,0:T(8,128)(2,1)} %get-tuple-element.110.refs_0_), channel_id=1, source_target_pairs={{0,4},{4,0},{8,12},{12,8},{16,20},{20,16},{24,28},{28,24},{1,5},{5... | collective-permute-start | bytes 1572872 | tf_op jit(solution)/shard_map/ppermute | solution.py:50
  68.3 12.5 %copy-start.13 = (bf16[512,512]{1,0:T(8,128)(2,1)}, bf16[512,512]{1,0:T(8,128)(2,1)S(1)}, u32[]{:S(2)}) copy-start(bf16[512,512]{1,0:T(8,128)(2,1)S(1)} %collective-permute-done.19.refs_6_) | copy-start | bytes 1572868
  68.3 13.6 %collective-permute-start.20 = (bf16[512,512]{1,0:T(8,128)(2,1)S(1)}, bf16[512,512]{1,0:T(8,128)(2,1)}, u32[]{:S(2)}, u32[]{:S(2)}) collective-permute-start(bf16[512,512]{1,0:T(8,128)(2,1)S(1)} %collective-permute-done.19.refs_6_), channel_id=1, source_target_pairs={{0,4},{4,0},{8,12},{12,8},{16,20},{20,16},{24,28},{28,24},{1,5},{5... | collective-permute-start | bytes 1572872 | tf_op jit(solution)/shard_map/ppermute | solution.py:50
  78.5 3.4 collective-permute-start.18
  78.6 3.3 collective-permute-start.16
  79.0 2.9 collective-permute-start.13
  99.1 104.8 %all-gather.2.cloned.1.call-start = ((), (), s32[]{:S(2)}) async-start(), calls=%async_computation.3 | async-start | bytes 21233664 | tf_op jit(solution)/shard_map/all_gather | solution.py:689
  99.7 221.7 %all-reduce.7.cloned.1.call-start = ((), (), s32[]{:S(2)}) async-start(), calls=%async_computation.4 | async-start | bytes 4194304 | tf_op jit(solution)/shard_map/psum | solution.py:780
  234.8 114.2 %reduce-scatter.3.cloned.1.call-start = ((), (), s32[]{:S(2)}) async-start(), calls=%async_computation.5 | async-start | bytes 14155776 | tf_op jit(solution)/shard_map/reduce_scatter | solution.py:803
  249.9 160.0 %all-reduce.9.cloned.1.call-start = ((), (), s32[]{:S(2)}) async-start(), calls=%async_computation.6 | async-start | bytes 4194304 | tf_op jit(solution)/shard_map/psum | solution.py:806
  321.5 107.6 %reduce-scatter.5.cloned.1.call-start = ((), (), s32[]{:S(2)}) async-start(), calls=%async_computation.8 | async-start | bytes 7077888 | tf_op jit(solution)/shard_map/reduce_scatter | solution.py:804
  322.1 204.2 %all-reduce.11.cloned.1.call-start = ((), (), s32[]{:S(2)}) async-start(), calls=%async_computation.7 | async-start | bytes 4194304 | tf_op jit(solution)/shard_map/psum | solution.py:913
  349.0 8.7 %collective-permute-start.22 = (bf16[512,512]{1,0:T(8,128)(2,1)}, bf16[512,512]{1,0:T(8,128)(2,1)S(1)}, u32[]{:S(2)}, u32[]{:S(2)}) collective-permute-start(bf16[512,512]{1,0:T(8,128)(2,1)} %get-tuple-element.155), channel_id=1, source_target_pairs={{0,4},{4,0},{8,12},{12,8},{16,20},{20,16},{24,28},{28,24},{1,5},{5... | collective-permute-start | bytes 1572872 | tf_op jit(solution)/shard_map/ppermute | solution.py:50
  349.8 12.0 %collective-permute-start.24 = (bf16[512,512]{1,0:T(8,128)(2,1)}, bf16[512,512]{1,0:T(8,128)(2,1)S(1)}, u32[]{:S(2)}, u32[]{:S(2)}) collective-permute-start(bf16[512,512]{1,0:T(8,128)(2,1)} %get-tuple-element.157), channel_id=1, source_target_pairs={{0,4},{4,0},{8,12},{12,8},{16,20},{20,16},{24,28},{28,24},{1,5},{5... | collective-permute-start | bytes 1572872 | tf_op jit(solution)/shard_map/ppermute | solution.py:50
  357.3 12.8 %collective-permute-start.21 = (bf16[512,512]{1,0:T(8,128)(2,1)}, bf16[512,512]{1,0:T(8,128)(2,1)S(1)}, u32[]{:S(2)}, u32[]{:S(2)}) collective-permute-start(bf16[512,512]{1,0:T(8,128)(2,1)} %get-tuple-element.153), channel_id=1, source_target_pairs={{0,4},{4,0},{8,12},{12,8},{16,20},{20,16},{24,28},{28,24},{1,5},{5... | collective-permute-start | bytes 1572872 | tf_op jit(solution)/shard_map/ppermute | solution.py:50
  357.6 6.1 %collective-permute-start.26 = (bf16[512,512]{1,0:T(8,128)(2,1)}, bf16[512,512]{1,0:T(8,128)(2,1)S(1)}, u32[]{:S(2)}, u32[]{:S(2)}) collective-permute-start(bf16[512,512]{1,0:T(8,128)(2,1)} %get-tuple-element.159), channel_id=1, source_target_pairs={{0,4},{4,0},{8,12},{12,8},{16,20},{20,16},{24,28},{28,24},{1,5},{5... | collective-permute-start | bytes 1572872 | tf_op jit(solution)/shard_map/ppermute | solution.py:50
  357.9 52.0 %collective-permute-start.23 = (bf16[512,512]{1,0:T(8,128)(2,1)S(1)}, bf16[512,512]{1,0:T(8,128)(2,1)S(1)}, u32[]{:S(2)}, u32[]{:S(2)}) collective-permute-start(bf16[512,512]{1,0:T(8,128)(2,1)S(1)} %add_convert_fusion.5), channel_id=1, source_target_pairs={{0,8},{4,12},{8,0},{12,4},{16,24},{20,28},{24,16},{28,20},{1,9},{5... | collective-permute-start | bytes 1572872 | tf_op jit(solution)/shard_map/ppermute | solution.py:50
  362.7 47.2 %collective-permute-start.25 = (bf16[512,512]{1,0:T(8,128)(2,1)}, bf16[512,512]{1,0:T(8,128)(2,1)S(1)}, u32[]{:S(2)}, u32[]{:S(2)}) collective-permute-start(bf16[512,512]{1,0:T(8,128)(2,1)} %add_convert_fusion.4), channel_id=1, source_target_pairs={{0,16},{4,20},{8,24},{12,28},{16,0},{20,4},{24,8},{28,12},{1,17},{... | collective-permute-start | bytes 1572872 | tf_op jit(solution)/shard_map/ppermute | solution.py:50
  364.6 45.3 %collective-permute-start.27 = (bf16[512,512]{1,0:T(8,128)(2,1)}, bf16[512,512]{1,0:T(8,128)(2,1)S(1)}, u32[]{:S(2)}, u32[]{:S(2)}) collective-permute-start(bf16[512,512]{1,0:T(8,128)(2,1)} %add_convert_fusion.3), channel_id=1, source_target_pairs={{0,24},{4,28},{8,16},{12,20},{16,8},{20,12},{24,0},{28,4},{1,25},{... | collective-permute-start | bytes 1572872 | tf_op jit(solution)/shard_map/ppermute | solution.py:50
  421.9 1.2 collective-permute-start.28
  423.8 3.8 collective-permute-start.29
  427.6 3.8 collective-permute-start.30
  431.4 4.7 collective-permute-start.31
  436.1 9.7 %collective-permute-start.37 = (bf16[4,256,512]{2,1,0:T(8,128)(2,1)}, bf16[4,256,512]{2,1,0:T(8,128)(2,1)}, u32[]{:S(2)}, u32[]{:S(2)}) collective-permute-start(bf16[4,256,512]{2,1,0:T(8,128)(2,1)} %bitcast.72), channel_id=1, source_target_pairs={{0,4},{4,0},{8,12},{12,8},{16,20},{20,16},{24,28},{28,24},{1,5},{5... | collective-permute-start | bytes 3145736 | tf_op jit(solution)/shard_map/ppermute | solution.py:50
  436.1 4.7 collective-permute-start.32
  439.5 11.5 %collective-permute-start.33 = (bf16[4,256,512]{2,1,0:T(8,128)(2,1)}, bf16[4,256,512]{2,1,0:T(8,128)(2,1)S(1)}, u32[]{:S(2)}, u32[]{:S(2)}) collective-permute-start(bf16[4,256,512]{2,1,0:T(8,128)(2,1)} %bitcast.71), channel_id=1, source_target_pairs={{0,4},{4,0},{8,12},{12,8},{16,20},{20,16},{24,28},{28,24},{1,5},{5... | collective-permute-start | bytes 3145736 | tf_op jit(solution)/shard_map/ppermute | solution.py:50
  439.8 13.2 %collective-permute-start.41 = (bf16[4,256,512]{2,1,0:T(8,128)(2,1)}, bf16[4,256,512]{2,1,0:T(8,128)(2,1)S(1)}, u32[]{:S(2)}, u32[]{:S(2)}) collective-permute-start(bf16[4,256,512]{2,1,0:T(8,128)(2,1)} %get-tuple-element.186), channel_id=1, source_target_pairs={{0,4},{4,0},{8,12},{12,8},{16,20},{20,16},{24,28},{28,24},{1,5},{5... | collective-permute-start | bytes 3145736 | tf_op jit(solution)/shard_map/ppermute | solution.py:50
  447.5 9.3 %collective-permute-start.38 = (bf16[256,512]{1,0:T(8,128)(2,1)S(1)}, bf16[256,512]{1,0:T(8,128)(2,1)S(1)}, u32[]{:S(2)}, u32[]{:S(2)}) collective-permute-start(bf16[256,512]{1,0:T(8,128)(2,1)S(1)} %get-tuple-element.209), channel_id=1, source_target_pairs={{0,8},{4,12},{8,0},{12,4},{16,24},{20,28},{24,16},{28,20},{1,9},{5... | collective-permute-start | bytes 786440 | tf_op jit(solution)/shard_map/ppermute | solution.py:50
  449.0 14.3 %collective-permute-start.40 = (bf16[256,512]{1,0:T(8,128)(2,1)S(1)}, bf16[256,512]{1,0:T(8,128)(2,1)S(1)}, u32[]{:S(2)}, u32[]{:S(2)}) collective-permute-start(bf16[256,512]{1,0:T(8,128)(2,1)S(1)} %get-tuple-element.210), channel_id=1, source_target_pairs={{0,24},{4,28},{8,16},{12,20},{16,8},{20,12},{24,0},{28,4},{1,25},{... | collective-permute-start | bytes 786440 | tf_op jit(solution)/shard_map/ppermute | solution.py:50
  450.5 14.8 %collective-permute-start.39 = (bf16[256,512]{1,0:T(8,128)(2,1)S(1)}, bf16[256,512]{1,0:T(8,128)(2,1)S(1)}, u32[]{:S(2)}, u32[]{:S(2)}) collective-permute-start(bf16[256,512]{1,0:T(8,128)(2,1)S(1)} %get-tuple-element.211), channel_id=1, source_target_pairs={{0,16},{4,20},{8,24},{12,28},{16,0},{20,4},{24,8},{28,12},{1,17},{... | collective-permute-start | bytes 786440 | tf_op jit(solution)/shard_map/ppermute | solution.py:50
  451.4 16.6 %collective-permute-start.34 = (bf16[256,512]{1,0:T(8,128)(2,1)S(1)}, bf16[256,512]{1,0:T(8,128)(2,1)S(1)}, u32[]{:S(2)}, u32[]{:S(2)}) collective-permute-start(bf16[256,512]{1,0:T(8,128)(2,1)S(1)} %get-tuple-element.212), channel_id=1, source_target_pairs={{0,8},{4,12},{8,0},{12,4},{16,24},{20,28},{24,16},{28,20},{1,9},{5... | collective-permute-start | bytes 786440 | tf_op jit(solution)/shard_map/ppermute | solution.py:50
  453.0 21.7 %collective-permute-start.36 = (bf16[256,512]{1,0:T(8,128)(2,1)S(1)}, bf16[256,512]{1,0:T(8,128)(2,1)S(1)}, u32[]{:S(2)}, u32[]{:S(2)}) collective-permute-start(bf16[256,512]{1,0:T(8,128)(2,1)S(1)} %get-tuple-element.213), channel_id=1, source_target_pairs={{0,24},{4,28},{8,16},{12,20},{16,8},{20,12},{24,0},{28,4},{1,25},{... | collective-permute-start | bytes 786440 | tf_op jit(solution)/shard_map/ppermute | solution.py:50
  456.8 19.7 %collective-permute-start.35 = (bf16[256,512]{1,0:T(8,128)(2,1)S(1)}, bf16[256,512]{1,0:T(8,128)(2,1)S(1)}, u32[]{:S(2)}, u32[]{:S(2)}) collective-permute-start(bf16[256,512]{1,0:T(8,128)(2,1)S(1)} %get-tuple-element.214), channel_id=1, source_target_pairs={{0,16},{4,20},{8,24},{12,28},{16,0},{20,4},{24,8},{28,12},{1,17},{... | collective-permute-start | bytes 786440 | tf_op jit(solution)/shard_map/ppermute | solution.py:50
  463.4 16.0 %collective-permute-start.42 = (bf16[256,512]{1,0:T(8,128)(2,1)S(1)}, bf16[256,512]{1,0:T(8,128)(2,1)S(1)}, u32[]{:S(2)}, u32[]{:S(2)}) collective-permute-start(bf16[256,512]{1,0:T(8,128)(2,1)S(1)} %get-tuple-element.206), channel_id=1, source_target_pairs={{0,8},{4,12},{8,0},{12,4},{16,24},{20,28},{24,16},{28,20},{1,9},{5... | collective-permute-start | bytes 786440 | tf_op jit(solution)/shard_map/ppermute | solution.py:50
  465.2 19.1 %collective-permute-start.44 = (bf16[256,512]{1,0:T(8,128)(2,1)S(1)}, bf16[256,512]{1,0:T(8,128)(2,1)S(1)}, u32[]{:S(2)}, u32[]{:S(2)}) collective-permute-start(bf16[256,512]{1,0:T(8,128)(2,1)S(1)} %get-tuple-element.207), channel_id=1, source_target_pairs={{0,24},{4,28},{8,16},{12,20},{16,8},{20,12},{24,0},{28,4},{1,25},{... | collective-permute-start | bytes 786440 | tf_op jit(solution)/shard_map/ppermute | solution.py:50
  468.1 17.6 %collective-permute-start.43 = (bf16[256,512]{1,0:T(8,128)(2,1)S(1)}, bf16[256,512]{1,0:T(8,128)(2,1)S(1)}, u32[]{:S(2)}, u32[]{:S(2)}) collective-permute-start(bf16[256,512]{1,0:T(8,128)(2,1)S(1)} %get-tuple-element.208), channel_id=1, source_target_pairs={{0,16},{4,20},{8,24},{12,28},{16,0},{20,4},{24,8},{28,12},{1,17},{... | collective-permute-start | bytes 786440 | tf_op jit(solution)/shard_map/ppermute | solution.py:50
  489.1 1.3 collective-permute-start.45
  491.0 3.7 collective-permute-start.46
  495.4 3.7 collective-permute-start.47
  499.7 3.9 collective-permute-start.48
  504.2 4.7 collective-permute-start.49
  510.3 15.3 %copy-start.27 = (f32[4352]{0:T(1024)S(1)}, f32[4352]{0:T(1024)}, u32[]{:S(2)}) copy-start(f32[4352]{0:T(1024)} %param.19) | copy-start | bytes 52228
  510.3 15.3 %copy-start.28 = (f32[4352]{0:T(1024)S(1)}, f32[4352]{0:T(1024)}, u32[]{:S(2)}) copy-start(f32[4352]{0:T(1024)} %param.18) | copy-start | bytes 52228
  (26 other events, 134.3 us)
Sparse Core Ops, SparseCore 0:
  99.3 89.6 all-reduce.4
  234.9 86.5 all-reduce.6
  324.4 85.4 all-reduce.8
  439.6 86.0 all-reduce.10
Sparse Core Ops, SparseCore 1:
  102.2 101.7 all-gather.1
  250.0 92.2 reduce-scatter.2
  346.1 76.3 reduce-scatter.4

commit v3 on v2

--- a/solution.py
+++ b/solution.py
@@ -82,8 +82,12 @@
     return me_ref[0] ^ k if parts > 1 else 0
 
 
-def columns_at(ref, block, width):
-    return ref[:, pl.ds(pl.multiple_of(block * width, width), width)]
+def in_order(me_ref, part_refs, whole_ref):
+    parts = len(part_refs)
+    rows = part_refs[0].shape[0]
+    for k, ref in enumerate(part_refs):
+        at = pl.multiple_of(place_of(me_ref, k, parts) * rows, rows)
+        whole_ref[pl.ds(at, rows), :] = ref[...]
 
 
 def turned(normed, cosine, sine):
@@ -104,14 +108,10 @@
 
 
 def project_kernel(parts, q_tiles, me_ref, h_ref, *refs):
-    w_refs = refs[:parts]
-    cos_ref, sin_ref, gain_ref, q_ref, kv_ref, lin_ref = refs[parts:]
+    cos_ref, sin_ref, gain_ref, q_ref, kv_ref, lin_ref, w_ref = refs[parts:]
     tile = pl.program_id(0)
-    depth = w_refs[0].shape[0]
-    total = None
-    for k, w_ref in enumerate(w_refs):
-        term = dot(columns_at(h_ref, place_of(me_ref, k, parts), depth), w_ref[...])
-        total = term if total is None else total + term
+    in_order(me_ref, refs[:parts], w_ref)
+    total = dot(h_ref[...], w_ref[...])
     per_tile = TILE // HD
 
     def normed_to(out_ref, gain):
@@ -242,14 +242,20 @@
             o_ref[:, pl.ds(at, block)] = term.astype(bf16)
 
 
-def mlp_kernel(x_ref, s_ref, gain_ref, c_ref, wg_ref, wu_ref, wd_ref, y_ref, h_ref, dg_ref, du_ref, a_ref):
+def plain_kernel(a_ref, w_ref, o_ref):
+    o_ref[...] = dot(a_ref[...], w_ref[...]).astype(bf16)
+
+
+def mlp_kernel(x_ref, s_ref, gain_ref, wg_ref, wu_ref, da_ref, y_ref, h_ref, scale_ref, dg_ref, du_ref, a_ref):
     @pl.when(pl.program_id(0) == 0)
     def _():
         def rows_of(r, unused):
             at = pl.ds(pl.multiple_of(r * 64, 64), 64)
             y = x_ref[at, :].astype(f32) + s_ref[at, :].astype(f32)
             y_ref[at, :] = y
-            h_ref[at, :] = (y * unit_scale(y) * gain_ref[...]).astype(bf16)
+            scale = unit_scale(y)
+            scale_ref[at, :] = scale
+            h_ref[at, :] = (y * scale * gain_ref[...]).astype(bf16)
             return unused
 
         lax.fori_loop(0, x_ref.shape[0] // 64, rows_of, 0, unroll=2)
@@ -257,7 +263,7 @@
     hidden = h_ref[...]
     gate = dot(hidden, wg_ref[...])
     up = dot(hidden, wu_ref[...])
-    grad = dot(c_ref[...], wd_ref[...])
+    grad = da_ref[...].astype(f32)
     sig = 1.0 / (1.0 + jnp.exp(-gate))
     silu = gate * sig
     a_ref[...] = (silu * up).astype(bf16)
@@ -273,19 +279,18 @@
     o_ref[...] = dot(a_ref[...], w_ref[...], last_dims).astype(bf16)
 
 
-def residual_back_kernel(parts, share, me_ref, y_ref, c_ref, s_ref, gain_ref, *refs):
-    out_parts = refs[:parts]
-    dy_ref, low_ref, do_ref, dgain_ref = refs[parts:]
+def residual_back_kernel(parts, share, me_ref, y_ref, scale_ref, c_ref, s_ref, gain_ref, *refs):
+    dy_ref, low_ref, do_ref, dgain_ref, w_ref = refs[parts:]
 
     @pl.when(pl.program_id(0) == 0)
     def _():
         dgain_ref[...] = jnp.zeros_like(dgain_ref)
+        in_order(me_ref, refs[:parts], w_ref)
 
     def rows_of(r, dgain):
         at = pl.ds(pl.multiple_of(r * 32, 32), 32)
-        y = y_ref[at, :]
-        scale = unit_scale(y)
-        unit = y * scale
+        scale = scale_ref[at, :]
+        unit = y_ref[at, :] * scale
         grad = s_ref[at, :].astype(f32)
         dy = c_ref[at, :].astype(f32) + norm_back(unit, scale, gain_ref[...], grad)
         dy_ref[at, :] = dy
@@ -294,12 +299,7 @@
 
     zeros = jnp.zeros(dgain_ref.shape, f32)
     dgain_ref[...] += share * lax.fori_loop(0, y_ref.shape[0] // 32, rows_of, zeros, unroll=2)
-    total = None
-    depth = out_parts[0].shape[0]
-    for k, w_ref in enumerate(out_parts):
-        term = dot(columns_at(low_ref, place_of(me_ref, k, parts), depth), w_ref[...])
-        total = term if total is None else total + term
-    do_ref[...] = total.astype(bf16)
+    do_ref[...] = dot(low_ref[...], w_ref[...]).astype(bf16)
 
 
 def attend_back_kernel(group, heads, parts, outs, own_ref, inverse_ref, starts_ref, q_ref, *refs):
@@ -380,9 +380,9 @@
 
 def key_back_kernel(parts, terms, kv_heads, me_ref, *refs):
     term_refs = refs[:terms]
-    lin_ref, cos_ref, sin_ref, gain_ref, dq_ref, x_ref = refs[terms : terms + 6]
-    w_refs = refs[terms + 6 : terms + 6 + parts]
-    dkv_ref, dgain_k_ref, dgain_ref, dh_ref, unit_ref = refs[terms + 6 + parts :]
+    lin_ref, cos_ref, sin_ref, gain_ref, dq_ref, x_ref, scale_ref = refs[terms : terms + 7]
+    w_refs = refs[terms + 7 : terms + 7 + parts]
+    dkv_ref, dgain_k_ref, dgain_ref, dh_ref = refs[terms + 7 + parts :]
     dgain = jnp.zeros((1, HD), f32)
 
     def total(begin):
@@ -403,13 +403,7 @@
         dkv_ref[:, (kv_heads + g) * HD : (kv_heads + g + 1) * HD] = total((2 * g + 1) * HD).astype(bf16)
     dgain_k_ref[...] = jnp.broadcast_to(dgain, dgain_k_ref.shape)
 
-    def rows_of(r, unused):
-        at = pl.ds(pl.multiple_of(r * 64, 64), 64)
-        x = x_ref[at, :].astype(f32)
-        unit_ref[at, :] = x * unit_scale(x)
-        return unused
-
-    lax.fori_loop(0, x_ref.shape[0] // 64, rows_of, 0, unroll=2)
+    scale = scale_ref[...]
     width = w_refs[0].shape[0]
     block = min(width, TILE)
     q_width = dq_ref.shape[1]
@@ -421,15 +415,15 @@
             term = dot(dq_ref[...], w_ref[rows, :q_width], last_dims)
             term = term + dot(dkv_ref[...], w_ref[rows, q_width:], last_dims)
             dh_ref[:, here] = term.astype(bf16)
-            dgain_ref[:, here] = jnp.sum(term * unit_ref[:, here], axis=0, keepdims=True)
-
-
-def input_back_kernel(dy_ref, x_ref, s_ref, gain_ref, o_ref):
+            unit = x_ref[:, here].astype(f32) * scale
+            dgain_ref[:, here] = jnp.sum(term * unit, axis=0, keepdims=True)
+
+
+def input_back_kernel(dy_ref, x_ref, scale_ref, s_ref, gain_ref, o_ref):
     def rows_of(r, unused):
         at = pl.ds(pl.multiple_of(r * 32, 32), 32)
-        x = x_ref[at, :].astype(f32)
-        scale = unit_scale(x)
-        back = norm_back(x * scale, scale, gain_ref[...], s_ref[at, :].astype(f32))
+        scale = scale_ref[at, :]
+        back = norm_back(x_ref[at, :].astype(f32) * scale, scale, gain_ref[...], s_ref[at, :].astype(f32))
         o_ref[at, :] = dy_ref[at, :] + back
         return unused
 
@@ -480,11 +474,10 @@
                 out_ref[0] = dot(lhs_ref[...], rhs_ref[...], first_dims).astype(bf16)
 
 
-def mlp_weight_grad_kernel(h_ref, c_ref, dg_ref, du_ref, a_ref, dgu_ref, down_ref):
+def mlp_weight_grad_kernel(h_ref, c_ref, dg_ref, du_ref, a_ref, o_ref):
     width = a_ref.shape[1]
-    dgu_ref[:, :width] = dot(h_ref[...], dg_ref[...], first_dims).astype(bf16)
-    dgu_ref[:, width:] = dot(h_ref[...], du_ref[...], first_dims).astype(bf16)
-    down_ref[...] = dot(c_ref[...], a_ref[...], first_dims).astype(bf16)
+    for k, (lhs_ref, rhs_ref) in enumerate(((h_ref, dg_ref), (h_ref, du_ref), (c_ref, a_ref))):
+        o_ref[:, k * width : (k + 1) * width] = dot(lhs_ref[...], rhs_ref[...], first_dims).astype(bf16)
 
 
 def weight_grad_turned_kernel(outs, lhs_ref, rhs_ref, *out_refs):
@@ -643,7 +636,8 @@
     sine = jnp.sin(angles) * jnp.where(jnp.arange(HD) < HD // 2, -1.0, 1.0)[None, :]
 
     inputs = block_input.astype(f32)
-    normed_low = (inputs * unit_scale(inputs) * gain_attn).astype(bf16)
+    scale_in = unit_scale(inputs)
+    normed_low = (inputs * scale_in * gain_attn).astype(bf16)
 
     normed_turned = transposed(me_array, normed_low, parts, row_count)
     if in_pairs:
@@ -667,6 +661,7 @@
                 pl.BlockSpec((tok_count, TILE), lambda n, *_: (0, jnp.maximum(n - q_tiles, 0))),
                 pl.BlockSpec((tok_count, TILE), lambda n, *_: (0, jnp.minimum(n, q_tiles))),
             ],
+            scratch_shapes=[pltpu.VMEM((model_width, TILE), bf16)],
         ),
         out_shape=(
             jax.ShapeDtypeStruct((tok_count, query_width), bf16),
@@ -740,24 +735,35 @@
     hidden_shape = jax.ShapeDtypeStruct((tok_count, ff_width), bf16)
     low_shape = jax.ShapeDtypeStruct((tok_count, model_width), bf16)
     wide_shape = jax.ShapeDtypeStruct((tok_count, model_width), f32)
-    residual, mlp_low, grad_gate, grad_up, hidden_low = pl.pallas_call(
+    scale_spec = pl.BlockSpec((tok_count, 1), lambda *_: (0, 0))
+    scale_shape = jax.ShapeDtypeStruct((tok_count, 1), f32)
+    grad_hidden = pl.pallas_call(
+        plain_kernel,
+        grid=(tiles,),
+        in_specs=[rows_all, pl.BlockSpec((model_width, TILE), lambda n: (0, n + 2 * tiles))],
+        out_specs=tile_spec,
+        out_shape=hidden_shape,
+        compiler_params=params(),
+        cost_estimate=cost(30),
+        name="grad_hidden",
+    )(cotangent, mlp_weights)
+    residual, mlp_low, scale_mlp, grad_gate, grad_up, hidden_low = pl.pallas_call(
         mlp_kernel,
         grid=(tiles,),
         in_specs=[
             rows_all,
             rows_all,
             gain_spec,
-            rows_all,
             pl.BlockSpec((model_width, TILE), lambda n: (0, n)),
             pl.BlockSpec((model_width, TILE), lambda n: (0, n + tiles)),
-            pl.BlockSpec((model_width, TILE), lambda n: (0, n + 2 * tiles)),
+            tile_spec,
         ],
-        out_specs=[rows_all, rows_all, tile_spec, tile_spec, tile_spec],
-        out_shape=(wide_shape, low_shape, hidden_shape, hidden_shape, hidden_shape),
+        out_specs=[rows_all, rows_all, scale_spec, tile_spec, tile_spec, tile_spec],
+        out_shape=(wide_shape, low_shape, scale_shape, hidden_shape, hidden_shape, hidden_shape),
         compiler_params=params(),
         cost_estimate=cost(18),
         name="mlp",
-    )(block_input, attn_sum, gain_mlp[None], cotangent, mlp_weights, mlp_weights, mlp_weights)
+    )(block_input, attn_sum, gain_mlp[None], mlp_weights, mlp_weights, grad_hidden)
 
     hidden_all = pl.BlockSpec((tok_count, ff_width), lambda n: (0, 0))
     out_tile = pl.BlockSpec((tok_count, 512), lambda n: (0, n))
@@ -780,12 +786,12 @@
     grad_mlp_sum = lax.psum(grad_mlp_part, "mp")
 
     row_tile = pl.BlockSpec((tok_count, TILE), lambda n: (0, n))
-    dw_gate_up, dw_down = pl.pallas_call(
+    dw_mlp = pl.pallas_call(
         mlp_weight_grad_kernel,
         grid=(model_width // TILE,),
         in_specs=[row_tile, row_tile, hidden_all, hidden_all, hidden_all],
-        out_specs=[pl.BlockSpec((TILE, k * ff_width), lambda n: (n, 0)) for k in (2, 1)],
-        out_shape=[jax.ShapeDtypeStruct((model_width, k * ff_width), bf16) for k in (2, 1)],
+        out_specs=pl.BlockSpec((TILE, 3 * ff_width), lambda n: (n, 0)),
+        out_shape=jax.ShapeDtypeStruct((model_width, 3 * ff_width), bf16),
         compiler_params=params(),
         cost_estimate=cost(1),
         name="mlp_weight_grad",
@@ -800,9 +806,8 @@
         cost_estimate=cost(1),
         name="mlp_out",
     )(hidden_low, mlp_weights)
-    gate_up_grads = lax.psum_scatter(dw_gate_up, "dp", scatter_dimension=0, tiled=True)
-    down_grads = lax.psum_scatter(dw_down, "dp", scatter_dimension=0, tiled=True)
-    grad_mlp_sum, mlp_part, dw_gate_up = lax.optimization_barrier((grad_mlp_sum, mlp_part, dw_gate_up))
+    mlp_grads = lax.psum_scatter(dw_mlp, "dp", scatter_dimension=0, tiled=True)
+    grad_mlp_sum, mlp_part, dw_mlp = lax.optimization_barrier((grad_mlp_sum, mlp_part, dw_mlp))
     mlp_sum = lax.psum(mlp_part, "mp")
 
     half_rows = tok_count // 2
@@ -812,9 +817,16 @@
         grid_spec=pltpu.PrefetchScalarGridSpec(
             num_scalar_prefetch=1,
             grid=(2,),
-            in_specs=[half_spec, half_spec, half_spec, gain_spec]
+            in_specs=[
+                half_spec,
+                pl.BlockSpec((half_rows, 1), lambda n, *_: (n, 0)),
+                half_spec,
+                half_spec,
+                gain_spec,
+            ]
             + [pl.BlockSpec((model_width // parts, query_width), lambda *_: (0, 0))] * parts,
             out_specs=[half_spec, half_spec, pl.BlockSpec((half_rows, query_width), lambda n, *_: (n, 0)), gain_spec],
+            scratch_shapes=[pltpu.VMEM((model_width, query_width), bf16)],
         ),
         out_shape=(
             wide_shape,
@@ -825,7 +837,7 @@
         compiler_params=params(),
         cost_estimate=cost(1),
         name="residual_back",
-    )(me_array, residual, cotangent, grad_mlp_sum, gain_mlp[None], *out_parts)
+    )(me_array, residual, scale_mlp, cotangent, grad_mlp_sum, gain_mlp[None], *out_parts)
     out_rows = token_total // parts
     dkv_spec = pl.BlockSpec((out_rows, 2 * heads * HD), lambda g, *_: (0, g))
     back = pl.pallas_call(
@@ -866,12 +878,12 @@
         sine,
         head_gains[:1],
     )
-    back, gate_up_grads = lax.optimization_barrier((back, gate_up_grads))
     grad_query_low, query_gain_grad = back[:2]
     query_gain_grad = jnp.sum(query_gain_grad, axis=0) / 8.0
     if in_pairs:
         came = [swap(back[2 + k], "dp", 1) for k in range(1, parts, 2)]
         halves = [add_pair(back[2 + 2 * k], came[k]) for k in range(parts // 2)]
+        halves, mlp_grads = lax.optimization_barrier((halves, mlp_grads))
         terms = [halves[0]] + [swap(halves[k], "dp", 2 * k) for k in range(1, parts // 2)]
     else:
         terms = [lax.psum_scatter(back[2], "dp", scatter_dimension=0, tiled=True)]
@@ -879,7 +891,15 @@
     [dw_query] = weight_grad(me_array, normed_turned, [grad_query_low], parts, row_count, True)
     [dw_out] = weight_grad(me_array, grad_res_low, [attended_low], parts, row_count)
 
-    terms, dw_query, dw_out, mlp_sum = lax.optimization_barrier((terms, dw_query, dw_out, mlp_sum))
+    def scattered(made):
+        if in_pairs:
+            return sum(term.astype(f32) for term in scatter_small(*made)).astype(bf16)
+        whole = made[0].reshape(model_width, -1)
+        return lax.psum_scatter(whole, "dp", scatter_dimension=0, tiled=True)
+
+    block_output = (residual + mlp_sum.astype(f32)).astype(bf16)
+    terms, block_output, dw_query, dw_out = lax.optimization_barrier((terms, block_output, dw_query, dw_out))
+    query_grads, out_grads = scattered(dw_query), scattered(dw_out)
     grad_kv_low, key_gain_grad, attn_gain_grad, grad_norm_part = pl.pallas_call(
         functools.partial(key_back_kernel, parts, len(terms), kv_heads),
         grid_spec=pltpu.PrefetchScalarGridSpec(
@@ -888,7 +908,7 @@
             in_specs=[pl.BlockSpec((tok_count, 2 * kv_width), lambda *_: (0, 0))] * len(terms)
             + [pl.BlockSpec((tok_count, kv_width), lambda *_: (0, query_width // kv_width))]
             + [angle_spec, angle_spec, pl.BlockSpec((1, HD), lambda *_: (0, 0))]
-            + [q_all, rows_all]
+            + [q_all, rows_all, scale_spec]
             + [pl.BlockSpec((model_width // parts, qkv_cols), lambda *_: (0, 0))] * parts,
             out_specs=[
                 pl.BlockSpec((tok_count, 2 * kv_width), lambda *_: (0, 0)),
@@ -896,7 +916,6 @@
                 gain_spec,
                 rows_all,
             ],
-            scratch_shapes=[pltpu.VMEM((tok_count, model_width), f32)],
         ),
         out_shape=[
             jax.ShapeDtypeStruct((tok_count, 2 * kv_width), bf16),
@@ -907,42 +926,38 @@
         compiler_params=params(),
         cost_estimate=cost(1),
         name="key_back",
-    )(me_array, *terms, lin, cosine, sine, head_gains[1:], grad_query_low, block_input, *qkv_parts)
+    )(me_array, *terms, lin, cosine, sine, head_gains[1:], grad_query_low, block_input, scale_in, *qkv_parts)
     [dw_kv] = weight_grad(me_array, normed_turned, [grad_kv_low], parts, row_count, True)
 
-    grad_norm_sum = lax.psum(grad_norm_part, "mp")
-    if in_pairs:
-        small = [scatter_small(*dw) for dw in (dw_query, dw_kv, dw_out)]
-        small = [sum(term.astype(f32) for term in piece).astype(bf16) for piece in small]
-    else:
-
-        def scattered(made):
-            whole = made[0].reshape(model_width, -1)
-            return lax.psum_scatter(whole, "dp", scatter_dimension=0, tiled=True)
-
-        small = [scattered(dw) for dw in (dw_query, dw_kv, dw_out)]
-    gain_grads = sum_all(
-        jnp.concatenate([attn_gain_grad[0], mlp_gain_grad[0], query_gain_grad, key_gain_grad[0]])
-    )
-    square = sum(jnp.sum(jnp.square(grad.astype(f32))) for grad in small + [gate_up_grads, down_grads])
-    square_total = sum_all(square.reshape(1, 1))[0, 0]
+    grad_norm_share = lax.psum_scatter(grad_norm_part, "mp", scatter_dimension=0, tiled=True)
+    weight_grads = [query_grads, scattered(dw_kv), out_grads, mlp_grads]
+    square = sum(jnp.sum(jnp.square(grad.astype(f32))) for grad in weight_grads)
+    square, grad_norm_share = lax.optimization_barrier((square, grad_norm_share))
+    grad_norm_sum = lax.all_gather(grad_norm_share, "mp", axis=0, tiled=True)
+    local = [attn_gain_grad[0], mlp_gain_grad[0], query_gain_grad, key_gain_grad[0]]
+    totals = sum_all(jnp.concatenate([jnp.broadcast_to(square, (HD,))] + local))
+    square_total, gain_grads = totals[0], totals[HD:]
     grad_norm = jnp.sqrt(square_total + jnp.sum(gain_grads * gain_grads))
     factor = 1.0 / jnp.maximum(grad_norm, 1.0)
-    new_weights, new_momentum, new_ema = update_weights(factor[None], weights, momentum, ema_weights, small + [gate_up_grads, down_grads])
-    gain_grads, mlp_sum = lax.optimization_barrier((gain_grads, mlp_sum))
-    block_output = (residual + mlp_sum.astype(f32)).astype(bf16)
+    new_weights, new_momentum, new_ema = update_weights(factor[None], weights, momentum, ema_weights, weight_grads)
     eighth = tok_count // 8
     eighth_spec = pl.BlockSpec((eighth, model_width), lambda n: (n, 0))
     grad_input = pl.pallas_call(
         input_back_kernel,
         grid=(8,),
-        in_specs=[eighth_spec, eighth_spec, eighth_spec, gain_spec],
+        in_specs=[
+            eighth_spec,
+            eighth_spec,
+            pl.BlockSpec((eighth, 1), lambda n: (n, 0)),
+            eighth_spec,
+            gain_spec,
+        ],
         out_specs=eighth_spec,
         out_shape=wide_shape,
         compiler_params=params(),
-        cost_estimate=cost(300),
+        cost_estimate=cost(8),
         name="input_back",
-    )(grad_residual, block_input, grad_norm_sum, gain_attn[None])
+    )(grad_residual, block_input, scale_in, grad_norm_sum, gain_attn[None])
     new_gains, new_gain_momentum, new_gain_ema = update(gains, gain_momentum, gain_ema, gain_grads, factor, gain_rate)
     return (
         block_output,

time: 544 us -> 520 us (0.956)
  starting transfers between devices: 52.7 us -> 37.9 us
    psum x1, waiting for transfers between devices: 89 us -> 0.89 us  [per_device(): attn_sum = lax.psum(attn_part, 'mp')]
    all_gather x1, waiting for transfers between devices: 15 us -> 82.1 us  [per_device(): mlp_weights = lax.all_gather(mlp_own, 'dp', axis=0, tiled=True)]
    reduce_scatter x2, waiting for transfers between devices: 0.03 us -> 15.3 us  [the longest x1 15.3 us: per_device(): mlp_grads = lax.psum_scatter(dw_mlp, 'dp', scatter_dimension=0, tiled=True)]
    ppermute x50 -> x45, starting transfers between devices: 52.2 us -> 37.1 us  [swap(): return lax.ppermute(array, axis, [(i, i ^ distance) for i in range(count)])]
    psum x1, waiting for transfers between devices: 38.9 us -> 28.5 us  [per_device(): mlp_sum = lax.psum(mlp_part, 'mp')]
    pallas_call x0 -> x1, Pallas kernels: none -> 8.35 us  [per_device(): pl.pallas_call(plain_kernel, grid=(tiles,), in_specs=[rows_all, pl.BlockS...]
    ppermute x50 -> x45, waiting for transfers between devices: 59.9 us -> 67.3 us  [swap(): return lax.ppermute(array, axis, [(i, i ^ distance) for i in range(count)])]
    all_gather x0 -> x1, waiting for transfers between devices: none -> 7.34 us  [per_device(): grad_norm_sum = lax.all_gather(grad_norm_share, 'mp', axis=0, tiled=True)]
  transfers between devices with their start and end apart: 57 -> 52, of which waited for: 28 -> 26; matrix products, arithmetic and copies ran while one was open for 6% -> 6% of each run, Pallas kernels for 19% -> 22%
where the time goes in v3:
time: 520 us; the launch traced here: 518 us
  waiting for transfers between devices  263 us (51%)
  Pallas kernels  161 us (31%)
  starting transfers between devices  37.9 us (7%)
  other arithmetic  23.8 us (5%)
  between operations  21.3 us (4%)
  local copies, waits for them, and re-layouts  10.9 us (2%)
    all_gather x1, waiting for transfers between devices, per_device(): mlp_weights = lax.all_gather(mlp_own, 'dp', axis=0, tiled=True)  82.1 us
    ppermute x45, waiting for transfers between devices, swap(): return lax.ppermute(array, axis, [(i, i ^ distance) for i in range(count)])  67.3 us
    psum x1, waiting for transfers between devices, per_device(): grad_mlp_sum = lax.psum(grad_mlp_part, 'mp')  61.6 us
    ppermute x45, starting transfers between devices, swap(): return lax.ppermute(array, axis, [(i, i ^ distance) for i in range(count)])  37.1 us
    psum x1, waiting for transfers between devices, per_device(): mlp_sum = lax.psum(mlp_part, 'mp')  28.5 us
    pallas_call x1, Pallas kernels, per_device(): pl.pallas_call(mlp_kernel, grid=(tiles,), in_specs=[rows_all, rows_all, g...  16.3 us
    pallas_call x1, Pallas kernels, per_device(): pl.pallas_call(mlp_weight_grad_kernel, grid=(model_width // TILE,), in_sp...  15.5 us
    reduce_scatter x1, waiting for transfers between devices, per_device(): mlp_grads = lax.psum_scatter(dw_mlp, 'dp', scatter_dimension=0, tiled=True)  15.3 us
  transfers between devices with their start and end apart: 52, of which 26 were waited for; matrix products, arithmetic and copies ran while one was open for 6% of the time, Pallas kernels for 22%

profile of v3, /device:TPU:0, one launch (start us, length us, event | category | flops | bytes accessed | tf_op | source)
XLA Modules:
  0.0 518.3 jit_solution(12835445873389367582)
XLA Ops:
  8.1 1.3 slice.162.refs_0_.refs_11_
  9.9 2.6 collective-permute-start.1
  12.5 1.5 collective-permute-start.3
  14.0 3.2 convert.12
  17.3 1.7 copy-done.1
  19.0 2.0 collective-permute-start.7
  22.9 1.9 fusion.2.x_ref.h_ref
  25.0 6.0 %transposed.1.lhs_ref = bf16[2048,512]{1,0:T(8,128)(2,1)} custom-call(s32[1]{0:T(128)} %bitcast.1.me_ref, bf16[512,2048]{1,0:T(8,128)(2,1)} %fusion.2.x_ref.h_ref), custom_call_target="tpu_custom_call" | custom-call | flops 5000000000 | bytes 17000000 | tf_op jit(solution)/shard_map/transposed/pallas_call | solution.py:440
  31.0 6.6 %collective-permute-done.3.refs_4_.refs_15_ = bf16[256,1024]{1,0:T(8,128)(2,1)} collective-permute-done((bf16[256,1024]{1,0:T(8,128)(2,1)S(1)}, bf16[256,1024]{1,0:T(8,128)(2,1)}, u32[]{:S(2)}, u32[]{:S(2)}) %collective-permute-start.3) | collective-permute-done | bytes 524320 | tf_op jit(solution)/shard_map/ppermute | solution.py:50
  38.7 1.8 fusion.13
  40.5 1.8 collective-permute-start.8
  44.5 8.4 %project.1 = (bf16[512,512]{1,0:T(8,128)(2,1)}, bf16[512,512]{1,0:T(8,128)(2,1)}, f32[512,768]{1,0:T(8,128)}) custom-call(s32[1]{0:T(128)} %bitcast.1.me_ref, bf16[512,2048]{1,0:T(8,128)(2,1)} %fusion.2.x_ref.h_ref, bf16[256,1024]{1,0:T(8,128)(2,1)} %copy-done.4, bf16[256,1024]{1,0:T(8,128)(2,1)} %copy-done.9, ...), custom_call_target="tpu_custom_call" | custom-call | flops 6000000000 | bytes 20400000 | tf_op jit(solution)/shard_map/project/pallas_call | solution.py:651
  52.9 2.1 collective-permute-done.8.refs_4_
  55.0 1.4 collective-permute-start.15
  57.0 1.5 collective-permute-start.19
  59.0 1.4 collective-permute-done.10.refs_1_
  60.9 9.2 %collective-permute-done.15.refs_2_ = bf16[512,512]{1,0:T(8,128)(2,1)S(1)} collective-permute-done((bf16[512,512]{1,0:T(8,128)(2,1)}, bf16[512,512]{1,0:T(8,128)(2,1)S(1)}, u32[]{:S(2)}, u32[]{:S(2)}) %collective-permute-start.15) | collective-permute-done | bytes 524320 | tf_op jit(solution)/shard_map/ppermute | solution.py:50
  70.0 11.2 %collective-permute-done.17.refs_4_ = bf16[512,512]{1,0:T(8,128)(2,1)} collective-permute-done((bf16[512,512]{1,0:T(8,128)(2,1)}, bf16[512,512]{1,0:T(8,128)(2,1)}, u32[]{:S(2)}, u32[]{:S(2)}) %collective-permute-start.17) | collective-permute-done | bytes 524320 | tf_op jit(solution)/shard_map/ppermute | solution.py:50
  81.9 1.6 slice.117
  85.4 10.7 %attend.1 = (f32[8,128,256]{2,1,0:T(8,128)}, bf16[512,512]{1,0:T(8,128)(2,1)}, f32[8,8,256]{2,1,0:T(8,128)}) custom-call(s32[4]{0:T(128)} %get-tuple-element.189.own_ref, s32[32]{0:T(128)} %fusion.14.inverse_ref, s32[8]{0:T(128)} %copy-done.31, bf16[512,512]{1,0:T(8,128)(2,1)} %get-tuple-element.95.q_ref, bf16[512,512]{1,0:T(8,128)(2,1)} %get-tuple-element.103.refs_0_, ...), custom_call_target="tpu_custom_call" | custom-call | flops 16000000000 | bytes 54400000 | tf_op jit(solution)/shard_map/attend/pallas_call | solution.py:694
  96.1 4.5 project_out.1
  100.9 82.1 %all-gather.3.cloned.1.call-done.w_ref.wg_ref.wu_ref = bf16[2048,4608]{1,0:T(8,128)(2,1)} async-done(((bf16[256,4608]{1,0:T(8,128)(2,1)}), bf16[2048,4608]{1,0:T(8,128)(2,1)}) %all-gather.3.cloned.1.call-update) | async-done | bytes 18874384 | tf_op jit(solution)/shard_map/all_gather | solution.py:684
  182.9 8.3 %grad_hidden.1.da_ref = bf16[512,1536]{1,0:T(8,128)(2,1)} custom-call(bf16[512,2048]{1,0:T(8,128)(2,1)} %c_ref.3, bf16[2048,4608]{1,0:T(8,128)(2,1)} %all-gather.3.cloned.1.call-done.w_ref.wg_ref.wu_ref), custom_call_target="tpu_custom_call" | custom-call | flops 30000001024 | bytes 102000000 | tf_op jit(solution)/shard_map/grad_hidden/pallas_call | solution.py:740
  192.2 16.3 %mlp.1 = (f32[512,2048]{1,0:T(8,128)}, bf16[512,2048]{1,0:T(8,128)(2,1)}, f32[512,1]{1,0:T(8,128)}, bf16[512,1536]{1,0:T(8,128)(2,1)}, bf16[512,1536]{1,0:T(8,128)(2,1)}, /*index=5*/bf16[512,1536]{1,0:T(8,128)(2,1)}) custom-call(bf16[512,2048]{1,0:T(8,128)(2,1)} %x_ref.3, bf16[512,2048]{1,0:T(8,128)(2,1)} %all-reduce.4.cloned.1.call-done.s_ref, ...), custom_call_target="tpu_custom_call" | custom-call | flops 17999998976 | bytes 61200000 | tf_op jit(solution)/shard_map/mlp/pallas_call | solution.py:750
  208.5 11.3 %mlp_back.1 = bf16[512,2048]{1,0:T(8,128)(2,1)} custom-call(bf16[512,1536]{1,0:T(8,128)(2,1)} %get-tuple-element.123.dg_ref, bf16[512,1536]{1,0:T(8,128)(2,1)} %get-tuple-element.124.du_ref, bf16[2048,4608]{1,0:T(8,128)(2,1)} %all-gather.3.cloned.1.call-done.w_ref.wg_ref.wu_ref, bf16[2048,4608]{1,0:T(8,128)(2,1)} %all-gather.3.cloned.1.call-done.w_ref.wg_ref.wu_ref), custom_call_target="tpu_custom_call" | custom-call | flops 11000000512 | bytes 37400000 | tf_op jit(solution)/shard_map/mlp_back/pallas_call | solution.py:770
  219.8 15.5 %mlp_weight_grad.1 = bf16[2048,4608]{1,0:T(8,128)(2,1)} custom-call(bf16[512,2048]{1,0:T(8,128)(2,1)} %get-tuple-element.129.h_ref, bf16[512,2048]{1,0:T(8,128)(2,1)} %c_ref.3, bf16[512,1536]{1,0:T(8,128)(2,1)} %get-tuple-element.123.dg_ref, bf16[512,1536]{1,0:T(8,128)(2,1)} %get-tuple-element.124.du_ref, bf16[512,1536]{1,0:T(8,128)(2,1)} %get-tuple-element.128.a_ref), custom_call_target="tpu_custom_call" | custom-call | flops 1000000000 | bytes 3400000 | tf_op jit(solution)/shard_map/mlp_weight_grad/pallas_call | solution.py:789
  235.4 7.9 %mlp_out.1 = bf16[512,2048]{1,0:T(8,128)(2,1)} custom-call(bf16[512,1536]{1,0:T(8,128)(2,1)} %get-tuple-element.128.a_ref, bf16[2048,4608]{1,0:T(8,128)(2,1)} %all-gather.3.cloned.1.call-done.w_ref.wg_ref.wu_ref), custom_call_target="tpu_custom_call" | custom-call | flops 1000000000 | bytes 3400000 | tf_op jit(solution)/shard_map/mlp_out/pallas_call | solution.py:799
  243.3 61.6 %all-reduce.6.cloned.1.call-done.s_ref = bf16[512,2048]{1,0:T(8,128)(2,1)} async-done(((bf16[512,2048]{1,0:T(8,128)(2,1)}), bf16[512,2048]{1,0:T(8,128)(2,1)}) %all-reduce.6.cloned.1.call-update) | async-done | bytes 2097168 | tf_op jit(solution)/shard_map/psum | solution.py:786
  305.6 8.8 %residual_back.1 = (f32[512,2048]{1,0:T(8,128)}, bf16[512,2048]{1,0:T(8,128)(2,1)}, bf16[512,512]{1,0:T(8,128)(2,1)}, f32[1,2048]{1,0:T(1,128)}) custom-call(s32[1]{0:T(128)} %bitcast.1.me_ref, f32[512,2048]{1,0:T(8,128)} %get-tuple-element.121.y_ref, f32[512,1]{1,0:T(8,128)} %get-tuple-element.122.scale_ref, bf16[512,2048]{1,0:T(8,128)(2,1)} %c_ref.3, ...), custom_call_target="tpu_custom_call" | custom-call | flops 1000000000 | bytes 3400000 | tf_op jit(solution)/shard_map/residual_back/pallas_call | solution.py:815
  314.4 15.3 %attend_back.1 = (bf16[512,512]{1,0:T(8,128)(2,1)}, f32[8,128]{1,0:T(8,128)}, bf16[512,512]{1,0:T(8,128)(2,1)}, bf16[512,512]{1,0:T(8,128)(2,1)}, bf16[512,512]{...) custom-call(s32[4]{0:T(128)} %get-tuple-element.189.own_ref, ...), custom_call_target="tpu_custom_call" | custom-call | flops 1000000000 | bytes 3400000 | tf_op jit(solution)/shard_map/attend_back/pallas_call | solution.py:843
  329.7 1.4 collective-permute-start.21
  332.6 7.1 %weight_grad.1 = (bf16[4,256,512]{2,1,0:T(8,128)(2,1)}, bf16[4,256,512]{2,1,0:T(8,128)(2,1)}) custom-call(s32[1]{0:T(128)} %bitcast.1.me_ref, bf16[512,2048]{1,0:T(8,128)(2,1)} %get-tuple-element.152.lhs_ref, bf16[512,512]{1,0:T(8,128)(2,1)} %get-tuple-element.111.low_ref.refs_0_), custom_call_target="tpu_custom_call" | custom-call | flops 1000000000 | bytes 3400000 | tf_op jit(solution)/shard_map/weight_grad/pallas_call | solution.py:516
  339.7 4.2 weight_grad_turned.2
  345.5 15.3 %reduce-scatter.3.cloned.1.call-done.refs_3_ = bf16[256,4608]{1,0:T(8,128)(2,1)} async-done(((bf16[2048,4608]{1,0:T(8,128)(2,1)}), bf16[256,4608]{1,0:T(8,128)(2,1)}) %reduce-scatter.3.cloned.1.call-update) | async-done | bytes 2359312 | tf_op jit(solution)/shard_map/reduce_scatter | solution.py:809
  360.8 1.4 collective-permute-start.25
  362.8 1.5 collective-permute-start.27
  364.3 28.5 %all-reduce.8.cloned.1.call-done = bf16[512,2048]{1,0:T(8,128)(2,1)} async-done(((bf16[512,2048]{1,0:T(8,128)(2,1)}), bf16[512,2048]{1,0:T(8,128)(2,1)}) %all-reduce.8.cloned.1.call-update) | async-done | bytes 2097168 | tf_op jit(solution)/shard_map/psum | solution.py:811
  392.8 4.9 add_convert_fusion
  398.9 9.0 %key_back.1 = (bf16[512,512]{1,0:T(8,128)(2,1)}, f32[8,128]{1,0:T(8,128)}, f32[1,2048]{1,0:T(1,128)}, bf16[512,2048]{1,0:T(8,128)(2,1)}) custom-call(s32[1]{0:T(128)} %bitcast.1.me_ref, bf16[512,512]{1,0:T(8,128)(2,1)} %add_convert_fusion.6.refs_0_, bf16[512,512]{1,0:T(8,128)(2,1)} %copy-done.18, bf16[512,512]{1,0:T(8,128)(2,1)} %copy-done.19, ...), custom_call_target="tpu_custom_call" | custom-call | flops 1000000000 | bytes 3400000 | tf_op jit(solution)/shard_map/key_back/pallas_call | solution.py:903
  408.3 4.4 weight_grad_turned.3
  412.9 1.8 multiply_reduce_fusion
  415.3 2.5 collective-permute-start.31
  419.3 2.5 collective-permute-start.35
  422.6 2.8 collective-permute-done.31
  425.5 1.5 collective-permute-start.33
  427.0 4.1 collective-permute-done.30
  431.1 2.4 collective-permute-start.39
  434.1 2.7 collective-permute-done.35
  436.8 1.5 collective-permute-start.37
  438.2 1.5 multiply_reduce_fusion.3
  439.7 2.7 collective-permute-done.34
  442.4 1.5 multiply_reduce_fusion.2
  445.2 2.9 collective-permute-done.39
  448.0 4.9 collective-permute-done.38
  453.0 1.5 multiply_reduce_fusion.1
  457.9 1.5 collective-permute-start.41
  459.3 2.3 collective-permute-done.41
  461.7 1.3 collective-permute-start.42
  463.0 2.4 collective-permute-done.42
  465.8 4.5 collective-permute-done.43
  471.2 4.4 collective-permute-done.44
  478.1 15.2 %update.1 = (f32[256,6144]{1,0:T(8,128)}, f32[256,6144]{1,0:T(8,128)}, f32[256,6144]{1,0:T(8,128)}) custom-call(f32[1]{0:T(128)} %bitcast.29.factor_ref, f32[256,6144]{1,0:T(8,128)} %w_ref.1, f32[256,6144]{1,0:T(8,128)} %m_ref.1, f32[256,6144]{1,0:T(8,128)} %e_ref.1, bf16[256,512]{1,0:T(8,128)(2,1)} %get-tuple-element.187.refs_0_, ...), custom_call_target="tpu_custom_call" | custom-call | flops 1000000000 | bytes 3400000 | tf_op jit(solution)/shard_map/update/pallas_call | solution.py:548
  493.9 7.3 %all-gather.5.cloned.1.call-done.s_ref = bf16[512,2048]{1,0:T(8,128)(2,1)} async-done(((bf16[128,2048]{1,0:T(8,128)(2,1)}), bf16[512,2048]{1,0:T(8,128)(2,1)}) %all-gather.5.cloned.1.call-update) | async-done | bytes 2097168 | tf_op jit(solution)/shard_map/all_gather | solution.py:936
  501.3 8.3 %input_back.1 = f32[512,2048]{1,0:T(8,128)} custom-call(f32[512,2048]{1,0:T(8,128)} %get-tuple-element.156.dy_ref, bf16[512,2048]{1,0:T(8,128)(2,1)} %x_ref.3, f32[512,1]{1,0:T(8,128)} %copy.22.refs_10_.scale_ref, bf16[512,2048]{1,0:T(8,128)(2,1)} %all-gather.5.cloned.1.call-done.s_ref, f32[1,2048]{1,0:T(1,128)} %bitcast.64), custom_call_target="tpu_custom_call" | custom-call | flops 8000000000 | bytes 27200000 | tf_op jit(solution)/shard_map/input_back/pallas_call | solution.py:945
  (184 shorter events, 26.1 us)
Async XLA Ops:
  8.0 174.9 %all-gather.3.cloned.1.call-start = ((), (), s32[]{:S(2)}) async-start(), calls=%async_computation.3 | async-start | bytes 21233664 | tf_op jit(solution)/shard_map/all_gather | solution.py:684
  9.4 11.6 %copy-start.34 = (s32[1,8]{1,0:T(1,128)S(1)}, s32[1,8]{1,0:T(1,128)}, u32[]{:S(2)}) copy-start(s32[1,8]{1,0:T(1,128)} %param.12) | copy-start | bytes 100
  9.4 11.7 %copy-start.24 = (f32[4352]{0:T(1024)S(1)}, f32[4352]{0:T(1024)}, u32[]{:S(2)}) copy-start(f32[4352]{0:T(1024)} %param.17) | copy-start | bytes 52228
  9.4 12.3 %copy-start = (bf16[512,2048]{1,0:T(8,128)(2,1)S(1)}, bf16[512,2048]{1,0:T(8,128)(2,1)}, u32[]{:S(2)}) copy-start(bf16[512,2048]{1,0:T(8,128)(2,1)} %x_ref.3) | copy-start | bytes 6291460
  9.4 31.1 %collective-permute-start = (bf16[256,1024]{1,0:T(8,128)(2,1)S(1)}, bf16[256,1024]{1,0:T(8,128)(2,1)S(1)}, u32[]{:S(2)}, u32[]{:S(2)}) collective-permute-start(bf16[256,1024]{1,0:T(8,128)(2,1)S(1)} %slice.162.refs_0_.refs_11_), channel_id=1, source_target_pairs={{0,4},{4,0},{8,12},{12,8},{16,20},{20,16},{24,28},{28,24},{1,5},{5... | collective-permute-start | bytes 1572872 | tf_op jit(solution)/shard_map/ppermute | solution.py:50
  9.9 21.1 %collective-permute-start.1 = (bf16[256,1024]{1,0:T(8,128)(2,1)S(1)}, bf16[256,1024]{1,0:T(8,128)(2,1)}, u32[]{:S(2)}, u32[]{:S(2)}) collective-permute-start(bf16[256,1024]{1,0:T(8,128)(2,1)S(1)} %slice.162.refs_0_.refs_11_), channel_id=1, source_target_pairs={{0,8},{4,12},{8,0},{12,4},{16,24},{20,28},{24,16},{28,20},{1,9},{5... | collective-permute-start | bytes 1572872 | tf_op jit(solution)/shard_map/ppermute | solution.py:50
  12.5 25.1 %collective-permute-start.3 = (bf16[256,1024]{1,0:T(8,128)(2,1)S(1)}, bf16[256,1024]{1,0:T(8,128)(2,1)}, u32[]{:S(2)}, u32[]{:S(2)}) collective-permute-start(bf16[256,1024]{1,0:T(8,128)(2,1)S(1)} %slice.162.refs_0_.refs_11_), channel_id=1, source_target_pairs={{0,16},{4,20},{8,24},{12,28},{16,0},{20,4},{24,8},{28,12},{1,17},{... | collective-permute-start | bytes 1572872 | tf_op jit(solution)/shard_map/ppermute | solution.py:50
  14.0 24.1 %collective-permute-start.5 = (bf16[256,1024]{1,0:T(8,128)(2,1)S(1)}, bf16[256,1024]{1,0:T(8,128)(2,1)}, u32[]{:S(2)}, u32[]{:S(2)}) collective-permute-start(bf16[256,1024]{1,0:T(8,128)(2,1)S(1)} %slice.162.refs_0_.refs_11_), channel_id=1, source_target_pairs={{0,24},{4,28},{8,16},{12,20},{16,8},{20,12},{24,0},{28,4},{1,25},{... | collective-permute-start | bytes 1572872 | tf_op jit(solution)/shard_map/ppermute | solution.py:50
  18.9 39.5 %copy-start.8 = (bf16[256,512]{1,0:T(8,128)(2,1)}, bf16[256,512]{1,0:T(8,128)(2,1)S(1)}, u32[]{:S(2)}) copy-start(bf16[256,512]{1,0:T(8,128)(2,1)S(1)} %slice.118.refs_0_) | copy-start | bytes 786436
  19.0 33.9 %collective-permute-start.7 = (bf16[256,512]{1,0:T(8,128)(2,1)S(1)}, bf16[256,512]{1,0:T(8,128)(2,1)}, u32[]{:S(2)}, u32[]{:S(2)}) collective-permute-start(bf16[256,512]{1,0:T(8,128)(2,1)S(1)} %slice.118.refs_0_), channel_id=1, source_target_pairs={{0,8},{4,12},{8,0},{12,4},{16,24},{20,28},{24,16},{28,20},{1,9},{5... | collective-permute-start | bytes 786440 | tf_op jit(solution)/shard_map/ppermute | solution.py:50
  31.0 11.3 %collective-permute-start.2 = (bf16[256,1024]{1,0:T(8,128)(2,1)}, bf16[256,1024]{1,0:T(8,128)(2,1)S(1)}, u32[]{:S(2)}, u32[]{:S(2)}) collective-permute-start(bf16[256,1024]{1,0:T(8,128)(2,1)} %collective-permute-done.1.refs_2_.refs_13_), channel_id=1, source_target_pairs={{0,4},{4,0},{8,12},{12,8},{16,20},{20,16},{24,28},{28,24},{1,5},{5... | collective-permute-start | bytes 1572872 | tf_op jit(solution)/shard_map/ppermute | solution.py:50
  37.6 5.9 %collective-permute-start.4 = (bf16[256,1024]{1,0:T(8,128)(2,1)}, bf16[256,1024]{1,0:T(8,128)(2,1)S(1)}, u32[]{:S(2)}, u32[]{:S(2)}) collective-permute-start(bf16[256,1024]{1,0:T(8,128)(2,1)} %collective-permute-done.3.refs_4_.refs_15_), channel_id=1, source_target_pairs={{0,4},{4,0},{8,12},{12,8},{16,20},{20,16},{24,28},{28,24},{1,5},{5... | collective-permute-start | bytes 1572872 | tf_op jit(solution)/shard_map/ppermute | solution.py:50
  38.1 5.4 %collective-permute-start.6 = (bf16[256,1024]{1,0:T(8,128)(2,1)}, bf16[256,1024]{1,0:T(8,128)(2,1)S(1)}, u32[]{:S(2)}, u32[]{:S(2)}) collective-permute-start(bf16[256,1024]{1,0:T(8,128)(2,1)} %collective-permute-done.5.refs_6_.refs_17_), channel_id=1, source_target_pairs={{0,4},{4,0},{8,12},{12,8},{16,20},{20,16},{24,28},{28,24},{1,5},{5... | collective-permute-start | bytes 1572872 | tf_op jit(solution)/shard_map/ppermute | solution.py:50
  40.5 14.5 %collective-permute-start.8 = (bf16[256,512]{1,0:T(8,128)(2,1)S(1)}, bf16[256,512]{1,0:T(8,128)(2,1)}, u32[]{:S(2)}, u32[]{:S(2)}) collective-permute-start(bf16[256,512]{1,0:T(8,128)(2,1)S(1)} %slice.118.refs_0_), channel_id=1, source_target_pairs={{0,16},{4,20},{8,24},{12,28},{16,0},{20,4},{24,8},{28,12},{1,17},{... | collective-permute-start | bytes 786440 | tf_op jit(solution)/shard_map/ppermute | solution.py:50
  42.3 12.6 %collective-permute-start.9 = (bf16[256,512]{1,0:T(8,128)(2,1)S(1)}, bf16[256,512]{1,0:T(8,128)(2,1)}, u32[]{:S(2)}, u32[]{:S(2)}) collective-permute-start(bf16[256,512]{1,0:T(8,128)(2,1)S(1)} %slice.118.refs_0_), channel_id=1, source_target_pairs={{0,24},{4,28},{8,16},{12,20},{16,8},{20,12},{24,0},{28,4},{1,25},{... | collective-permute-start | bytes 786440 | tf_op jit(solution)/shard_map/ppermute | solution.py:50
  44.5 37.4 %copy-start.2 = (bf16[256,6144]{1,0:T(8,128)(2,1)S(1)}, bf16[256,6144]{1,0:T(8,128)(2,1)}, u32[]{:S(2)}) copy-start(bf16[256,6144]{1,0:T(8,128)(2,1)} %copy-done.1) | copy-start | bytes 9437188
  55.0 15.0 %collective-permute-start.15 = (bf16[512,512]{1,0:T(8,128)(2,1)}, bf16[512,512]{1,0:T(8,128)(2,1)S(1)}, u32[]{:S(2)}, u32[]{:S(2)}) collective-permute-start(bf16[512,512]{1,0:T(8,128)(2,1)} %get-tuple-element.103.refs_0_), channel_id=1, source_target_pairs={{0,8},{4,12},{8,0},{12,4},{16,24},{20,28},{24,16},{28,20},{1,9},{5... | collective-permute-start | bytes 1572872 | tf_op jit(solution)/shard_map/ppermute | solution.py:50
  56.4 24.8 %collective-permute-start.17 = (bf16[512,512]{1,0:T(8,128)(2,1)}, bf16[512,512]{1,0:T(8,128)(2,1)}, u32[]{:S(2)}, u32[]{:S(2)}) collective-permute-start(bf16[512,512]{1,0:T(8,128)(2,1)} %get-tuple-element.103.refs_0_), channel_id=1, source_target_pairs={{0,16},{4,20},{8,24},{12,28},{16,0},{20,4},{24,8},{28,12},{1,17},{... | collective-permute-start | bytes 1572872 | tf_op jit(solution)/shard_map/ppermute | solution.py:50
  57.0 24.3 %collective-permute-start.19 = (bf16[512,512]{1,0:T(8,128)(2,1)}, bf16[512,512]{1,0:T(8,128)(2,1)}, u32[]{:S(2)}, u32[]{:S(2)}) collective-permute-start(bf16[512,512]{1,0:T(8,128)(2,1)} %get-tuple-element.103.refs_0_), channel_id=1, source_target_pairs={{0,24},{4,28},{8,16},{12,20},{16,8},{20,12},{24,0},{28,4},{1,25},{... | collective-permute-start | bytes 1572872 | tf_op jit(solution)/shard_map/ppermute | solution.py:50
  58.5 1.9 collective-permute-start.10
  58.5 2.1 collective-permute-start.11
  60.4 9.7 %copy-start.21 = (bf16[256,512]{1,0:T(8,128)(2,1)}, bf16[256,512]{1,0:T(8,128)(2,1)S(1)}, u32[]{:S(2)}) copy-start(bf16[256,512]{1,0:T(8,128)(2,1)S(1)} %collective-permute-done.10.refs_1_) | copy-start | bytes 786436
  60.4 24.3 %collective-permute-start.14 = (bf16[512,512]{1,0:T(8,128)(2,1)}, bf16[512,512]{1,0:T(8,128)(2,1)}, u32[]{:S(2)}, u32[]{:S(2)}) collective-permute-start(bf16[512,512]{1,0:T(8,128)(2,1)} %get-tuple-element.103.refs_0_), channel_id=1, source_target_pairs={{0,4},{4,0},{8,12},{12,8},{16,20},{20,16},{24,28},{28,24},{1,5},{5... | collective-permute-start | bytes 1572872 | tf_op jit(solution)/shard_map/ppermute | solution.py:50
  60.6 21.2 %collective-permute-start.12 = (bf16[256,512]{1,0:T(8,128)(2,1)}, bf16[256,512]{1,0:T(8,128)(2,1)S(1)}, u32[]{:S(2)}, u32[]{:S(2)}) collective-permute-start(bf16[256,512]{1,0:T(8,128)(2,1)} %collective-permute-done.8.refs_4_), channel_id=1, source_target_pairs={{0,4},{4,0},{8,12},{12,8},{16,20},{20,16},{24,28},{28,24},{1,5},{5... | collective-permute-start | bytes 786440 | tf_op jit(solution)/shard_map/ppermute | solution.py:50
  70.0 13.4 %copy-start.13 = (bf16[512,512]{1,0:T(8,128)(2,1)}, bf16[512,512]{1,0:T(8,128)(2,1)S(1)}, u32[]{:S(2)}) copy-start(bf16[512,512]{1,0:T(8,128)(2,1)S(1)} %collective-permute-done.15.refs_2_) | copy-start | bytes 1572868
  70.0 14.6 %collective-permute-start.16 = (bf16[512,512]{1,0:T(8,128)(2,1)S(1)}, bf16[512,512]{1,0:T(8,128)(2,1)}, u32[]{:S(2)}, u32[]{:S(2)}) collective-permute-start(bf16[512,512]{1,0:T(8,128)(2,1)S(1)} %collective-permute-done.15.refs_2_), channel_id=1, source_target_pairs={{0,4},{4,0},{8,12},{12,8},{16,20},{20,16},{24,28},{28,24},{1,5},{5... | collective-permute-start | bytes 1572872 | tf_op jit(solution)/shard_map/ppermute | solution.py:50
  81.3 3.4 collective-permute-start.18
  81.3 3.4 collective-permute-start.20
  81.8 2.9 collective-permute-start.13
  84.7 107.5 %all-reduce.4.cloned.1.call-start = ((), (), s32[]{:S(2)}) async-start(), calls=%async_computation.2 | async-start | bytes 4194304 | tf_op jit(solution)/shard_map/psum | solution.py:730
  100.6 204.3 %all-reduce.6.cloned.1.call-start = ((), (), s32[]{:S(2)}) async-start(), calls=%async_computation.4 | async-start | bytes 4194304 | tf_op jit(solution)/shard_map/psum | solution.py:786
  219.8 141.0 %reduce-scatter.3.cloned.1.call-start = ((), (), s32[]{:S(2)}) async-start(), calls=%async_computation.5 | async-start | bytes 21233664 | tf_op jit(solution)/shard_map/reduce_scatter | solution.py:809
  235.4 157.4 %all-reduce.8.cloned.1.call-start = ((), (), s32[]{:S(2)}) async-start(), calls=%async_computation.6 | async-start | bytes 4194304 | tf_op jit(solution)/shard_map/psum | solution.py:811
  305.0 150.9 %reduce-scatter.5.cloned.1.call-start = ((), (), s32[]{:S(2)}) async-start(), calls=%async_computation.7 | async-start | bytes 2621440 | tf_op jit(solution)/shard_map/reduce_scatter | solution.py:932
  329.7 14.2 %collective-permute-start.21 = (bf16[512,512]{1,0:T(8,128)(2,1)}, bf16[512,512]{1,0:T(8,128)(2,1)S(1)}, u32[]{:S(2)}, u32[]{:S(2)}) collective-permute-start(bf16[512,512]{1,0:T(8,128)(2,1)} %get-tuple-element.136), channel_id=1, source_target_pairs={{0,4},{4,0},{8,12},{12,8},{16,20},{20,16},{24,28},{28,24},{1,5},{5... | collective-permute-start | bytes 1572872 | tf_op jit(solution)/shard_map/ppermute | solution.py:50
  331.1 13.8 %collective-permute-start.22 = (bf16[512,512]{1,0:T(8,128)(2,1)}, bf16[512,512]{1,0:T(8,128)(2,1)S(1)}, u32[]{:S(2)}, u32[]{:S(2)}) collective-permute-start(bf16[512,512]{1,0:T(8,128)(2,1)} %get-tuple-element.138), channel_id=1, source_target_pairs={{0,4},{4,0},{8,12},{12,8},{16,20},{20,16},{24,28},{28,24},{1,5},{5... | collective-permute-start | bytes 1572872 | tf_op jit(solution)/shard_map/ppermute | solution.py:50
  332.1 13.0 %collective-permute-start.23 = (bf16[512,512]{1,0:T(8,128)(2,1)}, bf16[512,512]{1,0:T(8,128)(2,1)S(1)}, u32[]{:S(2)}, u32[]{:S(2)}) collective-permute-start(bf16[512,512]{1,0:T(8,128)(2,1)} %get-tuple-element.140), channel_id=1, source_target_pairs={{0,4},{4,0},{8,12},{12,8},{16,20},{20,16},{24,28},{28,24},{1,5},{5... | collective-permute-start | bytes 1572872 | tf_op jit(solution)/shard_map/ppermute | solution.py:50
  332.5 12.7 %collective-permute-start.24 = (bf16[512,512]{1,0:T(8,128)(2,1)}, bf16[512,512]{1,0:T(8,128)(2,1)S(1)}, u32[]{:S(2)}, u32[]{:S(2)}) collective-permute-start(bf16[512,512]{1,0:T(8,128)(2,1)} %get-tuple-element.142), channel_id=1, source_target_pairs={{0,4},{4,0},{8,12},{12,8},{16,20},{20,16},{24,28},{28,24},{1,5},{5... | collective-permute-start | bytes 1572872 | tf_op jit(solution)/shard_map/ppermute | solution.py:50
  360.8 36.9 %collective-permute-start.25 = (bf16[512,512]{1,0:T(8,128)(2,1)S(1)}, bf16[512,512]{1,0:T(8,128)(2,1)S(1)}, u32[]{:S(2)}, u32[]{:S(2)}) collective-permute-start(bf16[512,512]{1,0:T(8,128)(2,1)S(1)} %add_convert_fusion.5), channel_id=1, source_target_pairs={{0,8},{4,12},{8,0},{12,4},{16,24},{20,28},{24,16},{28,20},{1,9},{5... | collective-permute-start | bytes 1572872 | tf_op jit(solution)/shard_map/ppermute | solution.py:50
  362.1 35.5 %collective-permute-start.26 = (bf16[512,512]{1,0:T(8,128)(2,1)S(1)}, bf16[512,512]{1,0:T(8,128)(2,1)S(1)}, u32[]{:S(2)}, u32[]{:S(2)}) collective-permute-start(bf16[512,512]{1,0:T(8,128)(2,1)S(1)} %add_convert_fusion.4), channel_id=1, source_target_pairs={{0,16},{4,20},{8,24},{12,28},{16,0},{20,4},{24,8},{28,12},{1,17},{... | collective-permute-start | bytes 1572872 | tf_op jit(solution)/shard_map/ppermute | solution.py:50
  362.8 34.9 %collective-permute-start.27 = (bf16[512,512]{1,0:T(8,128)(2,1)S(1)}, bf16[512,512]{1,0:T(8,128)(2,1)S(1)}, u32[]{:S(2)}, u32[]{:S(2)}) collective-permute-start(bf16[512,512]{1,0:T(8,128)(2,1)S(1)} %add_convert_fusion.3), channel_id=1, source_target_pairs={{0,24},{4,28},{8,16},{12,20},{16,8},{20,12},{24,0},{28,4},{1,25},{... | collective-permute-start | bytes 1572872 | tf_op jit(solution)/shard_map/ppermute | solution.py:50
  407.9 93.4 %all-gather.5.cloned.1.call-start = ((), (), s32[]{:S(2)}) async-start(), calls=%async_computation.8 | async-start | bytes 2621440 | tf_op jit(solution)/shard_map/all_gather | solution.py:936
  408.2 6.8 %collective-permute-start.28 = (bf16[4,256,512]{2,1,0:T(8,128)(2,1)}, bf16[4,256,512]{2,1,0:T(8,128)(2,1)S(1)}, u32[]{:S(2)}, u32[]{:S(2)}) collective-permute-start(bf16[4,256,512]{2,1,0:T(8,128)(2,1)} %bitcast.70), channel_id=1, source_target_pairs={{0,4},{4,0},{8,12},{12,8},{16,20},{20,16},{24,28},{28,24},{1,5},{5... | collective-permute-start | bytes 3145736 | tf_op jit(solution)/shard_map/ppermute | solution.py:50
  412.6 6.3 %collective-permute-start.32 = (bf16[4,256,512]{2,1,0:T(8,128)(2,1)}, bf16[4,256,512]{2,1,0:T(8,128)(2,1)S(1)}, u32[]{:S(2)}, u32[]{:S(2)}) collective-permute-start(bf16[4,256,512]{2,1,0:T(8,128)(2,1)} %bitcast.71), channel_id=1, source_target_pairs={{0,4},{4,0},{8,12},{12,8},{16,20},{20,16},{24,28},{28,24},{1,5},{5... | collective-permute-start | bytes 3145736 | tf_op jit(solution)/shard_map/ppermute | solution.py:50
  414.7 7.0 %collective-permute-start.36 = (bf16[4,256,512]{2,1,0:T(8,128)(2,1)S(1)}, bf16[4,256,512]{2,1,0:T(8,128)(2,1)S(1)}, u32[]{:S(2)}, u32[]{:S(2)}) collective-permute-start(bf16[4,256,512]{2,1,0:T(8,128)(2,1)S(1)} %copy-done.33), channel_id=1, source_target_pairs={{0,4},{4,0},{8,12},{12,8},{16,20},{20,16},{24,28},{28,24},{1,5},{5... | collective-permute-start | bytes 3145736 | tf_op jit(solution)/shard_map/ppermute | solution.py:50
  415.3 10.1 %collective-permute-start.31 = (bf16[256,512]{1,0:T(8,128)(2,1)S(1)}, bf16[256,512]{1,0:T(8,128)(2,1)S(1)}, u32[]{:S(2)}, u32[]{:S(2)}) collective-permute-start(bf16[256,512]{1,0:T(8,128)(2,1)S(1)} %get-tuple-element.197), channel_id=1, source_target_pairs={{0,24},{4,28},{8,16},{12,20},{16,8},{20,12},{24,0},{28,4},{1,25},{... | collective-permute-start | bytes 786440 | tf_op jit(solution)/shard_map/ppermute | solution.py:50
  417.8 13.4 %collective-permute-start.30 = (bf16[256,512]{1,0:T(8,128)(2,1)S(1)}, bf16[256,512]{1,0:T(8,128)(2,1)S(1)}, u32[]{:S(2)}, u32[]{:S(2)}) collective-permute-start(bf16[256,512]{1,0:T(8,128)(2,1)S(1)} %get-tuple-element.198), channel_id=1, source_target_pairs={{0,16},{4,20},{8,24},{12,28},{16,0},{20,4},{24,8},{28,12},{1,17},{... | collective-permute-start | bytes 786440 | tf_op jit(solution)/shard_map/ppermute | solution.py:50
  418.3 15.2 %collective-permute-start.29 = (bf16[256,512]{1,0:T(8,128)(2,1)S(1)}, bf16[256,512]{1,0:T(8,128)(2,1)S(1)}, u32[]{:S(2)}, u32[]{:S(2)}) collective-permute-start(bf16[256,512]{1,0:T(8,128)(2,1)S(1)} %get-tuple-element.196), channel_id=1, source_target_pairs={{0,8},{4,12},{8,0},{12,4},{16,24},{20,28},{24,16},{28,20},{1,9},{5... | collective-permute-start | bytes 786440 | tf_op jit(solution)/shard_map/ppermute | solution.py:50
  419.3 17.5 %collective-permute-start.35 = (bf16[256,512]{1,0:T(8,128)(2,1)S(1)}, bf16[256,512]{1,0:T(8,128)(2,1)S(1)}, u32[]{:S(2)}, u32[]{:S(2)}) collective-permute-start(bf16[256,512]{1,0:T(8,128)(2,1)S(1)} %get-tuple-element.194), channel_id=1, source_target_pairs={{0,24},{4,28},{8,16},{12,20},{16,8},{20,12},{24,0},{28,4},{1,25},{... | collective-permute-start | bytes 786440 | tf_op jit(solution)/shard_map/ppermute | solution.py:50
  421.7 20.6 %collective-permute-start.34 = (bf16[256,512]{1,0:T(8,128)(2,1)S(1)}, bf16[256,512]{1,0:T(8,128)(2,1)S(1)}, u32[]{:S(2)}, u32[]{:S(2)}) collective-permute-start(bf16[256,512]{1,0:T(8,128)(2,1)S(1)} %get-tuple-element.195), channel_id=1, source_target_pairs={{0,16},{4,20},{8,24},{12,28},{16,0},{20,4},{24,8},{28,12},{1,17},{... | collective-permute-start | bytes 786440 | tf_op jit(solution)/shard_map/ppermute | solution.py:50
  425.5 16.9 %collective-permute-start.33 = (bf16[256,512]{1,0:T(8,128)(2,1)S(1)}, bf16[256,512]{1,0:T(8,128)(2,1)S(1)}, u32[]{:S(2)}, u32[]{:S(2)}) collective-permute-start(bf16[256,512]{1,0:T(8,128)(2,1)S(1)} %get-tuple-element.193), channel_id=1, source_target_pairs={{0,8},{4,12},{8,0},{12,4},{16,24},{20,28},{24,16},{28,20},{1,9},{5... | collective-permute-start | bytes 786440 | tf_op jit(solution)/shard_map/ppermute | solution.py:50
  431.1 16.9 %collective-permute-start.39 = (bf16[256,512]{1,0:T(8,128)(2,1)S(1)}, bf16[256,512]{1,0:T(8,128)(2,1)S(1)}, u32[]{:S(2)}, u32[]{:S(2)}) collective-permute-start(bf16[256,512]{1,0:T(8,128)(2,1)S(1)} %get-tuple-element.191), channel_id=1, source_target_pairs={{0,24},{4,28},{8,16},{12,20},{16,8},{20,12},{24,0},{28,4},{1,25},{... | collective-permute-start | bytes 786440 | tf_op jit(solution)/shard_map/ppermute | solution.py:50
  433.5 19.4 %collective-permute-start.38 = (bf16[256,512]{1,0:T(8,128)(2,1)S(1)}, bf16[256,512]{1,0:T(8,128)(2,1)S(1)}, u32[]{:S(2)}, u32[]{:S(2)}) collective-permute-start(bf16[256,512]{1,0:T(8,128)(2,1)S(1)} %get-tuple-element.192), channel_id=1, source_target_pairs={{0,16},{4,20},{8,24},{12,28},{16,0},{20,4},{24,8},{28,12},{1,17},{... | collective-permute-start | bytes 786440 | tf_op jit(solution)/shard_map/ppermute | solution.py:50
  436.8 19.1 %copy-start.30 = (f32[8,128]{1,0:T(8,128)S(1)}, f32[8,128]{1,0:T(8,128)}, u32[]{:S(2)}) copy-start(f32[8,128]{1,0:T(8,128)} %get-tuple-element.174) | copy-start | bytes 12292
  436.8 19.2 %copy-start.29 = (f32[1,2048]{1,0:T(1,128)S(1)}, f32[1,2048]{1,0:T(1,128)}, u32[]{:S(2)}) copy-start(f32[1,2048]{1,0:T(1,128)} %get-tuple-element.172) | copy-start | bytes 24580
  436.8 19.2 %copy-start.28 = (f32[1,2048]{1,0:T(1,128)S(1)}, f32[1,2048]{1,0:T(1,128)}, u32[]{:S(2)}) copy-start(f32[1,2048]{1,0:T(1,128)} %get-tuple-element.173) | copy-start | bytes 24580
  436.8 16.3 %collective-permute-start.37 = (bf16[256,512]{1,0:T(8,128)(2,1)S(1)}, bf16[256,512]{1,0:T(8,128)(2,1)S(1)}, u32[]{:S(2)}, u32[]{:S(2)}) collective-permute-start(bf16[256,512]{1,0:T(8,128)(2,1)S(1)} %get-tuple-element.190), channel_id=1, source_target_pairs={{0,8},{4,12},{8,0},{12,4},{16,24},{20,28},{24,16},{28,20},{1,9},{5... | collective-permute-start | bytes 786440 | tf_op jit(solution)/shard_map/ppermute | solution.py:50
  456.7 1.2 collective-permute-start.40
  457.9 3.8 collective-permute-start.41
  461.7 3.8 collective-permute-start.42
  465.4 4.9 collective-permute-start.43
  470.4 5.2 %collective-permute-start.44 = (f32[4480]{0:T(1024)S(1)}, f32[4480]{0:T(1024)S(1)}, u32[]{:S(2)}, u32[]{:S(2)}) collective-permute-start(f32[4480]{0:T(1024)S(1)} %add.194), channel_id=1, source_target_pairs={{0,2},{1,3},{2,0},{3,1},{4,6},{5,7},{6,4},{7,5},{8,10},{9,11},{10,... | collective-permute-start | bytes 53768 | tf_op jit(solution)/shard_map/ppermute | solution.py:50
  478.1 15.2 %copy-start.26 = (f32[4352]{0:T(1024)S(1)}, f32[4352]{0:T(1024)}, u32[]{:S(2)}) copy-start(f32[4352]{0:T(1024)} %param.19) | copy-start | bytes 52228
  478.1 15.2 %copy-start.27 = (f32[4352]{0:T(1024)S(1)}, f32[4352]{0:T(1024)}, u32[]{:S(2)}) copy-start(f32[4352]{0:T(1024)} %param.18) | copy-start | bytes 52228
  (23 other events, 69.8 us)
Sparse Core Ops, SparseCore 0:
  84.8 98.0 all-gather.2
  235.5 125.2 reduce-scatter.2
Sparse Core Ops, SparseCore 1:
  100.7 91.4 all-reduce.3
  219.9 85.0 all-reduce.5
  307.8 85.0 all-reduce.7
  407.9 42.5 reduce-scatter.4
  456.0 45.3 all-gather.4

commit v4 on v3

--- a/solution.py
+++ b/solution.py
@@ -107,32 +107,18 @@
     return scale * (e - unit * jnp.mean(e * unit, axis=-1, keepdims=True))
 
 
-def project_kernel(parts, q_tiles, me_ref, h_ref, *refs):
-    cos_ref, sin_ref, gain_ref, q_ref, kv_ref, lin_ref, w_ref = refs[parts:]
-    tile = pl.program_id(0)
+def project_kernel(parts, heads, me_ref, h_ref, *refs):
+    cos_ref, sin_ref, gain_ref, o_ref, lin_ref, w_ref = refs[parts:]
     in_order(me_ref, refs[:parts], w_ref)
     total = dot(h_ref[...], w_ref[...])
-    per_tile = TILE // HD
-
-    def normed_to(out_ref, gain):
-        for part in range(per_tile):
-            at = slice(part * HD, (part + 1) * HD)
-            values = total[:, at]
-            lin_ref[:, at] = values
-            normed = values * unit_scale(values) * gain
-            out_ref[:, at] = turned(normed, cos_ref[...], sin_ref[...]).astype(bf16)
-
-    @pl.when(tile < q_tiles)
-    def _():
-        normed_to(q_ref, gain_ref[0:1])
-
-    @pl.when(tile == q_tiles)
-    def _():
-        normed_to(kv_ref, gain_ref[1:2])
-
-    @pl.when(tile > q_tiles)
-    def _():
-        kv_ref[...] = total.astype(bf16)
+    for head in range(heads):
+        at = slice(head * HD, (head + 1) * HD)
+        values = total[:, at]
+        lin_ref[:, at] = values
+        normed = values * unit_scale(values) * gain_ref[...]
+        o_ref[:, at] = turned(normed, cos_ref[...], sin_ref[...]).astype(bf16)
+    if heads * HD < o_ref.shape[1]:
+        o_ref[:, heads * HD :] = total[:, heads * HD :].astype(bf16)
 
 
 def span_limits(own_ref, starts_ref, i, group):
@@ -240,6 +226,14 @@
             at = pl.multiple_of(first + b * block, block)
             term = dot(low_ref[...], w_ref[b * block : (b + 1) * block], last_dims)
             o_ref[:, pl.ds(at, block)] = term.astype(bf16)
+
+
+def output_first_kernel(y_ref, s_ref, o_ref):
+    o_ref[...] = (y_ref[...] + s_ref[...].astype(f32)).astype(bf16)
+
+
+def output_rest_kernel(y_ref, s_ref, made_ref, o_ref):
+    o_ref[...] = (y_ref[...] + s_ref[...].astype(f32)).astype(bf16)
 
 
 def plain_kernel(a_ref, w_ref, o_ref):
@@ -381,8 +375,9 @@
 def key_back_kernel(parts, terms, kv_heads, me_ref, *refs):
     term_refs = refs[:terms]
     lin_ref, cos_ref, sin_ref, gain_ref, dq_ref, x_ref, scale_ref = refs[terms : terms + 7]
-    w_refs = refs[terms + 7 : terms + 7 + parts]
-    dkv_ref, dgain_k_ref, dgain_ref, dh_ref = refs[terms + 7 + parts :]
+    wq_refs = refs[terms + 7 : terms + 7 + parts]
+    wkv_refs = refs[terms + 7 + parts : terms + 7 + 2 * parts]
+    dkv_ref, dgain_k_ref, dgain_ref, dh_ref = refs[terms + 7 + 2 * parts :]
     dgain = jnp.zeros((1, HD), f32)
 
     def total(begin):
@@ -404,16 +399,15 @@
     dgain_k_ref[...] = jnp.broadcast_to(dgain, dgain_k_ref.shape)
 
     scale = scale_ref[...]
-    width = w_refs[0].shape[0]
+    width = wq_refs[0].shape[0]
     block = min(width, TILE)
-    q_width = dq_ref.shape[1]
-    for k, w_ref in enumerate(w_refs):
+    for k in range(parts):
         first = place_of(me_ref, k, parts) * width
         for b in range(width // block):
             here = pl.ds(pl.multiple_of(first + b * block, block), block)
             rows = slice(b * block, (b + 1) * block)
-            term = dot(dq_ref[...], w_ref[rows, :q_width], last_dims)
-            term = term + dot(dkv_ref[...], w_ref[rows, q_width:], last_dims)
+            term = dot(dq_ref[...], wq_refs[k][rows, :], last_dims)
+            term = term + dot(dkv_ref[...], wkv_refs[k][rows, :], last_dims)
             dh_ref[:, here] = term.astype(bf16)
             unit = x_ref[:, here].astype(f32) * scale
             dgain_ref[:, here] = jnp.sum(term * unit, axis=0, keepdims=True)
@@ -421,13 +415,13 @@
 
 def input_back_kernel(dy_ref, x_ref, scale_ref, s_ref, gain_ref, o_ref):
     def rows_of(r, unused):
-        at = pl.ds(pl.multiple_of(r * 32, 32), 32)
+        at = pl.ds(pl.multiple_of(r * 16, 16), 16)
         scale = scale_ref[at, :]
         back = norm_back(x_ref[at, :].astype(f32) * scale, scale, gain_ref[...], s_ref[at, :].astype(f32))
         o_ref[at, :] = dy_ref[at, :] + back
         return unused
 
-    lax.fori_loop(0, x_ref.shape[0] // 32, rows_of, 0, unroll=2)
+    lax.fori_loop(0, x_ref.shape[0] // 16, rows_of, 0, unroll=4)
 
 
 def transpose_kernel(me_ref, x_ref, o_ref):
@@ -542,7 +536,7 @@
 
 def update_weights(factor, weights, momentum, average, pieces):
     rows, columns = weights.shape
-    step = 32
+    step = 64
     spec = pl.BlockSpec((step, columns), lambda n, _: (n, 0))
     shape = jax.ShapeDtypeStruct(weights.shape, f32)
     return pl.pallas_call(
@@ -607,16 +601,20 @@
     gain_mlp = gains[model_width : 2 * model_width]
     head_gains = gains[2 * model_width :].reshape(2, HD)
 
-    qkv_own = weights[:, :qkv_cols].astype(bf16)
+    kv_own = weights[:, query_width:qkv_cols].astype(bf16)
     if in_pairs:
-        qkv_outer = gather_chips(qkv_own)
-        later, qkv_own = lax.optimization_barrier((weights, qkv_own))
-        out_outer = gather_chips(later[:, qkv_cols:out_end].astype(bf16))
+        kv_outer = gather_chips(kv_own)
+        later, kv_own = lax.optimization_barrier((weights, kv_own))
+        qo_own = jnp.concatenate([later[:, :query_width], later[:, qkv_cols:out_end]], axis=1).astype(bf16)
+        qo_outer = gather_chips(qo_own)
+        later, qo_own = lax.optimization_barrier((later, qo_own))
+        mlp_own = later[:, out_end:].astype(bf16)
+        kv_outer[1], qo_own = lax.optimization_barrier((kv_outer[1], qo_own))
     else:
-        later = weights
-        qkv_parts = [lax.all_gather(qkv_own, "dp", axis=0, tiled=True)]
-        out_own = weights[:, qkv_cols:out_end].astype(bf16)
-        out_parts = [lax.all_gather(out_own, "dp", axis=0, tiled=True)]
+        mlp_own = weights[:, out_end:].astype(bf16)
+        qo_own = jnp.concatenate([weights[:, :query_width], weights[:, qkv_cols:out_end]], axis=1).astype(bf16)
+        qo_weights = [lax.all_gather(qo_own, "dp", axis=0, tiled=True)]
+        kv_weights = [lax.all_gather(kv_own, "dp", axis=0, tiled=True)]
 
     doc_ids = jnp.arange(doc_lengths.shape[1], dtype=jnp.int32)
     earlier = doc_ids[None, :] < doc_ids[:, None]
@@ -639,46 +637,55 @@
     scale_in = unit_scale(inputs)
     normed_low = (inputs * scale_in * gain_attn).astype(bf16)
 
-    normed_turned = transposed(me_array, normed_low, parts, row_count)
     if in_pairs:
-        normed_turned, qkv_outer[1] = lax.optimization_barrier((normed_turned, qkv_outer[1]))
-        qkv_parts = gather_cores(qkv_outer)
-
-    q_tiles = query_width // TILE
+        kv_weights = gather_cores(kv_outer)
+
     rows_all = pl.BlockSpec((tok_count, model_width), lambda *_: (0, 0))
     angle_spec = pl.BlockSpec((tok_count, HD), lambda *_: (0, 0))
-    part_tile = pl.BlockSpec((model_width // parts, TILE), lambda n, *_: (0, n))
-    queries, keys_values, lin = pl.pallas_call(
-        functools.partial(project_kernel, parts, q_tiles),
-        grid_spec=pltpu.PrefetchScalarGridSpec(
-            num_scalar_prefetch=1,
-            grid=(qkv_cols // TILE,),
-            in_specs=[rows_all]
-            + [part_tile] * parts
-            + [angle_spec, angle_spec, pl.BlockSpec((2, HD), lambda *_: (0, 0))],
-            out_specs=[
-                pl.BlockSpec((tok_count, TILE), lambda n, *_: (0, jnp.minimum(n, q_tiles - 1))),
-                pl.BlockSpec((tok_count, TILE), lambda n, *_: (0, jnp.maximum(n - q_tiles, 0))),
-                pl.BlockSpec((tok_count, TILE), lambda n, *_: (0, jnp.minimum(n, q_tiles))),
-            ],
-            scratch_shapes=[pltpu.VMEM((model_width, TILE), bf16)],
-        ),
-        out_shape=(
-            jax.ShapeDtypeStruct((tok_count, query_width), bf16),
-            jax.ShapeDtypeStruct((tok_count, 2 * kv_width), bf16),
-            jax.ShapeDtypeStruct((tok_count, query_width + kv_width), f32),
-        ),
-        compiler_params=params(),
-        cost_estimate=cost(6),
-        name="project",
-    )(me_array, normed_low, *qkv_parts, cosine, sine, head_gains)
-
-    mlp_own = later[:, out_end:].astype(bf16)
+    gain_head_spec = pl.BlockSpec((1, HD), lambda *_: (0, 0))
+
+    def project(weight_parts, width, head_count, gain):
+        lin_width = head_count * HD
+        return pl.pallas_call(
+            functools.partial(project_kernel, parts, head_count),
+            grid_spec=pltpu.PrefetchScalarGridSpec(
+                num_scalar_prefetch=1,
+                grid=(1,),
+                in_specs=[rows_all]
+                + [pl.BlockSpec((model_width // parts, width), lambda *_: (0, 0))] * parts
+                + [angle_spec, angle_spec, gain_head_spec],
+                out_specs=[
+                    pl.BlockSpec((tok_count, width), lambda *_: (0, 0)),
+                    pl.BlockSpec((tok_count, lin_width), lambda *_: (0, 0)),
+                ],
+                scratch_shapes=[pltpu.VMEM((model_width, width), bf16)],
+            ),
+            out_shape=(
+                jax.ShapeDtypeStruct((tok_count, width), bf16),
+                jax.ShapeDtypeStruct((tok_count, lin_width), f32),
+            ),
+            compiler_params=params(),
+            cost_estimate=cost(5),
+            name="project",
+        )(me_array, normed_low, *weight_parts, cosine, sine, gain)
+
+    keys_values, lin_k = project(kv_weights, 2 * kv_width, kv_heads, head_gains[1:])
     if in_pairs:
-        keys_values, out_outer = lax.optimization_barrier((keys_values, out_outer))
-        kv_parts = gather_cores(gather_chips(keys_values))
-        out_parts = gather_cores(out_outer)
-        mlp_own, out_parts, kv_parts = lax.optimization_barrier((mlp_own, out_parts, kv_parts))
+        keys_values, qo_outer = lax.optimization_barrier((keys_values, qo_outer))
+        qo_weights = gather_cores(qo_outer)
+        normed_there, qo_outer = lax.optimization_barrier((normed_low, qo_outer))
+        normed_turned = transposed(me_array, normed_there, parts, row_count)
+        mlp_own, normed_turned, qo_weights = lax.optimization_barrier((mlp_own, normed_turned, qo_weights))
+    else:
+        normed_turned = transposed(me_array, normed_low, parts, row_count)
+    queries, lin_q = project(qo_weights, query_width, q_heads, head_gains[:1])
+
+    if in_pairs:
+        kv_chips, queries, normed_turned, mlp_own = lax.optimization_barrier(
+            (gather_chips(keys_values), queries, normed_turned, mlp_own)
+        )
+        kv_parts = gather_cores(kv_chips)
+        mlp_own, kv_parts = lax.optimization_barrier((mlp_own, kv_parts))
     else:
         kv_parts = [lax.all_gather(keys_values, "dp", axis=0, tiled=True)]
     mlp_weights = lax.all_gather(mlp_own, "dp", axis=0, tiled=True)
@@ -712,20 +719,21 @@
         cost_estimate=cost(16),
         name="attend",
     )(own_spans, inverse, starts, queries, *kv_parts)
-    part_all = pl.BlockSpec((model_width // parts, query_width), lambda *_: (0, 0))
+    q_part = pl.BlockSpec((model_width // parts, query_width), lambda *_: (0, 0))
+    out_part = pl.BlockSpec((model_width // parts, query_width), lambda *_: (0, 1))
     attn_part = pl.pallas_call(
         functools.partial(project_out_kernel, parts),
         grid_spec=pltpu.PrefetchScalarGridSpec(
             num_scalar_prefetch=1,
             grid=(1,),
-            in_specs=[q_all] + [part_all] * parts,
+            in_specs=[q_all] + [out_part] * parts,
             out_specs=rows_all,
         ),
         out_shape=jax.ShapeDtypeStruct((tok_count, model_width), bf16),
         compiler_params=params(),
         cost_estimate=cost(4),
         name="project_out",
-    )(me_array, attended_low, *out_parts)
+    )(me_array, attended_low, *qo_weights)
 
     attn_sum = lax.psum(attn_part, "mp")
 
@@ -824,7 +832,7 @@
                 half_spec,
                 gain_spec,
             ]
-            + [pl.BlockSpec((model_width // parts, query_width), lambda *_: (0, 0))] * parts,
+            + [out_part] * parts,
             out_specs=[half_spec, half_spec, pl.BlockSpec((half_rows, query_width), lambda n, *_: (n, 0)), gain_spec],
             scratch_shapes=[pltpu.VMEM((model_width, query_width), bf16)],
         ),
@@ -837,7 +845,7 @@
         compiler_params=params(),
         cost_estimate=cost(1),
         name="residual_back",
-    )(me_array, residual, scale_mlp, cotangent, grad_mlp_sum, gain_mlp[None], *out_parts)
+    )(me_array, residual, scale_mlp, cotangent, grad_mlp_sum, gain_mlp[None], *qo_weights)
     out_rows = token_total // parts
     dkv_spec = pl.BlockSpec((out_rows, 2 * heads * HD), lambda g, *_: (0, g))
     back = pl.pallas_call(
@@ -873,7 +881,7 @@
         grad_att_low,
         attended,
         lse,
-        lin,
+        lin_q,
         cosine,
         sine,
         head_gains[:1],
@@ -897,7 +905,17 @@
         whole = made[0].reshape(model_width, -1)
         return lax.psum_scatter(whole, "dp", scatter_dimension=0, tiled=True)
 
-    block_output = (residual + mlp_sum.astype(f32)).astype(bf16)
+    first_spec = pl.BlockSpec((tok_count // 8, model_width), lambda n: (0, 0))
+    block_output = pl.pallas_call(
+        output_first_kernel,
+        grid=(1,),
+        in_specs=[first_spec, first_spec],
+        out_specs=first_spec,
+        out_shape=low_shape,
+        compiler_params=params(),
+        cost_estimate=cost(6),
+        name="output_first",
+    )(residual, mlp_sum)
     terms, block_output, dw_query, dw_out = lax.optimization_barrier((terms, block_output, dw_query, dw_out))
     query_grads, out_grads = scattered(dw_query), scattered(dw_out)
     grad_kv_low, key_gain_grad, attn_gain_grad, grad_norm_part = pl.pallas_call(
@@ -906,10 +924,11 @@
             num_scalar_prefetch=1,
             grid=(1,),
             in_specs=[pl.BlockSpec((tok_count, 2 * kv_width), lambda *_: (0, 0))] * len(terms)
-            + [pl.BlockSpec((tok_count, kv_width), lambda *_: (0, query_width // kv_width))]
+            + [pl.BlockSpec((tok_count, kv_width), lambda *_: (0, 0))]
             + [angle_spec, angle_spec, pl.BlockSpec((1, HD), lambda *_: (0, 0))]
             + [q_all, rows_all, scale_spec]
-            + [pl.BlockSpec((model_width // parts, qkv_cols), lambda *_: (0, 0))] * parts,
+            + [q_part] * parts
+            + [pl.BlockSpec((model_width // parts, 2 * kv_width), lambda *_: (0, 0))] * parts,
             out_specs=[
                 pl.BlockSpec((tok_count, 2 * kv_width), lambda *_: (0, 0)),
                 pl.BlockSpec((8, HD), lambda *_: (0, 0)),
@@ -926,13 +945,41 @@
         compiler_params=params(),
         cost_estimate=cost(1),
         name="key_back",
-    )(me_array, *terms, lin, cosine, sine, head_gains[1:], grad_query_low, block_input, scale_in, *qkv_parts)
+    )(
+        me_array,
+        *terms,
+        lin_k,
+        cosine,
+        sine,
+        head_gains[1:],
+        grad_query_low,
+        block_input,
+        scale_in,
+        *qo_weights,
+        *kv_weights,
+    )
     [dw_kv] = weight_grad(me_array, normed_turned, [grad_kv_low], parts, row_count, True)
 
     grad_norm_share = lax.psum_scatter(grad_norm_part, "mp", scatter_dimension=0, tiled=True)
-    weight_grads = [query_grads, scattered(dw_kv), out_grads, mlp_grads]
+    kv_grads = scattered(dw_kv)
+    mlp_sum, block_output, keys_done = lax.optimization_barrier((mlp_sum, block_output, grad_kv_low))
+    rest_spec = pl.BlockSpec((tok_count // 8, model_width), lambda n: (n + 1, 0))
+    block_output = pl.pallas_call(
+        output_rest_kernel,
+        grid=(7,),
+        in_specs=[rest_spec, rest_spec, anywhere],
+        out_specs=rest_spec,
+        out_shape=low_shape,
+        input_output_aliases={2: 0},
+        compiler_params=params(),
+        cost_estimate=cost(5),
+        name="output_rest",
+    )(residual, mlp_sum, block_output)
+    query_grads, kv_grads, out_grads, grad_norm_share, block_output = lax.optimization_barrier(
+        (query_grads, kv_grads, out_grads, grad_norm_share, block_output)
+    )
+    weight_grads = [query_grads, kv_grads, out_grads, mlp_grads]
     square = sum(jnp.sum(jnp.square(grad.astype(f32))) for grad in weight_grads)
-    square, grad_norm_share = lax.optimization_barrier((square, grad_norm_share))
     grad_norm_sum = lax.all_gather(grad_norm_share, "mp", axis=0, tiled=True)
     local = [attn_gain_grad[0], mlp_gain_grad[0], query_gain_grad, key_gain_grad[0]]
     totals = sum_all(jnp.concatenate([jnp.broadcast_to(square, (HD,))] + local))
@@ -940,19 +987,17 @@
     grad_norm = jnp.sqrt(square_total + jnp.sum(gain_grads * gain_grads))
     factor = 1.0 / jnp.maximum(grad_norm, 1.0)
     new_weights, new_momentum, new_ema = update_weights(factor[None], weights, momentum, ema_weights, weight_grads)
-    eighth = tok_count // 8
-    eighth_spec = pl.BlockSpec((eighth, model_width), lambda n: (n, 0))
     grad_input = pl.pallas_call(
         input_back_kernel,
-        grid=(8,),
+        grid=(2,),
         in_specs=[
-            eighth_spec,
-            eighth_spec,
-            pl.BlockSpec((eighth, 1), lambda n: (n, 0)),
-            eighth_spec,
+            half_spec,
+            half_spec,
+            pl.BlockSpec((half_rows, 1), lambda n: (n, 0)),
+            half_spec,
             gain_spec,
         ],
-        out_specs=eighth_spec,
+        out_specs=half_spec,
         out_shape=wide_shape,
         compiler_params=params(),
         cost_estimate=cost(8),

time: 520 us -> 526 us (1.012); the launches traced: 518 us -> 517 us
  Pallas kernels: 161 us -> 177 us
  waiting for transfers between devices: 263 us -> 251 us
  other arithmetic: 23.8 us -> 18.4 us
    pallas_call x2 -> x5, Pallas kernels: 16.7 us -> 25.2 us  [the longest x2 11.5 us: project(): pl.pallas_call(functools.partial(project_kernel, parts, head_count), grid...]
    all_gather x1, waiting for transfers between devices: 7.34 us -> 0.77 us  [per_device(): grad_norm_sum = lax.all_gather(grad_norm_share, 'mp', axis=0, tiled=True)]
  transfers between devices with their start and end apart: 52 -> 52, of which waited for: 26 -> 28; matrix products, arithmetic and copies ran while one was open for 6% -> 5% of each run, Pallas kernels for 22% -> 26%
where the time goes in v4:
time: 526 us; the launch traced here: 517 us
  waiting for transfers between devices  251 us (48%)
  Pallas kernels  177 us (34%)
  starting transfers between devices  38 us (7%)
  between operations  21.8 us (4%)
  other arithmetic  18.4 us (3%)
  local copies, waits for them, and re-layouts  10.7 us (2%)
    all_gather x1, waiting for transfers between devices, per_device(): mlp_weights = lax.all_gather(mlp_own, 'dp', axis=0, tiled=True)  78.2 us
    ppermute x45, waiting for transfers between devices, swap(): return lax.ppermute(array, axis, [(i, i ^ distance) for i in range(count)])  67.6 us
    psum x1, waiting for transfers between devices, per_device(): grad_mlp_sum = lax.psum(grad_mlp_part, 'mp')  62.8 us
    ppermute x45, starting transfers between devices, swap(): return lax.ppermute(array, axis, [(i, i ^ distance) for i in range(count)])  37.4 us
    psum x1, waiting for transfers between devices, per_device(): mlp_sum = lax.psum(mlp_part, 'mp')  28.5 us
    pallas_call x1, Pallas kernels, per_device(): pl.pallas_call(functools.partial(attend_back_kernel, group, heads, parts,...  19.9 us
    pallas_call x1, Pallas kernels, per_device(): pl.pallas_call(mlp_kernel, grid=(tiles,), in_specs=[rows_all, rows_all, g...  16.2 us
    pallas_call x1, Pallas kernels, per_device(): pl.pallas_call(functools.partial(attend_kernel, group, heads, parts), gri...  16 us
  transfers between devices with their start and end apart: 52, of which 28 were waited for; matrix products, arithmetic and copies ran while one was open for 5% of the time, Pallas kernels for 26%

profile of v4, /device:TPU:0, one launch (start us, length us, event | category | flops | bytes accessed | tf_op | source)
XLA Modules:
  0.0 516.5 jit_solution(5150324928502693831)
XLA Ops:
  8.1 1.1 slice.157.refs_0_.refs_19_
  9.1 4.0 collective-permute-start.5
  13.8 3.2 convert.17
  17.2 2.9 collective-permute-start.9
  22.0 1.9 fusion.2.h_ref.x_ref
  24.3 2.3 collective-permute-done.1.refs_2_.refs_21_
  27.1 1.8 fusion.13
  29.8 1.1 collective-permute-start.7
  32.3 5.4 %project.2 = (bf16[512,512]{1,0:T(8,128)(2,1)}, f32[512,256]{1,0:T(8,128)}) custom-call(s32[1]{0:T(128)} %bitcast.1.me_ref, bf16[512,2048]{1,0:T(8,128)(2,1)} %fusion.2.h_ref.x_ref, bf16[256,512]{1,0:T(8,128)(2,1)} %copy-done.14, bf16[256,512]{1,0:T(8,128)(2,1)} %collective-permute-done.refs_1_.refs_20_, ...), custom_call_target="tpu_custom_call" | custom-call | flops 5000000000 | bytes 17000000 | tf_op jit(solution)/shard_map/project/pallas_call | solution.py:649
  37.7 9.8 %collective-permute-done.8.refs_4_.refs_15_ = bf16[256,1024]{1,0:T(8,128)(2,1)S(1)} collective-permute-done((bf16[256,1024]{1,0:T(8,128)(2,1)S(1)}, bf16[256,1024]{1,0:T(8,128)(2,1)S(1)}, u32[]{:S(2)}, u32[]{:S(2)}) %collective-permute-start.8) | collective-permute-done | bytes 524320 | tf_op jit(solution)/shard_map/ppermute | solution.py:50
  48.9 4.0 slice.156
  52.8 2.5 collective-permute-start.12
  56.4 6.0 %transposed.1.lhs_ref = bf16[2048,512]{1,0:T(8,128)(2,1)} custom-call(s32[1]{0:T(128)} %bitcast.1.me_ref, bf16[512,2048]{1,0:T(8,128)(2,1)} %fusion.2.h_ref.x_ref), custom_call_target="tpu_custom_call" | custom-call | flops 5000000000 | bytes 17000000 | tf_op jit(solution)/shard_map/transposed/pallas_call | solution.py:434
  62.5 6.1 %project.3 = (bf16[512,512]{1,0:T(8,128)(2,1)}, f32[512,512]{1,0:T(8,128)}) custom-call(s32[1]{0:T(128)} %bitcast.1.me_ref, bf16[512,2048]{1,0:T(8,128)(2,1)} %fusion.2.h_ref.x_ref, bf16[256,1024]{1,0:T(8,128)(2,1)} %copy-done.2, bf16[256,1024]{1,0:T(8,128)(2,1)} %copy-done.9, bf16[256,1024]{1,0:T(8,128)(2,1)} %copy-done.8, bf16[256,1024]{1,0:T(8,128)(2,1)} %copy-done.10, ...), custom_call_target="tpu_custom_call" | custom-call | flops 5000000000 | bytes 17000000 | tf_op jit(solution)/shard_map/project/pallas_call | solution.py:649
  68.8 10.3 %collective-permute-done.11.refs_4_ = bf16[512,512]{1,0:T(8,128)(2,1)S(1)} collective-permute-done((bf16[512,512]{1,0:T(8,128)(2,1)}, bf16[512,512]{1,0:T(8,128)(2,1)S(1)}, u32[]{:S(2)}, u32[]{:S(2)}) %collective-permute-start.11) | collective-permute-done | bytes 524320 | tf_op jit(solution)/shard_map/ppermute | solution.py:50
  81.2 1.5 collective-permute-done.18.refs_3_
  84.2 16.0 %attend.1 = (f32[8,128,256]{2,1,0:T(8,128)}, bf16[512,512]{1,0:T(8,128)(2,1)}, f32[8,8,256]{2,1,0:T(8,128)}) custom-call(s32[4]{0:T(128)} %get-tuple-element.213.own_ref, s32[32]{0:T(128)} %fusion.14.inverse_ref, s32[8]{0:T(128)} %copy-done.40, bf16[512,512]{1,0:T(8,128)(2,1)} %get-tuple-element.129.q_ref, bf16[512,512]{1,0:T(8,128)(2,1)} %get-tuple-element.135.refs_0_, ...), custom_call_target="tpu_custom_call" | custom-call | flops 16000000000 | bytes 54400000 | tf_op jit(solution)/shard_map/attend/pallas_call | solution.py:701
  100.2 4.5 project_out.1
  104.7 78.2 %all-gather.3.cloned.1.call-done.w_ref.wg_ref.wu_ref = bf16[2048,4608]{1,0:T(8,128)(2,1)} async-done(((bf16[256,4608]{1,0:T(8,128)(2,1)}), bf16[2048,4608]{1,0:T(8,128)(2,1)}) %all-gather.3.cloned.1.call-update) | async-done | bytes 18874384 | tf_op jit(solution)/shard_map/all_gather | solution.py:691
  182.9 8.3 %grad_hidden.1.da_ref = bf16[512,1536]{1,0:T(8,128)(2,1)} custom-call(bf16[512,2048]{1,0:T(8,128)(2,1)} %c_ref.3, bf16[2048,4608]{1,0:T(8,128)(2,1)} %all-gather.3.cloned.1.call-done.w_ref.wg_ref.wu_ref), custom_call_target="tpu_custom_call" | custom-call | flops 30000001024 | bytes 102000000 | tf_op jit(solution)/shard_map/grad_hidden/pallas_call | solution.py:748
  191.3 16.2 %mlp.1 = (f32[512,2048]{1,0:T(8,128)}, bf16[512,2048]{1,0:T(8,128)(2,1)}, f32[512,1]{1,0:T(8,128)}, bf16[512,1536]{1,0:T(8,128)(2,1)}, bf16[512,1536]{1,0:T(8,128)(2,1)}, /*index=5*/bf16[512,1536]{1,0:T(8,128)(2,1)}) custom-call(bf16[512,2048]{1,0:T(8,128)(2,1)} %x_ref.3, bf16[512,2048]{1,0:T(8,128)(2,1)} %all-reduce.4.cloned.1.call-done.s_ref, ...), custom_call_target="tpu_custom_call" | custom-call | flops 17999998976 | bytes 61200000 | tf_op jit(solution)/shard_map/mlp/pallas_call | solution.py:758
  207.5 11.3 %mlp_back.1 = bf16[512,2048]{1,0:T(8,128)(2,1)} custom-call(bf16[512,1536]{1,0:T(8,128)(2,1)} %get-tuple-element.147.dg_ref, bf16[512,1536]{1,0:T(8,128)(2,1)} %get-tuple-element.148.du_ref, bf16[2048,4608]{1,0:T(8,128)(2,1)} %all-gather.3.cloned.1.call-done.w_ref.wg_ref.wu_ref, bf16[2048,4608]{1,0:T(8,128)(2,1)} %all-gather.3.cloned.1.call-done.w_ref.wg_ref.wu_ref), custom_call_target="tpu_custom_call" | custom-call | flops 11000000512 | bytes 37400000 | tf_op jit(solution)/shard_map/mlp_back/pallas_call | solution.py:778
  218.9 15.5 %mlp_weight_grad.1 = bf16[2048,4608]{1,0:T(8,128)(2,1)} custom-call(bf16[512,2048]{1,0:T(8,128)(2,1)} %get-tuple-element.153.h_ref, bf16[512,2048]{1,0:T(8,128)(2,1)} %c_ref.3, bf16[512,1536]{1,0:T(8,128)(2,1)} %get-tuple-element.147.dg_ref, bf16[512,1536]{1,0:T(8,128)(2,1)} %get-tuple-element.148.du_ref, bf16[512,1536]{1,0:T(8,128)(2,1)} %get-tuple-element.152.a_ref), custom_call_target="tpu_custom_call" | custom-call | flops 1000000000 | bytes 3400000 | tf_op jit(solution)/shard_map/mlp_weight_grad/pallas_call | solution.py:797
  234.5 7.6 %mlp_out.1 = bf16[512,2048]{1,0:T(8,128)(2,1)} custom-call(bf16[512,1536]{1,0:T(8,128)(2,1)} %get-tuple-element.152.a_ref, bf16[2048,4608]{1,0:T(8,128)(2,1)} %all-gather.3.cloned.1.call-done.w_ref.wg_ref.wu_ref), custom_call_target="tpu_custom_call" | custom-call | flops 1000000000 | bytes 3400000 | tf_op jit(solution)/shard_map/mlp_out/pallas_call | solution.py:807
  242.0 62.8 %all-reduce.6.cloned.1.call-done.s_ref = bf16[512,2048]{1,0:T(8,128)(2,1)} async-done(((bf16[512,2048]{1,0:T(8,128)(2,1)}), bf16[512,2048]{1,0:T(8,128)(2,1)}) %all-reduce.6.cloned.1.call-update) | async-done | bytes 2097168 | tf_op jit(solution)/shard_map/psum | solution.py:794
  304.9 8.6 %residual_back.1 = (f32[512,2048]{1,0:T(8,128)}, bf16[512,2048]{1,0:T(8,128)(2,1)}, bf16[512,512]{1,0:T(8,128)(2,1)}, f32[1,2048]{1,0:T(1,128)}) custom-call(s32[1]{0:T(128)} %bitcast.1.me_ref, f32[512,2048]{1,0:T(8,128)} %get-tuple-element.145.y_ref, f32[512,1]{1,0:T(8,128)} %get-tuple-element.146.scale_ref, bf16[512,2048]{1,0:T(8,128)(2,1)} %c_ref.3, ...), custom_call_target="tpu_custom_call" | custom-call | flops 1000000000 | bytes 3400000 | tf_op jit(solution)/shard_map/residual_back/pallas_call | solution.py:823
  313.5 19.9 %attend_back.1 = (bf16[512,512]{1,0:T(8,128)(2,1)}, f32[8,128]{1,0:T(8,128)}, bf16[512,512]{1,0:T(8,128)(2,1)}, bf16[512,512]{1,0:T(8,128)(2,1)}, bf16[512,512]{...) custom-call(s32[4]{0:T(128)} %get-tuple-element.213.own_ref, ...), custom_call_target="tpu_custom_call" | custom-call | flops 1000000000 | bytes 3400000 | tf_op jit(solution)/shard_map/attend_back/pallas_call | solution.py:851
  335.3 7.1 %weight_grad.1 = (bf16[4,256,512]{2,1,0:T(8,128)(2,1)}, bf16[4,256,512]{2,1,0:T(8,128)(2,1)}) custom-call(s32[1]{0:T(128)} %bitcast.1.me_ref, bf16[512,2048]{1,0:T(8,128)(2,1)} %get-tuple-element.176.lhs_ref, bf16[512,512]{1,0:T(8,128)(2,1)} %get-tuple-element.143.low_ref.refs_0_), custom_call_target="tpu_custom_call" | custom-call | flops 1000000000 | bytes 3400000 | tf_op jit(solution)/shard_map/weight_grad/pallas_call | solution.py:510
  342.4 4.2 weight_grad_turned.2
  348.2 12.5 %reduce-scatter.3.cloned.1.call-done.refs_3_ = bf16[256,4608]{1,0:T(8,128)(2,1)} async-done(((bf16[2048,4608]{1,0:T(8,128)(2,1)}), bf16[256,4608]{1,0:T(8,128)(2,1)}) %reduce-scatter.3.cloned.1.call-update) | async-done | bytes 2359312 | tf_op jit(solution)/shard_map/reduce_scatter | solution.py:817
  360.7 1.4 collective-permute-start.25
  362.7 1.5 collective-permute-start.27
  364.2 28.5 %all-reduce.8.cloned.1.call-done.s_ref = bf16[512,2048]{1,0:T(8,128)(2,1)} async-done(((bf16[512,2048]{1,0:T(8,128)(2,1)}), bf16[512,2048]{1,0:T(8,128)(2,1)}) %all-reduce.8.cloned.1.call-update) | async-done | bytes 2097168 | tf_op jit(solution)/shard_map/psum | solution.py:819
  392.7 1.9 output_first.1.made_ref
  395.8 8.9 %key_back.1 = (bf16[512,512]{1,0:T(8,128)(2,1)}, f32[8,128]{1,0:T(8,128)}, f32[1,2048]{1,0:T(1,128)}, bf16[512,2048]{1,0:T(8,128)(2,1)}) custom-call(s32[1]{0:T(128)} %bitcast.1.me_ref, bf16[512,512]{1,0:T(8,128)(2,1)} %add_convert_fusion.5.refs_0_, bf16[512,512]{1,0:T(8,128)(2,1)} %copy-done.26, bf16[512,512]{1,0:T(8,128)(2,1)} %copy-done.27, ...), custom_call_target="tpu_custom_call" | custom-call | flops 1000000000 | bytes 3400000 | tf_op jit(solution)/shard_map/key_back/pallas_call | solution.py:921
  405.0 4.2 weight_grad_turned.3
  409.7 6.0 %output_rest.1 = bf16[512,2048]{1,0:T(8,128)(2,1)} custom-call(f32[512,2048]{1,0:T(8,128)} %get-tuple-element.145.y_ref, bf16[512,2048]{1,0:T(8,128)(2,1)} %all-reduce.8.cloned.1.call-done.s_ref, bf16[512,2048]{1,0:T(8,128)(2,1)} %output_first.1.made_ref), custom_call_target="tpu_custom_call", output_to_operand_aliasing={{}: (2, {})} | custom-call | flops 5000000000 | bytes 17000000 | tf_op jit(solution)/shard_map/output_rest/pallas_call | solution.py:967
  415.7 1.6 fusion.3
  417.4 1.6 collective-permute-start.33
  419.0 1.5 collective-permute-start.35
  421.3 1.6 collective-permute-start.29
  422.9 1.5 collective-permute-start.31
  424.7 1.8 collective-permute-done.33
  426.5 1.6 collective-permute-start.30
  428.2 5.0 collective-permute-done.35
  433.3 1.4 collective-permute-start.37
  435.3 1.4 collective-permute-start.39
  436.8 1.1 collective-permute-done.29
  437.8 1.6 collective-permute-start.38
  439.6 4.9 collective-permute-done.31
  444.5 2.0 collective-permute-done.30
  446.7 2.4 collective-permute-done.37
  449.1 6.2 %collective-permute-done.39 = bf16[256,512]{1,0:T(8,128)(2,1)S(1)} collective-permute-done((bf16[256,512]{1,0:T(8,128)(2,1)S(1)}, bf16[256,512]{1,0:T(8,128)(2,1)S(1)}, u32[]{:S(2)}, u32[]{:S(2)}) %collective-permute-start.39) | collective-permute-done | bytes 262176 | tf_op jit(solution)/shard_map/ppermute | solution.py:50
  455.3 1.3 collective-permute-done.38
  456.9 1.8 multiply_reduce_fusion
  464.3 1.2 collective-permute-done.40
  465.4 1.5 collective-permute-start.41
  466.9 2.3 collective-permute-done.41
  469.8 3.3 collective-permute-done.42
  473.4 3.9 collective-permute-done.43
  477.2 1.4 collective-permute-start.44
  478.6 5.4 %collective-permute-done.44 = f32[4480]{0:T(1024)S(1)} collective-permute-done((f32[4480]{0:T(1024)S(1)}, f32[4480]{0:T(1024)S(1)}, u32[]{:S(2)}, u32[]{:S(2)}) %collective-permute-start.44) | collective-permute-done | bytes 17952 | tf_op jit(solution)/shard_map/ppermute | solution.py:50
  486.6 13.5 %update.1 = (f32[256,6144]{1,0:T(8,128)}, f32[256,6144]{1,0:T(8,128)}, f32[256,6144]{1,0:T(8,128)}) custom-call(f32[1]{0:T(128)} %bitcast.28.factor_ref, f32[256,6144]{1,0:T(8,128)} %w_ref.1, f32[256,6144]{1,0:T(8,128)} %m_ref.1, f32[256,6144]{1,0:T(8,128)} %e_ref.1, bf16[256,512]{1,0:T(8,128)(2,1)} %copy-done.4, bf16[256,512]{1,0:T(8,128)(2,1)} %copy-done.3, ...), custom_call_target="tpu_custom_call" | custom-call | flops 1000000000 | bytes 3400000 | tf_op jit(solution)/shard_map/update/pallas_call | solution.py:542
  501.5 5.8 %input_back.1 = f32[512,2048]{1,0:T(8,128)} custom-call(f32[512,2048]{1,0:T(8,128)} %get-tuple-element.196.dy_ref, bf16[512,2048]{1,0:T(8,128)(2,1)} %x_ref.3, f32[512,1]{1,0:T(8,128)} %copy.22.refs_10_.scale_ref, bf16[512,2048]{1,0:T(8,128)(2,1)} %all-gather.5.cloned.1.call-done.s_ref, f32[1,2048]{1,0:T(1,128)} %bitcast.59), custom_call_target="tpu_custom_call" | custom-call | flops 8000000000 | bytes 27200000 | tf_op jit(solution)/shard_map/input_back/pallas_call | solution.py:990
  (205 shorter events, 27.1 us)
Async XLA Ops:
  8.0 174.9 %all-gather.3.cloned.1.call-start = ((), (), s32[]{:S(2)}) async-start(), calls=%async_computation.3 | async-start | bytes 21233664 | tf_op jit(solution)/shard_map/all_gather | solution.py:691
  9.1 14.9 %collective-permute-start.5 = (bf16[256,512]{1,0:T(8,128)(2,1)S(1)}, bf16[256,512]{1,0:T(8,128)(2,1)}, u32[]{:S(2)}, u32[]{:S(2)}) collective-permute-start(bf16[256,512]{1,0:T(8,128)(2,1)S(1)} %slice.157.refs_0_.refs_19_), channel_id=1, source_target_pairs={{0,24},{4,28},{8,16},{12,20},{16,8},{20,12},{24,0},{28,4},{1,25},{... | collective-permute-start | bytes 786440 | tf_op jit(solution)/shard_map/ppermute | solution.py:50
  13.1 13.5 %collective-permute-start.3 = (bf16[256,512]{1,0:T(8,128)(2,1)S(1)}, bf16[256,512]{1,0:T(8,128)(2,1)}, u32[]{:S(2)}, u32[]{:S(2)}) collective-permute-start(bf16[256,512]{1,0:T(8,128)(2,1)S(1)} %slice.157.refs_0_.refs_19_), channel_id=1, source_target_pairs={{0,16},{4,20},{8,24},{12,28},{16,0},{20,4},{24,8},{28,12},{1,17},{... | collective-permute-start | bytes 786440 | tf_op jit(solution)/shard_map/ppermute | solution.py:50
  13.6 13.0 %collective-permute-start.1 = (bf16[256,512]{1,0:T(8,128)(2,1)S(1)}, bf16[256,512]{1,0:T(8,128)(2,1)}, u32[]{:S(2)}, u32[]{:S(2)}) collective-permute-start(bf16[256,512]{1,0:T(8,128)(2,1)S(1)} %slice.157.refs_0_.refs_19_), channel_id=1, source_target_pairs={{0,8},{4,12},{8,0},{12,4},{16,24},{20,28},{24,16},{28,20},{1,9},{5... | collective-permute-start | bytes 786440 | tf_op jit(solution)/shard_map/ppermute | solution.py:50
  13.7 15.2 %collective-permute-start = (bf16[256,512]{1,0:T(8,128)(2,1)S(1)}, bf16[256,512]{1,0:T(8,128)(2,1)}, u32[]{:S(2)}, u32[]{:S(2)}) collective-permute-start(bf16[256,512]{1,0:T(8,128)(2,1)S(1)} %slice.157.refs_0_.refs_19_), channel_id=1, source_target_pairs={{0,4},{4,0},{8,12},{12,8},{16,20},{20,16},{24,28},{28,24},{1,5},{5... | collective-permute-start | bytes 786440 | tf_op jit(solution)/shard_map/ppermute | solution.py:50
  17.1 30.7 %copy-start.2 = (bf16[256,1024]{1,0:T(8,128)(2,1)}, bf16[256,1024]{1,0:T(8,128)(2,1)S(1)}, u32[]{:S(2)}) copy-start(bf16[256,1024]{1,0:T(8,128)(2,1)S(1)} %pad_maximum_fusion.refs_0_.refs_11_) | copy-start | bytes 1572868
  17.2 20.5 %collective-permute-start.9 = (bf16[256,1024]{1,0:T(8,128)(2,1)S(1)}, bf16[256,1024]{1,0:T(8,128)(2,1)S(1)}, u32[]{:S(2)}, u32[]{:S(2)}) collective-permute-start(bf16[256,1024]{1,0:T(8,128)(2,1)S(1)} %pad_maximum_fusion.refs_0_.refs_11_), channel_id=1, source_target_pairs={{0,24},{4,28},{8,16},{12,20},{16,8},{20,12},{24,0},{28,4},{1,25},{... | collective-permute-start | bytes 1572872 | tf_op jit(solution)/shard_map/ppermute | solution.py:50
  24.0 5.7 %collective-permute-start.6 = (bf16[256,512]{1,0:T(8,128)(2,1)}, bf16[256,512]{1,0:T(8,128)(2,1)S(1)}, u32[]{:S(2)}, u32[]{:S(2)}) collective-permute-start(bf16[256,512]{1,0:T(8,128)(2,1)} %collective-permute-done.5.refs_6_.refs_25_), channel_id=1, source_target_pairs={{0,4},{4,0},{8,12},{12,8},{16,20},{20,16},{24,28},{28,24},{1,5},{5... | collective-permute-start | bytes 786440 | tf_op jit(solution)/shard_map/ppermute | solution.py:50
  26.6 4.9 collective-permute-start.2
  26.6 4.9 collective-permute-start.4
  28.9 18.6 %collective-permute-start.8 = (bf16[256,1024]{1,0:T(8,128)(2,1)S(1)}, bf16[256,1024]{1,0:T(8,128)(2,1)S(1)}, u32[]{:S(2)}, u32[]{:S(2)}) collective-permute-start(bf16[256,1024]{1,0:T(8,128)(2,1)S(1)} %pad_maximum_fusion.refs_0_.refs_11_), channel_id=1, source_target_pairs={{0,16},{4,20},{8,24},{12,28},{16,0},{20,4},{24,8},{28,12},{1,17},{... | collective-permute-start | bytes 1572872 | tf_op jit(solution)/shard_map/ppermute | solution.py:50
  29.8 18.1 %collective-permute-start.7 = (bf16[256,1024]{1,0:T(8,128)(2,1)S(1)}, bf16[256,1024]{1,0:T(8,128)(2,1)S(1)}, u32[]{:S(2)}, u32[]{:S(2)}) collective-permute-start(bf16[256,1024]{1,0:T(8,128)(2,1)S(1)} %pad_maximum_fusion.refs_0_.refs_11_), channel_id=1, source_target_pairs={{0,8},{4,12},{8,0},{12,4},{16,24},{20,28},{24,16},{28,20},{1,9},{5... | collective-permute-start | bytes 1572872 | tf_op jit(solution)/shard_map/ppermute | solution.py:50
  37.7 15.1 %copy-start.6 = (bf16[256,1024]{1,0:T(8,128)(2,1)}, bf16[256,1024]{1,0:T(8,128)(2,1)S(1)}, u32[]{:S(2)}) copy-start(bf16[256,1024]{1,0:T(8,128)(2,1)S(1)} %collective-permute-done.9.refs_6_.refs_17_) | copy-start | bytes 1572868
  47.8 7.5 %collective-permute-start.13 = (bf16[256,1024]{1,0:T(8,128)(2,1)S(1)}, bf16[256,1024]{1,0:T(8,128)(2,1)S(1)}, u32[]{:S(2)}, u32[]{:S(2)}) collective-permute-start(bf16[256,1024]{1,0:T(8,128)(2,1)S(1)} %pad_maximum_fusion.refs_0_.refs_11_), channel_id=1, source_target_pairs={{0,4},{4,0},{8,12},{12,8},{16,20},{20,16},{24,28},{28,24},{1,5},{5... | collective-permute-start | bytes 1572872 | tf_op jit(solution)/shard_map/ppermute | solution.py:50
  47.8 8.0 %collective-permute-start.14 = (bf16[256,1024]{1,0:T(8,128)(2,1)S(1)}, bf16[256,1024]{1,0:T(8,128)(2,1)S(1)}, u32[]{:S(2)}, u32[]{:S(2)}) collective-permute-start(bf16[256,1024]{1,0:T(8,128)(2,1)S(1)} %collective-permute-done.7.refs_2_.refs_13_), channel_id=1, source_target_pairs={{0,4},{4,0},{8,12},{12,8},{16,20},{20,16},{24,28},{28,24},{1,5},{5... | collective-permute-start | bytes 1572872 | tf_op jit(solution)/shard_map/ppermute | solution.py:50
  48.4 14.1 %collective-permute-start.15 = (bf16[256,1024]{1,0:T(8,128)(2,1)S(1)}, bf16[256,1024]{1,0:T(8,128)(2,1)}, u32[]{:S(2)}, u32[]{:S(2)}) collective-permute-start(bf16[256,1024]{1,0:T(8,128)(2,1)S(1)} %collective-permute-done.8.refs_4_.refs_15_), channel_id=1, source_target_pairs={{0,4},{4,0},{8,12},{12,8},{16,20},{20,16},{24,28},{28,24},{1,5},{5... | collective-permute-start | bytes 1572872 | tf_op jit(solution)/shard_map/ppermute | solution.py:50
  48.4 14.0 %collective-permute-start.16 = (bf16[256,1024]{1,0:T(8,128)(2,1)S(1)}, bf16[256,1024]{1,0:T(8,128)(2,1)}, u32[]{:S(2)}, u32[]{:S(2)}) collective-permute-start(bf16[256,1024]{1,0:T(8,128)(2,1)S(1)} %collective-permute-done.9.refs_6_.refs_17_), channel_id=1, source_target_pairs={{0,4},{4,0},{8,12},{12,8},{16,20},{20,16},{24,28},{28,24},{1,5},{5... | collective-permute-start | bytes 1572872 | tf_op jit(solution)/shard_map/ppermute | solution.py:50
  52.8 16.0 %collective-permute-start.12 = (bf16[512,512]{1,0:T(8,128)(2,1)}, bf16[512,512]{1,0:T(8,128)(2,1)S(1)}, u32[]{:S(2)}, u32[]{:S(2)}) collective-permute-start(bf16[512,512]{1,0:T(8,128)(2,1)} %get-tuple-element.135.refs_0_), channel_id=1, source_target_pairs={{0,24},{4,28},{8,16},{12,20},{16,8},{20,12},{24,0},{28,4},{1,25},{... | collective-permute-start | bytes 1572872 | tf_op jit(solution)/shard_map/ppermute | solution.py:50
  55.3 23.8 %collective-permute-start.11 = (bf16[512,512]{1,0:T(8,128)(2,1)}, bf16[512,512]{1,0:T(8,128)(2,1)S(1)}, u32[]{:S(2)}, u32[]{:S(2)}) collective-permute-start(bf16[512,512]{1,0:T(8,128)(2,1)} %get-tuple-element.135.refs_0_), channel_id=1, source_target_pairs={{0,16},{4,20},{8,24},{12,28},{16,0},{20,4},{24,8},{28,12},{1,17},{... | collective-permute-start | bytes 1572872 | tf_op jit(solution)/shard_map/ppermute | solution.py:50
  55.9 23.4 %collective-permute-start.10 = (bf16[512,512]{1,0:T(8,128)(2,1)}, bf16[512,512]{1,0:T(8,128)(2,1)S(1)}, u32[]{:S(2)}, u32[]{:S(2)}) collective-permute-start(bf16[512,512]{1,0:T(8,128)(2,1)} %get-tuple-element.135.refs_0_), channel_id=1, source_target_pairs={{0,8},{4,12},{8,0},{12,4},{16,24},{20,28},{24,16},{28,20},{1,9},{5... | collective-permute-start | bytes 1572872 | tf_op jit(solution)/shard_map/ppermute | solution.py:50
  62.5 16.8 %copy-start.15 = (bf16[512,512]{1,0:T(8,128)(2,1)S(1)}, bf16[512,512]{1,0:T(8,128)(2,1)}, u32[]{:S(2)}) copy-start(bf16[512,512]{1,0:T(8,128)(2,1)} %get-tuple-element.135.refs_0_) | copy-start | bytes 1572868
  68.8 12.3 %copy-start.16 = (bf16[512,512]{1,0:T(8,128)(2,1)}, bf16[512,512]{1,0:T(8,128)(2,1)S(1)}, u32[]{:S(2)}) copy-start(bf16[512,512]{1,0:T(8,128)(2,1)S(1)} %collective-permute-done.12.refs_6_) | copy-start | bytes 1572868
  79.2 1.9 collective-permute-start.17
  79.3 3.4 collective-permute-start.18
  79.8 3.6 collective-permute-start.19
  79.8 3.6 collective-permute-start.20
  83.4 107.8 %all-reduce.4.cloned.1.call-start = ((), (), s32[]{:S(2)}) async-start(), calls=%async_computation.2 | async-start | bytes 4194304 | tf_op jit(solution)/shard_map/psum | solution.py:738
  104.7 200.2 %all-reduce.6.cloned.1.call-start = ((), (), s32[]{:S(2)}) async-start(), calls=%async_computation.4 | async-start | bytes 4194304 | tf_op jit(solution)/shard_map/psum | solution.py:794
  218.8 141.9 %reduce-scatter.3.cloned.1.call-start = ((), (), s32[]{:S(2)}) async-start(), calls=%async_computation.5 | async-start | bytes 21233664 | tf_op jit(solution)/shard_map/reduce_scatter | solution.py:817
  234.4 158.3 %all-reduce.8.cloned.1.call-start = ((), (), s32[]{:S(2)}) async-start(), calls=%async_computation.6 | async-start | bytes 4194304 | tf_op jit(solution)/shard_map/psum | solution.py:819
  304.9 151.9 %reduce-scatter.5.cloned.1.call-start = ((), (), s32[]{:S(2)}) async-start(), calls=%async_computation.7 | async-start | bytes 2621440 | tf_op jit(solution)/shard_map/reduce_scatter | solution.py:963
  333.4 13.3 %collective-permute-start.21 = (bf16[512,512]{1,0:T(8,128)(2,1)}, bf16[512,512]{1,0:T(8,128)(2,1)S(1)}, u32[]{:S(2)}, u32[]{:S(2)}) collective-permute-start(bf16[512,512]{1,0:T(8,128)(2,1)} %get-tuple-element.160), channel_id=1, source_target_pairs={{0,4},{4,0},{8,12},{12,8},{16,20},{20,16},{24,28},{28,24},{1,5},{5... | collective-permute-start | bytes 1572872 | tf_op jit(solution)/shard_map/ppermute | solution.py:50
  333.5 14.2 %collective-permute-start.22 = (bf16[512,512]{1,0:T(8,128)(2,1)}, bf16[512,512]{1,0:T(8,128)(2,1)S(1)}, u32[]{:S(2)}, u32[]{:S(2)}) collective-permute-start(bf16[512,512]{1,0:T(8,128)(2,1)} %get-tuple-element.162), channel_id=1, source_target_pairs={{0,4},{4,0},{8,12},{12,8},{16,20},{20,16},{24,28},{28,24},{1,5},{5... | collective-permute-start | bytes 1572872 | tf_op jit(solution)/shard_map/ppermute | solution.py:50
  334.8 13.0 %collective-permute-start.23 = (bf16[512,512]{1,0:T(8,128)(2,1)}, bf16[512,512]{1,0:T(8,128)(2,1)S(1)}, u32[]{:S(2)}, u32[]{:S(2)}) collective-permute-start(bf16[512,512]{1,0:T(8,128)(2,1)} %get-tuple-element.164), channel_id=1, source_target_pairs={{0,4},{4,0},{8,12},{12,8},{16,20},{20,16},{24,28},{28,24},{1,5},{5... | collective-permute-start | bytes 1572872 | tf_op jit(solution)/shard_map/ppermute | solution.py:50
  334.9 13.1 %collective-permute-start.24 = (bf16[512,512]{1,0:T(8,128)(2,1)}, bf16[512,512]{1,0:T(8,128)(2,1)S(1)}, u32[]{:S(2)}, u32[]{:S(2)}) collective-permute-start(bf16[512,512]{1,0:T(8,128)(2,1)} %get-tuple-element.166), channel_id=1, source_target_pairs={{0,4},{4,0},{8,12},{12,8},{16,20},{20,16},{24,28},{28,24},{1,5},{5... | collective-permute-start | bytes 1572872 | tf_op jit(solution)/shard_map/ppermute | solution.py:50
  360.7 33.9 %collective-permute-start.25 = (bf16[512,512]{1,0:T(8,128)(2,1)S(1)}, bf16[512,512]{1,0:T(8,128)(2,1)S(1)}, u32[]{:S(2)}, u32[]{:S(2)}) collective-permute-start(bf16[512,512]{1,0:T(8,128)(2,1)S(1)} %add_convert_fusion.4), channel_id=1, source_target_pairs={{0,8},{4,12},{8,0},{12,4},{16,24},{20,28},{24,16},{28,20},{1,9},{5... | collective-permute-start | bytes 1572872 | tf_op jit(solution)/shard_map/ppermute | solution.py:50
  362.0 32.5 %collective-permute-start.26 = (bf16[512,512]{1,0:T(8,128)(2,1)S(1)}, bf16[512,512]{1,0:T(8,128)(2,1)S(1)}, u32[]{:S(2)}, u32[]{:S(2)}) collective-permute-start(bf16[512,512]{1,0:T(8,128)(2,1)S(1)} %add_convert_fusion.3), channel_id=1, source_target_pairs={{0,16},{4,20},{8,24},{12,28},{16,0},{20,4},{24,8},{28,12},{1,17},{... | collective-permute-start | bytes 1572872 | tf_op jit(solution)/shard_map/ppermute | solution.py:50
  362.7 31.9 %collective-permute-start.27 = (bf16[512,512]{1,0:T(8,128)(2,1)S(1)}, bf16[512,512]{1,0:T(8,128)(2,1)S(1)}, u32[]{:S(2)}, u32[]{:S(2)}) collective-permute-start(bf16[512,512]{1,0:T(8,128)(2,1)S(1)} %add_convert_fusion.2), channel_id=1, source_target_pairs={{0,24},{4,28},{8,16},{12,20},{16,8},{20,12},{24,0},{28,4},{1,25},{... | collective-permute-start | bytes 1572872 | tf_op jit(solution)/shard_map/ppermute | solution.py:50
  404.7 96.8 %all-gather.5.cloned.1.call-start = ((), (), s32[]{:S(2)}) async-start(), calls=%async_computation.8 | async-start | bytes 2621440 | tf_op jit(solution)/shard_map/all_gather | solution.py:983
  409.2 6.5 %collective-permute-start.32 = (bf16[4,256,512]{2,1,0:T(8,128)(2,1)}, bf16[4,256,512]{2,1,0:T(8,128)(2,1)}, u32[]{:S(2)}, u32[]{:S(2)}) collective-permute-start(bf16[4,256,512]{2,1,0:T(8,128)(2,1)} %bitcast.65), channel_id=1, source_target_pairs={{0,4},{4,0},{8,12},{12,8},{16,20},{20,16},{24,28},{28,24},{1,5},{5... | collective-permute-start | bytes 3145736 | tf_op jit(solution)/shard_map/ppermute | solution.py:50
  409.2 11.7 %collective-permute-start.28 = (bf16[4,256,512]{2,1,0:T(8,128)(2,1)}, bf16[4,256,512]{2,1,0:T(8,128)(2,1)S(1)}, u32[]{:S(2)}, u32[]{:S(2)}) collective-permute-start(bf16[4,256,512]{2,1,0:T(8,128)(2,1)} %bitcast.7), channel_id=1, source_target_pairs={{0,4},{4,0},{8,12},{12,8},{16,20},{20,16},{24,28},{28,24},{1,5},{5... | collective-permute-start | bytes 3145736 | tf_op jit(solution)/shard_map/ppermute | solution.py:50
  409.7 13.2 %collective-permute-start.36 = (bf16[4,256,512]{2,1,0:T(8,128)(2,1)}, bf16[4,256,512]{2,1,0:T(8,128)(2,1)S(1)}, u32[]{:S(2)}, u32[]{:S(2)}) collective-permute-start(bf16[4,256,512]{2,1,0:T(8,128)(2,1)} %get-tuple-element.190), channel_id=1, source_target_pairs={{0,4},{4,0},{8,12},{12,8},{16,20},{20,16},{24,28},{28,24},{1,5},{5... | collective-permute-start | bytes 3145736 | tf_op jit(solution)/shard_map/ppermute | solution.py:50
  417.4 9.2 %collective-permute-start.33 = (bf16[256,512]{1,0:T(8,128)(2,1)S(1)}, bf16[256,512]{1,0:T(8,128)(2,1)S(1)}, u32[]{:S(2)}, u32[]{:S(2)}) collective-permute-start(bf16[256,512]{1,0:T(8,128)(2,1)S(1)} %get-tuple-element.219), channel_id=1, source_target_pairs={{0,8},{4,12},{8,0},{12,4},{16,24},{20,28},{24,16},{28,20},{1,9},{5... | collective-permute-start | bytes 786440 | tf_op jit(solution)/shard_map/ppermute | solution.py:50
  419.0 14.3 %collective-permute-start.35 = (bf16[256,512]{1,0:T(8,128)(2,1)S(1)}, bf16[256,512]{1,0:T(8,128)(2,1)S(1)}, u32[]{:S(2)}, u32[]{:S(2)}) collective-permute-start(bf16[256,512]{1,0:T(8,128)(2,1)S(1)} %get-tuple-element.220), channel_id=1, source_target_pairs={{0,24},{4,28},{8,16},{12,20},{16,8},{20,12},{24,0},{28,4},{1,25},{... | collective-permute-start | bytes 786440 | tf_op jit(solution)/shard_map/ppermute | solution.py:50
  420.5 14.8 %collective-permute-start.34 = (bf16[256,512]{1,0:T(8,128)(2,1)S(1)}, bf16[256,512]{1,0:T(8,128)(2,1)S(1)}, u32[]{:S(2)}, u32[]{:S(2)}) collective-permute-start(bf16[256,512]{1,0:T(8,128)(2,1)S(1)} %get-tuple-element.221), channel_id=1, source_target_pairs={{0,16},{4,20},{8,24},{12,28},{16,0},{20,4},{24,8},{28,12},{1,17},{... | collective-permute-start | bytes 786440 | tf_op jit(solution)/shard_map/ppermute | solution.py:50
  421.3 16.5 %collective-permute-start.29 = (bf16[256,512]{1,0:T(8,128)(2,1)S(1)}, bf16[256,512]{1,0:T(8,128)(2,1)S(1)}, u32[]{:S(2)}, u32[]{:S(2)}) collective-permute-start(bf16[256,512]{1,0:T(8,128)(2,1)S(1)} %get-tuple-element.222), channel_id=1, source_target_pairs={{0,8},{4,12},{8,0},{12,4},{16,24},{20,28},{24,16},{28,20},{1,9},{5... | collective-permute-start | bytes 786440 | tf_op jit(solution)/shard_map/ppermute | solution.py:50
  422.9 21.6 %collective-permute-start.31 = (bf16[256,512]{1,0:T(8,128)(2,1)S(1)}, bf16[256,512]{1,0:T(8,128)(2,1)S(1)}, u32[]{:S(2)}, u32[]{:S(2)}) collective-permute-start(bf16[256,512]{1,0:T(8,128)(2,1)S(1)} %get-tuple-element.223), channel_id=1, source_target_pairs={{0,24},{4,28},{8,16},{12,20},{16,8},{20,12},{24,0},{28,4},{1,25},{... | collective-permute-start | bytes 786440 | tf_op jit(solution)/shard_map/ppermute | solution.py:50
  426.5 20.0 %collective-permute-start.30 = (bf16[256,512]{1,0:T(8,128)(2,1)S(1)}, bf16[256,512]{1,0:T(8,128)(2,1)S(1)}, u32[]{:S(2)}, u32[]{:S(2)}) collective-permute-start(bf16[256,512]{1,0:T(8,128)(2,1)S(1)} %get-tuple-element.224), channel_id=1, source_target_pairs={{0,16},{4,20},{8,24},{12,28},{16,0},{20,4},{24,8},{28,12},{1,17},{... | collective-permute-start | bytes 786440 | tf_op jit(solution)/shard_map/ppermute | solution.py:50
  433.3 15.8 %collective-permute-start.37 = (bf16[256,512]{1,0:T(8,128)(2,1)S(1)}, bf16[256,512]{1,0:T(8,128)(2,1)S(1)}, u32[]{:S(2)}, u32[]{:S(2)}) collective-permute-start(bf16[256,512]{1,0:T(8,128)(2,1)S(1)} %get-tuple-element.216), channel_id=1, source_target_pairs={{0,8},{4,12},{8,0},{12,4},{16,24},{20,28},{24,16},{28,20},{1,9},{5... | collective-permute-start | bytes 786440 | tf_op jit(solution)/shard_map/ppermute | solution.py:50
  435.3 20.0 %collective-permute-start.39 = (bf16[256,512]{1,0:T(8,128)(2,1)S(1)}, bf16[256,512]{1,0:T(8,128)(2,1)S(1)}, u32[]{:S(2)}, u32[]{:S(2)}) collective-permute-start(bf16[256,512]{1,0:T(8,128)(2,1)S(1)} %get-tuple-element.217), channel_id=1, source_target_pairs={{0,24},{4,28},{8,16},{12,20},{16,8},{20,12},{24,0},{28,4},{1,25},{... | collective-permute-start | bytes 786440 | tf_op jit(solution)/shard_map/ppermute | solution.py:50
  437.8 19.0 %copy-start.39 = (f32[8,128]{1,0:T(8,128)S(1)}, f32[8,128]{1,0:T(8,128)}, u32[]{:S(2)}) copy-start(f32[8,128]{1,0:T(8,128)} %get-tuple-element.204) | copy-start | bytes 12292
  437.8 19.0 %copy-start.1 = (bf16[256,4608]{1,0:T(8,128)(2,1)S(1)}, bf16[256,4608]{1,0:T(8,128)(2,1)}, u32[]{:S(2)}) copy-start(bf16[256,4608]{1,0:T(8,128)(2,1)} %reduce-scatter.3.cloned.1.call-done.refs_3_) | copy-start | bytes 7077892
  437.8 18.8 %collective-permute-start.38 = (bf16[256,512]{1,0:T(8,128)(2,1)S(1)}, bf16[256,512]{1,0:T(8,128)(2,1)S(1)}, u32[]{:S(2)}, u32[]{:S(2)}) collective-permute-start(bf16[256,512]{1,0:T(8,128)(2,1)S(1)} %get-tuple-element.218), channel_id=1, source_target_pairs={{0,16},{4,20},{8,24},{12,28},{16,0},{20,4},{24,8},{28,12},{1,17},{... | collective-permute-start | bytes 786440 | tf_op jit(solution)/shard_map/ppermute | solution.py:50
  439.6 19.1 %copy-start.3 = (bf16[256,512]{1,0:T(8,128)(2,1)}, bf16[256,512]{1,0:T(8,128)(2,1)S(1)}, u32[]{:S(2)}) copy-start(bf16[256,512]{1,0:T(8,128)(2,1)S(1)} %fusion.9.refs_1_) | copy-start | bytes 786436
  446.7 12.7 %copy-start.4 = (bf16[256,512]{1,0:T(8,128)(2,1)}, bf16[256,512]{1,0:T(8,128)(2,1)S(1)}, u32[]{:S(2)}) copy-start(bf16[256,512]{1,0:T(8,128)(2,1)S(1)} %fusion.12.refs_0_) | copy-start | bytes 786436
  456.7 29.8 %copy-start.5 = (bf16[256,512]{1,0:T(8,128)(2,1)}, bf16[256,512]{1,0:T(8,128)(2,1)S(1)}, u32[]{:S(2)}) copy-start(bf16[256,512]{1,0:T(8,128)(2,1)S(1)} %fusion.6.refs_2_) | copy-start | bytes 786436
  464.3 1.2 collective-permute-start.40
  465.4 3.8 collective-permute-start.41
  469.2 3.8 collective-permute-start.42
  473.0 4.2 collective-permute-start.43
  477.2 6.8 %collective-permute-start.44 = (f32[4480]{0:T(1024)S(1)}, f32[4480]{0:T(1024)S(1)}, u32[]{:S(2)}, u32[]{:S(2)}) collective-permute-start(f32[4480]{0:T(1024)S(1)} %add.190), channel_id=1, source_target_pairs={{0,2},{1,3},{2,0},{3,1},{4,6},{5,7},{6,4},{7,5},{8,10},{9,11},{10,... | collective-permute-start | bytes 53768 | tf_op jit(solution)/shard_map/ppermute | solution.py:50
  486.5 13.6 %copy-start.33 = (f32[4352]{0:T(1024)S(1)}, f32[4352]{0:T(1024)}, u32[]{:S(2)}) copy-start(f32[4352]{0:T(1024)} %param.17) | copy-start | bytes 52228
  486.6 13.5 %copy-start.35 = (f32[4352]{0:T(1024)S(1)}, f32[4352]{0:T(1024)}, u32[]{:S(2)}) copy-start(f32[4352]{0:T(1024)} %param.19) | copy-start | bytes 52228
  486.6 13.5 %copy-start.36 = (f32[4352]{0:T(1024)S(1)}, f32[4352]{0:T(1024)}, u32[]{:S(2)}) copy-start(f32[4352]{0:T(1024)} %param.18) | copy-start | bytes 52228
  (31 other events, 118.1 us)
Sparse Core Ops, SparseCore 0:
  83.6 99.3 all-gather.2
  234.5 126.1 reduce-scatter.2
Sparse Core Ops, SparseCore 1:
  104.8 85.4 all-reduce.3
  218.9 85.9 all-reduce.5
  307.7 85.0 all-reduce.7
  404.8 42.5 reduce-scatter.4
  456.9 44.6 all-gather.4

commit v5 on v3

--- a/solution.py
+++ b/solution.py
@@ -421,13 +421,13 @@
 
 def input_back_kernel(dy_ref, x_ref, scale_ref, s_ref, gain_ref, o_ref):
     def rows_of(r, unused):
-        at = pl.ds(pl.multiple_of(r * 32, 32), 32)
+        at = pl.ds(pl.multiple_of(r * 16, 16), 16)
         scale = scale_ref[at, :]
         back = norm_back(x_ref[at, :].astype(f32) * scale, scale, gain_ref[...], s_ref[at, :].astype(f32))
         o_ref[at, :] = dy_ref[at, :] + back
         return unused
 
-    lax.fori_loop(0, x_ref.shape[0] // 32, rows_of, 0, unroll=2)
+    lax.fori_loop(0, x_ref.shape[0] // 16, rows_of, 0, unroll=4)
 
 
 def transpose_kernel(me_ref, x_ref, o_ref):
@@ -542,7 +542,7 @@
 
 def update_weights(factor, weights, momentum, average, pieces):
     rows, columns = weights.shape
-    step = 32
+    step = 64
     spec = pl.BlockSpec((step, columns), lambda n, _: (n, 0))
     shape = jax.ShapeDtypeStruct(weights.shape, f32)
     return pl.pallas_call(
@@ -940,19 +940,17 @@
     grad_norm = jnp.sqrt(square_total + jnp.sum(gain_grads * gain_grads))
     factor = 1.0 / jnp.maximum(grad_norm, 1.0)
     new_weights, new_momentum, new_ema = update_weights(factor[None], weights, momentum, ema_weights, weight_grads)
-    eighth = tok_count // 8
-    eighth_spec = pl.BlockSpec((eighth, model_width), lambda n: (n, 0))
     grad_input = pl.pallas_call(
         input_back_kernel,
-        grid=(8,),
+        grid=(2,),
         in_specs=[
-            eighth_spec,
-            eighth_spec,
-            pl.BlockSpec((eighth, 1), lambda n: (n, 0)),
-            eighth_spec,
+            half_spec,
+            half_spec,
+            pl.BlockSpec((half_rows, 1), lambda n: (n, 0)),
+            half_spec,
             gain_spec,
         ],
-        out_specs=eighth_spec,
+        out_specs=half_spec,
         out_shape=wide_shape,
         compiler_params=params(),
         cost_estimate=cost(8),

time: 520 us -> 517 us (level)
  transfers between devices with their start and end apart: 52 -> 52, of which waited for: 26 -> 25; matrix products, arithmetic and copies ran while one was open for 6% -> 6% of each run, Pallas kernels for 22% -> 23%
where the time goes in v5:
time: 517 us; the launch traced here: 516 us
  waiting for transfers between devices  262 us (51%)
  Pallas kernels  161 us (31%)
  starting transfers between devices  37 us (7%)
  other arithmetic  23.8 us (5%)
  between operations  21.3 us (4%)
  local copies, waits for them, and re-layouts  10.9 us (2%)
    all_gather x1, waiting for transfers between devices, per_device(): mlp_weights = lax.all_gather(mlp_own, 'dp', axis=0, tiled=True)  80.1 us
    ppermute x45, waiting for transfers between devices, swap(): return lax.ppermute(array, axis, [(i, i ^ distance) for i in range(count)])  67.4 us
    psum x1, waiting for transfers between devices, per_device(): grad_mlp_sum = lax.psum(grad_mlp_part, 'mp')  62.8 us
    ppermute x45, starting transfers between devices, swap(): return lax.ppermute(array, axis, [(i, i ^ distance) for i in range(count)])  36.2 us
    psum x1, waiting for transfers between devices, per_device(): mlp_sum = lax.psum(mlp_part, 'mp')  28.5 us
    pallas_call x1, Pallas kernels, per_device(): pl.pallas_call(functools.partial(attend_back_kernel, group, heads, parts,...  17.1 us
    pallas_call x1, Pallas kernels, per_device(): pl.pallas_call(mlp_kernel, grid=(tiles,), in_specs=[rows_all, rows_all, g...  16.3 us
    pallas_call x1, Pallas kernels, per_device(): pl.pallas_call(mlp_weight_grad_kernel, grid=(model_width // TILE,), in_sp...  15.5 us
  transfers between devices with their start and end apart: 52, of which 25 were waited for; matrix products, arithmetic and copies ran while one was open for 6% of the time, Pallas kernels for 23%

profile of v5, /device:TPU:0, one launch (start us, length us, event | category | flops | bytes accessed | tf_op | source)
XLA Modules:
  0.0 515.8 jit_solution(4152273552214030132)
XLA Ops:
  8.1 1.3 slice.162.refs_0_.refs_11_
  9.9 2.6 collective-permute-start.1
  12.5 1.5 collective-permute-start.3
  14.0 3.2 convert.12
  17.3 1.7 copy-done.1
  19.0 2.0 collective-permute-start.7
  22.9 1.9 fusion.2.x_ref.h_ref
  25.0 6.0 %transposed.1.lhs_ref = bf16[2048,512]{1,0:T(8,128)(2,1)} custom-call(s32[1]{0:T(128)} %bitcast.1.me_ref, bf16[512,2048]{1,0:T(8,128)(2,1)} %fusion.2.x_ref.h_ref), custom_call_target="tpu_custom_call" | custom-call | flops 5000000000 | bytes 17000000 | tf_op jit(solution)/shard_map/transposed/pallas_call | solution.py:440
  31.0 6.6 %collective-permute-done.3.refs_4_.refs_15_ = bf16[256,1024]{1,0:T(8,128)(2,1)} collective-permute-done((bf16[256,1024]{1,0:T(8,128)(2,1)S(1)}, bf16[256,1024]{1,0:T(8,128)(2,1)}, u32[]{:S(2)}, u32[]{:S(2)}) %collective-permute-start.3) | collective-permute-done | bytes 524320 | tf_op jit(solution)/shard_map/ppermute | solution.py:50
  38.7 1.8 fusion.13
  40.5 1.8 collective-permute-start.8
  44.5 8.4 %project.1 = (bf16[512,512]{1,0:T(8,128)(2,1)}, bf16[512,512]{1,0:T(8,128)(2,1)}, f32[512,768]{1,0:T(8,128)}) custom-call(s32[1]{0:T(128)} %bitcast.1.me_ref, bf16[512,2048]{1,0:T(8,128)(2,1)} %fusion.2.x_ref.h_ref, bf16[256,1024]{1,0:T(8,128)(2,1)} %copy-done.4, bf16[256,1024]{1,0:T(8,128)(2,1)} %copy-done.9, ...), custom_call_target="tpu_custom_call" | custom-call | flops 6000000000 | bytes 20400000 | tf_op jit(solution)/shard_map/project/pallas_call | solution.py:651
  52.9 2.1 collective-permute-done.8.refs_4_
  55.0 1.4 collective-permute-start.15
  57.0 1.5 collective-permute-start.19
  59.0 1.4 collective-permute-done.10.refs_1_
  60.9 9.2 %collective-permute-done.15.refs_2_ = bf16[512,512]{1,0:T(8,128)(2,1)S(1)} collective-permute-done((bf16[512,512]{1,0:T(8,128)(2,1)}, bf16[512,512]{1,0:T(8,128)(2,1)S(1)}, u32[]{:S(2)}, u32[]{:S(2)}) %collective-permute-start.15) | collective-permute-done | bytes 524320 | tf_op jit(solution)/shard_map/ppermute | solution.py:50
  70.0 11.2 %collective-permute-done.17.refs_4_ = bf16[512,512]{1,0:T(8,128)(2,1)} collective-permute-done((bf16[512,512]{1,0:T(8,128)(2,1)}, bf16[512,512]{1,0:T(8,128)(2,1)}, u32[]{:S(2)}, u32[]{:S(2)}) %collective-permute-start.17) | collective-permute-done | bytes 524320 | tf_op jit(solution)/shard_map/ppermute | solution.py:50
  81.9 1.6 slice.117
  83.4 1.2 collective-permute-done.13.refs_7_
  85.4 12.8 %attend.1 = (f32[8,128,256]{2,1,0:T(8,128)}, bf16[512,512]{1,0:T(8,128)(2,1)}, f32[8,8,256]{2,1,0:T(8,128)}) custom-call(s32[4]{0:T(128)} %get-tuple-element.189.own_ref, s32[32]{0:T(128)} %fusion.14.inverse_ref, s32[8]{0:T(128)} %copy-done.31, bf16[512,512]{1,0:T(8,128)(2,1)} %get-tuple-element.95.q_ref, bf16[512,512]{1,0:T(8,128)(2,1)} %get-tuple-element.103.refs_0_, ...), custom_call_target="tpu_custom_call" | custom-call | flops 16000000000 | bytes 54400000 | tf_op jit(solution)/shard_map/attend/pallas_call | solution.py:694
  98.2 4.4 project_out.1
  102.9 80.1 %all-gather.3.cloned.1.call-done.w_ref.wg_ref.wu_ref = bf16[2048,4608]{1,0:T(8,128)(2,1)} async-done(((bf16[256,4608]{1,0:T(8,128)(2,1)}), bf16[2048,4608]{1,0:T(8,128)(2,1)}) %all-gather.3.cloned.1.call-update) | async-done | bytes 18874384 | tf_op jit(solution)/shard_map/all_gather | solution.py:684
  182.9 8.3 %grad_hidden.1.da_ref = bf16[512,1536]{1,0:T(8,128)(2,1)} custom-call(bf16[512,2048]{1,0:T(8,128)(2,1)} %c_ref.3, bf16[2048,4608]{1,0:T(8,128)(2,1)} %all-gather.3.cloned.1.call-done.w_ref.wg_ref.wu_ref), custom_call_target="tpu_custom_call" | custom-call | flops 30000001024 | bytes 102000000 | tf_op jit(solution)/shard_map/grad_hidden/pallas_call | solution.py:740
  191.3 16.3 %mlp.1 = (f32[512,2048]{1,0:T(8,128)}, bf16[512,2048]{1,0:T(8,128)(2,1)}, f32[512,1]{1,0:T(8,128)}, bf16[512,1536]{1,0:T(8,128)(2,1)}, bf16[512,1536]{1,0:T(8,128)(2,1)}, /*index=5*/bf16[512,1536]{1,0:T(8,128)(2,1)}) custom-call(bf16[512,2048]{1,0:T(8,128)(2,1)} %x_ref.3, bf16[512,2048]{1,0:T(8,128)(2,1)} %all-reduce.4.cloned.1.call-done.s_ref, ...), custom_call_target="tpu_custom_call" | custom-call | flops 17999998976 | bytes 61200000 | tf_op jit(solution)/shard_map/mlp/pallas_call | solution.py:750
  207.6 11.3 %mlp_back.1 = bf16[512,2048]{1,0:T(8,128)(2,1)} custom-call(bf16[512,1536]{1,0:T(8,128)(2,1)} %get-tuple-element.123.dg_ref, bf16[512,1536]{1,0:T(8,128)(2,1)} %get-tuple-element.124.du_ref, bf16[2048,4608]{1,0:T(8,128)(2,1)} %all-gather.3.cloned.1.call-done.w_ref.wg_ref.wu_ref, bf16[2048,4608]{1,0:T(8,128)(2,1)} %all-gather.3.cloned.1.call-done.w_ref.wg_ref.wu_ref), custom_call_target="tpu_custom_call" | custom-call | flops 11000000512 | bytes 37400000 | tf_op jit(solution)/shard_map/mlp_back/pallas_call | solution.py:770
  219.0 15.5 %mlp_weight_grad.1 = bf16[2048,4608]{1,0:T(8,128)(2,1)} custom-call(bf16[512,2048]{1,0:T(8,128)(2,1)} %get-tuple-element.129.h_ref, bf16[512,2048]{1,0:T(8,128)(2,1)} %c_ref.3, bf16[512,1536]{1,0:T(8,128)(2,1)} %get-tuple-element.123.dg_ref, bf16[512,1536]{1,0:T(8,128)(2,1)} %get-tuple-element.124.du_ref, bf16[512,1536]{1,0:T(8,128)(2,1)} %get-tuple-element.128.a_ref), custom_call_target="tpu_custom_call" | custom-call | flops 1000000000 | bytes 3400000 | tf_op jit(solution)/shard_map/mlp_weight_grad/pallas_call | solution.py:789
  234.5 7.6 %mlp_out.1 = bf16[512,2048]{1,0:T(8,128)(2,1)} custom-call(bf16[512,1536]{1,0:T(8,128)(2,1)} %get-tuple-element.128.a_ref, bf16[2048,4608]{1,0:T(8,128)(2,1)} %all-gather.3.cloned.1.call-done.w_ref.wg_ref.wu_ref), custom_call_target="tpu_custom_call" | custom-call | flops 1000000000 | bytes 3400000 | tf_op jit(solution)/shard_map/mlp_out/pallas_call | solution.py:799
  242.1 62.8 %all-reduce.6.cloned.1.call-done.s_ref = bf16[512,2048]{1,0:T(8,128)(2,1)} async-done(((bf16[512,2048]{1,0:T(8,128)(2,1)}), bf16[512,2048]{1,0:T(8,128)(2,1)}) %all-reduce.6.cloned.1.call-update) | async-done | bytes 2097168 | tf_op jit(solution)/shard_map/psum | solution.py:786
  305.6 8.8 %residual_back.1 = (f32[512,2048]{1,0:T(8,128)}, bf16[512,2048]{1,0:T(8,128)(2,1)}, bf16[512,512]{1,0:T(8,128)(2,1)}, f32[1,2048]{1,0:T(1,128)}) custom-call(s32[1]{0:T(128)} %bitcast.1.me_ref, f32[512,2048]{1,0:T(8,128)} %get-tuple-element.121.y_ref, f32[512,1]{1,0:T(8,128)} %get-tuple-element.122.scale_ref, bf16[512,2048]{1,0:T(8,128)(2,1)} %c_ref.3, ...), custom_call_target="tpu_custom_call" | custom-call | flops 1000000000 | bytes 3400000 | tf_op jit(solution)/shard_map/residual_back/pallas_call | solution.py:815
  314.4 17.1 %attend_back.1 = (bf16[512,512]{1,0:T(8,128)(2,1)}, f32[8,128]{1,0:T(8,128)}, bf16[512,512]{1,0:T(8,128)(2,1)}, bf16[512,512]{1,0:T(8,128)(2,1)}, bf16[512,512]{...) custom-call(s32[4]{0:T(128)} %get-tuple-element.189.own_ref, ...), custom_call_target="tpu_custom_call" | custom-call | flops 1000000000 | bytes 3400000 | tf_op jit(solution)/shard_map/attend_back/pallas_call | solution.py:843
  333.5 7.1 %weight_grad.1 = (bf16[4,256,512]{2,1,0:T(8,128)(2,1)}, bf16[4,256,512]{2,1,0:T(8,128)(2,1)}) custom-call(s32[1]{0:T(128)} %bitcast.1.me_ref, bf16[512,2048]{1,0:T(8,128)(2,1)} %get-tuple-element.152.lhs_ref, bf16[512,512]{1,0:T(8,128)(2,1)} %get-tuple-element.111.low_ref.refs_0_), custom_call_target="tpu_custom_call" | custom-call | flops 1000000000 | bytes 3400000 | tf_op jit(solution)/shard_map/weight_grad/pallas_call | solution.py:516
  340.6 4.3 weight_grad_turned.2
  346.5 14.3 %reduce-scatter.3.cloned.1.call-done.refs_3_ = bf16[256,4608]{1,0:T(8,128)(2,1)} async-done(((bf16[2048,4608]{1,0:T(8,128)(2,1)}), bf16[256,4608]{1,0:T(8,128)(2,1)}) %reduce-scatter.3.cloned.1.call-update) | async-done | bytes 2359312 | tf_op jit(solution)/shard_map/reduce_scatter | solution.py:809
  360.8 1.3 collective-permute-start.25
  362.8 1.5 collective-permute-start.27
  364.3 28.5 %all-reduce.8.cloned.1.call-done = bf16[512,2048]{1,0:T(8,128)(2,1)} async-done(((bf16[512,2048]{1,0:T(8,128)(2,1)}), bf16[512,2048]{1,0:T(8,128)(2,1)}) %all-reduce.8.cloned.1.call-update) | async-done | bytes 2097168 | tf_op jit(solution)/shard_map/psum | solution.py:811
  392.8 4.9 add_convert_fusion
  398.9 9.0 %key_back.1 = (bf16[512,512]{1,0:T(8,128)(2,1)}, f32[8,128]{1,0:T(8,128)}, f32[1,2048]{1,0:T(1,128)}, bf16[512,2048]{1,0:T(8,128)(2,1)}) custom-call(s32[1]{0:T(128)} %bitcast.1.me_ref, bf16[512,512]{1,0:T(8,128)(2,1)} %add_convert_fusion.6.refs_0_, bf16[512,512]{1,0:T(8,128)(2,1)} %copy-done.18, bf16[512,512]{1,0:T(8,128)(2,1)} %copy-done.19, ...), custom_call_target="tpu_custom_call" | custom-call | flops 1000000000 | bytes 3400000 | tf_op jit(solution)/shard_map/key_back/pallas_call | solution.py:903
  408.3 4.4 weight_grad_turned.3
  412.9 1.8 multiply_reduce_fusion
  415.3 2.5 collective-permute-start.31
  419.3 2.5 collective-permute-start.35
  422.6 2.8 collective-permute-done.31
  425.5 1.5 collective-permute-start.33
  427.0 4.1 collective-permute-done.30
  431.1 2.4 collective-permute-start.39
  434.1 2.7 collective-permute-done.35
  436.8 1.5 collective-permute-start.37
  438.2 1.5 multiply_reduce_fusion.3
  439.7 2.7 collective-permute-done.34
  442.4 1.5 multiply_reduce_fusion.2
  445.2 2.9 collective-permute-done.39
  448.0 4.9 collective-permute-done.38
  453.0 1.5 multiply_reduce_fusion.1
  457.9 1.5 collective-permute-start.41
  459.3 2.3 collective-permute-done.41
  461.6 1.3 collective-permute-start.42
  463.0 2.4 collective-permute-done.42
  465.8 4.6 collective-permute-done.43
  471.2 4.4 collective-permute-done.44
  478.1 13.5 %update.1 = (f32[256,6144]{1,0:T(8,128)}, f32[256,6144]{1,0:T(8,128)}, f32[256,6144]{1,0:T(8,128)}) custom-call(f32[1]{0:T(128)} %bitcast.29.factor_ref, f32[256,6144]{1,0:T(8,128)} %w_ref.1, f32[256,6144]{1,0:T(8,128)} %m_ref.1, f32[256,6144]{1,0:T(8,128)} %e_ref.1, bf16[256,512]{1,0:T(8,128)(2,1)} %get-tuple-element.187.refs_0_, ...), custom_call_target="tpu_custom_call" | custom-call | flops 1000000000 | bytes 3400000 | tf_op jit(solution)/shard_map/update/pallas_call | solution.py:548
  492.3 9.0 %all-gather.5.cloned.1.call-done.s_ref = bf16[512,2048]{1,0:T(8,128)(2,1)} async-done(((bf16[128,2048]{1,0:T(8,128)(2,1)}), bf16[512,2048]{1,0:T(8,128)(2,1)}) %all-gather.5.cloned.1.call-update) | async-done | bytes 2097168 | tf_op jit(solution)/shard_map/all_gather | solution.py:936
  501.3 5.8 %input_back.1 = f32[512,2048]{1,0:T(8,128)} custom-call(f32[512,2048]{1,0:T(8,128)} %get-tuple-element.156.dy_ref, bf16[512,2048]{1,0:T(8,128)(2,1)} %x_ref.3, f32[512,1]{1,0:T(8,128)} %copy.22.refs_10_.scale_ref, bf16[512,2048]{1,0:T(8,128)(2,1)} %all-gather.5.cloned.1.call-done.s_ref, f32[1,2048]{1,0:T(1,128)} %bitcast.64), custom_call_target="tpu_custom_call" | custom-call | flops 8000000000 | bytes 27200000 | tf_op jit(solution)/shard_map/input_back/pallas_call | solution.py:943
  (184 shorter events, 24.6 us)
Async XLA Ops:
  8.0 174.9 %all-gather.3.cloned.1.call-start = ((), (), s32[]{:S(2)}) async-start(), calls=%async_computation.3 | async-start | bytes 21233664 | tf_op jit(solution)/shard_map/all_gather | solution.py:684
  9.4 11.6 %copy-start.34 = (s32[1,8]{1,0:T(1,128)S(1)}, s32[1,8]{1,0:T(1,128)}, u32[]{:S(2)}) copy-start(s32[1,8]{1,0:T(1,128)} %param.12) | copy-start | bytes 100
  9.4 11.7 %copy-start.24 = (f32[4352]{0:T(1024)S(1)}, f32[4352]{0:T(1024)}, u32[]{:S(2)}) copy-start(f32[4352]{0:T(1024)} %param.17) | copy-start | bytes 52228
  9.4 12.3 %copy-start = (bf16[512,2048]{1,0:T(8,128)(2,1)S(1)}, bf16[512,2048]{1,0:T(8,128)(2,1)}, u32[]{:S(2)}) copy-start(bf16[512,2048]{1,0:T(8,128)(2,1)} %x_ref.3) | copy-start | bytes 6291460
  9.4 31.1 %collective-permute-start = (bf16[256,1024]{1,0:T(8,128)(2,1)S(1)}, bf16[256,1024]{1,0:T(8,128)(2,1)S(1)}, u32[]{:S(2)}, u32[]{:S(2)}) collective-permute-start(bf16[256,1024]{1,0:T(8,128)(2,1)S(1)} %slice.162.refs_0_.refs_11_), channel_id=1, source_target_pairs={{0,4},{4,0},{8,12},{12,8},{16,20},{20,16},{24,28},{28,24},{1,5},{5... | collective-permute-start | bytes 1572872 | tf_op jit(solution)/shard_map/ppermute | solution.py:50
  9.9 21.1 %collective-permute-start.1 = (bf16[256,1024]{1,0:T(8,128)(2,1)S(1)}, bf16[256,1024]{1,0:T(8,128)(2,1)}, u32[]{:S(2)}, u32[]{:S(2)}) collective-permute-start(bf16[256,1024]{1,0:T(8,128)(2,1)S(1)} %slice.162.refs_0_.refs_11_), channel_id=1, source_target_pairs={{0,8},{4,12},{8,0},{12,4},{16,24},{20,28},{24,16},{28,20},{1,9},{5... | collective-permute-start | bytes 1572872 | tf_op jit(solution)/shard_map/ppermute | solution.py:50
  12.5 25.1 %collective-permute-start.3 = (bf16[256,1024]{1,0:T(8,128)(2,1)S(1)}, bf16[256,1024]{1,0:T(8,128)(2,1)}, u32[]{:S(2)}, u32[]{:S(2)}) collective-permute-start(bf16[256,1024]{1,0:T(8,128)(2,1)S(1)} %slice.162.refs_0_.refs_11_), channel_id=1, source_target_pairs={{0,16},{4,20},{8,24},{12,28},{16,0},{20,4},{24,8},{28,12},{1,17},{... | collective-permute-start | bytes 1572872 | tf_op jit(solution)/shard_map/ppermute | solution.py:50
  14.0 24.1 %collective-permute-start.5 = (bf16[256,1024]{1,0:T(8,128)(2,1)S(1)}, bf16[256,1024]{1,0:T(8,128)(2,1)}, u32[]{:S(2)}, u32[]{:S(2)}) collective-permute-start(bf16[256,1024]{1,0:T(8,128)(2,1)S(1)} %slice.162.refs_0_.refs_11_), channel_id=1, source_target_pairs={{0,24},{4,28},{8,16},{12,20},{16,8},{20,12},{24,0},{28,4},{1,25},{... | collective-permute-start | bytes 1572872 | tf_op jit(solution)/shard_map/ppermute | solution.py:50
  18.9 39.5 %copy-start.8 = (bf16[256,512]{1,0:T(8,128)(2,1)}, bf16[256,512]{1,0:T(8,128)(2,1)S(1)}, u32[]{:S(2)}) copy-start(bf16[256,512]{1,0:T(8,128)(2,1)S(1)} %slice.118.refs_0_) | copy-start | bytes 786436
  19.0 33.9 %collective-permute-start.7 = (bf16[256,512]{1,0:T(8,128)(2,1)S(1)}, bf16[256,512]{1,0:T(8,128)(2,1)}, u32[]{:S(2)}, u32[]{:S(2)}) collective-permute-start(bf16[256,512]{1,0:T(8,128)(2,1)S(1)} %slice.118.refs_0_), channel_id=1, source_target_pairs={{0,8},{4,12},{8,0},{12,4},{16,24},{20,28},{24,16},{28,20},{1,9},{5... | collective-permute-start | bytes 786440 | tf_op jit(solution)/shard_map/ppermute | solution.py:50
  31.0 11.3 %collective-permute-start.2 = (bf16[256,1024]{1,0:T(8,128)(2,1)}, bf16[256,1024]{1,0:T(8,128)(2,1)S(1)}, u32[]{:S(2)}, u32[]{:S(2)}) collective-permute-start(bf16[256,1024]{1,0:T(8,128)(2,1)} %collective-permute-done.1.refs_2_.refs_13_), channel_id=1, source_target_pairs={{0,4},{4,0},{8,12},{12,8},{16,20},{20,16},{24,28},{28,24},{1,5},{5... | collective-permute-start | bytes 1572872 | tf_op jit(solution)/shard_map/ppermute | solution.py:50
  37.6 5.9 %collective-permute-start.4 = (bf16[256,1024]{1,0:T(8,128)(2,1)}, bf16[256,1024]{1,0:T(8,128)(2,1)S(1)}, u32[]{:S(2)}, u32[]{:S(2)}) collective-permute-start(bf16[256,1024]{1,0:T(8,128)(2,1)} %collective-permute-done.3.refs_4_.refs_15_), channel_id=1, source_target_pairs={{0,4},{4,0},{8,12},{12,8},{16,20},{20,16},{24,28},{28,24},{1,5},{5... | collective-permute-start | bytes 1572872 | tf_op jit(solution)/shard_map/ppermute | solution.py:50
  38.1 5.4 %collective-permute-start.6 = (bf16[256,1024]{1,0:T(8,128)(2,1)}, bf16[256,1024]{1,0:T(8,128)(2,1)S(1)}, u32[]{:S(2)}, u32[]{:S(2)}) collective-permute-start(bf16[256,1024]{1,0:T(8,128)(2,1)} %collective-permute-done.5.refs_6_.refs_17_), channel_id=1, source_target_pairs={{0,4},{4,0},{8,12},{12,8},{16,20},{20,16},{24,28},{28,24},{1,5},{5... | collective-permute-start | bytes 1572872 | tf_op jit(solution)/shard_map/ppermute | solution.py:50
  40.5 14.5 %collective-permute-start.8 = (bf16[256,512]{1,0:T(8,128)(2,1)S(1)}, bf16[256,512]{1,0:T(8,128)(2,1)}, u32[]{:S(2)}, u32[]{:S(2)}) collective-permute-start(bf16[256,512]{1,0:T(8,128)(2,1)S(1)} %slice.118.refs_0_), channel_id=1, source_target_pairs={{0,16},{4,20},{8,24},{12,28},{16,0},{20,4},{24,8},{28,12},{1,17},{... | collective-permute-start | bytes 786440 | tf_op jit(solution)/shard_map/ppermute | solution.py:50
  42.3 12.6 %collective-permute-start.9 = (bf16[256,512]{1,0:T(8,128)(2,1)S(1)}, bf16[256,512]{1,0:T(8,128)(2,1)}, u32[]{:S(2)}, u32[]{:S(2)}) collective-permute-start(bf16[256,512]{1,0:T(8,128)(2,1)S(1)} %slice.118.refs_0_), channel_id=1, source_target_pairs={{0,24},{4,28},{8,16},{12,20},{16,8},{20,12},{24,0},{28,4},{1,25},{... | collective-permute-start | bytes 786440 | tf_op jit(solution)/shard_map/ppermute | solution.py:50
  44.5 37.4 %copy-start.2 = (bf16[256,6144]{1,0:T(8,128)(2,1)S(1)}, bf16[256,6144]{1,0:T(8,128)(2,1)}, u32[]{:S(2)}) copy-start(bf16[256,6144]{1,0:T(8,128)(2,1)} %copy-done.1) | copy-start | bytes 9437188
  55.0 15.0 %collective-permute-start.15 = (bf16[512,512]{1,0:T(8,128)(2,1)}, bf16[512,512]{1,0:T(8,128)(2,1)S(1)}, u32[]{:S(2)}, u32[]{:S(2)}) collective-permute-start(bf16[512,512]{1,0:T(8,128)(2,1)} %get-tuple-element.103.refs_0_), channel_id=1, source_target_pairs={{0,8},{4,12},{8,0},{12,4},{16,24},{20,28},{24,16},{28,20},{1,9},{5... | collective-permute-start | bytes 1572872 | tf_op jit(solution)/shard_map/ppermute | solution.py:50
  56.4 24.8 %collective-permute-start.17 = (bf16[512,512]{1,0:T(8,128)(2,1)}, bf16[512,512]{1,0:T(8,128)(2,1)}, u32[]{:S(2)}, u32[]{:S(2)}) collective-permute-start(bf16[512,512]{1,0:T(8,128)(2,1)} %get-tuple-element.103.refs_0_), channel_id=1, source_target_pairs={{0,16},{4,20},{8,24},{12,28},{16,0},{20,4},{24,8},{28,12},{1,17},{... | collective-permute-start | bytes 1572872 | tf_op jit(solution)/shard_map/ppermute | solution.py:50
  57.0 24.3 %collective-permute-start.19 = (bf16[512,512]{1,0:T(8,128)(2,1)}, bf16[512,512]{1,0:T(8,128)(2,1)}, u32[]{:S(2)}, u32[]{:S(2)}) collective-permute-start(bf16[512,512]{1,0:T(8,128)(2,1)} %get-tuple-element.103.refs_0_), channel_id=1, source_target_pairs={{0,24},{4,28},{8,16},{12,20},{16,8},{20,12},{24,0},{28,4},{1,25},{... | collective-permute-start | bytes 1572872 | tf_op jit(solution)/shard_map/ppermute | solution.py:50
  58.5 1.9 collective-permute-start.10
  58.5 2.1 collective-permute-start.11
  60.4 9.7 %copy-start.21 = (bf16[256,512]{1,0:T(8,128)(2,1)}, bf16[256,512]{1,0:T(8,128)(2,1)S(1)}, u32[]{:S(2)}) copy-start(bf16[256,512]{1,0:T(8,128)(2,1)S(1)} %collective-permute-done.10.refs_1_) | copy-start | bytes 786436
  60.4 24.3 %collective-permute-start.14 = (bf16[512,512]{1,0:T(8,128)(2,1)}, bf16[512,512]{1,0:T(8,128)(2,1)}, u32[]{:S(2)}, u32[]{:S(2)}) collective-permute-start(bf16[512,512]{1,0:T(8,128)(2,1)} %get-tuple-element.103.refs_0_), channel_id=1, source_target_pairs={{0,4},{4,0},{8,12},{12,8},{16,20},{20,16},{24,28},{28,24},{1,5},{5... | collective-permute-start | bytes 1572872 | tf_op jit(solution)/shard_map/ppermute | solution.py:50
  60.6 21.2 %collective-permute-start.12 = (bf16[256,512]{1,0:T(8,128)(2,1)}, bf16[256,512]{1,0:T(8,128)(2,1)S(1)}, u32[]{:S(2)}, u32[]{:S(2)}) collective-permute-start(bf16[256,512]{1,0:T(8,128)(2,1)} %collective-permute-done.8.refs_4_), channel_id=1, source_target_pairs={{0,4},{4,0},{8,12},{12,8},{16,20},{20,16},{24,28},{28,24},{1,5},{5... | collective-permute-start | bytes 786440 | tf_op jit(solution)/shard_map/ppermute | solution.py:50
  70.0 13.4 %copy-start.13 = (bf16[512,512]{1,0:T(8,128)(2,1)}, bf16[512,512]{1,0:T(8,128)(2,1)S(1)}, u32[]{:S(2)}) copy-start(bf16[512,512]{1,0:T(8,128)(2,1)S(1)} %collective-permute-done.15.refs_2_) | copy-start | bytes 1572868
  70.0 14.6 %collective-permute-start.16 = (bf16[512,512]{1,0:T(8,128)(2,1)S(1)}, bf16[512,512]{1,0:T(8,128)(2,1)}, u32[]{:S(2)}, u32[]{:S(2)}) collective-permute-start(bf16[512,512]{1,0:T(8,128)(2,1)S(1)} %collective-permute-done.15.refs_2_), channel_id=1, source_target_pairs={{0,4},{4,0},{8,12},{12,8},{16,20},{20,16},{24,28},{28,24},{1,5},{5... | collective-permute-start | bytes 1572872 | tf_op jit(solution)/shard_map/ppermute | solution.py:50
  81.3 3.4 collective-permute-start.18
  81.3 3.4 collective-permute-start.20
  81.8 2.9 collective-permute-start.13
  84.7 106.6 %all-reduce.4.cloned.1.call-start = ((), (), s32[]{:S(2)}) async-start(), calls=%async_computation.2 | async-start | bytes 4194304 | tf_op jit(solution)/shard_map/psum | solution.py:730
  102.6 202.3 %all-reduce.6.cloned.1.call-start = ((), (), s32[]{:S(2)}) async-start(), calls=%async_computation.4 | async-start | bytes 4194304 | tf_op jit(solution)/shard_map/psum | solution.py:786
  218.9 141.9 %reduce-scatter.3.cloned.1.call-start = ((), (), s32[]{:S(2)}) async-start(), calls=%async_computation.5 | async-start | bytes 21233664 | tf_op jit(solution)/shard_map/reduce_scatter | solution.py:809
  234.5 158.3 %all-reduce.8.cloned.1.call-start = ((), (), s32[]{:S(2)}) async-start(), calls=%async_computation.6 | async-start | bytes 4194304 | tf_op jit(solution)/shard_map/psum | solution.py:811
  305.0 150.9 %reduce-scatter.5.cloned.1.call-start = ((), (), s32[]{:S(2)}) async-start(), calls=%async_computation.7 | async-start | bytes 2621440 | tf_op jit(solution)/shard_map/reduce_scatter | solution.py:932
  331.4 13.5 %collective-permute-start.21 = (bf16[512,512]{1,0:T(8,128)(2,1)}, bf16[512,512]{1,0:T(8,128)(2,1)S(1)}, u32[]{:S(2)}, u32[]{:S(2)}) collective-permute-start(bf16[512,512]{1,0:T(8,128)(2,1)} %get-tuple-element.136), channel_id=1, source_target_pairs={{0,4},{4,0},{8,12},{12,8},{16,20},{20,16},{24,28},{28,24},{1,5},{5... | collective-permute-start | bytes 1572872 | tf_op jit(solution)/shard_map/ppermute | solution.py:50
  332.0 13.9 %collective-permute-start.22 = (bf16[512,512]{1,0:T(8,128)(2,1)}, bf16[512,512]{1,0:T(8,128)(2,1)S(1)}, u32[]{:S(2)}, u32[]{:S(2)}) collective-permute-start(bf16[512,512]{1,0:T(8,128)(2,1)} %get-tuple-element.138), channel_id=1, source_target_pairs={{0,4},{4,0},{8,12},{12,8},{16,20},{20,16},{24,28},{28,24},{1,5},{5... | collective-permute-start | bytes 1572872 | tf_op jit(solution)/shard_map/ppermute | solution.py:50
  333.0 13.1 %collective-permute-start.23 = (bf16[512,512]{1,0:T(8,128)(2,1)}, bf16[512,512]{1,0:T(8,128)(2,1)S(1)}, u32[]{:S(2)}, u32[]{:S(2)}) collective-permute-start(bf16[512,512]{1,0:T(8,128)(2,1)} %get-tuple-element.140), channel_id=1, source_target_pairs={{0,4},{4,0},{8,12},{12,8},{16,20},{20,16},{24,28},{28,24},{1,5},{5... | collective-permute-start | bytes 1572872 | tf_op jit(solution)/shard_map/ppermute | solution.py:50
  333.4 12.8 %collective-permute-start.24 = (bf16[512,512]{1,0:T(8,128)(2,1)}, bf16[512,512]{1,0:T(8,128)(2,1)S(1)}, u32[]{:S(2)}, u32[]{:S(2)}) collective-permute-start(bf16[512,512]{1,0:T(8,128)(2,1)} %get-tuple-element.142), channel_id=1, source_target_pairs={{0,4},{4,0},{8,12},{12,8},{16,20},{20,16},{24,28},{28,24},{1,5},{5... | collective-permute-start | bytes 1572872 | tf_op jit(solution)/shard_map/ppermute | solution.py:50
  360.8 36.9 %collective-permute-start.25 = (bf16[512,512]{1,0:T(8,128)(2,1)S(1)}, bf16[512,512]{1,0:T(8,128)(2,1)S(1)}, u32[]{:S(2)}, u32[]{:S(2)}) collective-permute-start(bf16[512,512]{1,0:T(8,128)(2,1)S(1)} %add_convert_fusion.5), channel_id=1, source_target_pairs={{0,8},{4,12},{8,0},{12,4},{16,24},{20,28},{24,16},{28,20},{1,9},{5... | collective-permute-start | bytes 1572872 | tf_op jit(solution)/shard_map/ppermute | solution.py:50
  362.1 35.6 %collective-permute-start.26 = (bf16[512,512]{1,0:T(8,128)(2,1)S(1)}, bf16[512,512]{1,0:T(8,128)(2,1)S(1)}, u32[]{:S(2)}, u32[]{:S(2)}) collective-permute-start(bf16[512,512]{1,0:T(8,128)(2,1)S(1)} %add_convert_fusion.4), channel_id=1, source_target_pairs={{0,16},{4,20},{8,24},{12,28},{16,0},{20,4},{24,8},{28,12},{1,17},{... | collective-permute-start | bytes 1572872 | tf_op jit(solution)/shard_map/ppermute | solution.py:50
  362.8 34.9 %collective-permute-start.27 = (bf16[512,512]{1,0:T(8,128)(2,1)S(1)}, bf16[512,512]{1,0:T(8,128)(2,1)S(1)}, u32[]{:S(2)}, u32[]{:S(2)}) collective-permute-start(bf16[512,512]{1,0:T(8,128)(2,1)S(1)} %add_convert_fusion.3), channel_id=1, source_target_pairs={{0,24},{4,28},{8,16},{12,20},{16,8},{20,12},{24,0},{28,4},{1,25},{... | collective-permute-start | bytes 1572872 | tf_op jit(solution)/shard_map/ppermute | solution.py:50
  407.9 93.4 %all-gather.5.cloned.1.call-start = ((), (), s32[]{:S(2)}) async-start(), calls=%async_computation.8 | async-start | bytes 2621440 | tf_op jit(solution)/shard_map/all_gather | solution.py:936
  408.2 6.8 %collective-permute-start.28 = (bf16[4,256,512]{2,1,0:T(8,128)(2,1)}, bf16[4,256,512]{2,1,0:T(8,128)(2,1)S(1)}, u32[]{:S(2)}, u32[]{:S(2)}) collective-permute-start(bf16[4,256,512]{2,1,0:T(8,128)(2,1)} %bitcast.70), channel_id=1, source_target_pairs={{0,4},{4,0},{8,12},{12,8},{16,20},{20,16},{24,28},{28,24},{1,5},{5... | collective-permute-start | bytes 3145736 | tf_op jit(solution)/shard_map/ppermute | solution.py:50
  412.6 6.3 %collective-permute-start.32 = (bf16[4,256,512]{2,1,0:T(8,128)(2,1)}, bf16[4,256,512]{2,1,0:T(8,128)(2,1)S(1)}, u32[]{:S(2)}, u32[]{:S(2)}) collective-permute-start(bf16[4,256,512]{2,1,0:T(8,128)(2,1)} %bitcast.71), channel_id=1, source_target_pairs={{0,4},{4,0},{8,12},{12,8},{16,20},{20,16},{24,28},{28,24},{1,5},{5... | collective-permute-start | bytes 3145736 | tf_op jit(solution)/shard_map/ppermute | solution.py:50
  414.7 7.0 %collective-permute-start.36 = (bf16[4,256,512]{2,1,0:T(8,128)(2,1)S(1)}, bf16[4,256,512]{2,1,0:T(8,128)(2,1)S(1)}, u32[]{:S(2)}, u32[]{:S(2)}) collective-permute-start(bf16[4,256,512]{2,1,0:T(8,128)(2,1)S(1)} %copy-done.33), channel_id=1, source_target_pairs={{0,4},{4,0},{8,12},{12,8},{16,20},{20,16},{24,28},{28,24},{1,5},{5... | collective-permute-start | bytes 3145736 | tf_op jit(solution)/shard_map/ppermute | solution.py:50
  415.3 10.1 %collective-permute-start.31 = (bf16[256,512]{1,0:T(8,128)(2,1)S(1)}, bf16[256,512]{1,0:T(8,128)(2,1)S(1)}, u32[]{:S(2)}, u32[]{:S(2)}) collective-permute-start(bf16[256,512]{1,0:T(8,128)(2,1)S(1)} %get-tuple-element.197), channel_id=1, source_target_pairs={{0,24},{4,28},{8,16},{12,20},{16,8},{20,12},{24,0},{28,4},{1,25},{... | collective-permute-start | bytes 786440 | tf_op jit(solution)/shard_map/ppermute | solution.py:50
  417.8 13.4 %collective-permute-start.30 = (bf16[256,512]{1,0:T(8,128)(2,1)S(1)}, bf16[256,512]{1,0:T(8,128)(2,1)S(1)}, u32[]{:S(2)}, u32[]{:S(2)}) collective-permute-start(bf16[256,512]{1,0:T(8,128)(2,1)S(1)} %get-tuple-element.198), channel_id=1, source_target_pairs={{0,16},{4,20},{8,24},{12,28},{16,0},{20,4},{24,8},{28,12},{1,17},{... | collective-permute-start | bytes 786440 | tf_op jit(solution)/shard_map/ppermute | solution.py:50
  418.3 15.2 %collective-permute-start.29 = (bf16[256,512]{1,0:T(8,128)(2,1)S(1)}, bf16[256,512]{1,0:T(8,128)(2,1)S(1)}, u32[]{:S(2)}, u32[]{:S(2)}) collective-permute-start(bf16[256,512]{1,0:T(8,128)(2,1)S(1)} %get-tuple-element.196), channel_id=1, source_target_pairs={{0,8},{4,12},{8,0},{12,4},{16,24},{20,28},{24,16},{28,20},{1,9},{5... | collective-permute-start | bytes 786440 | tf_op jit(solution)/shard_map/ppermute | solution.py:50
  419.3 17.5 %collective-permute-start.35 = (bf16[256,512]{1,0:T(8,128)(2,1)S(1)}, bf16[256,512]{1,0:T(8,128)(2,1)S(1)}, u32[]{:S(2)}, u32[]{:S(2)}) collective-permute-start(bf16[256,512]{1,0:T(8,128)(2,1)S(1)} %get-tuple-element.194), channel_id=1, source_target_pairs={{0,24},{4,28},{8,16},{12,20},{16,8},{20,12},{24,0},{28,4},{1,25},{... | collective-permute-start | bytes 786440 | tf_op jit(solution)/shard_map/ppermute | solution.py:50
  421.7 20.6 %collective-permute-start.34 = (bf16[256,512]{1,0:T(8,128)(2,1)S(1)}, bf16[256,512]{1,0:T(8,128)(2,1)S(1)}, u32[]{:S(2)}, u32[]{:S(2)}) collective-permute-start(bf16[256,512]{1,0:T(8,128)(2,1)S(1)} %get-tuple-element.195), channel_id=1, source_target_pairs={{0,16},{4,20},{8,24},{12,28},{16,0},{20,4},{24,8},{28,12},{1,17},{... | collective-permute-start | bytes 786440 | tf_op jit(solution)/shard_map/ppermute | solution.py:50
  425.5 16.9 %collective-permute-start.33 = (bf16[256,512]{1,0:T(8,128)(2,1)S(1)}, bf16[256,512]{1,0:T(8,128)(2,1)S(1)}, u32[]{:S(2)}, u32[]{:S(2)}) collective-permute-start(bf16[256,512]{1,0:T(8,128)(2,1)S(1)} %get-tuple-element.193), channel_id=1, source_target_pairs={{0,8},{4,12},{8,0},{12,4},{16,24},{20,28},{24,16},{28,20},{1,9},{5... | collective-permute-start | bytes 786440 | tf_op jit(solution)/shard_map/ppermute | solution.py:50
  431.1 16.9 %collective-permute-start.39 = (bf16[256,512]{1,0:T(8,128)(2,1)S(1)}, bf16[256,512]{1,0:T(8,128)(2,1)S(1)}, u32[]{:S(2)}, u32[]{:S(2)}) collective-permute-start(bf16[256,512]{1,0:T(8,128)(2,1)S(1)} %get-tuple-element.191), channel_id=1, source_target_pairs={{0,24},{4,28},{8,16},{12,20},{16,8},{20,12},{24,0},{28,4},{1,25},{... | collective-permute-start | bytes 786440 | tf_op jit(solution)/shard_map/ppermute | solution.py:50
  433.5 19.4 %collective-permute-start.38 = (bf16[256,512]{1,0:T(8,128)(2,1)S(1)}, bf16[256,512]{1,0:T(8,128)(2,1)S(1)}, u32[]{:S(2)}, u32[]{:S(2)}) collective-permute-start(bf16[256,512]{1,0:T(8,128)(2,1)S(1)} %get-tuple-element.192), channel_id=1, source_target_pairs={{0,16},{4,20},{8,24},{12,28},{16,0},{20,4},{24,8},{28,12},{1,17},{... | collective-permute-start | bytes 786440 | tf_op jit(solution)/shard_map/ppermute | solution.py:50
  436.8 19.1 %copy-start.30 = (f32[8,128]{1,0:T(8,128)S(1)}, f32[8,128]{1,0:T(8,128)}, u32[]{:S(2)}) copy-start(f32[8,128]{1,0:T(8,128)} %get-tuple-element.174) | copy-start | bytes 12292
  436.8 19.2 %copy-start.29 = (f32[1,2048]{1,0:T(1,128)S(1)}, f32[1,2048]{1,0:T(1,128)}, u32[]{:S(2)}) copy-start(f32[1,2048]{1,0:T(1,128)} %get-tuple-element.172) | copy-start | bytes 24580
  436.8 19.2 %copy-start.28 = (f32[1,2048]{1,0:T(1,128)S(1)}, f32[1,2048]{1,0:T(1,128)}, u32[]{:S(2)}) copy-start(f32[1,2048]{1,0:T(1,128)} %get-tuple-element.173) | copy-start | bytes 24580
  436.8 16.3 %collective-permute-start.37 = (bf16[256,512]{1,0:T(8,128)(2,1)S(1)}, bf16[256,512]{1,0:T(8,128)(2,1)S(1)}, u32[]{:S(2)}, u32[]{:S(2)}) collective-permute-start(bf16[256,512]{1,0:T(8,128)(2,1)S(1)} %get-tuple-element.190), channel_id=1, source_target_pairs={{0,8},{4,12},{8,0},{12,4},{16,24},{20,28},{24,16},{28,20},{1,9},{5... | collective-permute-start | bytes 786440 | tf_op jit(solution)/shard_map/ppermute | solution.py:50
  456.7 1.2 collective-permute-start.40
  457.9 3.8 collective-permute-start.41
  461.6 3.8 collective-permute-start.42
  465.4 4.9 collective-permute-start.43
  470.4 5.2 %collective-permute-start.44 = (f32[4480]{0:T(1024)S(1)}, f32[4480]{0:T(1024)S(1)}, u32[]{:S(2)}, u32[]{:S(2)}) collective-permute-start(f32[4480]{0:T(1024)S(1)} %add.194), channel_id=1, source_target_pairs={{0,2},{1,3},{2,0},{3,1},{4,6},{5,7},{6,4},{7,5},{8,10},{9,11},{10,... | collective-permute-start | bytes 53768 | tf_op jit(solution)/shard_map/ppermute | solution.py:50
  478.1 13.6 %copy-start.26 = (f32[4352]{0:T(1024)S(1)}, f32[4352]{0:T(1024)}, u32[]{:S(2)}) copy-start(f32[4352]{0:T(1024)} %param.19) | copy-start | bytes 52228
  478.1 13.6 %copy-start.27 = (f32[4352]{0:T(1024)S(1)}, f32[4352]{0:T(1024)}, u32[]{:S(2)}) copy-start(f32[4352]{0:T(1024)} %param.18) | copy-start | bytes 52228
  (23 other events, 69.9 us)
Sparse Core Ops, SparseCore 0:
  84.8 98.0 all-gather.2
  234.6 126.1 reduce-scatter.2
Sparse Core Ops, SparseCore 1:
  102.7 88.4 all-reduce.3
  219.0 85.9 all-reduce.5
  307.8 85.0 all-reduce.7
  407.9 42.5 reduce-scatter.4
  455.9 45.3 all-gather.4

commit v6 on v5

--- a/solution.py
+++ b/solution.py
@@ -240,6 +240,14 @@
             at = pl.multiple_of(first + b * block, block)
             term = dot(low_ref[...], w_ref[b * block : (b + 1) * block], last_dims)
             o_ref[:, pl.ds(at, block)] = term.astype(bf16)
+
+
+def output_first_kernel(y_ref, s_ref, o_ref):
+    o_ref[...] = (y_ref[...] + s_ref[...].astype(f32)).astype(bf16)
+
+
+def output_rest_kernel(y_ref, s_ref, made_ref, o_ref):
+    o_ref[...] = (y_ref[...] + s_ref[...].astype(f32)).astype(bf16)
 
 
 def plain_kernel(a_ref, w_ref, o_ref):
@@ -897,7 +905,17 @@
         whole = made[0].reshape(model_width, -1)
         return lax.psum_scatter(whole, "dp", scatter_dimension=0, tiled=True)
 
-    block_output = (residual + mlp_sum.astype(f32)).astype(bf16)
+    first_spec = pl.BlockSpec((tok_count // 8, model_width), lambda n: (0, 0))
+    block_output = pl.pallas_call(
+        output_first_kernel,
+        grid=(1,),
+        in_specs=[first_spec, first_spec],
+        out_specs=first_spec,
+        out_shape=low_shape,
+        compiler_params=params(),
+        cost_estimate=cost(6),
+        name="output_first",
+    )(residual, mlp_sum)
     terms, block_output, dw_query, dw_out = lax.optimization_barrier((terms, block_output, dw_query, dw_out))
     query_grads, out_grads = scattered(dw_query), scattered(dw_out)
     grad_kv_low, key_gain_grad, attn_gain_grad, grad_norm_part = pl.pallas_call(
@@ -930,9 +948,22 @@
     [dw_kv] = weight_grad(me_array, normed_turned, [grad_kv_low], parts, row_count, True)
 
     grad_norm_share = lax.psum_scatter(grad_norm_part, "mp", scatter_dimension=0, tiled=True)
+    mlp_sum, block_output, keys_done = lax.optimization_barrier((mlp_sum, block_output, grad_kv_low))
+    rest_spec = pl.BlockSpec((tok_count // 8, model_width), lambda n: (n + 1, 0))
+    block_output = pl.pallas_call(
+        output_rest_kernel,
+        grid=(7,),
+        in_specs=[rest_spec, rest_spec, anywhere],
+        out_specs=rest_spec,
+        out_shape=low_shape,
+        input_output_aliases={2: 0},
+        compiler_params=params(),
+        cost_estimate=cost(5),
+        name="output_rest",
+    )(residual, mlp_sum, block_output)
     weight_grads = [query_grads, scattered(dw_kv), out_grads, mlp_grads]
     square = sum(jnp.sum(jnp.square(grad.astype(f32))) for grad in weight_grads)
-    square, grad_norm_share = lax.optimization_barrier((square, grad_norm_share))
+    square, grad_norm_share, block_output = lax.optimization_barrier((square, grad_norm_share, block_output))
     grad_norm_sum = lax.all_gather(grad_norm_share, "mp", axis=0, tiled=True)
     local = [attn_gain_grad[0], mlp_gain_grad[0], query_gain_grad, key_gain_grad[0]]
     totals = sum_all(jnp.concatenate([jnp.broadcast_to(square, (HD,))] + local))

time: 517 us -> 521 us (level)
  Pallas kernels: 161 us -> 167 us
    pallas_call x0 -> x2, Pallas kernels: none -> 7.83 us  [the longest x1 5.98 us: per_device(): pl.pallas_call(output_rest_kernel, grid=(7,), in_specs=[rest_spec, rest_s...]
  transfers between devices with their start and end apart: 52 -> 52, of which waited for: 25 -> 26; matrix products, arithmetic and copies ran while one was open for 6% -> 5% of each run, Pallas kernels for 23% -> 24%
where the time goes in v6:
time: 521 us; the launch traced here: 520 us
  waiting for transfers between devices  264 us (51%)
  Pallas kernels  167 us (32%)
  starting transfers between devices  36.6 us (7%)
  between operations  21.3 us (4%)
  other arithmetic  20.1 us (4%)
  local copies, waits for them, and re-layouts  10.9 us (2%)
    all_gather x1, waiting for transfers between devices, per_device(): mlp_weights = lax.all_gather(mlp_own, 'dp', axis=0, tiled=True)  81 us
    ppermute x45, waiting for transfers between devices, swap(): return lax.ppermute(array, axis, [(i, i ^ distance) for i in range(count)])  67.9 us
    psum x1, waiting for transfers between devices, per_device(): grad_mlp_sum = lax.psum(grad_mlp_part, 'mp')  61.7 us
    ppermute x45, starting transfers between devices, swap(): return lax.ppermute(array, axis, [(i, i ^ distance) for i in range(count)])  35.8 us
    psum x1, waiting for transfers between devices, per_device(): mlp_sum = lax.psum(mlp_part, 'mp')  28.5 us
    pallas_call x1, Pallas kernels, per_device(): pl.pallas_call(mlp_kernel, grid=(tiles,), in_specs=[rows_all, rows_all, g...  16.2 us
    pallas_call x1, Pallas kernels, per_device(): pl.pallas_call(functools.partial(attend_back_kernel, group, heads, parts,...  16.2 us
    pallas_call x1, Pallas kernels, per_device(): pl.pallas_call(mlp_weight_grad_kernel, grid=(model_width // TILE,), in_sp...  15.5 us
  transfers between devices with their start and end apart: 52, of which 26 were waited for; matrix products, arithmetic and copies ran while one was open for 5% of the time, Pallas kernels for 24%

profile of v6, /device:TPU:0, one launch (start us, length us, event | category | flops | bytes accessed | tf_op | source)
XLA Modules:
  0.0 520.0 jit_solution(11609003262252232777)
XLA Ops:
  9.9 2.6 collective-permute-start.1
  12.5 1.5 collective-permute-start.3
  14.0 3.2 convert.12
  17.3 1.7 copy-done.1
  19.0 2.0 collective-permute-start.7
  22.9 1.9 fusion.2.x_ref.h_ref
  24.9 6.0 %transposed.1.lhs_ref = bf16[2048,512]{1,0:T(8,128)(2,1)} custom-call(s32[1]{0:T(128)} %bitcast.1.me_ref, bf16[512,2048]{1,0:T(8,128)(2,1)} %fusion.2.x_ref.h_ref), custom_call_target="tpu_custom_call" | custom-call | flops 5000000000 | bytes 17000000 | tf_op jit(solution)/shard_map/transposed/pallas_call | solution.py:448
  30.9 6.7 %collective-permute-done.3.refs_4_.refs_15_ = bf16[256,1024]{1,0:T(8,128)(2,1)} collective-permute-done((bf16[256,1024]{1,0:T(8,128)(2,1)S(1)}, bf16[256,1024]{1,0:T(8,128)(2,1)}, u32[]{:S(2)}, u32[]{:S(2)}) %collective-permute-start.3) | collective-permute-done | bytes 524320 | tf_op jit(solution)/shard_map/ppermute | solution.py:50
  38.7 1.8 fusion.13
  40.5 1.8 collective-permute-start.8
  44.4 8.4 %project.1 = (bf16[512,512]{1,0:T(8,128)(2,1)}, bf16[512,512]{1,0:T(8,128)(2,1)}, f32[512,768]{1,0:T(8,128)}) custom-call(s32[1]{0:T(128)} %bitcast.1.me_ref, bf16[512,2048]{1,0:T(8,128)(2,1)} %fusion.2.x_ref.h_ref, bf16[256,1024]{1,0:T(8,128)(2,1)} %copy-done.4, bf16[256,1024]{1,0:T(8,128)(2,1)} %collective-permute-done.refs_1_.refs_12_, ...), custom_call_target="tpu_custom_call" | custom-call | flops 6000000000 | bytes 20400000 | tf_op jit(solution)/shard_map/project/pallas_call | solution.py:659
  52.8 2.1 collective-permute-done.8.refs_4_
  54.9 1.4 collective-permute-start.15
  56.9 1.5 collective-permute-start.19
  58.9 1.4 collective-permute-done.10.refs_1_
  60.8 9.2 %collective-permute-done.15.refs_2_ = bf16[512,512]{1,0:T(8,128)(2,1)S(1)} collective-permute-done((bf16[512,512]{1,0:T(8,128)(2,1)}, bf16[512,512]{1,0:T(8,128)(2,1)S(1)}, u32[]{:S(2)}, u32[]{:S(2)}) %collective-permute-start.15) | collective-permute-done | bytes 524320 | tf_op jit(solution)/shard_map/ppermute | solution.py:50
  70.0 11.2 %collective-permute-done.17.refs_4_ = bf16[512,512]{1,0:T(8,128)(2,1)} collective-permute-done((bf16[512,512]{1,0:T(8,128)(2,1)}, bf16[512,512]{1,0:T(8,128)(2,1)}, u32[]{:S(2)}, u32[]{:S(2)}) %collective-permute-start.17) | collective-permute-done | bytes 524320 | tf_op jit(solution)/shard_map/ppermute | solution.py:50
  81.8 1.6 slice.117
  85.4 11.8 %attend.1 = (f32[8,128,256]{2,1,0:T(8,128)}, bf16[512,512]{1,0:T(8,128)(2,1)}, f32[8,8,256]{2,1,0:T(8,128)}) custom-call(s32[4]{0:T(128)} %get-tuple-element.195.own_ref, s32[32]{0:T(128)} %fusion.14.inverse_ref, s32[8]{0:T(128)} %copy-done.30, bf16[512,512]{1,0:T(8,128)(2,1)} %get-tuple-element.98.q_ref, bf16[512,512]{1,0:T(8,128)(2,1)} %get-tuple-element.106.refs_0_, ...), custom_call_target="tpu_custom_call" | custom-call | flops 16000000000 | bytes 54400000 | tf_op jit(solution)/shard_map/attend/pallas_call | solution.py:702
  97.2 4.4 project_out.1
  101.9 81.0 %all-gather.3.cloned.1.call-done.w_ref.wg_ref.wu_ref = bf16[2048,4608]{1,0:T(8,128)(2,1)} async-done(((bf16[256,4608]{1,0:T(8,128)(2,1)}), bf16[2048,4608]{1,0:T(8,128)(2,1)}) %all-gather.3.cloned.1.call-update) | async-done | bytes 18874384 | tf_op jit(solution)/shard_map/all_gather | solution.py:692
  182.9 8.3 %grad_hidden.1.da_ref = bf16[512,1536]{1,0:T(8,128)(2,1)} custom-call(bf16[512,2048]{1,0:T(8,128)(2,1)} %c_ref.3, bf16[2048,4608]{1,0:T(8,128)(2,1)} %all-gather.3.cloned.1.call-done.w_ref.wg_ref.wu_ref), custom_call_target="tpu_custom_call" | custom-call | flops 30000001024 | bytes 102000000 | tf_op jit(solution)/shard_map/grad_hidden/pallas_call | solution.py:748
  192.0 16.2 %mlp.1 = (f32[512,2048]{1,0:T(8,128)}, bf16[512,2048]{1,0:T(8,128)(2,1)}, f32[512,1]{1,0:T(8,128)}, bf16[512,1536]{1,0:T(8,128)(2,1)}, bf16[512,1536]{1,0:T(8,128)(2,1)}, /*index=5*/bf16[512,1536]{1,0:T(8,128)(2,1)}) custom-call(bf16[512,2048]{1,0:T(8,128)(2,1)} %x_ref.3, bf16[512,2048]{1,0:T(8,128)(2,1)} %all-reduce.4.cloned.1.call-done.s_ref, ...), custom_call_target="tpu_custom_call" | custom-call | flops 17999998976 | bytes 61200000 | tf_op jit(solution)/shard_map/mlp/pallas_call | solution.py:758
  208.2 11.3 %mlp_back.1 = bf16[512,2048]{1,0:T(8,128)(2,1)} custom-call(bf16[512,1536]{1,0:T(8,128)(2,1)} %get-tuple-element.126.dg_ref, bf16[512,1536]{1,0:T(8,128)(2,1)} %get-tuple-element.127.du_ref, bf16[2048,4608]{1,0:T(8,128)(2,1)} %all-gather.3.cloned.1.call-done.w_ref.wg_ref.wu_ref, bf16[2048,4608]{1,0:T(8,128)(2,1)} %all-gather.3.cloned.1.call-done.w_ref.wg_ref.wu_ref), custom_call_target="tpu_custom_call" | custom-call | flops 11000000512 | bytes 37400000 | tf_op jit(solution)/shard_map/mlp_back/pallas_call | solution.py:778
  219.6 15.5 %mlp_weight_grad.1 = bf16[2048,4608]{1,0:T(8,128)(2,1)} custom-call(bf16[512,2048]{1,0:T(8,128)(2,1)} %get-tuple-element.132.h_ref, bf16[512,2048]{1,0:T(8,128)(2,1)} %c_ref.3, bf16[512,1536]{1,0:T(8,128)(2,1)} %get-tuple-element.126.dg_ref, bf16[512,1536]{1,0:T(8,128)(2,1)} %get-tuple-element.127.du_ref, bf16[512,1536]{1,0:T(8,128)(2,1)} %get-tuple-element.131.a_ref), custom_call_target="tpu_custom_call" | custom-call | flops 1000000000 | bytes 3400000 | tf_op jit(solution)/shard_map/mlp_weight_grad/pallas_call | solution.py:797
  235.2 7.9 %mlp_out.1 = bf16[512,2048]{1,0:T(8,128)(2,1)} custom-call(bf16[512,1536]{1,0:T(8,128)(2,1)} %get-tuple-element.131.a_ref, bf16[2048,4608]{1,0:T(8,128)(2,1)} %all-gather.3.cloned.1.call-done.w_ref.wg_ref.wu_ref), custom_call_target="tpu_custom_call" | custom-call | flops 1000000000 | bytes 3400000 | tf_op jit(solution)/shard_map/mlp_out/pallas_call | solution.py:807
  243.1 61.7 %all-reduce.6.cloned.1.call-done.s_ref = bf16[512,2048]{1,0:T(8,128)(2,1)} async-done(((bf16[512,2048]{1,0:T(8,128)(2,1)}), bf16[512,2048]{1,0:T(8,128)(2,1)}) %all-reduce.6.cloned.1.call-update) | async-done | bytes 2097168 | tf_op jit(solution)/shard_map/psum | solution.py:794
  305.5 8.7 %residual_back.1 = (f32[512,2048]{1,0:T(8,128)}, bf16[512,2048]{1,0:T(8,128)(2,1)}, bf16[512,512]{1,0:T(8,128)(2,1)}, f32[1,2048]{1,0:T(1,128)}) custom-call(s32[1]{0:T(128)} %bitcast.1.me_ref, f32[512,2048]{1,0:T(8,128)} %get-tuple-element.124.y_ref, f32[512,1]{1,0:T(8,128)} %get-tuple-element.125.scale_ref, bf16[512,2048]{1,0:T(8,128)(2,1)} %c_ref.3, ...), custom_call_target="tpu_custom_call" | custom-call | flops 1000000000 | bytes 3400000 | tf_op jit(solution)/shard_map/residual_back/pallas_call | solution.py:823
  314.2 16.2 %attend_back.1 = (bf16[512,512]{1,0:T(8,128)(2,1)}, f32[8,128]{1,0:T(8,128)}, bf16[512,512]{1,0:T(8,128)(2,1)}, bf16[512,512]{1,0:T(8,128)(2,1)}, bf16[512,512]{...) custom-call(s32[4]{0:T(128)} %get-tuple-element.195.own_ref, ...), custom_call_target="tpu_custom_call" | custom-call | flops 1000000000 | bytes 3400000 | tf_op jit(solution)/shard_map/attend_back/pallas_call | solution.py:851
  332.3 7.1 %weight_grad.1 = (bf16[4,256,512]{2,1,0:T(8,128)(2,1)}, bf16[4,256,512]{2,1,0:T(8,128)(2,1)}) custom-call(s32[1]{0:T(128)} %bitcast.1.me_ref, bf16[512,2048]{1,0:T(8,128)(2,1)} %get-tuple-element.155.lhs_ref, bf16[512,512]{1,0:T(8,128)(2,1)} %get-tuple-element.114.low_ref.refs_0_), custom_call_target="tpu_custom_call" | custom-call | flops 1000000000 | bytes 3400000 | tf_op jit(solution)/shard_map/weight_grad/pallas_call | solution.py:524
  339.4 4.3 weight_grad_turned.2
  345.3 15.3 %reduce-scatter.3.cloned.1.call-done.refs_3_ = bf16[256,4608]{1,0:T(8,128)(2,1)} async-done(((bf16[2048,4608]{1,0:T(8,128)(2,1)}), bf16[256,4608]{1,0:T(8,128)(2,1)}) %reduce-scatter.3.cloned.1.call-update) | async-done | bytes 2359312 | tf_op jit(solution)/shard_map/reduce_scatter | solution.py:817
  360.6 1.3 collective-permute-start.25
  362.6 1.5 collective-permute-start.27
  364.1 28.5 %all-reduce.8.cloned.1.call-done.s_ref = bf16[512,2048]{1,0:T(8,128)(2,1)} async-done(((bf16[512,2048]{1,0:T(8,128)(2,1)}), bf16[512,2048]{1,0:T(8,128)(2,1)}) %all-reduce.8.cloned.1.call-update) | async-done | bytes 2097168 | tf_op jit(solution)/shard_map/psum | solution.py:819
  392.6 1.9 output_first.1.made_ref
  395.7 9.0 %key_back.1 = (bf16[512,512]{1,0:T(8,128)(2,1)}, f32[8,128]{1,0:T(8,128)}, f32[1,2048]{1,0:T(1,128)}, bf16[512,2048]{1,0:T(8,128)(2,1)}) custom-call(s32[1]{0:T(128)} %bitcast.1.me_ref, bf16[512,512]{1,0:T(8,128)(2,1)} %add_convert_fusion.5.refs_0_, bf16[512,512]{1,0:T(8,128)(2,1)} %copy-done.17, bf16[512,512]{1,0:T(8,128)(2,1)} %copy-done.18, ...), custom_call_target="tpu_custom_call" | custom-call | flops 1000000000 | bytes 3400000 | tf_op jit(solution)/shard_map/key_back/pallas_call | solution.py:921
  405.1 4.4 weight_grad_turned.3
  409.7 1.8 multiply_reduce_fusion
  411.8 6.0 %output_rest.1 = bf16[512,2048]{1,0:T(8,128)(2,1)} custom-call(f32[512,2048]{1,0:T(8,128)} %get-tuple-element.124.y_ref, bf16[512,2048]{1,0:T(8,128)(2,1)} %all-reduce.8.cloned.1.call-done.s_ref, bf16[512,2048]{1,0:T(8,128)(2,1)} %output_first.1.made_ref), custom_call_target="tpu_custom_call", output_to_operand_aliasing={{}: (2, {})} | custom-call | flops 5000000000 | bytes 17000000 | tf_op jit(solution)/shard_map/output_rest/pallas_call | solution.py:953
  417.8 1.6 add_convert_fusion.1
  419.4 2.4 collective-permute-start.31
  423.3 2.4 collective-permute-start.35
  426.7 2.9 collective-permute-done.31
  429.6 1.5 collective-permute-start.33
  431.1 4.2 collective-permute-done.30
  435.2 2.4 collective-permute-start.39
  438.2 2.7 collective-permute-done.35
  440.9 1.5 collective-permute-start.37
  442.3 1.5 multiply_reduce_fusion.3
  443.8 2.7 collective-permute-done.34
  446.5 1.5 multiply_reduce_fusion.2
  449.3 2.9 collective-permute-done.39
  452.1 4.8 collective-permute-done.38
  457.1 1.5 multiply_reduce_fusion.1
  461.9 1.5 collective-permute-start.41
  463.3 2.3 collective-permute-done.41
  465.7 1.3 collective-permute-start.42
  467.0 2.4 collective-permute-done.42
  469.8 4.8 collective-permute-done.43
  475.2 4.6 collective-permute-done.44
  482.3 13.5 %update.1 = (f32[256,6144]{1,0:T(8,128)}, f32[256,6144]{1,0:T(8,128)}, f32[256,6144]{1,0:T(8,128)}) custom-call(f32[1]{0:T(128)} %bitcast.29.factor_ref, f32[256,6144]{1,0:T(8,128)} %w_ref.1, f32[256,6144]{1,0:T(8,128)} %m_ref.1, f32[256,6144]{1,0:T(8,128)} %e_ref.1, bf16[256,512]{1,0:T(8,128)(2,1)} %get-tuple-element.193.refs_0_, ...), custom_call_target="tpu_custom_call" | custom-call | flops 1000000000 | bytes 3400000 | tf_op jit(solution)/shard_map/update/pallas_call | solution.py:556
  496.5 8.9 %all-gather.5.cloned.1.call-done.s_ref = bf16[512,2048]{1,0:T(8,128)(2,1)} async-done(((bf16[128,2048]{1,0:T(8,128)(2,1)}), bf16[512,2048]{1,0:T(8,128)(2,1)}) %all-gather.5.cloned.1.call-update) | async-done | bytes 2097168 | tf_op jit(solution)/shard_map/all_gather | solution.py:967
  505.4 5.8 %input_back.1 = f32[512,2048]{1,0:T(8,128)} custom-call(f32[512,2048]{1,0:T(8,128)} %get-tuple-element.175.dy_ref, bf16[512,2048]{1,0:T(8,128)(2,1)} %x_ref.3, f32[512,1]{1,0:T(8,128)} %copy.22.refs_10_.scale_ref, bf16[512,2048]{1,0:T(8,128)(2,1)} %all-gather.5.cloned.1.call-done.s_ref, f32[1,2048]{1,0:T(1,128)} %bitcast.64), custom_call_target="tpu_custom_call" | custom-call | flops 8000000000 | bytes 27200000 | tf_op jit(solution)/shard_map/input_back/pallas_call | solution.py:974
  (181 shorter events, 27.1 us)
Async XLA Ops:
  8.0 174.9 %all-gather.3.cloned.1.call-start = ((), (), s32[]{:S(2)}) async-start(), calls=%async_computation.3 | async-start | bytes 21233664 | tf_op jit(solution)/shard_map/all_gather | solution.py:692
  9.4 11.6 %copy-start.32 = (s32[1,8]{1,0:T(1,128)S(1)}, s32[1,8]{1,0:T(1,128)}, u32[]{:S(2)}) copy-start(s32[1,8]{1,0:T(1,128)} %param.12) | copy-start | bytes 100
  9.4 11.7 %copy-start.23 = (f32[4352]{0:T(1024)S(1)}, f32[4352]{0:T(1024)}, u32[]{:S(2)}) copy-start(f32[4352]{0:T(1024)} %param.17) | copy-start | bytes 52228
  9.4 12.3 %copy-start = (bf16[512,2048]{1,0:T(8,128)(2,1)S(1)}, bf16[512,2048]{1,0:T(8,128)(2,1)}, u32[]{:S(2)}) copy-start(bf16[512,2048]{1,0:T(8,128)(2,1)} %x_ref.3) | copy-start | bytes 6291460
  9.4 31.1 %collective-permute-start = (bf16[256,1024]{1,0:T(8,128)(2,1)S(1)}, bf16[256,1024]{1,0:T(8,128)(2,1)}, u32[]{:S(2)}, u32[]{:S(2)}) collective-permute-start(bf16[256,1024]{1,0:T(8,128)(2,1)S(1)} %slice.162.refs_0_.refs_11_), channel_id=1, source_target_pairs={{0,4},{4,0},{8,12},{12,8},{16,20},{20,16},{24,28},{28,24},{1,5},{5... | collective-permute-start | bytes 1572872 | tf_op jit(solution)/shard_map/ppermute | solution.py:50
  9.9 21.0 %collective-permute-start.1 = (bf16[256,1024]{1,0:T(8,128)(2,1)S(1)}, bf16[256,1024]{1,0:T(8,128)(2,1)}, u32[]{:S(2)}, u32[]{:S(2)}) collective-permute-start(bf16[256,1024]{1,0:T(8,128)(2,1)S(1)} %slice.162.refs_0_.refs_11_), channel_id=1, source_target_pairs={{0,8},{4,12},{8,0},{12,4},{16,24},{20,28},{24,16},{28,20},{1,9},{5... | collective-permute-start | bytes 1572872 | tf_op jit(solution)/shard_map/ppermute | solution.py:50
  12.5 25.1 %collective-permute-start.3 = (bf16[256,1024]{1,0:T(8,128)(2,1)S(1)}, bf16[256,1024]{1,0:T(8,128)(2,1)}, u32[]{:S(2)}, u32[]{:S(2)}) collective-permute-start(bf16[256,1024]{1,0:T(8,128)(2,1)S(1)} %slice.162.refs_0_.refs_11_), channel_id=1, source_target_pairs={{0,16},{4,20},{8,24},{12,28},{16,0},{20,4},{24,8},{28,12},{1,17},{... | collective-permute-start | bytes 1572872 | tf_op jit(solution)/shard_map/ppermute | solution.py:50
  14.0 24.1 %collective-permute-start.5 = (bf16[256,1024]{1,0:T(8,128)(2,1)S(1)}, bf16[256,1024]{1,0:T(8,128)(2,1)}, u32[]{:S(2)}, u32[]{:S(2)}) collective-permute-start(bf16[256,1024]{1,0:T(8,128)(2,1)S(1)} %slice.162.refs_0_.refs_11_), channel_id=1, source_target_pairs={{0,24},{4,28},{8,16},{12,20},{16,8},{20,12},{24,0},{28,4},{1,25},{... | collective-permute-start | bytes 1572872 | tf_op jit(solution)/shard_map/ppermute | solution.py:50
  18.9 39.5 %copy-start.8 = (bf16[256,512]{1,0:T(8,128)(2,1)}, bf16[256,512]{1,0:T(8,128)(2,1)S(1)}, u32[]{:S(2)}) copy-start(bf16[256,512]{1,0:T(8,128)(2,1)S(1)} %slice.118.refs_0_) | copy-start | bytes 786436
  19.0 33.9 %collective-permute-start.7 = (bf16[256,512]{1,0:T(8,128)(2,1)S(1)}, bf16[256,512]{1,0:T(8,128)(2,1)}, u32[]{:S(2)}, u32[]{:S(2)}) collective-permute-start(bf16[256,512]{1,0:T(8,128)(2,1)S(1)} %slice.118.refs_0_), channel_id=1, source_target_pairs={{0,8},{4,12},{8,0},{12,4},{16,24},{20,28},{24,16},{28,20},{1,9},{5... | collective-permute-start | bytes 786440 | tf_op jit(solution)/shard_map/ppermute | solution.py:50
  30.9 11.3 %collective-permute-start.2 = (bf16[256,1024]{1,0:T(8,128)(2,1)}, bf16[256,1024]{1,0:T(8,128)(2,1)S(1)}, u32[]{:S(2)}, u32[]{:S(2)}) collective-permute-start(bf16[256,1024]{1,0:T(8,128)(2,1)} %collective-permute-done.1.refs_2_.refs_13_), channel_id=1, source_target_pairs={{0,4},{4,0},{8,12},{12,8},{16,20},{20,16},{24,28},{28,24},{1,5},{5... | collective-permute-start | bytes 1572872 | tf_op jit(solution)/shard_map/ppermute | solution.py:50
  37.6 5.8 %collective-permute-start.4 = (bf16[256,1024]{1,0:T(8,128)(2,1)}, bf16[256,1024]{1,0:T(8,128)(2,1)S(1)}, u32[]{:S(2)}, u32[]{:S(2)}) collective-permute-start(bf16[256,1024]{1,0:T(8,128)(2,1)} %collective-permute-done.3.refs_4_.refs_15_), channel_id=1, source_target_pairs={{0,4},{4,0},{8,12},{12,8},{16,20},{20,16},{24,28},{28,24},{1,5},{5... | collective-permute-start | bytes 1572872 | tf_op jit(solution)/shard_map/ppermute | solution.py:50
  38.1 5.3 %collective-permute-start.6 = (bf16[256,1024]{1,0:T(8,128)(2,1)}, bf16[256,1024]{1,0:T(8,128)(2,1)S(1)}, u32[]{:S(2)}, u32[]{:S(2)}) collective-permute-start(bf16[256,1024]{1,0:T(8,128)(2,1)} %collective-permute-done.5.refs_6_.refs_17_), channel_id=1, source_target_pairs={{0,4},{4,0},{8,12},{12,8},{16,20},{20,16},{24,28},{28,24},{1,5},{5... | collective-permute-start | bytes 1572872 | tf_op jit(solution)/shard_map/ppermute | solution.py:50
  40.5 14.4 %collective-permute-start.8 = (bf16[256,512]{1,0:T(8,128)(2,1)S(1)}, bf16[256,512]{1,0:T(8,128)(2,1)}, u32[]{:S(2)}, u32[]{:S(2)}) collective-permute-start(bf16[256,512]{1,0:T(8,128)(2,1)S(1)} %slice.118.refs_0_), channel_id=1, source_target_pairs={{0,16},{4,20},{8,24},{12,28},{16,0},{20,4},{24,8},{28,12},{1,17},{... | collective-permute-start | bytes 786440 | tf_op jit(solution)/shard_map/ppermute | solution.py:50
  42.3 12.6 %collective-permute-start.9 = (bf16[256,512]{1,0:T(8,128)(2,1)S(1)}, bf16[256,512]{1,0:T(8,128)(2,1)}, u32[]{:S(2)}, u32[]{:S(2)}) collective-permute-start(bf16[256,512]{1,0:T(8,128)(2,1)S(1)} %slice.118.refs_0_), channel_id=1, source_target_pairs={{0,24},{4,28},{8,16},{12,20},{16,8},{20,12},{24,0},{28,4},{1,25},{... | collective-permute-start | bytes 786440 | tf_op jit(solution)/shard_map/ppermute | solution.py:50
  44.4 37.4 %copy-start.2 = (bf16[256,6144]{1,0:T(8,128)(2,1)S(1)}, bf16[256,6144]{1,0:T(8,128)(2,1)}, u32[]{:S(2)}) copy-start(bf16[256,6144]{1,0:T(8,128)(2,1)} %copy-done.1) | copy-start | bytes 9437188
  54.9 15.0 %collective-permute-start.15 = (bf16[512,512]{1,0:T(8,128)(2,1)}, bf16[512,512]{1,0:T(8,128)(2,1)S(1)}, u32[]{:S(2)}, u32[]{:S(2)}) collective-permute-start(bf16[512,512]{1,0:T(8,128)(2,1)} %get-tuple-element.106.refs_0_), channel_id=1, source_target_pairs={{0,8},{4,12},{8,0},{12,4},{16,24},{20,28},{24,16},{28,20},{1,9},{5... | collective-permute-start | bytes 1572872 | tf_op jit(solution)/shard_map/ppermute | solution.py:50
  56.4 24.8 %collective-permute-start.17 = (bf16[512,512]{1,0:T(8,128)(2,1)}, bf16[512,512]{1,0:T(8,128)(2,1)}, u32[]{:S(2)}, u32[]{:S(2)}) collective-permute-start(bf16[512,512]{1,0:T(8,128)(2,1)} %get-tuple-element.106.refs_0_), channel_id=1, source_target_pairs={{0,16},{4,20},{8,24},{12,28},{16,0},{20,4},{24,8},{28,12},{1,17},{... | collective-permute-start | bytes 1572872 | tf_op jit(solution)/shard_map/ppermute | solution.py:50
  56.9 24.3 %collective-permute-start.19 = (bf16[512,512]{1,0:T(8,128)(2,1)}, bf16[512,512]{1,0:T(8,128)(2,1)}, u32[]{:S(2)}, u32[]{:S(2)}) collective-permute-start(bf16[512,512]{1,0:T(8,128)(2,1)} %get-tuple-element.106.refs_0_), channel_id=1, source_target_pairs={{0,24},{4,28},{8,16},{12,20},{16,8},{20,12},{24,0},{28,4},{1,25},{... | collective-permute-start | bytes 1572872 | tf_op jit(solution)/shard_map/ppermute | solution.py:50
  58.4 1.9 collective-permute-start.10
  58.4 2.1 collective-permute-start.11
  60.3 9.7 %copy-start.20 = (bf16[256,512]{1,0:T(8,128)(2,1)}, bf16[256,512]{1,0:T(8,128)(2,1)S(1)}, u32[]{:S(2)}) copy-start(bf16[256,512]{1,0:T(8,128)(2,1)S(1)} %collective-permute-done.10.refs_1_) | copy-start | bytes 786436
  60.3 24.3 %collective-permute-start.14 = (bf16[512,512]{1,0:T(8,128)(2,1)}, bf16[512,512]{1,0:T(8,128)(2,1)}, u32[]{:S(2)}, u32[]{:S(2)}) collective-permute-start(bf16[512,512]{1,0:T(8,128)(2,1)} %get-tuple-element.106.refs_0_), channel_id=1, source_target_pairs={{0,4},{4,0},{8,12},{12,8},{16,20},{20,16},{24,28},{28,24},{1,5},{5... | collective-permute-start | bytes 1572872 | tf_op jit(solution)/shard_map/ppermute | solution.py:50
  60.5 21.2 %collective-permute-start.12 = (bf16[256,512]{1,0:T(8,128)(2,1)}, bf16[256,512]{1,0:T(8,128)(2,1)S(1)}, u32[]{:S(2)}, u32[]{:S(2)}) collective-permute-start(bf16[256,512]{1,0:T(8,128)(2,1)} %collective-permute-done.8.refs_4_), channel_id=1, source_target_pairs={{0,4},{4,0},{8,12},{12,8},{16,20},{20,16},{24,28},{28,24},{1,5},{5... | collective-permute-start | bytes 786440 | tf_op jit(solution)/shard_map/ppermute | solution.py:50
  70.0 13.4 %copy-start.12 = (bf16[512,512]{1,0:T(8,128)(2,1)}, bf16[512,512]{1,0:T(8,128)(2,1)S(1)}, u32[]{:S(2)}) copy-start(bf16[512,512]{1,0:T(8,128)(2,1)S(1)} %collective-permute-done.15.refs_2_) | copy-start | bytes 1572868
  70.0 14.6 %collective-permute-start.16 = (bf16[512,512]{1,0:T(8,128)(2,1)S(1)}, bf16[512,512]{1,0:T(8,128)(2,1)}, u32[]{:S(2)}, u32[]{:S(2)}) collective-permute-start(bf16[512,512]{1,0:T(8,128)(2,1)S(1)} %collective-permute-done.15.refs_2_), channel_id=1, source_target_pairs={{0,4},{4,0},{8,12},{12,8},{16,20},{20,16},{24,28},{28,24},{1,5},{5... | collective-permute-start | bytes 1572872 | tf_op jit(solution)/shard_map/ppermute | solution.py:50
  81.2 3.4 collective-permute-start.18
  81.2 3.4 collective-permute-start.20
  81.7 2.9 collective-permute-start.13
  84.6 107.4 %all-reduce.4.cloned.1.call-start = ((), (), s32[]{:S(2)}) async-start(), calls=%async_computation.2 | async-start | bytes 4194304 | tf_op jit(solution)/shard_map/psum | solution.py:738
  101.6 203.2 %all-reduce.6.cloned.1.call-start = ((), (), s32[]{:S(2)}) async-start(), calls=%async_computation.4 | async-start | bytes 4194304 | tf_op jit(solution)/shard_map/psum | solution.py:794
  219.5 141.1 %reduce-scatter.3.cloned.1.call-start = ((), (), s32[]{:S(2)}) async-start(), calls=%async_computation.5 | async-start | bytes 21233664 | tf_op jit(solution)/shard_map/reduce_scatter | solution.py:817
  235.1 157.5 %all-reduce.8.cloned.1.call-start = ((), (), s32[]{:S(2)}) async-start(), calls=%async_computation.6 | async-start | bytes 4194304 | tf_op jit(solution)/shard_map/psum | solution.py:819
  304.8 155.0 %reduce-scatter.5.cloned.1.call-start = ((), (), s32[]{:S(2)}) async-start(), calls=%async_computation.7 | async-start | bytes 2621440 | tf_op jit(solution)/shard_map/reduce_scatter | solution.py:950
  330.4 13.4 %collective-permute-start.21 = (bf16[512,512]{1,0:T(8,128)(2,1)}, bf16[512,512]{1,0:T(8,128)(2,1)S(1)}, u32[]{:S(2)}, u32[]{:S(2)}) collective-permute-start(bf16[512,512]{1,0:T(8,128)(2,1)} %get-tuple-element.139), channel_id=1, source_target_pairs={{0,4},{4,0},{8,12},{12,8},{16,20},{20,16},{24,28},{28,24},{1,5},{5... | collective-permute-start | bytes 1572872 | tf_op jit(solution)/shard_map/ppermute | solution.py:50
  330.5 14.2 %collective-permute-start.22 = (bf16[512,512]{1,0:T(8,128)(2,1)}, bf16[512,512]{1,0:T(8,128)(2,1)S(1)}, u32[]{:S(2)}, u32[]{:S(2)}) collective-permute-start(bf16[512,512]{1,0:T(8,128)(2,1)} %get-tuple-element.141), channel_id=1, source_target_pairs={{0,4},{4,0},{8,12},{12,8},{16,20},{20,16},{24,28},{28,24},{1,5},{5... | collective-permute-start | bytes 1572872 | tf_op jit(solution)/shard_map/ppermute | solution.py:50
  331.8 13.0 %collective-permute-start.23 = (bf16[512,512]{1,0:T(8,128)(2,1)}, bf16[512,512]{1,0:T(8,128)(2,1)S(1)}, u32[]{:S(2)}, u32[]{:S(2)}) collective-permute-start(bf16[512,512]{1,0:T(8,128)(2,1)} %get-tuple-element.143), channel_id=1, source_target_pairs={{0,4},{4,0},{8,12},{12,8},{16,20},{20,16},{24,28},{28,24},{1,5},{5... | collective-permute-start | bytes 1572872 | tf_op jit(solution)/shard_map/ppermute | solution.py:50
  331.9 13.1 %collective-permute-start.24 = (bf16[512,512]{1,0:T(8,128)(2,1)}, bf16[512,512]{1,0:T(8,128)(2,1)S(1)}, u32[]{:S(2)}, u32[]{:S(2)}) collective-permute-start(bf16[512,512]{1,0:T(8,128)(2,1)} %get-tuple-element.145), channel_id=1, source_target_pairs={{0,4},{4,0},{8,12},{12,8},{16,20},{20,16},{24,28},{28,24},{1,5},{5... | collective-permute-start | bytes 1572872 | tf_op jit(solution)/shard_map/ppermute | solution.py:50
  360.6 33.9 %collective-permute-start.25 = (bf16[512,512]{1,0:T(8,128)(2,1)S(1)}, bf16[512,512]{1,0:T(8,128)(2,1)S(1)}, u32[]{:S(2)}, u32[]{:S(2)}) collective-permute-start(bf16[512,512]{1,0:T(8,128)(2,1)S(1)} %add_convert_fusion.4), channel_id=1, source_target_pairs={{0,8},{4,12},{8,0},{12,4},{16,24},{20,28},{24,16},{28,20},{1,9},{5... | collective-permute-start | bytes 1572872 | tf_op jit(solution)/shard_map/ppermute | solution.py:50
  362.0 32.5 %collective-permute-start.26 = (bf16[512,512]{1,0:T(8,128)(2,1)S(1)}, bf16[512,512]{1,0:T(8,128)(2,1)S(1)}, u32[]{:S(2)}, u32[]{:S(2)}) collective-permute-start(bf16[512,512]{1,0:T(8,128)(2,1)S(1)} %add_convert_fusion.3), channel_id=1, source_target_pairs={{0,16},{4,20},{8,24},{12,28},{16,0},{20,4},{24,8},{28,12},{1,17},{... | collective-permute-start | bytes 1572872 | tf_op jit(solution)/shard_map/ppermute | solution.py:50
  362.6 31.9 %collective-permute-start.27 = (bf16[512,512]{1,0:T(8,128)(2,1)S(1)}, bf16[512,512]{1,0:T(8,128)(2,1)S(1)}, u32[]{:S(2)}, u32[]{:S(2)}) collective-permute-start(bf16[512,512]{1,0:T(8,128)(2,1)S(1)} %add_convert_fusion.2), channel_id=1, source_target_pairs={{0,24},{4,28},{8,16},{12,20},{16,8},{20,12},{24,0},{28,4},{1,25},{... | collective-permute-start | bytes 1572872 | tf_op jit(solution)/shard_map/ppermute | solution.py:50
  404.7 100.8 %all-gather.5.cloned.1.call-start = ((), (), s32[]{:S(2)}) async-start(), calls=%async_computation.8 | async-start | bytes 2621440 | tf_op jit(solution)/shard_map/all_gather | solution.py:967
  405.0 12.8 %collective-permute-start.28 = (bf16[4,256,512]{2,1,0:T(8,128)(2,1)}, bf16[4,256,512]{2,1,0:T(8,128)(2,1)}, u32[]{:S(2)}, u32[]{:S(2)}) collective-permute-start(bf16[4,256,512]{2,1,0:T(8,128)(2,1)} %bitcast.7), channel_id=1, source_target_pairs={{0,4},{4,0},{8,12},{12,8},{16,20},{20,16},{24,28},{28,24},{1,5},{5... | collective-permute-start | bytes 3145736 | tf_op jit(solution)/shard_map/ppermute | solution.py:50
  409.4 13.6 %collective-permute-start.32 = (bf16[4,256,512]{2,1,0:T(8,128)(2,1)}, bf16[4,256,512]{2,1,0:T(8,128)(2,1)S(1)}, u32[]{:S(2)}, u32[]{:S(2)}) collective-permute-start(bf16[4,256,512]{2,1,0:T(8,128)(2,1)} %bitcast.70), channel_id=1, source_target_pairs={{0,4},{4,0},{8,12},{12,8},{16,20},{20,16},{24,28},{28,24},{1,5},{5... | collective-permute-start | bytes 3145736 | tf_op jit(solution)/shard_map/ppermute | solution.py:50
  411.5 14.3 %collective-permute-start.36 = (bf16[4,256,512]{2,1,0:T(8,128)(2,1)}, bf16[4,256,512]{2,1,0:T(8,128)(2,1)S(1)}, u32[]{:S(2)}, u32[]{:S(2)}) collective-permute-start(bf16[4,256,512]{2,1,0:T(8,128)(2,1)} %get-tuple-element.168), channel_id=1, source_target_pairs={{0,4},{4,0},{8,12},{12,8},{16,20},{20,16},{24,28},{28,24},{1,5},{5... | collective-permute-start | bytes 3145736 | tf_op jit(solution)/shard_map/ppermute | solution.py:50
  419.4 10.1 %collective-permute-start.31 = (bf16[256,512]{1,0:T(8,128)(2,1)S(1)}, bf16[256,512]{1,0:T(8,128)(2,1)S(1)}, u32[]{:S(2)}, u32[]{:S(2)}) collective-permute-start(bf16[256,512]{1,0:T(8,128)(2,1)S(1)} %get-tuple-element.203), channel_id=1, source_target_pairs={{0,24},{4,28},{8,16},{12,20},{16,8},{20,12},{24,0},{28,4},{1,25},{... | collective-permute-start | bytes 786440 | tf_op jit(solution)/shard_map/ppermute | solution.py:50
  421.9 13.4 %collective-permute-start.30 = (bf16[256,512]{1,0:T(8,128)(2,1)S(1)}, bf16[256,512]{1,0:T(8,128)(2,1)S(1)}, u32[]{:S(2)}, u32[]{:S(2)}) collective-permute-start(bf16[256,512]{1,0:T(8,128)(2,1)S(1)} %get-tuple-element.204), channel_id=1, source_target_pairs={{0,16},{4,20},{8,24},{12,28},{16,0},{20,4},{24,8},{28,12},{1,17},{... | collective-permute-start | bytes 786440 | tf_op jit(solution)/shard_map/ppermute | solution.py:50
  422.4 15.2 %collective-permute-start.29 = (bf16[256,512]{1,0:T(8,128)(2,1)S(1)}, bf16[256,512]{1,0:T(8,128)(2,1)S(1)}, u32[]{:S(2)}, u32[]{:S(2)}) collective-permute-start(bf16[256,512]{1,0:T(8,128)(2,1)S(1)} %get-tuple-element.202), channel_id=1, source_target_pairs={{0,8},{4,12},{8,0},{12,4},{16,24},{20,28},{24,16},{28,20},{1,9},{5... | collective-permute-start | bytes 786440 | tf_op jit(solution)/shard_map/ppermute | solution.py:50
  423.3 17.5 %collective-permute-start.35 = (bf16[256,512]{1,0:T(8,128)(2,1)S(1)}, bf16[256,512]{1,0:T(8,128)(2,1)S(1)}, u32[]{:S(2)}, u32[]{:S(2)}) collective-permute-start(bf16[256,512]{1,0:T(8,128)(2,1)S(1)} %get-tuple-element.200), channel_id=1, source_target_pairs={{0,24},{4,28},{8,16},{12,20},{16,8},{20,12},{24,0},{28,4},{1,25},{... | collective-permute-start | bytes 786440 | tf_op jit(solution)/shard_map/ppermute | solution.py:50
  425.8 20.7 %collective-permute-start.34 = (bf16[256,512]{1,0:T(8,128)(2,1)S(1)}, bf16[256,512]{1,0:T(8,128)(2,1)S(1)}, u32[]{:S(2)}, u32[]{:S(2)}) collective-permute-start(bf16[256,512]{1,0:T(8,128)(2,1)S(1)} %get-tuple-element.201), channel_id=1, source_target_pairs={{0,16},{4,20},{8,24},{12,28},{16,0},{20,4},{24,8},{28,12},{1,17},{... | collective-permute-start | bytes 786440 | tf_op jit(solution)/shard_map/ppermute | solution.py:50
  429.6 16.9 %collective-permute-start.33 = (bf16[256,512]{1,0:T(8,128)(2,1)S(1)}, bf16[256,512]{1,0:T(8,128)(2,1)S(1)}, u32[]{:S(2)}, u32[]{:S(2)}) collective-permute-start(bf16[256,512]{1,0:T(8,128)(2,1)S(1)} %get-tuple-element.199), channel_id=1, source_target_pairs={{0,8},{4,12},{8,0},{12,4},{16,24},{20,28},{24,16},{28,20},{1,9},{5... | collective-permute-start | bytes 786440 | tf_op jit(solution)/shard_map/ppermute | solution.py:50
  435.2 16.9 %collective-permute-start.39 = (bf16[256,512]{1,0:T(8,128)(2,1)S(1)}, bf16[256,512]{1,0:T(8,128)(2,1)S(1)}, u32[]{:S(2)}, u32[]{:S(2)}) collective-permute-start(bf16[256,512]{1,0:T(8,128)(2,1)S(1)} %get-tuple-element.197), channel_id=1, source_target_pairs={{0,24},{4,28},{8,16},{12,20},{16,8},{20,12},{24,0},{28,4},{1,25},{... | collective-permute-start | bytes 786440 | tf_op jit(solution)/shard_map/ppermute | solution.py:50
  437.6 19.3 %collective-permute-start.38 = (bf16[256,512]{1,0:T(8,128)(2,1)S(1)}, bf16[256,512]{1,0:T(8,128)(2,1)S(1)}, u32[]{:S(2)}, u32[]{:S(2)}) collective-permute-start(bf16[256,512]{1,0:T(8,128)(2,1)S(1)} %get-tuple-element.198), channel_id=1, source_target_pairs={{0,16},{4,20},{8,24},{12,28},{16,0},{20,4},{24,8},{28,12},{1,17},{... | collective-permute-start | bytes 786440 | tf_op jit(solution)/shard_map/ppermute | solution.py:50
  440.8 19.0 %copy-start.29 = (f32[8,128]{1,0:T(8,128)S(1)}, f32[8,128]{1,0:T(8,128)}, u32[]{:S(2)}) copy-start(f32[8,128]{1,0:T(8,128)} %get-tuple-element.180) | copy-start | bytes 12292
  440.9 19.1 %copy-start.28 = (f32[1,2048]{1,0:T(1,128)S(1)}, f32[1,2048]{1,0:T(1,128)}, u32[]{:S(2)}) copy-start(f32[1,2048]{1,0:T(1,128)} %get-tuple-element.178) | copy-start | bytes 24580
  440.9 19.1 %copy-start.27 = (f32[1,2048]{1,0:T(1,128)S(1)}, f32[1,2048]{1,0:T(1,128)}, u32[]{:S(2)}) copy-start(f32[1,2048]{1,0:T(1,128)} %get-tuple-element.179) | copy-start | bytes 24580
  440.9 16.2 %collective-permute-start.37 = (bf16[256,512]{1,0:T(8,128)(2,1)S(1)}, bf16[256,512]{1,0:T(8,128)(2,1)S(1)}, u32[]{:S(2)}, u32[]{:S(2)}) collective-permute-start(bf16[256,512]{1,0:T(8,128)(2,1)S(1)} %get-tuple-element.196), channel_id=1, source_target_pairs={{0,8},{4,12},{8,0},{12,4},{16,24},{20,28},{24,16},{28,20},{1,9},{5... | collective-permute-start | bytes 786440 | tf_op jit(solution)/shard_map/ppermute | solution.py:50
  460.7 1.2 collective-permute-start.40
  461.9 3.8 collective-permute-start.41
  465.7 3.8 collective-permute-start.42
  469.5 5.2 collective-permute-start.43
  474.6 5.2 collective-permute-start.44
  482.3 13.6 %copy-start.25 = (f32[4352]{0:T(1024)S(1)}, f32[4352]{0:T(1024)}, u32[]{:S(2)}) copy-start(f32[4352]{0:T(1024)} %param.19) | copy-start | bytes 52228
  482.3 13.6 %copy-start.26 = (f32[4352]{0:T(1024)S(1)}, f32[4352]{0:T(1024)}, u32[]{:S(2)}) copy-start(f32[4352]{0:T(1024)} %param.18) | copy-start | bytes 52228
  (21 other events, 68.5 us)
Sparse Core Ops, SparseCore 0:
  84.7 98.0 all-gather.2
  235.2 125.3 reduce-scatter.2
Sparse Core Ops, SparseCore 1:
  101.7 90.2 all-reduce.3
  219.6 85.2 all-reduce.5
  307.6 85.0 all-reduce.7
  404.7 42.5 reduce-scatter.4
  460.0 45.4 all-gather.4
